TPU v7x, 32 devices: a whole 2x2x4 slice. The times are simulated.
32 devices in a mesh: dp: 8 (over z, x), seq: 4 (over y, core).
Axes of the slice: x: 2, y: 2, z: 4, core: 2. Of those that a mesh axis runs over, the one named last changes fastest.
Arguments:
- words: bfloat16 [32, 1024, 1024], P('dp', 'seq'), may hold values from -6 to 6
- patches: bfloat16 [32, 2048, 1024], P('dp', 'seq'), may hold values from -6 to 6
- proj: bfloat16 [1024, 1024], P('dp'), may hold values from -0.1875 to 0.1875
- routes: int32 [32, 1024, 1], P('dp', 'seq'), may hold values from 0 to 3; in each aligned block of 256 rows (0 to 255, 256 to 511, ..., all dimensions but the last counted through in order) at most 128 rows name the same one
- targets: int32 [32, 1024], P('dp', 'seq'), may hold values from 0 to 511
- counts: int32 [32], P('dp'), may hold values from 512 to 1024
- flags: int32 [32, 16, 32], P('dp'), may hold values 0 or 1
Outputs:
- word_loss: float32 [32, 1024], P('dp', 'seq')
- proj_grad: float32 [1024, 1024], P('dp', 'seq')
Inputs may be any that keep to these rules, and one draw needn't show every extreme that they name: `routes`: among the 256 words of one page held by one index of seq, at most 128 name the same shard; some block reaches 128.
All inputs are finite; a program needn't handle non-finite values. No bound on the sum of `flags` on one device may be relied on, other than what follows from the above.
Results may differ from a plain program's by a relative error of at most 0.0065.
Values may be sent and summed in bfloat16 or wider, within the bound.
No kernel may reach another device: no remote copies, remote signals or barrier semaphores. Data moves between devices by JAX's collectives and lax.ppermute only.
A program may use at most 64 MiB of HBM per device.

v0:
```python
import math

import jax
import jax.numpy as jnp
from jax import lax
from jax.sharding import PartitionSpec as P

MARGIN_BLOCK_SIZE = 64


def local(words, patches, proj, routes, targets, counts, flags):
    pages, wdev, width = words.shape
    ppsz = patches.shape[1]
    nblk = flags.shape[1]
    nseq = lax.axis_size("seq")
    mine = lax.axis_index("seq")
    capacity_limit = 2 * wdev // nseq
    bps = ppsz // MARGIN_BLOCK_SIZE
    scale = 2.0 / math.sqrt(width)
    flat_rows = words.reshape(pages * wdev, width)
    columns = flat_rows
    query = jnp.dot(
        columns, lax.all_gather(proj, "dp", axis=0, tiled=True), preferred_element_type=jnp.float32
    )
    query = query.astype(jnp.bfloat16).reshape(pages, wdev, width)
    destination_slot = routes[:, :, 0]
    onehot = (
        destination_slot[:, :, None] == jnp.arange(nseq, dtype=jnp.int32)[None, None, :]
    ).astype(jnp.int32)
    rank = jnp.cumsum(onehot, axis=1) - onehot
    slot = jnp.sum(rank * onehot, axis=2)
    slot_hit = (
        slot[:, :, None] == jnp.arange(capacity_limit, dtype=jnp.int32)[None, None, :]
    ).astype(jnp.int32)
    dispatch = onehot[:, :, :, None] * slot_hit[:, :, None, :]
    dispatch_bf = dispatch.astype(jnp.bfloat16)
    word_idx = mine * wdev + jnp.arange(wdev, dtype=jnp.int32)
    q_buf = jnp.einsum(
        "pwhc,pwd->hpcd", dispatch_bf, query, preferred_element_type=jnp.float32
    ).astype(jnp.bfloat16)
    tgt_buf = jnp.einsum("pwhc,pw->hpc", dispatch, targets)
    idx_buf = jnp.einsum("pwhc,w->hpc", dispatch, word_idx + 1) - 1
    q_in, tgt_in, idx_in = (
        lax.all_to_all(q_buf, "seq", split_axis=0, concat_axis=0, tiled=True),
        lax.all_to_all(tgt_buf, "seq", split_axis=0, concat_axis=0, tiled=True),
        lax.all_to_all(idx_buf, "seq", split_axis=0, concat_axis=0, tiled=True),
    )
    scores = jnp.einsum("hpcd,pkd->hpck", q_in, patches, preferred_element_type=jnp.float32) * scale
    own = lax.dynamic_slice_in_dim(flags, mine * bps, bps, 2)
    word_block = jnp.maximum(idx_in, 0) // MARGIN_BLOCK_SIZE
    picked = (word_block[..., None] == jnp.arange(nblk, dtype=jnp.int32)).astype(jnp.int32)
    hit = jnp.sum(picked[..., None] * own[None, :, None, :, :], axis=-2)
    allowed = (hit > 0) | (
        (tgt_in // MARGIN_BLOCK_SIZE)[..., None] == jnp.arange(bps, dtype=jnp.int32)
    )
    mask = jnp.broadcast_to(allowed[..., None], allowed.shape + (MARGIN_BLOCK_SIZE,)).reshape(
        scores.shape
    )
    expo = jnp.where(mask, jnp.exp(scores), jnp.float32(0.0))
    total = jnp.sum(expo, axis=-1)
    is_target = jnp.arange(ppsz, dtype=jnp.int32) == tgt_in[..., None]
    target_score = jnp.sum(jnp.where(is_target, scores, jnp.float32(0.0)), axis=-1)
    valid_mask = (idx_in >= 0) & (idx_in < counts[None, :, None])
    loss_out = jnp.where(valid_mask, jnp.log(total) - target_score, jnp.float32(0.0))
    coef = jnp.where(
        valid_mask, jnp.float32(64.0) / counts.astype(jnp.float32)[None, :, None], jnp.float32(0.0)
    )
    dscore = (coef[..., None] * (expo / total[..., None] - is_target.astype(jnp.float32))).astype(
        jnp.bfloat16
    )
    dquery = (
        jnp.einsum("hpck,pkd->hpcd", dscore, patches, preferred_element_type=jnp.float32) * scale
    ).astype(jnp.bfloat16)
    loss_home = lax.all_to_all(loss_out, "seq", split_axis=0, concat_axis=0, tiled=True)
    dq_home = lax.all_to_all(dquery, "seq", split_axis=0, concat_axis=0, tiled=True)
    right = (
        jnp.einsum("pwhc,hpcd->pwd", dispatch_bf, dq_home, preferred_element_type=jnp.float32)
        .astype(jnp.bfloat16)
        .reshape(-1, width)
    )
    word_loss = jnp.einsum("pwhc,hpc->pw", dispatch.astype(jnp.float32), loss_home)
    columns = flat_rows
    partial_rows = lax.psum_scatter(
        jnp.einsum("rc,rd->cd", columns, right, preferred_element_type=jnp.float32),
        "dp",
        scatter_dimension=0,
        tiled=True,
    )
    proj_grad = lax.psum_scatter(partial_rows, "seq", scatter_dimension=1, tiled=True)
    return (word_loss, proj_grad)


def solution(mesh):
    in_specs = (
        P("dp", "seq", None),
        P("dp", "seq", None),
        P("dp", None),
        P("dp", "seq", None),
        P("dp", "seq"),
        P("dp"),
        P("dp", None, None),
    )
    out_specs = (P("dp", "seq"), P("dp", "seq"))
    return jax.shard_map(local, mesh=mesh, in_specs=in_specs, out_specs=out_specs, check_vma=False)
```

profile of v0, /device:TPU:0, one launch (start us, length us, event | category | flops | bytes accessed | tf_op | source)
XLA Modules:
  0.0 325.5 jit_solution(17133190436435363246)
XLA Ops:
  7.2 0.0 copy-start
  7.2 0.0 all-gather.2.cloned.1.call-start
  7.2 0.7 all-gather.2.cloned.1.call-update
  7.9 0.7 copy.102
  8.6 0.7 compare_convert_fusion
  9.3 4.8 %reduce-window.6 = s32[4,4,2,128]{3,2,1,0:T(2,128)S(1)} reduce-window(s32[4,4,2,128]{3,2,1,0:T(2,128)S(1)} %compare_convert_fusion, s32[]{:T(128)} %constant.40.clone.1), window={size=1x1x1x128 pad=0_0x0_0x0_0x127_0}, to_apply=%region_0.0 | reduce-window | flops 520192 | bytes 32772 | tf_op jit(solution)/shard_map/reduce-window
  14.1 0.1 slice.8
  14.2 0.1 copy.44
  14.4 0.1 copy.45
  14.5 0.1 broadcast_add_fusion
  14.6 0.2 fusion.39
  14.8 2.9 fusion
  17.7 0.6 copy.101
  18.3 4.2 %all-to-all-start.1 = ((s32[4,4,128]{2,1,0:T(4,128)}), s32[4,4,128]{2,1,0:T(4,128)S(1)}, u32[]{:S(2)}, u32[]{:S(2)}) async-start(s32[4,4,128]{2,1,0:T(4,128)} %bitcast.76), calls=%async_computation.1 | async-start | bytes 16384 | tf_op jit(solution)/shard_map/all_to_all | solution.py:45
  22.6 2.6 fusion.2
  25.1 0.6 fusion.46
  25.7 36.6 %all-gather.2.cloned.1.call-done = bf16[1024,1024]{1,0:T(8,128)(2,1)} async-done(((bf16[128,1024]{1,0:T(8,128)(2,1)}), bf16[1024,1024]{1,0:T(8,128)(2,1)}) %all-gather.2.cloned.1.call-update) | async-done | bytes 2097168 | tf_op jit(solution)/shard_map/all_gather | solution.py:23
  62.3 0.0 copy-done
  62.3 5.3 %convolution_convert_fusion = bf16[1024,1024]{1,0:T(8,128)(2,1)} fusion(bf16[1024,1024]{1,0:T(8,128)(2,1)S(1)} %bitcast.79, bf16[1024,1024]{1,0:T(8,128)(2,1)} %all-gather.2.cloned.1.call-done), kind=kOutput, calls=%fused_computation.31 | convolution fusion | flops 2148532224 | bytes 6291456 | tf_op jit(solution)/shard_map/dot_general | solution.py:22
  67.6 0.0 all-to-all-done.1
  67.6 3.2 all-to-all-start
  70.9 5.2 %convert_bitcast_fusion = bf16[4,4,128,1024]{2,3,0,1:T(8,128)(2,1)} fusion(bf16[4,256,1024,1]{2,1,3,0:T(8,128)(2,1)} %bitcast.80, s32[4,256,128]{2,1,0:T(8,128)S(1)} %fusion.39, s32[4,256,4]{1,2,0:T(4,128)S(1)} %fusion.44), kind=kOutput, calls=%fused_computation.22 | convolution fusion | flops 1076887552 | bytes 6832128 | tf_op jit(solution)/shard_map/pwhc,pwd->hpcd/dot_general | solution.py:38
  76.1 6.3 %copy.56 = bf16[4,4,128,1024]{3,2,1,0:T(8,128)(2,1)} copy(bf16[4,4,128,1024]{2,3,0,1:T(8,128)(2,1)} %convert_bitcast_fusion) | data formatting | bytes 8388608 | tf_op jit(solution)/shard_map/convert_element_type | solution.py:40
  82.4 0.0 all-to-all-done
  82.4 5.0 %all-to-all-start.2 = ((bf16[4,4,128,1024]{3,2,1,0:T(8,128)(2,1)}), bf16[4,4,128,1024]{3,2,1,0:T(8,128)(2,1)}, u32[]{:S(2)}, u32[]{:S(2)}) async-start(bf16[4,4,128,1024]{3,2,1,0:T(8,128)(2,1)} %copy.56), calls=%async_computation.2 | async-start | bytes 8388608 | tf_op jit(solution)/shard_map/all_to_all | solution.py:44
  87.4 0.2 reduce-scatter.3.cloned.1.call-start
  87.7 0.0 copy-done.2
  87.7 0.1 constant_dynamic-slice_fusion
  87.8 0.0 copy-done.3
  87.9 0.1 multiply_reduce_fusion
  88.0 0.3 broadcast_in_dim.15
  88.3 2.3 copy.58
  90.6 0.1 broadcast_select_fusion
  90.7 45.0 %all-to-all-done.2 = bf16[4,4,128,1024]{3,2,1,0:T(8,128)(2,1)} async-done(((bf16[4,4,128,1024]{3,2,1,0:T(8,128)(2,1)}), bf16[4,4,128,1024]{3,2,1,0:T(8,128)(2,1)}, u32[]{:S(2)}, u32[]{:S(2)}) %all-to-all-start.2) | async-done | bytes 4194336 | tf_op jit(solution)/shard_map/all_to_all | solution.py:44
  135.7 7.2 %fusion.14 = (f32[4,4,128]{2,0,1:T(4,128)S(1)}, f32[4,4,128]{2,0,1:T(4,128)S(1)}, f32[4,4,128,512]{3,2,1,0:T(8,128)S(1)}) fusion(pred[4,4,128,512]{3,2,0,1:T(32,128)(4,1)} %copy.58, s32[4,4,128]{2,0,1:T(4,128)S(1)} %get-tuple-element.14, bf16[4,512,1024]{2,1,0:T(8,128)(2,1)} %param.8, bf16[4,4,128,1024]{3,2,1,0:T(8,128)(2,1)} %all-to-all-done.2), kind=kOutput, calls=%fused_computation.23 | convolution fusion | flops 2153771008 | bytes 13656064 | tf_op jit(solution)/shard_map/hpcd,pkd->hpck/dot_general | solution.py:48
  142.9 4.2 %fusion.4 = bf16[4,4,128,1024]{3,2,0,1:T(8,128)(2,1)S(1)} fusion(bf16[4,512,1024]{2,1,0:T(8,128)(2,1)S(1)} %copy-done.4, pred[4,4,128,512]{3,2,0,1:T(32,128)(4,1)S(1)} %copy-done.1, f32[4,4,128,512]{3,2,1,0:T(8,128)S(1)} %get-tuple-element.16, f32[4,4,128]{2,0,1:T(4,128)S(1)} %get-tuple-element.10, f32[4,4,128]{2,0,1:T(4,128)S(1)} %get-tuple-element.12, ...), kind=kOutput, calls=%fused_computation.7 | convolution fusion | flops 2160066560 | bytes 13656064 | tf_op jit(solution)/shard_map/hpck,pkd->hpcd/dot_general | solution.py:72
  147.2 0.6 copy.61
  147.8 51.6 %all_to_all.25 = bf16[4,4,128,1024]{3,2,1,0:T(8,128)(2,1)} all-to-all(bf16[4,4,128,1024]{3,2,1,0:T(8,128)(2,1)S(1)} %copy.61), channel_id=1, replica_groups=mesh['dp'=8,'seq'=4] {'seq'}, dimensions={0} | all-to-all | bytes 8388608 | tf_op jit(solution)/shard_map/all_to_all | solution.py:75
  199.3 7.6 %convolution_bitcast_fusion = f32[1024,1024]{0,1:T(8,128)} fusion(bf16[4,256,1024]{2,1,0:T(8,128)(2,1)S(1)} %copy-done, bf16[4,4,128,1024]{3,2,1,0:T(8,128)(2,1)} %all_to_all.25, s32[4,256,128]{2,1,0:T(8,128)S(1)} %fusion.39, s32[4,256,4]{1,2,0:T(4,128)S(1)} %fusion.44), kind=kOutput, calls=%fused_computation.24 | convolution fusion | flops 3223322624 | bytes 11026432 | tf_op jit(solution)/shard_map/rc,rd->cd/dot_general | solution.py:84
  207.0 0.0 reduce-scatter.3.cloned.1.call-update
  207.0 0.0 reduce-scatter.5.cloned.1.call-start
  207.0 86.2 %reduce-scatter.3.cloned.1.call-done = f32[128,1024]{0,1:T(8,128)} async-done(((f32[1024,1024]{0,1:T(8,128)}), f32[128,1024]{0,1:T(8,128)}) %reduce-scatter.3.cloned.1.call-update) | async-done | bytes 524304 | tf_op jit(solution)/shard_map/reduce_scatter | solution.py:83
  293.2 0.0 reduce-scatter.5.cloned.1.call-update
  293.3 6.3 %all_to_all.26 = bf16[4,4,128]{2,1,0:T(4,128)(2,1)S(1)} all-to-all(bf16[4,4,128]{2,1,0:T(4,128)(2,1)S(1)} %copy.60), channel_id=1, replica_groups=mesh['dp'=8,'seq'=4] {'seq'}, dimensions={0} | all-to-all | bytes 8192 | tf_op jit(solution)/shard_map/all_to_all | solution.py:74
  299.6 0.9 fusion.17
  300.5 0.6 copy.103
  301.1 16.2 %reduce-scatter.5.cloned.1.call-done = f32[128,256]{0,1:T(8,128)} async-done(((f32[128,1024]{0,1:T(8,128)}), f32[128,256]{0,1:T(8,128)}) %reduce-scatter.5.cloned.1.call-update) | async-done | bytes 131088 | tf_op jit(solution)/shard_map/reduce_scatter | solution.py:89
  317.3 1.7 copy.64
  (21 shorter events, 0.2 us)
Async XLA Ops:
  7.2 55.2 %copy-start = (bf16[4,256,1024]{2,1,0:T(8,128)(2,1)S(1)}, bf16[4,256,1024]{2,1,0:T(8,128)(2,1)}, u32[]{:S(2)}) copy-start(bf16[4,256,1024]{2,1,0:T(8,128)(2,1)} %param.7) | copy-start | bytes 6291460
  7.2 55.2 %all-gather.2.cloned.1.call-start = ((), (), s32[]{:S(2)}) async-start(), calls=%async_computation.7 | async-start | bytes 2359296 | tf_op jit(solution)/shard_map/all_gather | solution.py:23
  18.3 49.3 %all-to-all-start.1 = ((s32[4,4,128]{2,1,0:T(4,128)}), s32[4,4,128]{2,1,0:T(4,128)S(1)}, u32[]{:S(2)}, u32[]{:S(2)}) async-start(s32[4,4,128]{2,1,0:T(4,128)} %bitcast.76), calls=%async_computation.1 | async-start | bytes 16384 | tf_op jit(solution)/shard_map/all_to_all | solution.py:45
  67.6 14.8 %all-to-all-start = ((s32[4,4,128]{2,1,0:T(4,128)}), s32[4,4,128]{2,1,0:T(4,128)S(1)}, u32[]{:S(2)}, u32[]{:S(2)}) async-start(s32[4,4,128]{2,1,0:T(4,128)} %fusion.46), calls=%async_computation | async-start | bytes 16384 | tf_op jit(solution)/shard_map/all_to_all | solution.py:46
  82.4 5.2 %copy-start.2 = (s32[4,16,32]{2,1,0:T(8,128)S(1)}, s32[4,16,32]{2,1,0:T(8,128)}, u32[]{:S(2)}) copy-start(s32[4,16,32]{2,1,0:T(8,128)} %param.13) | copy-start | bytes 24580
  82.4 5.3 %copy-start.3 = (s32[4]{0:T(128)S(1)}, s32[4]{0:T(128)}, u32[]{:S(2)}) copy-start(s32[4]{0:T(128)} %param.12) | copy-start | bytes 52
  82.4 53.2 %all-to-all-start.2 = ((bf16[4,4,128,1024]{3,2,1,0:T(8,128)(2,1)}), bf16[4,4,128,1024]{3,2,1,0:T(8,128)(2,1)}, u32[]{:S(2)}, u32[]{:S(2)}) async-start(bf16[4,4,128,1024]{3,2,1,0:T(8,128)(2,1)} %copy.56), calls=%async_computation.2 | async-start | bytes 8388608 | tf_op jit(solution)/shard_map/all_to_all | solution.py:44
  87.4 205.8 %reduce-scatter.3.cloned.1.call-start = ((), (), s32[]{:S(2)}) async-start(), calls=%async_computation.8 | async-start | bytes 4718592 | tf_op jit(solution)/shard_map/reduce_scatter | solution.py:83
  135.7 7.3 %copy-start.1 = (pred[4,4,128,512]{3,2,0,1:T(32,128)(4,1)S(1)}, pred[4,4,128,512]{3,2,0,1:T(32,128)(4,1)}, u32[]{:S(2)}) copy-start(pred[4,4,128,512]{3,2,0,1:T(32,128)(4,1)} %copy.58) | copy-start | bytes 3145732
  135.7 7.3 %copy-start.4 = (bf16[4,512,1024]{2,1,0:T(8,128)(2,1)S(1)}, bf16[4,512,1024]{2,1,0:T(8,128)(2,1)}, u32[]{:S(2)}) copy-start(bf16[4,512,1024]{2,1,0:T(8,128)(2,1)} %param.8) | copy-start | bytes 12582916
  207.0 110.3 %reduce-scatter.5.cloned.1.call-start = ((), (), s32[]{:S(2)}) async-start(), calls=%async_computation.9 | async-start | bytes 655360 | tf_op jit(solution)/shard_map/reduce_scatter | solution.py:89
Sparse Core Ops, SparseCore 0:
  10.1 52.1 all-gather.1
  207.1 86.0 reduce-scatter.2
  295.8 21.4 reduce-scatter.4
where the time goes:
time: 326 us
  waiting for transfers between devices  185 us (57%)
  blocking collectives  57.9 us (18%)
  matrix products  35.9 us (11%)
  between operations  13.9 us (4%)
  local copies, waits for them, and re-layouts  13.5 us (4%)
  starting transfers between devices  12.8 us (4%)
  other arithmetic  6.74 us (2%)
    reduce_scatter x1, waiting for transfers between devices, local(): lax.psum_scatter(jnp.einsum('rc,rd->cd', columns, right, preferred_elemen...  86.2 us
    all_to_all x1, blocking collectives, local(): lax.all_to_all(dquery, 'seq', split_axis=0, concat_axis=0, tiled=True)  51.6 us
    all_to_all x1, waiting for transfers between devices, local(): lax.all_to_all(q_buf, 'seq', split_axis=0, concat_axis=0, tiled=True)  45 us
    all_gather x1, waiting for transfers between devices, local(): lax.all_gather(proj, 'dp', axis=0, tiled=True)  36.6 us
    reduce_scatter x1, waiting for transfers between devices, local(): lax.psum_scatter(partial_rows, 'seq', scatter_dimension=1, tiled=True)  16.2 us
    dot_general x1, matrix products, local(): jnp.einsum('rc,rd->cd', columns, right, preferred_element_type=jnp.float32)  7.62 us
    dot_general x1, matrix products, local(): jnp.einsum('hpcd,pkd->hpck', q_in, patches, preferred_element_type=jnp.fl...  7.24 us
  transfers between devices with their start and end apart: 6, of which 4 were waited for; matrix products, arithmetic and copies ran while one was open for 11% of the time, Pallas kernels for 0%

commit v1 on v0

v1 whole, which is shorter than its diff:
```python
import functools
import math

import jax
import jax.numpy as jnp
from jax import lax
from jax.experimental import pallas as pl
from jax.experimental.pallas import tpu as pltpu
from jax.sharding import PartitionSpec as P

MARGIN_BLOCK_SIZE = 64
VMEM_LIMIT = 48 * 1024 * 1024


def page_kernel(n_homes, n_proj, cap, first, scale, info, *refs):
    refs = list(refs)
    meta, fexp, patches = refs[:3]
    words = refs[3 : 3 + n_homes]
    gathered = refs[3 + n_homes : 3 + n_homes + n_proj]
    rest = refs[3 + n_homes + n_proj :]
    acc_in = None
    if not first:
        acc_in, rest = rest[0], rest[1:]
    acc, loss, proj, rows_x, rows_dq, sems = rest
    page = pl.program_id(0)
    me, my_dp, core = info[0], info[1], info[2]
    wdev = meta.shape[-1]
    pps = patches.shape[-2]
    nblk = fexp.shape[-2]
    n_cols, _, wcol = acc.shape
    half = proj.shape[-1]

    def proj_copies():
        copies = []
        for g, ref in enumerate(gathered):
            other_core, low = g // 2, g % 2
            for hi in range(ref.shape[0]):
                shard = jnp.bitwise_xor(my_dp, hi * 2 + low)
                rows = ref.shape[1]
                copies.append(
                    pltpu.make_async_copy(
                        ref.at[hi],
                        proj.at[
                            jnp.bitwise_xor(core, other_core),
                            pl.ds(pl.multiple_of(shard * rows, rows), rows),
                        ],
                        sems.at[len(copies)],
                    )
                )
        return copies

    @pl.when(page == 0)
    def _():
        for copy in proj_copies():
            copy.start()
        if first:
            acc[...] = jnp.zeros_like(acc)
        else:
            acc[...] = acc_in[...]

    m = (meta[0, 0] == me).astype(jnp.float32)
    before = lax.broadcasted_iota(jnp.int32, (wdev, wdev), 0) < lax.broadcasted_iota(
        jnp.int32, (wdev, wdev), 1
    )
    rank = jnp.dot(
        m.astype(jnp.bfloat16), before.astype(jnp.bfloat16), preferred_element_type=jnp.float32
    )
    rank = jnp.where(m > 0, rank, -1.0)
    slots = lax.broadcasted_iota(jnp.int32, (cap, wdev), 0).astype(jnp.float32)
    here = lax.broadcasted_iota(jnp.int32, (cap, wdev), 1)
    picks, t_rows, i_rows = [], [], []
    for r in range(n_homes):
        pick = (slots == rank[r : r + 1, :]).astype(jnp.float32)
        rows_x[pl.ds(r * cap, cap), :] = jnp.dot(
            pick.astype(jnp.bfloat16),
            words[r][...].reshape(wdev, -1),
            preferred_element_type=jnp.float32,
        ).astype(jnp.bfloat16)
        target = meta[0, 1][r : r + 1, :].astype(jnp.float32)
        place = (here + info[4 + r] * wdev + 1).astype(jnp.float32)
        t_rows.append(jnp.sum(pick * target, axis=1, keepdims=True))
        i_rows.append(jnp.sum(pick * place, axis=1, keepdims=True))
        picks.append(pick)
    t = jnp.concatenate(t_rows, axis=0).astype(jnp.int32)
    idx = jnp.concatenate(i_rows, axis=0).astype(jnp.int32) - 1
    n_rows = n_homes * cap

    @pl.when(page == 0)
    def _():
        for copy in proj_copies():
            copy.wait()

    x = rows_x[...]
    pat = patches[...].reshape(pps, -1)
    scores = jnp.zeros((n_rows, pps), jnp.float32)
    for h in range(2):
        q = jnp.dot(x, proj[h], preferred_element_type=jnp.float32).astype(jnp.bfloat16)
        scores = scores + lax.dot_general(
            q,
            pat[:, h * half : (h + 1) * half],
            (((1,), (1,)), ((), ())),
            preferred_element_type=jnp.float32,
        )
    scores = scores * scale
    blocks = lax.broadcasted_iota(jnp.int32, (n_rows, nblk), 1)
    word_block = (jnp.maximum(idx, 0) // MARGIN_BLOCK_SIZE == blocks).astype(jnp.bfloat16)
    hit = jnp.dot(word_block, fexp[0], preferred_element_type=jnp.float32)
    k = lax.broadcasted_iota(jnp.int32, (n_rows, pps), 1)
    allowed = (hit > 0.5) | (k // MARGIN_BLOCK_SIZE == t // MARGIN_BLOCK_SIZE)
    is_target = k == t
    top = jnp.max(jnp.where(allowed, scores, -jnp.inf), axis=1, keepdims=True)
    expo = jnp.where(allowed, jnp.exp(scores - top), 0.0)
    total = jnp.sum(expo, axis=1, keepdims=True)
    target_score = jnp.sum(jnp.where(is_target, scores, 0.0), axis=1, keepdims=True)
    count = info[4 + n_homes + page]
    valid = (idx >= 0) & (idx < count)
    row_loss = jnp.where(valid, top + jnp.log(total) - target_score, 0.0)
    coef = jnp.where(valid, 64.0 / count.astype(jnp.float32), 0.0)
    dscore = (coef * (expo * (1.0 / total) - is_target.astype(jnp.float32))).astype(jnp.bfloat16)
    for r in range(n_homes):
        loss[0, r : r + 1, :] = jnp.sum(
            picks[r] * row_loss[r * cap : (r + 1) * cap], axis=0, keepdims=True
        )
    rows_dq[...] = (
        jnp.dot(dscore, pat, preferred_element_type=jnp.float32) * scale
    ).astype(jnp.bfloat16)
    for j in range(n_cols):
        acc[j] += lax.dot_general(
            x,
            rows_dq[:, j * wcol : (j + 1) * wcol],
            (((0,), (0,)), ((), ())),
            preferred_element_type=jnp.float32,
        )


def run_pages(info, meta, fexp, patches, words, gathered, acc, cap, n_cols, first_page, n_pages):
    n_homes = len(words)
    wdev, width = words[0].shape[-2:]
    pps = patches.shape[1]
    nblk = fexp.shape[1]
    wcol = width // n_cols
    rows = n_homes * cap
    first = acc is None
    n_copies = sum(g.shape[0] for g in gathered)
    take = lambda p, info: (p + first_page, 0, 0)
    any_space = pl.BlockSpec(memory_space=pl.ANY)
    in_specs = [
        pl.BlockSpec((1,) + meta.shape[1:], lambda p, info: (p + first_page, 0, 0, 0)),
        pl.BlockSpec((1, nblk, pps), take),
        pl.BlockSpec((1, pps, width), take),
    ]
    for w in words:
        if w.shape[0] == 1:
            in_specs.append(pl.BlockSpec((1, wdev, width), lambda p, info: (0, 0, 0)))
        else:
            in_specs.append(pl.BlockSpec((1, wdev, width), take))
    in_specs += [any_space] * len(gathered)
    whole = pl.BlockSpec((n_cols, width, wcol), lambda p, info: (0, 0, 0))
    operands = [info, meta, fexp, patches, *words, *gathered]
    aliases = {}
    if not first:
        in_specs.append(whole)
        operands.append(acc)
        aliases = {len(operands) - 1: 0}
    flops = 2 * n_pages * rows * width * (2 * width + 2 * pps + wdev)
    bytes_accessed = n_pages * (n_homes * wdev + pps) * width * 2 + 2 * width * width + 8 * width * width
    return pl.pallas_call(
        functools.partial(
            page_kernel, n_homes, len(gathered), cap, first, 2.0 / math.sqrt(width)
        ),
        grid_spec=pltpu.PrefetchScalarGridSpec(
            num_scalar_prefetch=1,
            grid=(n_pages,),
            in_specs=in_specs,
            out_specs=[
                whole,
                pl.BlockSpec((1, n_homes, wdev), lambda p, info: (p, 0, 0)),
            ],
            scratch_shapes=[
                pltpu.VMEM((2, width, width // 2), jnp.bfloat16),
                pltpu.VMEM((rows, width), jnp.bfloat16),
                pltpu.VMEM((rows, width), jnp.bfloat16),
                pltpu.SemaphoreType.DMA((n_copies,)),
            ],
        ),
        out_shape=[
            jax.ShapeDtypeStruct((n_cols, width, wcol), jnp.float32),
            jax.ShapeDtypeStruct((n_pages, n_homes, wdev), jnp.float32),
        ],
        input_output_aliases=aliases,
        compiler_params=pltpu.CompilerParams(vmem_limit_bytes=VMEM_LIMIT),
        cost_estimate=pl.CostEstimate(
            flops=flops, bytes_accessed=bytes_accessed, transcendentals=n_pages * rows * pps
        ),
    )(*operands)


def exchange(x, axis, offset):
    n = lax.axis_size(axis)
    return lax.ppermute(x, axis, [(i, i ^ offset) for i in range(n)])


def local(words, patches, proj, routes, targets, counts, flags):
    pages, wdev, width = words.shape
    pps = patches.shape[1]
    n_seq = lax.axis_size("seq")
    n_dp = lax.axis_size("dp")
    me = lax.axis_index("seq")
    my_dp = lax.axis_index("dp")
    core = me % 2
    n_y = n_seq // 2
    cap = 2 * wdev // n_seq
    bps = pps // MARGIN_BLOCK_SIZE
    half = width // 2
    shard_rows = proj.shape[0]

    far = [[exchange(words[p : p + 1], "seq", 2 * k) for k in range(1, n_y)] for p in range(pages)]
    near = exchange(words, "seq", 1)

    mine = lax.dynamic_slice_in_dim(proj, core * half, half, 1)
    low0 = [mine] + [exchange(mine, "dp", 2 * k) for k in range(1, n_dp // 2)]
    low1 = [exchange(piece, "dp", 1) for piece in low0]
    low0, low1 = jnp.stack(low0), jnp.stack(low1)
    gathered = [low0, low1, exchange(low0, "seq", 1), exchange(low1, "seq", 1)]

    pair = jnp.stack([routes[:, :, 0], targets], axis=1)
    metas = jnp.stack([pair] + [exchange(pair, "seq", r) for r in range(1, n_seq)], axis=2)
    pad = lambda a: jnp.pad(a, ((0, 0), (0, 0), (0, -a.shape[2] % 8), (0, 0)), constant_values=-1)
    homes = jnp.bitwise_xor(me, jnp.arange(n_seq, dtype=jnp.int32))
    own = lax.dynamic_slice_in_dim(flags, me * bps, bps, 2)
    fexp = jnp.repeat(own, MARGIN_BLOCK_SIZE, axis=2).astype(jnp.bfloat16)
    base = jnp.stack([me, my_dp, core, jnp.zeros_like(me)]).astype(jnp.int32)

    info = jnp.concatenate([base, homes[:2], counts])
    acc, loss_near = run_pages(
        info, pad(metas[:, :, :2]), fexp, patches, [words, near], gathered, None, cap, n_seq, 0, pages
    )
    far_meta = pad(metas[:, :, 2:])
    losses = []
    for p in range(pages):
        blocks = []
        for block in far[p]:
            blocks += [block, exchange(block, "seq", 1)]
        info = jnp.concatenate([base, homes[2:], counts[p : p + 1]])
        acc, loss = run_pages(
            info, far_meta, fexp, patches, blocks, gathered, acc, cap, n_seq, p, 1
        )
        losses.append(loss)
    loss_far = jnp.concatenate(losses, axis=0)

    acc = acc.reshape(n_y, 2, width, width // n_seq)
    pick = lambda a, i, axis: lax.dynamic_index_in_dim(a, i, axis, keepdims=False)
    part = pick(acc, core, 1) + exchange(pick(acc, 1 - core, 1).astype(jnp.bfloat16), "seq", 1)
    y = me // 2
    total = pick(part, y, 0)
    for k in range(1, n_y):
        total = total + exchange(pick(part, jnp.bitwise_xor(y, k), 0).astype(jnp.bfloat16), "seq", 2 * k)
    total = total.reshape(n_dp, shard_rows, width // n_seq)
    grad = pick(total, my_dp, 0)
    for k in range(1, n_dp):
        grad = grad + exchange(pick(total, jnp.bitwise_xor(my_dp, k), 0).astype(jnp.bfloat16), "dp", k)

    word_loss = loss_near[:, 0] + exchange(loss_near[:, 1], "seq", 1)
    for r in range(2, n_seq):
        word_loss = word_loss + exchange(loss_far[:, r - 2], "seq", r)
    return (word_loss, grad)


def solution(mesh):
    in_specs = (
        P("dp", "seq", None),
        P("dp", "seq", None),
        P("dp", None),
        P("dp", "seq", None),
        P("dp", "seq"),
        P("dp"),
        P("dp", None, None),
    )
    out_specs = (P("dp", "seq"), P("dp", "seq"))
    return jax.shard_map(local, mesh=mesh, in_specs=in_specs, out_specs=out_specs, check_vma=False)
```

time: 326 us -> 169 us (0.52)
  waiting for transfers between devices: 185 us -> 51.9 us
  Pallas kernels: 0 us -> 63.9 us
  blocking collectives: 57.9 us -> 0 us
  matrix products: 35.9 us -> 0 us
  starting transfers between devices: 12.8 us -> 34.2 us
  between operations: 13.9 us -> 0.91 us
    reduce_scatter x2 -> x0, waiting for transfers between devices: 102 us -> none  [the longest x1 86.2 us: local(): lax.psum_scatter(jnp.einsum('rc,rd->cd', columns, right, preferred_elemen...]
    pallas_call x0 -> x5, Pallas kernels: none -> 63.9 us  [run_pages(): pl.pallas_call(functools.partial(page_kernel, n_homes, len(gathered), cap...]
    all_to_all x2 -> x0, blocking collectives: 57.9 us -> none  [the longest x1 51.6 us: local(): lax.all_to_all(dquery, 'seq', split_axis=0, concat_axis=0, tiled=True)]
    ppermute x0 -> x33, waiting for transfers between devices: none -> 51.9 us  [exchange(): return lax.ppermute(x, axis, [(i, i ^ offset) for i in range(n)])]
    all_to_all x3 -> x0, waiting for transfers between devices: 45 us -> none  [the longest x1 45 us: local(): lax.all_to_all(q_buf, 'seq', split_axis=0, concat_axis=0, tiled=True)]
    all_gather x1 -> x0, waiting for transfers between devices: 36.6 us -> none  [local(): lax.all_gather(proj, 'dp', axis=0, tiled=True)]
    dot_general x8 -> x0, matrix products: 35.9 us -> none  [the longest x1 7.62 us: local(): jnp.einsum('rc,rd->cd', columns, right, preferred_element_type=jnp.float32)]
    ppermute x0 -> x33, starting transfers between devices: none -> 34.2 us  [exchange(): return lax.ppermute(x, axis, [(i, i ^ offset) for i in range(n)])]
  transfers between devices with their start and end apart: 6 -> 33, of which waited for: 4 -> 10; matrix products, arithmetic and copies ran while one was open for 11% -> 7% of each run, Pallas kernels for 0% -> 31%
where the time goes in v1:
time: 169 us; the launch traced here: 168 us
  Pallas kernels  63.9 us (38%)
  waiting for transfers between devices  51.9 us (31%)
  starting transfers between devices  34.2 us (20%)
  local copies, waits for them, and re-layouts  11.4 us (7%)
  other arithmetic  6.2 us (4%)
    pallas_call x5, Pallas kernels, run_pages(): pl.pallas_call(functools.partial(page_kernel, n_homes, len(gathered), cap...  63.9 us
    ppermute x33, waiting for transfers between devices, exchange(): return lax.ppermute(x, axis, [(i, i ^ offset) for i in range(n)])  51.9 us
    ppermute x33, starting transfers between devices, exchange(): return lax.ppermute(x, axis, [(i, i ^ offset) for i in range(n)])  34.2 us
  transfers between devices with their start and end apart: 33, of which 10 were waited for; matrix products, arithmetic and copies ran while one was open for 7% of the time, Pallas kernels for 31%

profile of v1, /device:TPU:0, one launch (start us, length us, event | category | flops | bytes accessed | tf_op | source)
XLA Modules:
  0.0 168.5 jit_solution(14138810536162561872)
XLA Ops:
  1.6 3.1 %collective-permute-start.2 = (bf16[128,512]{1,0:T(8,128)(2,1)S(1)}, bf16[128,512]{1,0:T(8,128)(2,1)S(1)}, u32[]{:S(2)}, u32[]{:S(2)}) collective-permute-start(bf16[128,512]{1,0:T(8,128)(2,1)S(1)} %constant_dynamic-slice_fusion), channel_id=1, source_target_pairs={{0,8},{4,12},{8,0},{12,4},{16,24},{20,28},{24,16},{28,20},{1,9},{5... | collective-permute-start | bytes 393224 | tf_op jit(solution)/shard_map/ppermute | solution.py:200
  4.7 2.6 %collective-permute-start.3 = (bf16[128,512]{1,0:T(8,128)(2,1)S(1)}, bf16[128,512]{1,0:T(8,128)(2,1)}, u32[]{:S(2)}, u32[]{:S(2)}) collective-permute-start(bf16[128,512]{1,0:T(8,128)(2,1)S(1)} %constant_dynamic-slice_fusion), channel_id=1, source_target_pairs={{0,16},{4,20},{8,24},{12,28},{16,0},{20,4},{24,8},{28,12},{1,17},{... | collective-permute-start | bytes 393224 | tf_op jit(solution)/shard_map/ppermute | solution.py:200
  7.3 0.7 stack.66
  8.0 0.7 fusion.18
  8.8 2.7 %fusion.19 = (bf16[1,256,1024]{2,1,0:T(8,128)(2,1)}, bf16[1,256,1024]{2,1,0:T(8,128)(2,1)S(1)}, bf16[1,256,1024]{2,1,0:T(8,128)(2,1)S(1)}, bf16[1,256,1024]{2,1,0:T(8,128)(2,1)}) fusion(bf16[4,256,1024]{2,1,0:T(8,128)(2,1)} %refs_3_.1), kind=kLoop, calls=%fused_computation.47 | loop fusion | bytes 4194304 | tf_op jit(solution)/shard_map/slice | solution.py:217
  11.5 1.7 %collective-permute-start.5 = (bf16[128,512]{1,0:T(8,128)(2,1)S(1)}, bf16[128,512]{1,0:T(8,128)(2,1)S(1)}, u32[]{:S(2)}, u32[]{:S(2)}) collective-permute-start(bf16[128,512]{1,0:T(8,128)(2,1)S(1)} %constant_dynamic-slice_fusion), channel_id=1, source_target_pairs={{0,4},{4,0},{8,12},{12,8},{16,20},{20,16},{24,28},{28,24},{1,5},{5... | collective-permute-start | bytes 393224 | tf_op jit(solution)/shard_map/ppermute | solution.py:200
  13.2 1.5 collective-permute-start.14
  14.7 3.0 %collective-permute-done.3 = bf16[128,512]{1,0:T(8,128)(2,1)} collective-permute-done((bf16[128,512]{1,0:T(8,128)(2,1)S(1)}, bf16[128,512]{1,0:T(8,128)(2,1)}, u32[]{:S(2)}, u32[]{:S(2)}) %collective-permute-start.3) | collective-permute-done | bytes 131104 | tf_op jit(solution)/shard_map/ppermute | solution.py:200
  17.7 1.5 collective-permute-start.16
  19.2 1.5 collective-permute-start.6
  20.9 0.6 collective-permute-start.7
  21.5 3.1 %collective-permute-done.6 = bf16[128,512]{1,0:T(8,128)(2,1)S(1)} collective-permute-done((bf16[128,512]{1,0:T(8,128)(2,1)S(1)}, bf16[128,512]{1,0:T(8,128)(2,1)S(1)}, u32[]{:S(2)}, u32[]{:S(2)}) %collective-permute-start.6) | collective-permute-done | bytes 131104 | tf_op jit(solution)/shard_map/ppermute | solution.py:200
  24.5 1.5 collective-permute-start.8
  26.3 1.0 pad_maximum_fusion.refs_5_
  27.3 1.6 collective-permute-start.12
  28.9 0.7 collective-permute-done.8
  29.6 1.2 pad_maximum_fusion.1.refs_6_
  30.8 8.0 %collective-permute-done.12 = s32[4,2,256]{2,1,0:T(2,128)S(1)} collective-permute-done((s32[4,2,256]{2,1,0:T(2,128)S(1)}, s32[4,2,256]{2,1,0:T(2,128)S(1)}, u32[]{:S(2)}, u32[]{:S(2)}) %collective-permute-start.12) | collective-permute-done | bytes 8224 | tf_op jit(solution)/shard_map/ppermute | solution.py:200
  38.7 1.5 collective-permute-start.18
  41.4 0.7 fusion.21
  42.1 0.7 concatenate.26.info
  42.8 0.8 concatenate.27.info
  43.6 0.8 concatenate.28.info
  44.3 0.7 concatenate.29.info
  45.2 8.7 %collective-permute-done.18.refs_3_ = bf16[1,256,1024]{2,1,0:T(8,128)(2,1)} collective-permute-done((bf16[1,256,1024]{2,1,0:T(8,128)(2,1)}, bf16[1,256,1024]{2,1,0:T(8,128)(2,1)}, u32[]{:S(2)}, u32[]{:S(2)}) %collective-permute-start.18) | collective-permute-done | bytes 524320 | tf_op jit(solution)/shard_map/ppermute | solution.py:200
  53.9 9.5 %collective-permute-done.20.refs_3_ = bf16[1,256,1024]{2,1,0:T(8,128)(2,1)} collective-permute-done((bf16[1,256,1024]{2,1,0:T(8,128)(2,1)}, bf16[1,256,1024]{2,1,0:T(8,128)(2,1)}, u32[]{:S(2)}, u32[]{:S(2)}) %collective-permute-start.20) | collective-permute-done | bytes 524320 | tf_op jit(solution)/shard_map/ppermute | solution.py:200
  64.0 1.6 copy-done.1
  65.6 19.1 %shard_map.86 = (f32[4,1024,256]{2,1,0:T(8,128)}, f32[4,2,256]{2,1,0:T(2,128)S(1)}) custom-call(s32[10]{0:T(128)S(1)} %concatenate.25.info, s32[4,2,8,256]{3,2,1,0:T(8,128)S(1)} %pad.7.clone.refs_0_, bf16[4,16,512]{2,1,0:T(8,128)(2,1)S(1)} %convert_element_type.87.refs_1_, bf16[4,512,1024]{2,1,0:T(8,128)(2,1)} %refs_2_.9, ...), custom_call_target="tpu_custom_call" | custom-call | flops 6979321856 | bytes 18874368 | tf_op jit(solution)/shard_map/pallas_call | solution.py:167
  84.7 11.1 %shard_map.87 = (f32[4,1024,256]{2,1,0:T(8,128)}, f32[1,2,256]{2,1,0:T(2,128)S(1)}) custom-call(s32[7]{0:T(128)S(1)} %concatenate.26.info, s32[4,2,8,256]{3,2,1,0:T(8,128)S(1)} %pad.8.refs_0_, bf16[4,16,512]{2,1,0:T(8,128)(2,1)S(1)} %convert_element_type.87.refs_1_, bf16[4,512,1024]{2,1,0:T(8,128)(2,1)} %refs_2_.9, ...), custom_call_target="tpu_custom_call", output_to_operand_aliasing={{0}: (10, {})} | custom-call | flops 1744830464 | bytes 12582912 | tf_op jit(solution)/shard_map/pallas_call | solution.py:167
  95.8 11.1 %shard_map.88 = (f32[4,1024,256]{2,1,0:T(8,128)}, f32[1,2,256]{2,1,0:T(2,128)S(1)}) custom-call(s32[7]{0:T(128)S(1)} %concatenate.27.info, s32[4,2,8,256]{3,2,1,0:T(8,128)S(1)} %pad.8.refs_0_, bf16[4,16,512]{2,1,0:T(8,128)(2,1)S(1)} %convert_element_type.87.refs_1_, bf16[4,512,1024]{2,1,0:T(8,128)(2,1)} %refs_2_.9, ...), custom_call_target="tpu_custom_call", output_to_operand_aliasing={{0}: (10, {})} | custom-call | flops 1744830464 | bytes 12582912 | tf_op jit(solution)/shard_map/pallas_call | solution.py:167
  106.9 11.2 %shard_map.89 = (f32[4,1024,256]{2,1,0:T(8,128)}, f32[1,2,256]{2,1,0:T(2,128)S(1)}) custom-call(s32[7]{0:T(128)S(1)} %concatenate.28.info, s32[4,2,8,256]{3,2,1,0:T(8,128)S(1)} %pad.8.refs_0_, bf16[4,16,512]{2,1,0:T(8,128)(2,1)S(1)} %convert_element_type.87.refs_1_, bf16[4,512,1024]{2,1,0:T(8,128)(2,1)} %refs_2_.9, ...), custom_call_target="tpu_custom_call", output_to_operand_aliasing={{0}: (10, {})} | custom-call | flops 1744830464 | bytes 12582912 | tf_op jit(solution)/shard_map/pallas_call | solution.py:167
  118.1 11.4 %shard_map.90 = (f32[4,1024,256]{2,1,0:T(8,128)}, f32[1,2,256]{2,1,0:T(2,128)S(1)}) custom-call(s32[7]{0:T(128)S(1)} %concatenate.29.info, s32[4,2,8,256]{3,2,1,0:T(8,128)S(1)} %pad.8.refs_0_, bf16[4,16,512]{2,1,0:T(8,128)(2,1)S(1)} %convert_element_type.87.refs_1_, bf16[4,512,1024]{2,1,0:T(8,128)(2,1)} %refs_2_.9, ...), custom_call_target="tpu_custom_call", output_to_operand_aliasing={{0}: (10, {})} | custom-call | flops 1744830464 | bytes 12582912 | tf_op jit(solution)/shard_map/pallas_call | solution.py:167
  129.6 1.7 %fusion = bf16[2,1024,256]{2,1,0:T(8,128)(2,1)S(1)} fusion(f32[2,2,1024,256]{3,2,1,0:T(8,128)} %bitcast.73, s32[]{:T(128)S(6)} %select_n.60), kind=kLoop, calls=%fused_computation.2 | loop fusion | bytes 2097156 | tf_op jit(solution)/shard_map/convert_element_type | solution.py:253
  131.8 2.3 %collective-permute-done.24 = bf16[2,1024,256]{2,1,0:T(8,128)(2,1)S(1)} collective-permute-done((bf16[2,1024,256]{2,1,0:T(8,128)(2,1)S(1)}, bf16[2,1024,256]{2,1,0:T(8,128)(2,1)S(1)}, u32[]{:S(2)}, u32[]{:S(2)}) %collective-permute-start.24) | collective-permute-done | bytes 1048608 | tf_op jit(solution)/shard_map/ppermute | solution.py:200
  134.1 1.8 %bitcast_add_fusion = f32[2,1024,256]{2,1,0:T(8,128)S(1)} fusion(bf16[2,1024,256]{2,1,0:T(8,128)(2,1)S(1)} %collective-permute-done.24, f32[2,2,1024,256]{3,2,1,0:T(8,128)} %bitcast.74, s32[]{:T(128)S(6)} %select_n.59), kind=kLoop, calls=%fused_computation | loop fusion | flops 1048576 | bytes 5242884 | tf_op jit(solution)/shard_map/add | solution.py:253
  136.0 1.6 collective-permute-start.25
  138.2 0.9 collective-permute-start.23
  139.1 11.2 %collective-permute-done.25 = bf16[1024,256]{1,0:T(8,128)(2,1)S(1)} collective-permute-done((bf16[1024,256]{1,0:T(8,128)(2,1)S(1)}, bf16[1024,256]{1,0:T(8,128)(2,1)S(1)}, u32[]{:S(2)}, u32[]{:S(2)}) %collective-permute-start.25) | collective-permute-done | bytes 524320 | tf_op jit(solution)/shard_map/ppermute | solution.py:200
  151.0 0.8 collective-permute-start.27
  151.8 2.3 %collective-permute-start.28 = (bf16[128,256]{1,0:T(8,128)(2,1)S(1)}, bf16[128,256]{1,0:T(8,128)(2,1)S(1)}, u32[]{:S(2)}, u32[]{:S(2)}) collective-permute-start(bf16[128,256]{1,0:T(8,128)(2,1)S(1)} %get-tuple-element.31), channel_id=1, source_target_pairs={{0,12},{4,8},{8,4},{12,0},{16,28},{20,24},{24,20},{28,16},{1,13},{... | collective-permute-start | bytes 196616 | tf_op jit(solution)/shard_map/ppermute | solution.py:200
  154.1 2.2 %collective-permute-start.29 = (bf16[128,256]{1,0:T(8,128)(2,1)S(1)}, bf16[128,256]{1,0:T(8,128)(2,1)S(1)}, u32[]{:S(2)}, u32[]{:S(2)}) collective-permute-start(bf16[128,256]{1,0:T(8,128)(2,1)S(1)} %get-tuple-element.30), channel_id=1, source_target_pairs={{0,16},{4,20},{8,24},{12,28},{16,0},{20,4},{24,8},{28,12},{1,17},{... | collective-permute-start | bytes 196616 | tf_op jit(solution)/shard_map/ppermute | solution.py:200
  156.3 1.1 collective-permute-start.30
  157.4 3.3 %collective-permute-start.31 = (bf16[128,256]{1,0:T(8,128)(2,1)S(1)}, bf16[128,256]{1,0:T(8,128)(2,1)S(1)}, u32[]{:S(2)}, u32[]{:S(2)}) collective-permute-start(bf16[128,256]{1,0:T(8,128)(2,1)S(1)} %get-tuple-element.28), channel_id=1, source_target_pairs={{0,24},{4,28},{8,16},{12,20},{16,8},{20,12},{24,0},{28,4},{1,25},{... | collective-permute-start | bytes 196616 | tf_op jit(solution)/shard_map/ppermute | solution.py:200
  160.7 1.2 collective-permute-start.32
  161.8 0.6 fusion.17
  162.4 4.2 %collective-permute-done.30 = bf16[128,256]{1,0:T(8,128)(2,1)S(1)} collective-permute-done((bf16[128,256]{1,0:T(8,128)(2,1)S(1)}, bf16[128,256]{1,0:T(8,128)(2,1)S(1)}, u32[]{:S(2)}, u32[]{:S(2)}) %collective-permute-start.30) | collective-permute-done | bytes 65568 | tf_op jit(solution)/shard_map/ppermute | solution.py:200
  166.6 1.1 collective-permute-done.32
  167.7 0.7 fusion.7
  (76 shorter events, 5.1 us)
Async XLA Ops:
  0.6 1.0 copy-start
  0.6 63.4 %collective-permute-start.1 = (bf16[4,256,1024]{2,1,0:T(8,128)(2,1)}, bf16[4,256,1024]{2,1,0:T(8,128)(2,1)}, u32[]{:S(2)}, u32[]{:S(2)}) collective-permute-start(bf16[4,256,1024]{2,1,0:T(8,128)(2,1)} %refs_3_.1), channel_id=1, source_target_pairs={{0,1},{1,0},{2,3},{3,2},{4,5},{5,4},{6,7},{7,6},{8,9},{9,8},{10,11... | collective-permute-start | bytes 6291464 | tf_op jit(solution)/shard_map/ppermute | solution.py:200
  1.6 11.6 %collective-permute-start.2 = (bf16[128,512]{1,0:T(8,128)(2,1)S(1)}, bf16[128,512]{1,0:T(8,128)(2,1)S(1)}, u32[]{:S(2)}, u32[]{:S(2)}) collective-permute-start(bf16[128,512]{1,0:T(8,128)(2,1)S(1)} %constant_dynamic-slice_fusion), channel_id=1, source_target_pairs={{0,8},{4,12},{8,0},{12,4},{16,24},{20,28},{24,16},{28,20},{1,9},{5... | collective-permute-start | bytes 393224 | tf_op jit(solution)/shard_map/ppermute | solution.py:200
  4.7 13.0 %collective-permute-start.3 = (bf16[128,512]{1,0:T(8,128)(2,1)S(1)}, bf16[128,512]{1,0:T(8,128)(2,1)}, u32[]{:S(2)}, u32[]{:S(2)}) collective-permute-start(bf16[128,512]{1,0:T(8,128)(2,1)S(1)} %constant_dynamic-slice_fusion), channel_id=1, source_target_pairs={{0,16},{4,20},{8,24},{12,28},{16,0},{20,4},{24,8},{28,12},{1,17},{... | collective-permute-start | bytes 393224 | tf_op jit(solution)/shard_map/ppermute | solution.py:200
  7.3 12.0 %collective-permute-start.4 = (bf16[128,512]{1,0:T(8,128)(2,1)S(1)}, bf16[128,512]{1,0:T(8,128)(2,1)S(1)}, u32[]{:S(2)}, u32[]{:S(2)}) collective-permute-start(bf16[128,512]{1,0:T(8,128)(2,1)S(1)} %constant_dynamic-slice_fusion), channel_id=1, source_target_pairs={{0,24},{4,28},{8,16},{12,20},{16,8},{20,12},{24,0},{28,4},{1,25},{... | collective-permute-start | bytes 393224 | tf_op jit(solution)/shard_map/ppermute | solution.py:200
  8.7 12.1 %copy-start.4 = (s32[4,16,32]{2,1,0:T(8,128)S(1)}, s32[4,16,32]{2,1,0:T(8,128)}, u32[]{:S(2)}) copy-start(s32[4,16,32]{2,1,0:T(8,128)} %param.13) | copy-start | bytes 24580
  8.7 2.8 %collective-permute-start = (s32[4,2,256]{2,1,0:T(2,128)S(1)}, s32[4,2,256]{2,1,0:T(2,128)S(1)}, u32[]{:S(2)}, u32[]{:S(2)}) collective-permute-start(s32[4,2,256]{2,1,0:T(2,128)S(1)} %get-tuple-element.36), channel_id=1, source_target_pairs={{0,1},{1,0},{2,3},{3,2},{4,5},{5,4},{6,7},{7,6},{8,9},{9,8},{10,11... | collective-permute-start | bytes 24584 | tf_op jit(solution)/shard_map/ppermute | solution.py:200
  11.5 29.9 %copy-start.5 = (s32[4]{0:T(128)S(1)}, s32[4]{0:T(128)}, u32[]{:S(2)}) copy-start(s32[4]{0:T(128)} %param.12) | copy-start | bytes 52
  11.5 9.4 %collective-permute-start.5 = (bf16[128,512]{1,0:T(8,128)(2,1)S(1)}, bf16[128,512]{1,0:T(8,128)(2,1)S(1)}, u32[]{:S(2)}, u32[]{:S(2)}) collective-permute-start(bf16[128,512]{1,0:T(8,128)(2,1)S(1)} %constant_dynamic-slice_fusion), channel_id=1, source_target_pairs={{0,4},{4,0},{8,12},{12,8},{16,20},{20,16},{24,28},{28,24},{1,5},{5... | collective-permute-start | bytes 393224 | tf_op jit(solution)/shard_map/ppermute | solution.py:200
  13.2 27.6 %collective-permute-start.14 = (bf16[1,256,1024]{2,1,0:T(8,128)(2,1)S(1)}, bf16[1,256,1024]{2,1,0:T(8,128)(2,1)S(1)}, u32[]{:S(2)}, u32[]{:S(2)}) collective-permute-start(bf16[1,256,1024]{2,1,0:T(8,128)(2,1)S(1)} %get-tuple-element.24), channel_id=1, source_target_pairs={{0,2},{1,3},{2,0},{3,1},{4,6},{5,7},{6,4},{7,5},{8,10},{9,11},{10,... | collective-permute-start | bytes 1572872 | tf_op jit(solution)/shard_map/ppermute | solution.py:200
  17.7 23.0 %collective-permute-start.16 = (bf16[1,256,1024]{2,1,0:T(8,128)(2,1)S(1)}, bf16[1,256,1024]{2,1,0:T(8,128)(2,1)S(1)}, u32[]{:S(2)}, u32[]{:S(2)}) collective-permute-start(bf16[1,256,1024]{2,1,0:T(8,128)(2,1)S(1)} %get-tuple-element.23), channel_id=1, source_target_pairs={{0,2},{1,3},{2,0},{3,1},{4,6},{5,7},{6,4},{7,5},{8,10},{9,11},{10,... | collective-permute-start | bytes 1572872 | tf_op jit(solution)/shard_map/ppermute | solution.py:200
  19.2 5.3 %collective-permute-start.6 = (bf16[128,512]{1,0:T(8,128)(2,1)S(1)}, bf16[128,512]{1,0:T(8,128)(2,1)S(1)}, u32[]{:S(2)}, u32[]{:S(2)}) collective-permute-start(bf16[128,512]{1,0:T(8,128)(2,1)S(1)} %collective-permute-done.2), channel_id=1, source_target_pairs={{0,4},{4,0},{8,12},{12,8},{16,20},{20,16},{24,28},{28,24},{1,5},{5... | collective-permute-start | bytes 393224 | tf_op jit(solution)/shard_map/ppermute | solution.py:200
  20.8 5.2 %copy-start.2 = (bf16[128,512]{1,0:T(8,128)(2,1)}, bf16[128,512]{1,0:T(8,128)(2,1)S(1)}, u32[]{:S(2)}) copy-start(bf16[128,512]{1,0:T(8,128)(2,1)S(1)} %collective-permute-done.5) | copy-start | bytes 393220
  20.9 6.4 %collective-permute-start.7 = (bf16[128,512]{1,0:T(8,128)(2,1)}, bf16[128,512]{1,0:T(8,128)(2,1)}, u32[]{:S(2)}, u32[]{:S(2)}) collective-permute-start(bf16[128,512]{1,0:T(8,128)(2,1)} %collective-permute-done.3), channel_id=1, source_target_pairs={{0,4},{4,0},{8,12},{12,8},{16,20},{20,16},{24,28},{28,24},{1,5},{5... | collective-permute-start | bytes 393224 | tf_op jit(solution)/shard_map/ppermute | solution.py:200
  24.5 1.8 %copy-start.3 = (bf16[128,512]{1,0:T(8,128)(2,1)}, bf16[128,512]{1,0:T(8,128)(2,1)S(1)}, u32[]{:S(2)}) copy-start(bf16[128,512]{1,0:T(8,128)(2,1)S(1)} %collective-permute-done.6) | copy-start | bytes 393220
  24.5 5.1 %collective-permute-start.8 = (bf16[128,512]{1,0:T(8,128)(2,1)S(1)}, bf16[128,512]{1,0:T(8,128)(2,1)}, u32[]{:S(2)}, u32[]{:S(2)}) collective-permute-start(bf16[128,512]{1,0:T(8,128)(2,1)S(1)} %collective-permute-done.4), channel_id=1, source_target_pairs={{0,4},{4,0},{8,12},{12,8},{16,20},{20,16},{24,28},{28,24},{1,5},{5... | collective-permute-start | bytes 393224 | tf_op jit(solution)/shard_map/ppermute | solution.py:200
  27.3 11.4 %collective-permute-start.12 = (s32[4,2,256]{2,1,0:T(2,128)S(1)}, s32[4,2,256]{2,1,0:T(2,128)S(1)}, u32[]{:S(2)}, u32[]{:S(2)}) collective-permute-start(s32[4,2,256]{2,1,0:T(2,128)S(1)} %get-tuple-element.36), channel_id=1, source_target_pairs={{0,2},{1,3},{2,0},{3,1},{4,6},{5,7},{6,4},{7,5},{8,10},{9,11},{10,... | collective-permute-start | bytes 24584 | tf_op jit(solution)/shard_map/ppermute | solution.py:200
  29.6 10.6 %collective-permute-start.13 = (s32[4,2,256]{2,1,0:T(2,128)S(1)}, s32[4,2,256]{2,1,0:T(2,128)S(1)}, u32[]{:S(2)}, u32[]{:S(2)}) collective-permute-start(s32[4,2,256]{2,1,0:T(2,128)S(1)} %get-tuple-element.36), channel_id=1, source_target_pairs={{0,3},{1,2},{2,1},{3,0},{4,7},{5,6},{6,5},{7,4},{8,11},{9,10},{10,... | collective-permute-start | bytes 24584 | tf_op jit(solution)/shard_map/ppermute | solution.py:200
  38.7 15.2 %collective-permute-start.18 = (bf16[1,256,1024]{2,1,0:T(8,128)(2,1)}, bf16[1,256,1024]{2,1,0:T(8,128)(2,1)}, u32[]{:S(2)}, u32[]{:S(2)}) collective-permute-start(bf16[1,256,1024]{2,1,0:T(8,128)(2,1)} %get-tuple-element.25), channel_id=1, source_target_pairs={{0,2},{1,3},{2,0},{3,1},{4,6},{5,7},{6,4},{7,5},{8,10},{9,11},{10,... | collective-permute-start | bytes 1572872 | tf_op jit(solution)/shard_map/ppermute | solution.py:200
  40.2 23.2 %collective-permute-start.20 = (bf16[1,256,1024]{2,1,0:T(8,128)(2,1)}, bf16[1,256,1024]{2,1,0:T(8,128)(2,1)}, u32[]{:S(2)}, u32[]{:S(2)}) collective-permute-start(bf16[1,256,1024]{2,1,0:T(8,128)(2,1)} %get-tuple-element.22), channel_id=1, source_target_pairs={{0,2},{1,3},{2,0},{3,1},{4,6},{5,7},{6,4},{7,5},{8,10},{9,11},{10,... | collective-permute-start | bytes 1572872 | tf_op jit(solution)/shard_map/ppermute | solution.py:200
  40.8 22.7 %collective-permute-start.9 = (bf16[4,128,512]{2,1,0:T(8,128)(2,1)S(1)}, bf16[4,128,512]{2,1,0:T(8,128)(2,1)S(1)}, u32[]{:S(2)}, u32[]{:S(2)}) collective-permute-start(bf16[4,128,512]{2,1,0:T(8,128)(2,1)S(1)} %pad_maximum_fusion.refs_5_), channel_id=1, source_target_pairs={{0,1},{1,0},{2,3},{3,2},{4,5},{5,4},{6,7},{7,6},{8,9},{9,8},{10,11... | collective-permute-start | bytes 1572872 | tf_op jit(solution)/shard_map/ppermute | solution.py:200
  40.8 23.2 %collective-permute-start.10 = (bf16[4,128,512]{2,1,0:T(8,128)(2,1)S(1)}, bf16[4,128,512]{2,1,0:T(8,128)(2,1)S(1)}, u32[]{:S(2)}, u32[]{:S(2)}) collective-permute-start(bf16[4,128,512]{2,1,0:T(8,128)(2,1)S(1)} %pad_maximum_fusion.1.refs_6_), channel_id=1, source_target_pairs={{0,1},{1,0},{2,3},{3,2},{4,5},{5,4},{6,7},{7,6},{8,9},{9,8},{10,11... | collective-permute-start | bytes 1572872 | tf_op jit(solution)/shard_map/ppermute | solution.py:200
  53.9 30.8 %collective-permute-start.15 = (bf16[1,256,1024]{2,1,0:T(8,128)(2,1)S(1)}, bf16[1,256,1024]{2,1,0:T(8,128)(2,1)S(1)}, u32[]{:S(2)}, u32[]{:S(2)}) collective-permute-start(bf16[1,256,1024]{2,1,0:T(8,128)(2,1)S(1)} %collective-permute-done.14.refs_3_), channel_id=1, source_target_pairs={{0,1},{1,0},{2,3},{3,2},{4,5},{5,4},{6,7},{7,6},{8,9},{9,8},{10,11... | collective-permute-start | bytes 1572872 | tf_op jit(solution)/shard_map/ppermute | solution.py:200
  63.4 32.4 %collective-permute-start.17 = (bf16[1,256,1024]{2,1,0:T(8,128)(2,1)S(1)}, bf16[1,256,1024]{2,1,0:T(8,128)(2,1)S(1)}, u32[]{:S(2)}, u32[]{:S(2)}) collective-permute-start(bf16[1,256,1024]{2,1,0:T(8,128)(2,1)S(1)} %collective-permute-done.16.refs_3_), channel_id=1, source_target_pairs={{0,1},{1,0},{2,3},{3,2},{4,5},{5,4},{6,7},{7,6},{8,9},{9,8},{10,11... | collective-permute-start | bytes 1572872 | tf_op jit(solution)/shard_map/ppermute | solution.py:200
  63.4 43.5 %collective-permute-start.19 = (bf16[1,256,1024]{2,1,0:T(8,128)(2,1)}, bf16[1,256,1024]{2,1,0:T(8,128)(2,1)S(1)}, u32[]{:S(2)}, u32[]{:S(2)}) collective-permute-start(bf16[1,256,1024]{2,1,0:T(8,128)(2,1)} %collective-permute-done.18.refs_3_), channel_id=1, source_target_pairs={{0,1},{1,0},{2,3},{3,2},{4,5},{5,4},{6,7},{7,6},{8,9},{9,8},{10,11... | collective-permute-start | bytes 1572872 | tf_op jit(solution)/shard_map/ppermute | solution.py:200
  63.9 54.2 %collective-permute-start.21 = (bf16[1,256,1024]{2,1,0:T(8,128)(2,1)}, bf16[1,256,1024]{2,1,0:T(8,128)(2,1)S(1)}, u32[]{:S(2)}, u32[]{:S(2)}) collective-permute-start(bf16[1,256,1024]{2,1,0:T(8,128)(2,1)} %collective-permute-done.20.refs_3_), channel_id=1, source_target_pairs={{0,1},{1,0},{2,3},{3,2},{4,5},{5,4},{6,7},{7,6},{8,9},{9,8},{10,11... | collective-permute-start | bytes 1572872 | tf_op jit(solution)/shard_map/ppermute | solution.py:200
  64.0 1.6 copy-start.1
  131.3 2.8 %collective-permute-start.24 = (bf16[2,1024,256]{2,1,0:T(8,128)(2,1)S(1)}, bf16[2,1024,256]{2,1,0:T(8,128)(2,1)S(1)}, u32[]{:S(2)}, u32[]{:S(2)}) collective-permute-start(bf16[2,1024,256]{2,1,0:T(8,128)(2,1)S(1)} %fusion), channel_id=1, source_target_pairs={{0,1},{1,0},{2,3},{3,2},{4,5},{5,4},{6,7},{7,6},{8,9},{9,8},{10,11... | collective-permute-start | bytes 3145736 | tf_op jit(solution)/shard_map/ppermute | solution.py:200
  136.0 14.4 %collective-permute-start.25 = (bf16[1024,256]{1,0:T(8,128)(2,1)S(1)}, bf16[1024,256]{1,0:T(8,128)(2,1)S(1)}, u32[]{:S(2)}, u32[]{:S(2)}) collective-permute-start(bf16[1024,256]{1,0:T(8,128)(2,1)S(1)} %fusion.1), channel_id=1, source_target_pairs={{0,2},{1,3},{2,0},{3,1},{4,6},{5,7},{6,4},{7,5},{8,10},{9,11},{10,... | collective-permute-start | bytes 1572872 | tf_op jit(solution)/shard_map/ppermute | solution.py:200
  137.6 14.2 %collective-permute-start.22 = (f32[4,256]{1,0:T(4,128)S(1)}, f32[4,256]{1,0:T(4,128)S(1)}, u32[]{:S(2)}, u32[]{:S(2)}) collective-permute-start(f32[4,256]{1,0:T(4,128)S(1)} %bitcast.84), channel_id=1, source_target_pairs={{0,2},{1,3},{2,0},{3,1},{4,6},{5,7},{6,4},{7,5},{8,10},{9,11},{10,... | collective-permute-start | bytes 12296 | tf_op jit(solution)/shard_map/ppermute | solution.py:200
  138.2 16.0 %collective-permute-start.23 = (f32[4,256]{1,0:T(4,128)S(1)}, f32[4,256]{1,0:T(4,128)S(1)}, u32[]{:S(2)}, u32[]{:S(2)}) collective-permute-start(f32[4,256]{1,0:T(4,128)S(1)} %bitcast.83), channel_id=1, source_target_pairs={{0,3},{1,2},{2,1},{3,0},{4,7},{5,6},{6,5},{7,4},{8,11},{9,10},{10,... | collective-permute-start | bytes 12296 | tf_op jit(solution)/shard_map/ppermute | solution.py:200
  150.5 6.9 %collective-permute-start.26 = (bf16[128,256]{1,0:T(8,128)(2,1)S(1)}, bf16[128,256]{1,0:T(8,128)(2,1)S(1)}, u32[]{:S(2)}, u32[]{:S(2)}) collective-permute-start(bf16[128,256]{1,0:T(8,128)(2,1)S(1)} %get-tuple-element.26), channel_id=1, source_target_pairs={{0,4},{4,0},{8,12},{12,8},{16,20},{20,16},{24,28},{28,24},{1,5},{5... | collective-permute-start | bytes 196616 | tf_op jit(solution)/shard_map/ppermute | solution.py:200
  151.0 9.7 %collective-permute-start.27 = (bf16[128,256]{1,0:T(8,128)(2,1)S(1)}, bf16[128,256]{1,0:T(8,128)(2,1)S(1)}, u32[]{:S(2)}, u32[]{:S(2)}) collective-permute-start(bf16[128,256]{1,0:T(8,128)(2,1)S(1)} %get-tuple-element.32), channel_id=1, source_target_pairs={{0,8},{4,12},{8,0},{12,4},{16,24},{20,28},{24,16},{28,20},{1,9},{5... | collective-permute-start | bytes 196616 | tf_op jit(solution)/shard_map/ppermute | solution.py:200
  151.8 4.5 %collective-permute-start.11 = (f32[4,256]{1,0:T(4,128)S(1)}, f32[4,256]{1,0:T(4,128)S(1)}, u32[]{:S(2)}, u32[]{:S(2)}) collective-permute-start(f32[4,256]{1,0:T(4,128)S(1)} %slice_bitcast_fusion), channel_id=1, source_target_pairs={{0,1},{1,0},{2,3},{3,2},{4,5},{5,4},{6,7},{7,6},{8,9},{9,8},{10,11... | collective-permute-start | bytes 12296 | tf_op jit(solution)/shard_map/ppermute | solution.py:200
  151.8 10.6 %collective-permute-start.28 = (bf16[128,256]{1,0:T(8,128)(2,1)S(1)}, bf16[128,256]{1,0:T(8,128)(2,1)S(1)}, u32[]{:S(2)}, u32[]{:S(2)}) collective-permute-start(bf16[128,256]{1,0:T(8,128)(2,1)S(1)} %get-tuple-element.31), channel_id=1, source_target_pairs={{0,12},{4,8},{8,4},{12,0},{16,28},{20,24},{24,20},{28,16},{1,13},{... | collective-permute-start | bytes 196616 | tf_op jit(solution)/shard_map/ppermute | solution.py:200
  154.1 8.3 %collective-permute-start.29 = (bf16[128,256]{1,0:T(8,128)(2,1)S(1)}, bf16[128,256]{1,0:T(8,128)(2,1)S(1)}, u32[]{:S(2)}, u32[]{:S(2)}) collective-permute-start(bf16[128,256]{1,0:T(8,128)(2,1)S(1)} %get-tuple-element.30), channel_id=1, source_target_pairs={{0,16},{4,20},{8,24},{12,28},{16,0},{20,4},{24,8},{28,12},{1,17},{... | collective-permute-start | bytes 196616 | tf_op jit(solution)/shard_map/ppermute | solution.py:200
  156.3 10.3 %collective-permute-start.30 = (bf16[128,256]{1,0:T(8,128)(2,1)S(1)}, bf16[128,256]{1,0:T(8,128)(2,1)S(1)}, u32[]{:S(2)}, u32[]{:S(2)}) collective-permute-start(bf16[128,256]{1,0:T(8,128)(2,1)S(1)} %get-tuple-element.29), channel_id=1, source_target_pairs={{0,20},{4,16},{8,28},{12,24},{16,4},{20,0},{24,12},{28,8},{1,21},{... | collective-permute-start | bytes 196616 | tf_op jit(solution)/shard_map/ppermute | solution.py:200
  157.4 9.2 %collective-permute-start.31 = (bf16[128,256]{1,0:T(8,128)(2,1)S(1)}, bf16[128,256]{1,0:T(8,128)(2,1)S(1)}, u32[]{:S(2)}, u32[]{:S(2)}) collective-permute-start(bf16[128,256]{1,0:T(8,128)(2,1)S(1)} %get-tuple-element.28), channel_id=1, source_target_pairs={{0,24},{4,28},{8,16},{12,20},{16,8},{20,12},{24,0},{28,4},{1,25},{... | collective-permute-start | bytes 196616 | tf_op jit(solution)/shard_map/ppermute | solution.py:200
  160.7 7.1 %collective-permute-start.32 = (bf16[128,256]{1,0:T(8,128)(2,1)S(1)}, bf16[128,256]{1,0:T(8,128)(2,1)S(1)}, u32[]{:S(2)}, u32[]{:S(2)}) collective-permute-start(bf16[128,256]{1,0:T(8,128)(2,1)S(1)} %get-tuple-element.27), channel_id=1, source_target_pairs={{0,28},{4,24},{8,20},{12,16},{16,12},{20,8},{24,4},{28,0},{1,29},{... | collective-permute-start | bytes 196616 | tf_op jit(solution)/shard_map/ppermute | solution.py:200

commit v2 on v0

v2 whole, which is shorter than its diff:
```python
import functools
import math

import jax
import jax.numpy as jnp
from jax import lax
from jax.experimental import pallas as pl
from jax.experimental.pallas import tpu as pltpu
from jax.sharding import PartitionSpec as P

MARGIN_BLOCK_SIZE = 64
VMEM_LIMIT = 40 * 1024 * 1024
ME, CORE, COUNTS = 0, 1, 2


def ranks(hits):
    n = hits.shape[1]
    before = lax.broadcasted_iota(jnp.int32, (n, n), 0) < lax.broadcasted_iota(jnp.int32, (n, n), 1)
    count = jnp.dot(
        hits.astype(jnp.bfloat16), before.astype(jnp.bfloat16), preferred_element_type=jnp.float32
    )
    return jnp.where(hits > 0, count, -1.0)


def dispatch_kernel(offsets, cap, info, routes, words, *outs):
    wdev = words.shape[1]
    route = jnp.broadcast_to(routes[0], (8, wdev))
    slots = lax.broadcasted_iota(jnp.int32, (cap, wdev), 0).astype(jnp.float32)
    row = lax.broadcasted_iota(jnp.int32, (8, wdev), 0)
    picks = []
    for first in range(0, len(offsets), 8):
        some = offsets[first : first + 8]
        to = jnp.full((8, wdev), -1, jnp.int32)
        for i, offset in enumerate(some):
            to = jnp.where(row == i, jnp.bitwise_xor(info[ME], offset), to)
        rank = ranks((route == to).astype(jnp.float32))
        picks += [(slots == rank[i : i + 1]).astype(jnp.bfloat16) for i in range(len(some))]
    rows = jnp.dot(
        jnp.concatenate(picks, axis=0), words[0], preferred_element_type=jnp.float32
    ).astype(jnp.bfloat16)
    for i, out in enumerate(outs):
        out[0] = rows[i * cap : (i + 1) * cap]


def dispatch(info, routes, words, offsets, cap, first_page, n_pages):
    _, wdev, width = words.shape
    n = len(offsets)
    take = lambda p, info: (p + first_page, 0, 0)
    return pl.pallas_call(
        functools.partial(dispatch_kernel, offsets, cap),
        grid_spec=pltpu.PrefetchScalarGridSpec(
            num_scalar_prefetch=1,
            grid=(n_pages,),
            in_specs=[pl.BlockSpec((1, 1, wdev), take), pl.BlockSpec((1, wdev, width), take)],
            out_specs=[pl.BlockSpec((1, cap, width), lambda p, info: (p, 0, 0))] * n,
        ),
        out_shape=[jax.ShapeDtypeStruct((n_pages, cap, width), jnp.bfloat16)] * n,
        compiler_params=pltpu.CompilerParams(vmem_limit_bytes=VMEM_LIMIT),
        cost_estimate=pl.CostEstimate(
            flops=0, bytes_accessed=0, transcendentals=0
        ),
    )(info, routes, words)


def page_kernel(offsets, n_proj, first_page, n_pages, has_acc, last, scale, info, *refs):
    n_homes = len(offsets)
    refs = list(refs)
    meta, flags, patches = refs[:3]
    words = refs[3 : 3 + n_homes]
    gathered = refs[3 + n_homes : 3 + n_homes + n_proj]
    rest = refs[3 + n_homes + n_proj :]
    acc_in = rest.pop(0) if has_acc else None
    outs, rest = (rest[:2], rest[2:]) if last else (rest[:1], rest[1:])
    loss, proj, x_t, dqs, sems = rest[:5]
    acc = rest[5] if has_acc else None
    page = pl.program_id(0)
    me, core = info[ME], info[CORE]
    wdev = meta.shape[-1]
    pps, width = patches.shape[-2:]
    nblk, all_blk = flags.shape[-2:]
    cap = words[0].shape[1]
    n_rows = n_homes * cap
    n_cols = meta.shape[0]
    wcol = width // n_cols
    half = width // 2
    bps = pps // MARGIN_BLOCK_SIZE

    def proj_copies():
        return [
            pltpu.make_async_copy(ref, proj.at[jnp.bitwise_xor(core, g)], sems.at[g])
            for g, ref in enumerate(gathered)
        ]

    acc_copy = lambda: pltpu.make_async_copy(acc_in, acc, sems.at[n_proj])

    @pl.when(page == 0)
    def _():
        for copy in proj_copies():
            copy.start()
        if has_acc:
            acc_copy().start()

    slots = lax.broadcasted_iota(jnp.int32, (cap, wdev), 0).astype(jnp.float32)
    here = lax.broadcasted_iota(jnp.int32, (cap, wdev), 1)
    row = lax.broadcasted_iota(jnp.int32, (8, wdev), 0)
    picks, t_rows, i_rows = [], [], []
    for first in range(0, n_homes, 8):
        some = offsets[first : first + 8]
        hits = jnp.zeros((8, wdev), jnp.float32)
        for i, offset in enumerate(some):
            route = meta[jnp.bitwise_xor(me, offset), page + first_page, 0:1, :]
            hits = jnp.where((row == i) & (route == me), 1.0, hits)
        rank = ranks(hits)
        for i, offset in enumerate(some):
            home = jnp.bitwise_xor(me, offset)
            pick = (slots == rank[i : i + 1]).astype(jnp.float32)
            target = meta[home, page + first_page, 1:2, :].astype(jnp.float32)
            place = (here + (home * wdev + 1)).astype(jnp.float32)
            t_rows.append(jnp.sum(pick * target, axis=1, keepdims=True))
            i_rows.append(jnp.sum(pick * place, axis=1, keepdims=True))
            picks.append(pick)
    t = jnp.concatenate(t_rows, axis=0).astype(jnp.int32)
    idx = jnp.concatenate(i_rows, axis=0).astype(jnp.int32) - 1

    x = jnp.concatenate([w[0] for w in words], axis=0)
    if x_t.shape[0] == n_pages:
        x_t[page] = x.T
    else:
        x_t[0, :, pl.ds(pl.multiple_of(page * n_rows, n_rows), n_rows)] = x.T

    blocks = lax.broadcasted_iota(jnp.int32, (n_rows, nblk), 1)
    word_block = (jnp.maximum(idx, 0) // MARGIN_BLOCK_SIZE == blocks).astype(jnp.bfloat16)
    margin = jnp.dot(
        word_block, flags[0].astype(jnp.bfloat16), preferred_element_type=jnp.float32
    ).astype(jnp.bfloat16)
    spread = (
        lax.broadcasted_iota(jnp.int32, (all_blk, pps), 0)
        == me * bps + lax.broadcasted_iota(jnp.int32, (all_blk, pps), 1) // MARGIN_BLOCK_SIZE
    ).astype(jnp.bfloat16)
    hit = jnp.dot(margin, spread, preferred_element_type=jnp.float32)
    k = lax.broadcasted_iota(jnp.int32, (n_rows, pps), 1)
    allowed = (hit > 0.5) | (k // MARGIN_BLOCK_SIZE == t // MARGIN_BLOCK_SIZE)
    is_target = k == t

    @pl.when(page == 0)
    def _():
        for copy in proj_copies():
            copy.wait()

    pat = patches[0]
    scores = jnp.zeros((n_rows, pps), jnp.float32)
    for h in range(2):
        q = jnp.dot(x, proj[h], preferred_element_type=jnp.float32).astype(jnp.bfloat16)
        scores = scores + lax.dot_general(
            q,
            pat[:, h * half : (h + 1) * half],
            (((1,), (1,)), ((), ())),
            preferred_element_type=jnp.float32,
        )
    scores = scores * scale
    top = jnp.max(jnp.where(allowed, scores, -jnp.inf), axis=1, keepdims=True)
    expo = jnp.where(allowed, jnp.exp(scores - top), 0.0)
    total = jnp.sum(expo, axis=1, keepdims=True)
    target_score = jnp.sum(jnp.where(is_target, scores, 0.0), axis=1, keepdims=True)
    count = info[COUNTS + first_page + page]
    valid = (idx >= 0) & (idx < count)
    row_loss = jnp.where(valid, top + jnp.log(total) - target_score, 0.0)
    coef = jnp.where(valid, 64.0 / count.astype(jnp.float32), 0.0)
    share = expo * (1.0 / total)
    dscore = (coef * jnp.where(is_target, share - 1.0, share)).astype(jnp.bfloat16)
    for r in range(n_homes):
        loss[0, r : r + 1, :] = jnp.sum(
            picks[r] * row_loss[r * cap : (r + 1) * cap], axis=0, keepdims=True
        )
    dqs[pl.ds(pl.multiple_of(page * n_rows, n_rows), n_rows), :] = (
        jnp.dot(dscore, pat, preferred_element_type=jnp.float32) * scale
    ).astype(jnp.bfloat16)

    @pl.when(page == n_pages - 1)
    def _():
        if has_acc:
            acc_copy().wait()

        def gradient(j):
            got = acc[j] if has_acc else 0.0
            depth = x_t.shape[2]
            for g in range(x_t.shape[0]):
                got += jnp.dot(
                    x_t[g],
                    dqs[g * depth : (g + 1) * depth, pl.ds(pl.multiple_of(j * wcol, wcol), wcol)],
                    preferred_element_type=jnp.float32,
                )
            return got

        def store(out, y, got):
            halves, _, lows, highs, cut, _ = out.shape
            for part in range(halves * lows * highs):
                high, low, h = part // (2 * lows), part // 2 % lows, part % 2
                out[h, y, low, high] = got[part * cut : (part + 1) * cut].astype(out.dtype)

        if last:
            keep, send = outs
            for y in range(n_cols // 2):
                store(send, y, gradient(2 * y + 1 - core))
            for y in range(n_cols // 2):
                store(keep, y, gradient(2 * y + core))
        else:
            for j in range(n_cols):
                outs[0][j] = gradient(j)


def run_pages(
    n_high, info, meta, flags, patches, words, offsets, gathered, acc, first_page, last
):
    n_pages, cap, width = words[0].shape
    n_seq, _, _, wdev = meta.shape
    pps = patches.shape[1]
    n_homes = len(offsets)
    wcol = width // n_seq
    n_rows = n_homes * cap
    has_acc = acc is not None
    take = lambda p, info: (p + first_page, 0, 0)
    in_specs = [
        pl.BlockSpec(meta.shape, lambda p, info: (0, 0, 0, 0)),
        pl.BlockSpec((1,) + flags.shape[1:], take),
        pl.BlockSpec((1, pps, width), take),
    ]
    in_specs += [pl.BlockSpec((1, cap, width), lambda p, info: (p, 0, 0))] * n_homes
    in_specs += [pl.BlockSpec(memory_space=pl.ANY)] * (len(gathered) + has_acc)
    operands = [info, meta, flags, patches, *words, *gathered] + ([acc] if has_acc else [])
    if last:
        form = (2, n_seq // 2, 2, n_high, width // (4 * n_high), wcol)
        out_shape = [jax.ShapeDtypeStruct(form, t) for t in (jnp.float32, jnp.bfloat16)]
    else:
        out_shape = [jax.ShapeDtypeStruct((n_seq, width, wcol), jnp.float32)]
    out_specs = [pl.BlockSpec(o.shape, lambda p, info, o=o: (0,) * len(o.shape)) for o in out_shape]
    groups = 1 if n_rows % 128 == 0 else n_pages
    scratch = [
        pltpu.VMEM((2, width, width // 2), jnp.bfloat16),
        pltpu.VMEM((groups, width, n_pages * n_rows // groups), jnp.bfloat16),
        pltpu.VMEM((n_pages * n_rows, width), jnp.bfloat16),
        pltpu.SemaphoreType.DMA((len(gathered) + 1,)),
    ]
    if has_acc:
        scratch.append(pltpu.VMEM((n_seq, width, wcol), jnp.float32))
    return pl.pallas_call(
        functools.partial(
            page_kernel,
            offsets,
            len(gathered),
            first_page,
            n_pages,
            has_acc,
            last,
            2.0 / math.sqrt(width),
        ),
        grid_spec=pltpu.PrefetchScalarGridSpec(
            num_scalar_prefetch=1,
            grid=(n_pages,),
            in_specs=in_specs,
            out_specs=out_specs
            + [pl.BlockSpec((1, n_homes, wdev), lambda p, info: (p, 0, 0))],
            scratch_shapes=scratch,
        ),
        out_shape=out_shape + [jax.ShapeDtypeStruct((n_pages, n_homes, wdev), jnp.float32)],
        compiler_params=pltpu.CompilerParams(vmem_limit_bytes=VMEM_LIMIT),
        cost_estimate=pl.CostEstimate(
            flops=0, bytes_accessed=0, transcendentals=0
        ),
    )(*operands)


def exchange(x, axis, offset):
    n = lax.axis_size(axis)
    return lax.ppermute(x, axis, [(i, i ^ offset) for i in range(n)])


def pick(x, i, axis=0):
    return lax.dynamic_index_in_dim(x, i, axis, keepdims=False)


def pick_sum(terms, i, axis=0):
    return sum(pick(t, i, axis).astype(jnp.float32) for t in terms)


def local(words, patches, proj, routes, targets, counts, flags):
    pages, wdev, width = words.shape
    n_seq = lax.axis_size("seq")
    n_dp = lax.axis_size("dp")
    me = lax.axis_index("seq")
    my_dp = lax.axis_index("dp")
    core, y, low, high = me % 2, me // 2, my_dp % 2, my_dp // 2
    n_y, n_high = n_seq // 2, n_dp // 2
    cap = 2 * wdev // n_seq
    half = width // 2
    shard_rows = proj.shape[0]
    wcol = width // n_seq
    near, far = (0, 1), tuple(range(2, n_seq))

    info = jnp.concatenate([jnp.stack([me, core]).astype(jnp.int32), counts])
    routes = routes.reshape(pages, 1, wdev)

    chunks = [(0, pages // 2)] + [(p, 1) for p in range(pages // 2, pages)]
    held = info
    arrived = []
    for first_page, n_pages in chunks:
        rows = dispatch(held, routes, words, far, cap, first_page, n_pages)
        held, rows = lax.optimization_barrier((held, rows))
        arrived.append([exchange(x, "seq", r) for x, r in zip(rows, far)])
    stay, across = dispatch(held, routes, words, near, cap, 0, pages)
    across = exchange(across, "seq", 1)

    pair = jnp.concatenate([routes, targets.reshape(pages, 1, wdev)], axis=1)
    meta = lax.all_to_all(jnp.broadcast_to(pair, (n_seq,) + pair.shape), "seq", 0, 0, tiled=True)

    mine = lax.dynamic_slice_in_dim(proj, core * half, half, 1)
    mine = lax.all_gather(mine, "dp", axis=0, tiled=True)
    mine, meta, arrived[0] = lax.optimization_barrier((mine, meta, arrived[0]))
    gathered = [mine, exchange(mine, "seq", 1)]

    run = functools.partial(run_pages, n_high, info, meta, flags, patches)
    acc, loss = run([stay, across], near, gathered, None, 0, False)
    word_loss = [loss[:, 0], exchange(loss[:, 1], "seq", 1)]
    losses = []
    for (first_page, n_pages), rows in zip(chunks, arrived):
        last = first_page + n_pages == pages
        *out, loss = run(rows, far, gathered, acc, first_page, last)
        acc = out[0]
        losses.append(loss)
    keep, send = out
    losses = jnp.concatenate(losses, axis=0)

    terms = [keep, exchange(send, "seq", 1)]

    def over_y(terms):
        total = pick_sum(terms, y)
        for k in range(1, n_y):
            other = pick_sum(terms, jnp.bitwise_xor(y, k)).astype(jnp.bfloat16)
            total = total + exchange(other, "seq", 2 * k)
        return total

    def over_low(terms, axis):
        other = pick_sum(terms, 1 - low, axis).astype(jnp.bfloat16)
        return pick_sum(terms, low, axis) + exchange(other, "dp", 1)

    one = over_low([over_y([t[0] for t in terms])], 0)
    two = over_y([over_low([t[1] for t in terms], 1)])
    grad = jnp.concatenate([pick(one, high), pick(two, high)], axis=0)
    for k in range(1, n_high):
        to = jnp.bitwise_xor(high, k)
        other = jnp.concatenate([pick(one, to), pick(two, to)], axis=0).astype(jnp.bfloat16)
        grad = grad + exchange(other, "dp", 2 * k)

    for i, r in enumerate(far):
        word_loss.append(exchange(losses[:, i], "seq", r))
    return (sum(word_loss), grad)


def solution(mesh):
    in_specs = (
        P("dp", "seq", None),
        P("dp", "seq", None),
        P("dp", None),
        P("dp", "seq", None),
        P("dp", "seq"),
        P("dp"),
        P("dp", None, None),
    )
    out_specs = (P("dp", "seq"), P("dp", "seq"))
    return jax.shard_map(local, mesh=mesh, in_specs=in_specs, out_specs=out_specs, check_vma=False)
```

time: 326 us -> 129 us (0.40)
  waiting for transfers between devices: 185 us -> 29.8 us
  blocking collectives: 57.9 us -> 16.5 us
  matrix products: 35.9 us -> 0 us
  Pallas kernels: 0 us -> 31.9 us
  starting transfers between devices: 12.8 us -> 17.2 us
  other arithmetic: 6.74 us -> 2.46 us
    reduce_scatter x2 -> x0, waiting for transfers between devices: 102 us -> none  [the longest x1 86.2 us: local(): lax.psum_scatter(jnp.einsum('rc,rd->cd', columns, right, preferred_elemen...]
    all_to_all x3 -> x0, waiting for transfers between devices: 45 us -> none  [the longest x1 45 us: local(): lax.all_to_all(q_buf, 'seq', split_axis=0, concat_axis=0, tiled=True)]
    all_to_all x2 -> x1, blocking collectives: 57.9 us -> 16.5 us  [local(): lax.all_to_all(jnp.broadcast_to(pair, (n_seq,) + pair.shape), 'seq', 0, 0...]
    dot_general x8 -> x0, matrix products: 35.9 us -> none  [the longest x1 7.62 us: local(): jnp.einsum('rc,rd->cd', columns, right, preferred_element_type=jnp.float32)]
    pallas_call x0 -> x7, Pallas kernels: none -> 31.9 us  [the longest x3 25.2 us: run_pages(): pl.pallas_call(functools.partial(page_kernel, offsets, len(gathered), fir...]
    all_gather x1, waiting for transfers between devices: 36.6 us -> 13.8 us  [local(): mine = lax.all_gather(mine, 'dp', axis=0, tiled=True)]
    ppermute x0 -> x19, starting transfers between devices: none -> 17.1 us  [exchange(): return lax.ppermute(x, axis, [(i, i ^ offset) for i in range(n)])]
    ppermute x0 -> x19, waiting for transfers between devices: none -> 16 us  [exchange(): return lax.ppermute(x, axis, [(i, i ^ offset) for i in range(n)])]
  transfers between devices with their start and end apart: 6 -> 20, of which waited for: 4 -> 8; matrix products, arithmetic and copies ran while one was open for 11% -> 6% of each run, Pallas kernels for 0% -> 21%
where the time goes in v2:
time: 129 us
  Pallas kernels  31.9 us (25%)
  waiting for transfers between devices  29.8 us (23%)
  starting transfers between devices  17.2 us (13%)
  local copies, waits for them, and re-layouts  16.5 us (13%)
  blocking collectives  16.5 us (13%)
  between operations  14.4 us (11%)
  other arithmetic  2.46 us (2%)
    pallas_call x3, Pallas kernels, run_pages(): pl.pallas_call(functools.partial(page_kernel, offsets, len(gathered), fir...  25.2 us
    ppermute x19, starting transfers between devices, exchange(): return lax.ppermute(x, axis, [(i, i ^ offset) for i in range(n)])  17.1 us
    all_to_all x1, blocking collectives, local(): lax.all_to_all(jnp.broadcast_to(pair, (n_seq,) + pair.shape), 'seq', 0, 0...  16.5 us
    ppermute x19, waiting for transfers between devices, exchange(): return lax.ppermute(x, axis, [(i, i ^ offset) for i in range(n)])  16 us
    all_gather x1, waiting for transfers between devices, local(): mine = lax.all_gather(mine, 'dp', axis=0, tiled=True)  13.8 us
    unnamed x31, local copies, waits for them, and re-layouts  9.97 us
    pallas_call x4, Pallas kernels, dispatch(): pl.pallas_call(functools.partial(dispatch_kernel, offsets, cap), grid_spe...  6.71 us
    pallas_call x3, local copies, waits for them, and re-layouts, run_pages(): pl.pallas_call(functools.partial(page_kernel, offsets, len(gathered), fir...  4.32 us
  transfers between devices with their start and end apart: 20, of which 8 were waited for; matrix products, arithmetic and copies ran while one was open for 6% of the time, Pallas kernels for 21%

profile of v2, /device:TPU:0, one launch (start us, length us, event | category | flops | bytes accessed | tf_op | source)
XLA Modules:
  0.0 128.8 jit_solution(18398975300197788625)
XLA Ops:
  7.3 0.9 copy-done
  8.1 0.7 constant_dynamic-slice_fusion
  8.8 0.7 pad_add_fusion.1.info
  9.5 1.6 %copy-done.3 = bf16[4,256,1024]{2,1,0:T(8,128)(2,1)S(1)} copy-done((bf16[4,256,1024]{2,1,0:T(8,128)(2,1)S(1)}, bf16[4,256,1024]{2,1,0:T(8,128)(2,1)}, u32[]{:S(2)}) %copy-start.3) | copy-done | bytes 2097176
  11.1 0.7 copy-done.7
  11.8 1.4 %shard_map.86 = (bf16[2,128,1024]{2,1,0:T(8,128)(2,1)S(1)}, bf16[2,128,1024]{2,1,0:T(8,128)(2,1)S(1)}) custom-call(s32[6]{0:T(128)S(1)} %pad_add_fusion.1.info, s32[4,1,256]{2,1,0:T(1,128)S(1)} %bitcast.59, bf16[4,256,1024]{2,1,0:T(8,128)(2,1)S(1)} %copy-done.3), custom_call_target="tpu_custom_call" | custom-call | tf_op jit(solution)/shard_map/pallas_call | solution.py:49
  13.3 3.0 %collective-permute-start = (bf16[2,128,1024]{2,1,0:T(8,128)(2,1)S(1)}, bf16[2,128,1024]{2,1,0:T(8,128)(2,1)S(1)}, u32[]{:S(2)}, u32[]{:S(2)}) collective-permute-start(bf16[2,128,1024]{2,1,0:T(8,128)(2,1)S(1)} %get-tuple-element.34), channel_id=1, source_target_pairs={{0,2},{1,3},{2,0},{3,1},{4,6},{5,7},{6,4},{7,5},{8,10},{9,11},{10,... | collective-permute-start | bytes 1572872 | tf_op jit(solution)/shard_map/ppermute | solution.py:275
  16.3 1.0 shard_map.87
  17.3 0.7 copy-done.12
  18.0 0.7 copy-done.11
  18.7 1.0 shard_map.88
  19.7 3.3 %shard_map.89 = (bf16[4,128,1024]{2,1,0:T(8,128)(2,1)S(1)}, bf16[4,128,1024]{2,1,0:T(8,128)(2,1)}) custom-call(s32[6]{0:T(128)S(1)} %pad_add_fusion.1.info, s32[4,1,256]{2,1,0:T(1,128)S(1)} %bitcast.62, bf16[4,256,1024]{2,1,0:T(8,128)(2,1)S(1)} %copy-done.3), custom_call_target="tpu_custom_call" | custom-call | tf_op jit(solution)/shard_map/pallas_call | solution.py:49
  23.0 0.2 collective-permute-start.2
  23.3 16.5 %all_to_all.5.refs_0_ = s32[4,4,2,256]{3,2,1,0:T(2,128)S(1)} all-to-all(s32[4,4,2,256]{3,2,1,0:T(2,128)S(1)} %broadcast_in_dim.3), channel_id=1, replica_groups=mesh['dp'=8,'seq'=4] {'seq'}, dimensions={0} | all-to-all | bytes 65536 | tf_op jit(solution)/shard_map/all_to_all | solution.py:314
  39.8 13.8 %all-gather.2.cloned.1.call-done.refs_5_ = bf16[1024,512]{1,0:T(8,128)(2,1)} async-done(((bf16[128,512]{1,0:T(8,128)(2,1)}), bf16[1024,512]{1,0:T(8,128)(2,1)}) %all-gather.2.cloned.1.call-update) | async-done | bytes 1048592 | tf_op jit(solution)/shard_map/all_gather | solution.py:317
  53.7 1.5 %collective-permute-start.5 = (bf16[1,128,1024]{2,1,0:T(8,128)(2,1)}, bf16[1,128,1024]{2,1,0:T(8,128)(2,1)S(1)}, u32[]{:S(2)}, u32[]{:S(2)}) collective-permute-start(bf16[1,128,1024]{2,1,0:T(8,128)(2,1)} %copy-done.12), channel_id=1, source_target_pairs={{0,2},{1,3},{2,0},{3,1},{4,6},{5,7},{6,4},{7,5},{8,10},{9,11},{10,... | collective-permute-start | bytes 786440 | tf_op jit(solution)/shard_map/ppermute | solution.py:275
  55.2 0.4 collective-permute-start.6
  55.5 1.5 %collective-permute-start.7 = (bf16[1,128,1024]{2,1,0:T(8,128)(2,1)}, bf16[1,128,1024]{2,1,0:T(8,128)(2,1)S(1)}, u32[]{:S(2)}, u32[]{:S(2)}) collective-permute-start(bf16[1,128,1024]{2,1,0:T(8,128)(2,1)} %copy-done.10), channel_id=1, source_target_pairs={{0,2},{1,3},{2,0},{3,1},{4,6},{5,7},{6,4},{7,5},{8,10},{9,11},{10,... | collective-permute-start | bytes 786440 | tf_op jit(solution)/shard_map/ppermute | solution.py:275
  57.0 0.2 collective-permute-start.8
  57.2 2.2 %copy-done.1 = bf16[4,512,1024]{2,1,0:T(8,128)(2,1)S(1)} copy-done((bf16[4,512,1024]{2,1,0:T(8,128)(2,1)S(1)}, bf16[4,512,1024]{2,1,0:T(8,128)(2,1)}, u32[]{:S(2)}) %copy-start.1) | copy-done | bytes 4194328
  59.4 1.2 copy-done.4
  60.6 13.0 %shard_map.90 = (f32[4,1024,256]{2,1,0:T(8,128)S(1)}, f32[4,2,256]{2,1,0:T(2,128)S(1)}) custom-call(s32[6]{0:T(128)S(1)} %pad_add_fusion.1.info, s32[4,4,2,256]{3,2,1,0:T(2,128)S(1)} %all_to_all.5.refs_0_, s32[4,16,32]{2,1,0:T(8,128)S(1)} %copy-done.6, bf16[4,512,1024]{2,1,0:T(8,128)(2,1)S(1)} %copy-done.1, ...), custom_call_target="tpu_custom_call" | custom-call | tf_op jit(solution)/shard_map/pallas_call | solution.py:246
  73.7 2.0 %copy-done.5 = f32[4,1024,256]{2,1,0:T(8,128)} copy-done((f32[4,1024,256]{2,1,0:T(8,128)}, f32[4,1024,256]{2,1,0:T(8,128)S(1)}, u32[]{:S(2)}) %copy-start.5) | copy-done | bytes 4194328
  75.6 7.0 %shard_map.91 = (f32[4,1024,256]{2,1,0:T(8,128)S(1)}, f32[2,2,256]{2,1,0:T(2,128)S(1)}) custom-call(s32[6]{0:T(128)S(1)} %pad_add_fusion.1.info, s32[4,4,2,256]{3,2,1,0:T(2,128)S(1)} %all_to_all.5.refs_0_, s32[4,16,32]{2,1,0:T(8,128)S(1)} %copy-done.6, bf16[4,512,1024]{2,1,0:T(8,128)(2,1)S(1)} %copy-done.2, ...), custom_call_target="tpu_custom_call" | custom-call | tf_op jit(solution)/shard_map/pallas_call | solution.py:246
  82.7 4.2 %shard_map.93 = (f32[4,2,256]{2,1,0:T(2,128)S(1)}, f32[4,1024,256]{2,1,0:T(8,128)S(1)}) fusion(f32[4,2,256]{2,1,0:T(2,128)S(1)} %constant_dynamic-update-slice_fusion.2, s32[6]{0:T(128)S(1)} %pad_add_fusion.1.info, s32[4,4,2,256]{3,2,1,0:T(2,128)S(1)} %all_to_all.5.refs_0_, s32[4,16,32]{2,1,0:T(8,128)S(1)} %copy-done.6, ...), kind=kCustom, calls=%fused_computation.35 | custom fusion | bytes 15272448 | tf_op jit(solution)/shard_map/pallas_call | solution.py:246
  86.9 5.2 %shard_map.92 = (f32[2,2,2,4,64,256]{5,4,3,2,1,0:T(8,128)S(1)}, bf16[2,2,2,4,64,256]{5,4,3,2,1,0:T(8,128)(2,1)}, f32[1,2,256]{2,1,0:T(2,128)S(1)}) custom-call(s32[6]{0:T(128)S(1)} %pad_add_fusion.1.info, s32[4,4,2,256]{3,2,1,0:T(2,128)S(1)} %all_to_all.5.refs_0_, s32[4,16,32]{2,1,0:T(8,128)S(1)} %copy-done.6, bf16[4,512,1024]{2,1,0:T(8,128)(2,1)S(1)} %copy-done.2, ...), custom_call_target="tpu_custom_call" | custom-call | tf_op jit(solution)/shard_map/pallas_call | solution.py:246
  92.1 0.6 collective-permute-start.11
  92.7 0.1 copy.12
  93.0 1.2 collective-permute-start.10
  94.2 0.5 collective-permute-start.9
  94.8 0.2 collective-permute-start.4
  94.9 0.3 collective-permute-done.11
  95.3 1.3 fusion.19
  96.6 1.6 %collective-permute-start.12 = (bf16[2,4,64,256]{3,2,1,0:T(8,128)(2,1)S(1)}, bf16[2,4,64,256]{3,2,1,0:T(8,128)(2,1)S(1)}, u32[]{:S(2)}, u32[]{:S(2)}) collective-permute-start(bf16[2,4,64,256]{3,2,1,0:T(8,128)(2,1)S(1)} %fusion.1), channel_id=1, source_target_pairs={{0,2},{1,3},{2,0},{3,1},{4,6},{5,7},{6,4},{7,5},{8,10},{9,11},{10,... | collective-permute-start | bytes 786440 | tf_op jit(solution)/shard_map/ppermute | solution.py:275
  98.2 0.6 fusion.15
  98.9 0.6 collective-permute-start.14
  99.5 5.8 %collective-permute-done.12 = bf16[2,4,64,256]{3,2,1,0:T(8,128)(2,1)S(1)} collective-permute-done((bf16[2,4,64,256]{3,2,1,0:T(8,128)(2,1)S(1)}, bf16[2,4,64,256]{3,2,1,0:T(8,128)(2,1)S(1)}, u32[]{:S(2)}, u32[]{:S(2)}) %collective-permute-start.12) | collective-permute-done | bytes 262176 | tf_op jit(solution)/shard_map/ppermute | solution.py:275
  105.4 0.6 collective-permute-start.13
  106.0 1.2 collective-permute-done.14
  107.4 0.6 collective-permute-start.15
  108.0 2.5 %collective-permute-done.13 = bf16[4,64,256]{2,1,0:T(8,128)(2,1)S(1)} collective-permute-done((bf16[4,64,256]{2,1,0:T(8,128)(2,1)S(1)}, bf16[4,64,256]{2,1,0:T(8,128)(2,1)S(1)}, u32[]{:S(2)}, u32[]{:S(2)}) %collective-permute-start.13) | collective-permute-done | bytes 131104 | tf_op jit(solution)/shard_map/ppermute | solution.py:275
  110.5 1.9 %collective-permute-done.15 = bf16[4,64,256]{2,1,0:T(8,128)(2,1)S(1)} collective-permute-done((bf16[4,64,256]{2,1,0:T(8,128)(2,1)S(1)}, bf16[4,64,256]{2,1,0:T(8,128)(2,1)S(1)}, u32[]{:S(2)}, u32[]{:S(2)}) %collective-permute-start.15) | collective-permute-done | bytes 131104 | tf_op jit(solution)/shard_map/ppermute | solution.py:275
  112.5 0.6 collective-permute-start.16
  113.1 2.1 %collective-permute-start.17 = (bf16[128,256]{1,0:T(8,128)(2,1)S(1)}, bf16[128,256]{1,0:T(8,128)(2,1)S(1)}, u32[]{:S(2)}, u32[]{:S(2)}) collective-permute-start(bf16[128,256]{1,0:T(8,128)(2,1)S(1)} %pad_maximum_fusion.1), channel_id=1, source_target_pairs={{0,16},{4,20},{8,24},{12,28},{16,0},{20,4},{24,8},{28,12},{1,17},{... | collective-permute-start | bytes 196616 | tf_op jit(solution)/shard_map/ppermute | solution.py:275
  115.2 1.7 %collective-permute-start.18 = (bf16[128,256]{1,0:T(8,128)(2,1)S(1)}, bf16[128,256]{1,0:T(8,128)(2,1)S(1)}, u32[]{:S(2)}, u32[]{:S(2)}) collective-permute-start(bf16[128,256]{1,0:T(8,128)(2,1)S(1)} %pad_maximum_fusion.2), channel_id=1, source_target_pairs={{0,24},{4,28},{8,16},{12,20},{16,8},{20,12},{24,0},{28,4},{1,25},{... | collective-permute-start | bytes 196616 | tf_op jit(solution)/shard_map/ppermute | solution.py:275
  117.0 2.4 %collective-permute-done.17 = bf16[128,256]{1,0:T(8,128)(2,1)S(1)} collective-permute-done((bf16[128,256]{1,0:T(8,128)(2,1)S(1)}, bf16[128,256]{1,0:T(8,128)(2,1)S(1)}, u32[]{:S(2)}, u32[]{:S(2)}) %collective-permute-start.17) | collective-permute-done | bytes 65568 | tf_op jit(solution)/shard_map/ppermute | solution.py:275
  119.3 1.9 %collective-permute-done.18 = bf16[128,256]{1,0:T(8,128)(2,1)S(1)} collective-permute-done((bf16[128,256]{1,0:T(8,128)(2,1)S(1)}, bf16[128,256]{1,0:T(8,128)(2,1)S(1)}, u32[]{:S(2)}, u32[]{:S(2)}) %collective-permute-start.18) | collective-permute-done | bytes 65568 | tf_op jit(solution)/shard_map/ppermute | solution.py:275
  121.3 0.7 fusion.6
  (63 shorter events, 0.9 us)
Async XLA Ops:
  7.2 1.0 copy-start
  7.2 12.5 %copy-start.8 = (s32[4,256,1]{1,2,0:T(1,128)S(1)}, s32[4,256,1]{1,2,0:T(1,128)}, u32[]{:S(2)}) copy-start(s32[4,256,1]{1,2,0:T(1,128)} %param.10) | copy-start | bytes 12292
  7.2 46.5 %all-gather.2.cloned.1.call-start = ((), (), s32[]{:S(2)}) async-start(), calls=%async_computation.1 | async-start | bytes 1179648 | tf_op jit(solution)/shard_map/all_gather | solution.py:317
  9.5 1.6 %copy-start.3 = (bf16[4,256,1024]{2,1,0:T(8,128)(2,1)S(1)}, bf16[4,256,1024]{2,1,0:T(8,128)(2,1)}, u32[]{:S(2)}) copy-start(bf16[4,256,1024]{2,1,0:T(8,128)(2,1)} %words.7) | copy-start | bytes 6291460
  11.1 0.7 copy-start.7
  11.8 11.4 %copy-start.13 = (s32[4,256]{1,0:T(4,128)S(1)}, s32[4,256]{1,0:T(4,128)}, u32[]{:S(2)}) copy-start(s32[4,256]{1,0:T(4,128)} %param.11) | copy-start | bytes 12292
  11.8 45.4 %copy-start.6 = (s32[4,16,32]{2,1,0:T(8,128)S(1)}, s32[4,16,32]{2,1,0:T(8,128)}, u32[]{:S(2)}) copy-start(s32[4,16,32]{2,1,0:T(8,128)} %refs_1_.6) | copy-start | bytes 24580
  13.3 26.5 %collective-permute-start = (bf16[2,128,1024]{2,1,0:T(8,128)(2,1)S(1)}, bf16[2,128,1024]{2,1,0:T(8,128)(2,1)S(1)}, u32[]{:S(2)}, u32[]{:S(2)}) collective-permute-start(bf16[2,128,1024]{2,1,0:T(8,128)(2,1)S(1)} %get-tuple-element.34), channel_id=1, source_target_pairs={{0,2},{1,3},{2,0},{3,1},{4,6},{5,7},{6,4},{7,5},{8,10},{9,11},{10,... | collective-permute-start | bytes 1572872 | tf_op jit(solution)/shard_map/ppermute | solution.py:275
  16.3 23.5 %collective-permute-start.1 = (bf16[2,128,1024]{2,1,0:T(8,128)(2,1)S(1)}, bf16[2,128,1024]{2,1,0:T(8,128)(2,1)S(1)}, u32[]{:S(2)}, u32[]{:S(2)}) collective-permute-start(bf16[2,128,1024]{2,1,0:T(8,128)(2,1)S(1)} %get-tuple-element.35), channel_id=1, source_target_pairs={{0,3},{1,2},{2,1},{3,0},{4,7},{5,6},{6,5},{7,4},{8,11},{9,10},{10,... | collective-permute-start | bytes 1572872 | tf_op jit(solution)/shard_map/ppermute | solution.py:275
  17.3 0.7 copy-start.12
  18.0 0.7 copy-start.11
  19.7 20.1 %copy-start.9 = (bf16[1,128,1024]{2,1,0:T(8,128)(2,1)}, bf16[1,128,1024]{2,1,0:T(8,128)(2,1)S(1)}, u32[]{:S(2)}) copy-start(bf16[1,128,1024]{2,1,0:T(8,128)(2,1)S(1)} %get-tuple-element.57) | copy-start | bytes 786436
  19.7 20.1 %copy-start.10 = (bf16[1,128,1024]{2,1,0:T(8,128)(2,1)}, bf16[1,128,1024]{2,1,0:T(8,128)(2,1)S(1)}, u32[]{:S(2)}) copy-start(bf16[1,128,1024]{2,1,0:T(8,128)(2,1)S(1)} %get-tuple-element.56) | copy-start | bytes 786436
  23.0 34.0 %collective-permute-start.2 = (bf16[4,128,1024]{2,1,0:T(8,128)(2,1)}, bf16[4,128,1024]{2,1,0:T(8,128)(2,1)S(1)}, u32[]{:S(2)}, u32[]{:S(2)}) collective-permute-start(bf16[4,128,1024]{2,1,0:T(8,128)(2,1)} %get-tuple-element.45), channel_id=1, source_target_pairs={{0,1},{1,0},{2,3},{3,2},{4,5},{5,4},{6,7},{7,6},{8,9},{9,8},{10,11... | collective-permute-start | bytes 3145736 | tf_op jit(solution)/shard_map/ppermute | solution.py:275
  53.7 3.5 %collective-permute-start.3 = (bf16[1024,512]{1,0:T(8,128)(2,1)}, bf16[1024,512]{1,0:T(8,128)(2,1)S(1)}, u32[]{:S(2)}, u32[]{:S(2)}) collective-permute-start(bf16[1024,512]{1,0:T(8,128)(2,1)} %all-gather.2.cloned.1.call-done.refs_5_), channel_id=1, source_target_pairs={{0,1},{1,0},{2,3},{3,2},{4,5},{5,4},{6,7},{7,6},{8,9},{9,8},{10,11... | collective-permute-start | bytes 3145736 | tf_op jit(solution)/shard_map/ppermute | solution.py:275
  53.7 29.0 %collective-permute-start.5 = (bf16[1,128,1024]{2,1,0:T(8,128)(2,1)}, bf16[1,128,1024]{2,1,0:T(8,128)(2,1)S(1)}, u32[]{:S(2)}, u32[]{:S(2)}) collective-permute-start(bf16[1,128,1024]{2,1,0:T(8,128)(2,1)} %copy-done.12), channel_id=1, source_target_pairs={{0,2},{1,3},{2,0},{3,1},{4,6},{5,7},{6,4},{7,5},{8,10},{9,11},{10,... | collective-permute-start | bytes 786440 | tf_op jit(solution)/shard_map/ppermute | solution.py:275
  55.2 27.5 %collective-permute-start.6 = (bf16[1,128,1024]{2,1,0:T(8,128)(2,1)}, bf16[1,128,1024]{2,1,0:T(8,128)(2,1)S(1)}, u32[]{:S(2)}, u32[]{:S(2)}) collective-permute-start(bf16[1,128,1024]{2,1,0:T(8,128)(2,1)} %copy-done.11), channel_id=1, source_target_pairs={{0,3},{1,2},{2,1},{3,0},{4,7},{5,6},{6,5},{7,4},{8,11},{9,10},{10,... | collective-permute-start | bytes 786440 | tf_op jit(solution)/shard_map/ppermute | solution.py:275
  55.5 31.3 %collective-permute-start.7 = (bf16[1,128,1024]{2,1,0:T(8,128)(2,1)}, bf16[1,128,1024]{2,1,0:T(8,128)(2,1)S(1)}, u32[]{:S(2)}, u32[]{:S(2)}) collective-permute-start(bf16[1,128,1024]{2,1,0:T(8,128)(2,1)} %copy-done.10), channel_id=1, source_target_pairs={{0,2},{1,3},{2,0},{3,1},{4,6},{5,7},{6,4},{7,5},{8,10},{9,11},{10,... | collective-permute-start | bytes 786440 | tf_op jit(solution)/shard_map/ppermute | solution.py:275
  57.0 29.8 %collective-permute-start.8 = (bf16[1,128,1024]{2,1,0:T(8,128)(2,1)}, bf16[1,128,1024]{2,1,0:T(8,128)(2,1)S(1)}, u32[]{:S(2)}, u32[]{:S(2)}) collective-permute-start(bf16[1,128,1024]{2,1,0:T(8,128)(2,1)} %copy-done.9), channel_id=1, source_target_pairs={{0,3},{1,2},{2,1},{3,0},{4,7},{5,6},{6,5},{7,4},{8,11},{9,10},{10,... | collective-permute-start | bytes 786440 | tf_op jit(solution)/shard_map/ppermute | solution.py:275
  57.2 2.2 %copy-start.1 = (bf16[4,512,1024]{2,1,0:T(8,128)(2,1)S(1)}, bf16[4,512,1024]{2,1,0:T(8,128)(2,1)}, u32[]{:S(2)}) copy-start(bf16[4,512,1024]{2,1,0:T(8,128)(2,1)} %refs_2_.6) | copy-start | bytes 12582916
  59.4 1.2 copy-start.4
  60.6 15.0 %copy-start.2 = (bf16[4,512,1024]{2,1,0:T(8,128)(2,1)S(1)}, bf16[4,512,1024]{2,1,0:T(8,128)(2,1)}, u32[]{:S(2)}) copy-start(bf16[4,512,1024]{2,1,0:T(8,128)(2,1)} %refs_2_.6) | copy-start | bytes 12582916
  73.7 2.0 %copy-start.5 = (f32[4,1024,256]{2,1,0:T(8,128)}, f32[4,1024,256]{2,1,0:T(8,128)S(1)}, u32[]{:S(2)}) copy-start(f32[4,1024,256]{2,1,0:T(8,128)S(1)} %get-tuple-element.50.refs_7_) | copy-start | bytes 12582916
  92.1 3.2 %collective-permute-start.11 = (bf16[2,2,2,4,64,256]{5,4,3,2,1,0:T(8,128)(2,1)}, bf16[2,2,2,4,64,256]{5,4,3,2,1,0:T(8,128)(2,1)}, u32[]{:S(2)}, u32[]{:S(2)}) collective-permute-start(bf16[2,2,2,4,64,256]{5,4,3,2,1,0:T(8,128)(2,1)} %get-tuple-element.61), channel_id=1, source_target_pairs={{0,1},{1,0},{2,3},{3,2},{4,5},{5,4},{6,7},{7,6},{8,9},{9,8},{10,11... | collective-permute-start | bytes 3145736 | tf_op jit(solution)/shard_map/ppermute | solution.py:275
  93.0 5.2 %collective-permute-start.10 = (f32[4,256]{1,0:T(4,128)S(1)}, f32[4,256]{1,0:T(4,128)S(1)}, u32[]{:S(2)}, u32[]{:S(2)}) collective-permute-start(f32[4,256]{1,0:T(4,128)S(1)} %bitcast.64), channel_id=1, source_target_pairs={{0,3},{1,2},{2,1},{3,0},{4,7},{5,6},{6,5},{7,4},{8,11},{9,10},{10,... | collective-permute-start | bytes 12296 | tf_op jit(solution)/shard_map/ppermute | solution.py:275
  94.2 3.9 %collective-permute-start.9 = (f32[4,256]{1,0:T(4,128)S(1)}, f32[4,256]{1,0:T(4,128)S(1)}, u32[]{:S(2)}, u32[]{:S(2)}) collective-permute-start(f32[4,256]{1,0:T(4,128)S(1)} %bitcast.65), channel_id=1, source_target_pairs={{0,2},{1,3},{2,0},{3,1},{4,6},{5,7},{6,4},{7,5},{8,10},{9,11},{10,... | collective-permute-start | bytes 12296 | tf_op jit(solution)/shard_map/ppermute | solution.py:275
  94.8 3.4 %collective-permute-start.4 = (f32[4,256]{1,0:T(4,128)S(1)}, f32[4,256]{1,0:T(4,128)S(1)}, u32[]{:S(2)}, u32[]{:S(2)}) collective-permute-start(f32[4,256]{1,0:T(4,128)S(1)} %slice_bitcast_fusion), channel_id=1, source_target_pairs={{0,1},{1,0},{2,3},{3,2},{4,5},{5,4},{6,7},{7,6},{8,9},{9,8},{10,11... | collective-permute-start | bytes 12296 | tf_op jit(solution)/shard_map/ppermute | solution.py:275
  96.6 8.7 %collective-permute-start.12 = (bf16[2,4,64,256]{3,2,1,0:T(8,128)(2,1)S(1)}, bf16[2,4,64,256]{3,2,1,0:T(8,128)(2,1)S(1)}, u32[]{:S(2)}, u32[]{:S(2)}) collective-permute-start(bf16[2,4,64,256]{3,2,1,0:T(8,128)(2,1)S(1)} %fusion.1), channel_id=1, source_target_pairs={{0,2},{1,3},{2,0},{3,1},{4,6},{5,7},{6,4},{7,5},{8,10},{9,11},{10,... | collective-permute-start | bytes 786440 | tf_op jit(solution)/shard_map/ppermute | solution.py:275
  98.9 8.4 %collective-permute-start.14 = (bf16[2,4,64,256]{3,2,1,0:T(8,128)(2,1)S(1)}, bf16[2,4,64,256]{3,2,1,0:T(8,128)(2,1)S(1)}, u32[]{:S(2)}, u32[]{:S(2)}) collective-permute-start(bf16[2,4,64,256]{3,2,1,0:T(8,128)(2,1)S(1)} %fusion.2), channel_id=1, source_target_pairs={{0,4},{4,0},{8,12},{12,8},{16,20},{20,16},{24,28},{28,24},{1,5},{5... | collective-permute-start | bytes 786440 | tf_op jit(solution)/shard_map/ppermute | solution.py:275
  105.4 5.0 %collective-permute-start.13 = (bf16[4,64,256]{2,1,0:T(8,128)(2,1)S(1)}, bf16[4,64,256]{2,1,0:T(8,128)(2,1)S(1)}, u32[]{:S(2)}, u32[]{:S(2)}) collective-permute-start(bf16[4,64,256]{2,1,0:T(8,128)(2,1)S(1)} %fusion.3), channel_id=1, source_target_pairs={{0,4},{4,0},{8,12},{12,8},{16,20},{20,16},{24,28},{28,24},{1,5},{5... | collective-permute-start | bytes 393224 | tf_op jit(solution)/shard_map/ppermute | solution.py:275
  107.4 5.0 %collective-permute-start.15 = (bf16[4,64,256]{2,1,0:T(8,128)(2,1)S(1)}, bf16[4,64,256]{2,1,0:T(8,128)(2,1)S(1)}, u32[]{:S(2)}, u32[]{:S(2)}) collective-permute-start(bf16[4,64,256]{2,1,0:T(8,128)(2,1)S(1)} %fusion.4), channel_id=1, source_target_pairs={{0,2},{1,3},{2,0},{3,1},{4,6},{5,7},{6,4},{7,5},{8,10},{9,11},{10,... | collective-permute-start | bytes 393224 | tf_op jit(solution)/shard_map/ppermute | solution.py:275
  112.5 4.5 %collective-permute-start.16 = (bf16[128,256]{1,0:T(8,128)(2,1)S(1)}, bf16[128,256]{1,0:T(8,128)(2,1)S(1)}, u32[]{:S(2)}, u32[]{:S(2)}) collective-permute-start(bf16[128,256]{1,0:T(8,128)(2,1)S(1)} %pad_maximum_fusion), channel_id=1, source_target_pairs={{0,8},{4,12},{8,0},{12,4},{16,24},{20,28},{24,16},{28,20},{1,9},{5... | collective-permute-start | bytes 196616 | tf_op jit(solution)/shard_map/ppermute | solution.py:275
  113.1 6.2 %collective-permute-start.17 = (bf16[128,256]{1,0:T(8,128)(2,1)S(1)}, bf16[128,256]{1,0:T(8,128)(2,1)S(1)}, u32[]{:S(2)}, u32[]{:S(2)}) collective-permute-start(bf16[128,256]{1,0:T(8,128)(2,1)S(1)} %pad_maximum_fusion.1), channel_id=1, source_target_pairs={{0,16},{4,20},{8,24},{12,28},{16,0},{20,4},{24,8},{28,12},{1,17},{... | collective-permute-start | bytes 196616 | tf_op jit(solution)/shard_map/ppermute | solution.py:275
  115.2 6.1 %collective-permute-start.18 = (bf16[128,256]{1,0:T(8,128)(2,1)S(1)}, bf16[128,256]{1,0:T(8,128)(2,1)S(1)}, u32[]{:S(2)}, u32[]{:S(2)}) collective-permute-start(bf16[128,256]{1,0:T(8,128)(2,1)S(1)} %pad_maximum_fusion.2), channel_id=1, source_target_pairs={{0,24},{4,28},{8,16},{12,20},{16,8},{20,12},{24,0},{28,4},{1,25},{... | collective-permute-start | bytes 196616 | tf_op jit(solution)/shard_map/ppermute | solution.py:275
Sparse Core Ops, SparseCore 0:
  10.7 42.9 all-gather.1

commit v3 on v0

v3 whole, which is shorter than its diff:
```python
import functools
import math

import jax
import jax.numpy as jnp
from jax import lax
from jax.experimental import pallas as pl
from jax.experimental.pallas import tpu as pltpu
from jax.sharding import PartitionSpec as P

MARGIN_BLOCK_SIZE = 64
VMEM_LIMIT = 28 * 1024 * 1024
ME, CORE, DP, COUNTS = 0, 1, 2, 3
TARGET, COEF = 0, 1
FREE = pl.CostEstimate(flops=0, bytes_accessed=0, transcendentals=0)
F32, BF16 = jnp.float32, jnp.bfloat16


def dot(a, b, contract=((1,), (0,))):
    return lax.dot_general(a, b, (contract, ((), ())), preferred_element_type=F32)


def iota(shape, axis):
    return lax.broadcasted_iota(jnp.int32, shape, axis)


def ranks(hits):
    n = hits.shape[1]
    before = (iota((n, n), 0) < iota((n, n), 1)).astype(BF16)
    return jnp.where(hits > 0, dot(hits.astype(BF16), before), -1.0)


def call(kernel, n_pages, in_specs, out_specs, out_shape, operands, scratch=(), cost=FREE):
    return pl.pallas_call(
        kernel,
        grid_spec=pltpu.PrefetchScalarGridSpec(
            num_scalar_prefetch=1,
            grid=(n_pages,),
            in_specs=in_specs,
            out_specs=out_specs,
            scratch_shapes=scratch,
        ),
        out_shape=out_shape,
        compiler_params=pltpu.CompilerParams(vmem_limit_bytes=VMEM_LIMIT),
        cost_estimate=cost,
    )(*operands)


def page_of(array, first_page=0):
    rest = array.shape[1:]
    return pl.BlockSpec((1,) + rest, lambda p, info: (p + first_page,) + (0,) * len(rest))


def all_of(array):
    return pl.BlockSpec(array.shape, lambda p, info: (0,) * len(array.shape))


def dispatch_kernel(offsets, cap, info, routes, words, *outs):
    wdev = words.shape[1]
    route = jnp.broadcast_to(routes[0], (8, wdev))
    slots = iota((cap, wdev), 0).astype(F32)
    row = iota((8, wdev), 0)
    to = jnp.full((8, wdev), -1, jnp.int32)
    for i, offset in enumerate(offsets):
        to = jnp.where(row == i, jnp.bitwise_xor(info[ME], offset), to)
    rank = ranks((route == to).astype(F32))
    picks = [(slots == rank[i : i + 1]).astype(BF16) for i in range(len(offsets))]
    rows = dot(jnp.concatenate(picks, axis=0), words[0]).astype(BF16)
    n = len(offsets) // len(outs)
    for i in range(len(offsets)):
        outs[i // n][i % n, 0] = rows[i * cap : (i + 1) * cap]


def dispatch(info, routes, words, offsets, cap, first_page, n_pages, together=1):
    width = words.shape[2]
    n = len(offsets) // together
    out = jax.ShapeDtypeStruct((together, n_pages, cap, width), BF16)
    spec = pl.BlockSpec((together, 1, cap, width), lambda p, info: (0, p, 0, 0))
    return call(
        functools.partial(dispatch_kernel, offsets, cap),
        n_pages,
        [page_of(routes, first_page), page_of(words, first_page)],
        [spec] * n,
        [out] * n,
        (info, routes, words),
    )


def table_kernel(offsets, cap, info, meta, flags, bias, table, rank_out):
    page = pl.program_id(0)
    me = info[ME]
    wdev = meta.shape[-1]
    nblk, all_blk = flags.shape[1:]
    n_rows, pps = bias.shape[1:]
    slots = iota((cap, wdev), 0).astype(F32)
    row = iota((8, wdev), 0)
    hits = jnp.zeros((8, wdev), F32)
    for i in range(len(offsets)):
        hits = jnp.where((row == i) & (meta[i, 0, 0:1, :] == me), 1.0, hits)
    rank = ranks(hits)
    rank_out[0] = rank
    t, idx = [], []
    for i, offset in enumerate(offsets):
        pick = (slots == rank[i : i + 1]).astype(F32)
        target = meta[i, 0, 1:2, :].astype(F32)
        place = iota((cap, wdev), 1) + (jnp.bitwise_xor(me, offset) * wdev + 1)
        t.append(jnp.sum(pick * target, axis=1, keepdims=True))
        idx.append(jnp.sum(pick * place.astype(F32), axis=1, keepdims=True))
    t = jnp.concatenate(t, axis=0).astype(jnp.int32)
    idx = jnp.concatenate(idx, axis=0).astype(jnp.int32) - 1
    word_block = (jnp.maximum(idx, 0) // MARGIN_BLOCK_SIZE == iota((n_rows, nblk), 1)).astype(BF16)
    margin = dot(word_block, flags[0].astype(BF16)).astype(BF16)
    first = me * (pps // MARGIN_BLOCK_SIZE)
    block = iota((all_blk, pps), 1) // MARGIN_BLOCK_SIZE
    hit = dot(margin, (iota((all_blk, pps), 0) == first + block).astype(BF16))
    own = iota((n_rows, pps), 1) // MARGIN_BLOCK_SIZE == t // MARGIN_BLOCK_SIZE
    bias[0] = jnp.where((hit > 0.5) | own, 0.0, -jnp.inf).astype(BF16)
    count = info[COUNTS + page]
    valid = (idx >= 0) & (idx < count)
    coef = jnp.where(valid, 64.0 / count.astype(F32), 0.0)
    lane = iota((n_rows, 128), 1)
    table[0] = jnp.where(lane == TARGET, t.astype(F32), jnp.where(lane == COEF, coef, 0.0))


def tables(info, meta, flags, offsets, cap, pps):
    n_homes, pages, _, wdev = meta.shape
    out = [
        jax.ShapeDtypeStruct((pages, n_homes * cap, pps), BF16),
        jax.ShapeDtypeStruct((pages, n_homes * cap, 128), F32),
        jax.ShapeDtypeStruct((pages, 8, wdev), F32),
    ]
    return call(
        functools.partial(table_kernel, offsets, cap),
        pages,
        [
            pl.BlockSpec((n_homes, 1, 2, wdev), lambda p, info: (0, p, 0, 0)),
            page_of(flags),
        ],
        [page_of(o) for o in out],
        out,
        (info, meta, flags),
    )


def weights_kernel(offsets, info, patches, *refs):
    *gathered, out, proj, sems = refs
    half = proj.shape[2]

    def copies():
        for g, ref in enumerate(gathered):
            rows = ref.shape[1]
            core = g // len(offsets)
            for i, offset in enumerate(offsets[g % len(offsets)]):
                shard = jnp.bitwise_xor(info[DP], offset)
                to = proj.at[
                    jnp.bitwise_xor(info[CORE], core),
                    pl.ds(pl.multiple_of(shard * rows, rows), rows),
                ]
                yield ref.at[i], to

    @pl.when(pl.program_id(0) == 0)
    def _():
        started = [
            pltpu.make_async_copy(a, b, sems.at[i]) for i, (a, b) in enumerate(copies())
        ]
        for copy in started:
            copy.start()
        for copy in started:
            copy.wait()

    pat = patches[0]
    out[0] = sum(
        dot(proj[h], pat[:, h * half : (h + 1) * half], ((1,), (1,))) for h in range(2)
    ).astype(BF16)


def weights(info, patches, gathered, offsets):
    pages, pps, width = patches.shape
    out = jax.ShapeDtypeStruct((pages, width, pps), BF16)
    return call(
        functools.partial(weights_kernel, offsets),
        pages,
        [page_of(patches)] + [pl.BlockSpec(memory_space=pl.ANY)] * len(gathered),
        page_of(out),
        out,
        (info, patches, *gathered),
        [
            pltpu.VMEM((2, width, width // 2), BF16),
            pltpu.SemaphoreType.DMA((sum(g.shape[0] for g in gathered),)),
        ],
    )


def page_kernel(n_homes, n_pages, has_acc, last, info, bias, table, rank, weight, patches, *refs):
    refs = list(refs)
    words, rest = refs[:n_homes], refs[n_homes:]
    acc_in = rest.pop(0) if has_acc else None
    n_outs = 4 if last else 1
    outs, (loss, x_t, dqs, *rest) = rest[:n_outs], rest[n_outs:]
    page = pl.program_id(0)
    pps, width = patches.shape[1:]
    cap = words[0].shape[2]
    n_rows = n_homes * cap
    wcol = outs[0].shape[-1]
    n_cols = width // wcol
    scale = 2.0 / math.sqrt(width)
    if has_acc:
        acc, sem = rest
        acc_copy = pltpu.make_async_copy(acc_in, acc, sem)

        @pl.when(page == 0)
        def _():
            acc_copy.start()

    x = jnp.concatenate([w[0, 0] for w in words], axis=0)
    if x_t.shape[0] == n_pages:
        x_t[page] = x.T
    else:
        x_t[0, :, pl.ds(pl.multiple_of(page * n_rows, n_rows), n_rows)] = x.T
    pat = patches[0]
    scores = dot(x, weight[0]) * scale
    is_target = iota((n_rows, pps), 1) == table[0, :, TARGET : TARGET + 1].astype(jnp.int32)
    coef = table[0, :, COEF : COEF + 1]
    masked = scores + bias[0].astype(F32)
    top = jnp.max(masked, axis=1, keepdims=True)
    expo = jnp.exp(masked - top)
    total = jnp.sum(expo, axis=1, keepdims=True)
    target_score = jnp.sum(jnp.where(is_target, scores, 0.0), axis=1, keepdims=True)
    row_loss = jnp.where(coef > 0, top + jnp.log(total) - target_score, 0.0)
    share = expo * (1.0 / total)
    dscore = (coef * jnp.where(is_target, share - 1.0, share)).astype(BF16)
    dqs[pl.ds(pl.multiple_of(page * n_rows, n_rows), n_rows), :] = (
        dot(dscore, pat) * scale
    ).astype(BF16)
    slots = iota((cap, rank.shape[2]), 0).astype(F32)
    for r in range(n_homes):
        picked = jnp.where(slots == rank[0, r : r + 1, :], row_loss[r * cap : (r + 1) * cap], 0.0)
        loss[0, r : r + 1, :] = jnp.sum(picked, axis=0, keepdims=True)

    @pl.when(page == n_pages - 1)
    def _():
        if has_acc:
            acc_copy.wait()

        def gradient(j):
            got = acc[j] if has_acc else 0.0
            depth = x_t.shape[2]
            for g in range(x_t.shape[0]):
                some = pl.ds(pl.multiple_of(j * wcol, wcol), wcol)
                got += dot(x_t[g], dqs[g * depth : (g + 1) * depth, some])
            return got

        def store(halves, y, got):
            _, lows, highs, cut, _ = halves[0].shape
            for part in range(2 * lows * highs):
                rows = got[part * cut : (part + 1) * cut]
                out = halves[part % 2]
                out[y, part // 2 % lows, part // (2 * lows)] = rows.astype(out.dtype)

        if last:
            for y in range(n_cols // 2):
                store(outs[2:], y, gradient(2 * y + 1 - info[CORE]))
            for y in range(n_cols // 2):
                store(outs[:2], y, gradient(2 * y + info[CORE]))
        else:
            for j in range(n_cols):
                outs[0][j] = gradient(j)


def run_pages(n_seq, n_high, info, weight, patches, table, words, acc, first_page, last):
    _, n_pages, cap, width = words[0].shape
    n_homes = len(words)
    n_rows = n_homes * cap
    wdev = table[2].shape[2]
    wcol = width // n_seq
    has_acc = acc is not None
    if last:
        form = (n_seq // 2, 2, n_high, width // (4 * n_high), wcol)
        out = [jax.ShapeDtypeStruct(form, t) for t in (F32, F32, BF16, BF16)]
    else:
        out = [jax.ShapeDtypeStruct((n_seq, width, wcol), F32)]
    loss = jax.ShapeDtypeStruct((n_pages, n_homes, wdev), F32)
    groups = 1 if n_rows % 128 == 0 else n_pages
    scratch = [
        pltpu.VMEM((groups, width, n_pages * n_rows // groups), BF16),
        pltpu.VMEM((n_pages * n_rows, width), BF16),
    ]
    if has_acc:
        scratch += [pltpu.VMEM((n_seq, width, wcol), F32), pltpu.SemaphoreType.DMA(())]
    return call(
        functools.partial(page_kernel, n_homes, n_pages, has_acc, last),
        n_pages,
        [page_of(a, first_page) for a in (*table, weight, patches)]
        + [pl.BlockSpec((1, 1, cap, width), lambda p, info: (0, p, 0, 0))] * n_homes
        + [pl.BlockSpec(memory_space=pl.ANY)] * has_acc,
        [all_of(o) for o in out] + [page_of(loss)],
        out + [loss],
        (info, *table, weight, patches, *words) + ((acc,) if has_acc else ()),
        scratch,
    )


def exchange(x, axis, offset):
    n = lax.axis_size(axis)
    return lax.ppermute(x, axis, [(i, i ^ offset) for i in range(n)])


def pick(x, i, axis=0):
    return lax.dynamic_index_in_dim(x, i, axis, keepdims=False)


def pick_sum(terms, i, axis=0):
    return sum(pick(t, i, axis).astype(F32) for t in terms)


def local(words, patches, proj, routes, targets, counts, flags):
    pages, wdev, width = words.shape
    pps = patches.shape[1]
    n_seq = lax.axis_size("seq")
    n_dp = lax.axis_size("dp")
    me = lax.axis_index("seq")
    my_dp = lax.axis_index("dp")
    core, y, low, high = me % 2, me // 2, my_dp % 2, my_dp // 2
    n_y, n_high = n_seq // 2, n_dp // 2
    cap = 2 * wdev // n_seq
    half = width // 2
    near, far = (0, 1), tuple(range(2, n_seq))

    info = jnp.concatenate([jnp.stack([me, core, my_dp]).astype(jnp.int32), counts])
    routes = routes.reshape(pages, 1, wdev)

    cut = pages - 1
    both = dispatch(info, routes, words, far, cap, 0, cut, 2)
    held, proj, both = lax.optimization_barrier((info, proj, both))
    rest = dispatch(held, routes, words, far, cap, cut, pages - cut)
    stay, across = dispatch(held, routes, words, near, cap, 0, pages)
    both = [exchange(rows, "seq", 2 * (k + 1)) for k, rows in enumerate(both)]

    pair = jnp.concatenate([routes, targets.reshape(pages, 1, wdev)], axis=1)
    meta_near = jnp.stack([pair, exchange(pair, "seq", 1)])
    table_near = tables(info, meta_near, flags, near, cap, pps)
    meta_far = jnp.concatenate([exchange(meta_near, "seq", 2 * k) for k in range(1, n_y)], axis=0)

    piece, bit = lax.dynamic_slice_in_dim(proj, core * half, half, 1)[None], 1
    pieces = [(piece, 0)]
    while bit < n_high:
        other = exchange(piece, "dp", 2 * bit)
        pieces = [(piece, 0), (other, bit)]
        bit *= 2
        if bit < n_high:
            piece = jnp.concatenate([piece, other], axis=0)
    gathered, offsets = [], []
    for piece, start in pieces:
        gathered += [piece, exchange(piece, "dp", 1)]
        offsets += [[2 * (start + i) + low for i in range(piece.shape[0])] for low in range(2)]
    gathered, rest, across, table_near = lax.optimization_barrier(
        (gathered, rest, across, table_near)
    )
    gathered += [exchange(piece, "seq", 1) for piece in gathered]
    rest = [exchange(rows, "seq", r) for rows, r in zip(rest, far)]
    across = exchange(across, "seq", 1)

    weight = weights(info, patches, gathered, offsets)
    both, weight, meta_far = lax.optimization_barrier((both, weight, meta_far))
    table_far = tables(info, meta_far, flags, far, cap, pps)
    first = [x for rows in both for x in (rows, exchange(rows[1:], "seq", 1))]
    run = functools.partial(run_pages, n_seq, n_high, info, weight, patches)
    acc, loss = run(table_near, [stay, across], None, 0, False)
    word_loss = [loss[:, 0], exchange(loss[:, 1], "seq", 1)]
    acc, loss_a = run(table_far, first, acc, 0, False)
    *out, loss_b = run(table_far, rest, acc, cut, True)
    losses = jnp.concatenate([loss_a, loss_b], axis=0)

    terms = [[out[h], exchange(out[2 + h], "seq", 1)] for h in range(2)]

    def over_y(terms):
        total = pick_sum(terms, y)
        for k in range(1, n_y):
            other = pick_sum(terms, jnp.bitwise_xor(y, k)).astype(BF16)
            total = total + exchange(other, "seq", 2 * k)
        return total

    def over_low(terms, axis):
        other = pick_sum(terms, 1 - low, axis).astype(BF16)
        return pick_sum(terms, low, axis) + exchange(other, "dp", 1)

    one = over_low([over_y(terms[0])], 0)
    two = over_y([over_low(terms[1], 1)])
    grad = jnp.concatenate([pick(one, high), pick(two, high)], axis=0)
    for k in range(1, n_high):
        to = jnp.bitwise_xor(high, k)
        other = jnp.concatenate([pick(one, to), pick(two, to)], axis=0).astype(BF16)
        grad = grad + exchange(other, "dp", 2 * k)

    for i, r in enumerate(far):
        word_loss.append(exchange(losses[:, i], "seq", r))
    return (sum(word_loss), grad)


def solution(mesh):
    in_specs = (
        P("dp", "seq", None),
        P("dp", "seq", None),
        P("dp", None),
        P("dp", "seq", None),
        P("dp", "seq"),
        P("dp"),
        P("dp", None, None),
    )
    out_specs = (P("dp", "seq"), P("dp", "seq"))
    return jax.shard_map(local, mesh=mesh, in_specs=in_specs, out_specs=out_specs, check_vma=False)
```

time: 326 us -> 116 us (0.36)
  waiting for transfers between devices: 185 us -> 31.8 us
  blocking collectives: 57.9 us -> 0 us
  Pallas kernels: 0 us -> 42.6 us
  matrix products: 35.9 us -> 0 us
  between operations: 13.9 us -> 0.94 us
  starting transfers between devices: 12.8 us -> 24.7 us
  other arithmetic: 6.74 us -> 2.49 us
    reduce_scatter x2 -> x0, waiting for transfers between devices: 102 us -> none  [the longest x1 86.2 us: local(): lax.psum_scatter(jnp.einsum('rc,rd->cd', columns, right, preferred_elemen...]
    all_to_all x2 -> x0, blocking collectives: 57.9 us -> none  [the longest x1 51.6 us: local(): lax.all_to_all(dquery, 'seq', split_axis=0, concat_axis=0, tiled=True)]
    all_to_all x3 -> x0, waiting for transfers between devices: 45 us -> none  [the longest x1 45 us: local(): lax.all_to_all(q_buf, 'seq', split_axis=0, concat_axis=0, tiled=True)]
    pallas_call x0 -> x9, Pallas kernels: none -> 42.6 us  [call(): pl.pallas_call(kernel, grid_spec=pltpu.PrefetchScalarGridSpec(num_scalar_...]
    all_gather x1 -> x0, waiting for transfers between devices: 36.6 us -> none  [local(): lax.all_gather(proj, 'dp', axis=0, tiled=True)]
    dot_general x8 -> x0, matrix products: 35.9 us -> none  [the longest x1 7.62 us: local(): jnp.einsum('rc,rd->cd', columns, right, preferred_element_type=jnp.float32)]
    ppermute x0 -> x27, waiting for transfers between devices: none -> 31.8 us  [exchange(): return lax.ppermute(x, axis, [(i, i ^ offset) for i in range(n)])]
    ppermute x0 -> x27, starting transfers between devices: none -> 24.7 us  [exchange(): return lax.ppermute(x, axis, [(i, i ^ offset) for i in range(n)])]
  transfers between devices with their start and end apart: 6 -> 27, of which waited for: 4 -> 12; matrix products, arithmetic and copies ran while one was open for 11% -> 3% of each run, Pallas kernels for 0% -> 31%
where the time goes in v3:
time: 116 us; the launch traced here: 115 us
  Pallas kernels  42.6 us (37%)
  waiting for transfers between devices  31.8 us (27%)
  starting transfers between devices  24.7 us (21%)
  local copies, waits for them, and re-layouts  12.7 us (11%)
  other arithmetic  2.49 us (2%)
    pallas_call x9, Pallas kernels, call(): pl.pallas_call(kernel, grid_spec=pltpu.PrefetchScalarGridSpec(num_scalar_...  42.6 us
    ppermute x27, waiting for transfers between devices, exchange(): return lax.ppermute(x, axis, [(i, i ^ offset) for i in range(n)])  31.8 us
    ppermute x27, starting transfers between devices, exchange(): return lax.ppermute(x, axis, [(i, i ^ offset) for i in range(n)])  24.7 us
    unnamed x31, local copies, waits for them, and re-layouts  10.5 us
  transfers between devices with their start and end apart: 27, of which 12 were waited for; matrix products, arithmetic and copies ran while one was open for 3% of the time, Pallas kernels for 31%

profile of v3, /device:TPU:0, one launch (start us, length us, event | category | flops | bytes accessed | tf_op | source)
XLA Modules:
  0.0 115.2 jit_solution(962702578473482207)
XLA Ops:
  0.7 0.8 pad_add_fusion.2.info
  1.5 1.6 %copy-done.6 = bf16[4,256,1024]{2,1,0:T(8,128)(2,1)S(1)} copy-done((bf16[4,256,1024]{2,1,0:T(8,128)(2,1)S(1)}, bf16[4,256,1024]{2,1,0:T(8,128)(2,1)}, u32[]{:S(2)}) %copy-start.6) | copy-done | bytes 2097176
  3.0 0.7 copy-done.11
  3.7 3.1 %shard_map.86 = bf16[2,3,128,1024]{3,2,1,0:T(8,128)(2,1)} custom-call(s32[7]{0:T(128)S(1)} %pad_add_fusion.2.info, s32[4,1,256]{2,1,0:T(1,128)S(1)} %bitcast.59, bf16[4,256,1024]{2,1,0:T(8,128)(2,1)S(1)} %copy-done.6), custom_call_target="tpu_custom_call" | custom-call | tf_op jit(solution)/shard_map/pallas_call | solution.py:34
  6.8 3.0 %collective-permute-start.5 = (bf16[2,3,128,1024]{3,2,1,0:T(8,128)(2,1)}, bf16[2,3,128,1024]{3,2,1,0:T(8,128)(2,1)}, u32[]{:S(2)}, u32[]{:S(2)}) collective-permute-start(bf16[2,3,128,1024]{3,2,1,0:T(8,128)(2,1)} %shard_map.86), channel_id=1, source_target_pairs={{0,2},{1,3},{2,0},{3,1},{4,6},{5,7},{6,4},{7,5},{8,10},{9,11},{10,... | collective-permute-start | bytes 4718600 | tf_op jit(solution)/shard_map/ppermute | solution.py:305
  9.8 1.6 %collective-permute-start = (bf16[1,128,512]{2,1,0:T(8,128)(2,1)S(1)}, bf16[1,128,512]{2,1,0:T(8,128)(2,1)S(1)}, u32[]{:S(2)}, u32[]{:S(2)}) collective-permute-start(bf16[1,128,512]{2,1,0:T(8,128)(2,1)S(1)} %dynamic-slice_bitcast_fusion), channel_id=1, source_target_pairs={{0,8},{4,12},{8,0},{12,4},{16,24},{20,28},{24,16},{28,20},{1,9},{5... | collective-permute-start | bytes 393224 | tf_op jit(solution)/shard_map/ppermute | solution.py:305
  11.4 3.4 %collective-permute-done = bf16[1,128,512]{2,1,0:T(8,128)(2,1)S(1)} collective-permute-done((bf16[1,128,512]{2,1,0:T(8,128)(2,1)S(1)}, bf16[1,128,512]{2,1,0:T(8,128)(2,1)S(1)}, u32[]{:S(2)}, u32[]{:S(2)}) %collective-permute-start) | collective-permute-done | bytes 131104 | tf_op jit(solution)/shard_map/ppermute | solution.py:305
  14.9 2.7 %collective-permute-start.2 = (bf16[2,128,512]{2,1,0:T(8,128)(2,1)S(1)}, bf16[2,128,512]{2,1,0:T(8,128)(2,1)S(1)}, u32[]{:S(2)}, u32[]{:S(2)}) collective-permute-start(bf16[2,128,512]{2,1,0:T(8,128)(2,1)S(1)} %pad_maximum_fusion.refs_0_), channel_id=1, source_target_pairs={{0,16},{4,20},{8,24},{12,28},{16,0},{20,4},{24,8},{28,12},{1,17},{... | collective-permute-start | bytes 786440 | tf_op jit(solution)/shard_map/ppermute | solution.py:305
  17.5 1.5 %collective-permute-start.1 = (bf16[2,128,512]{2,1,0:T(8,128)(2,1)S(1)}, bf16[2,128,512]{2,1,0:T(8,128)(2,1)S(1)}, u32[]{:S(2)}, u32[]{:S(2)}) collective-permute-start(bf16[2,128,512]{2,1,0:T(8,128)(2,1)S(1)} %pad_maximum_fusion.refs_0_), channel_id=1, source_target_pairs={{0,4},{4,0},{8,12},{12,8},{16,20},{20,16},{24,28},{28,24},{1,5},{5... | collective-permute-start | bytes 786440 | tf_op jit(solution)/shard_map/ppermute | solution.py:305
  19.0 9.5 %collective-permute-done.2.refs_2_ = bf16[2,128,512]{2,1,0:T(8,128)(2,1)S(1)} collective-permute-done((bf16[2,128,512]{2,1,0:T(8,128)(2,1)S(1)}, bf16[2,128,512]{2,1,0:T(8,128)(2,1)S(1)}, u32[]{:S(2)}, u32[]{:S(2)}) %collective-permute-start.2) | collective-permute-done | bytes 262176 | tf_op jit(solution)/shard_map/ppermute | solution.py:305
  28.5 1.5 %collective-permute-start.3 = (bf16[2,128,512]{2,1,0:T(8,128)(2,1)S(1)}, bf16[2,128,512]{2,1,0:T(8,128)(2,1)S(1)}, u32[]{:S(2)}, u32[]{:S(2)}) collective-permute-start(bf16[2,128,512]{2,1,0:T(8,128)(2,1)S(1)} %collective-permute-done.2.refs_2_), channel_id=1, source_target_pairs={{0,4},{4,0},{8,12},{12,8},{16,20},{20,16},{24,28},{28,24},{1,5},{5... | collective-permute-start | bytes 786440 | tf_op jit(solution)/shard_map/ppermute | solution.py:305
  30.1 3.4 %shard_map.88 = (bf16[1,4,128,1024]{3,2,1,0:T(8,128)(2,1)S(1)}, bf16[1,4,128,1024]{3,2,1,0:T(8,128)(2,1)}) custom-call(s32[7]{0:T(128)S(1)} %pad_add_fusion.2.info, s32[4,1,256]{2,1,0:T(1,128)S(1)} %bitcast.61, bf16[4,256,1024]{2,1,0:T(8,128)(2,1)S(1)} %copy-done.7), custom_call_target="tpu_custom_call" | custom-call | tf_op jit(solution)/shard_map/pallas_call | solution.py:34
  33.4 1.7 %shard_map.87 = (bf16[1,1,128,1024]{3,2,1,0:T(8,128)(2,1)}, bf16[1,1,128,1024]{3,2,1,0:T(8,128)(2,1)}) custom-call(s32[7]{0:T(128)S(1)} %pad_add_fusion.2.info, s32[4,1,256]{2,1,0:T(1,128)S(1)} %bitcast.62, bf16[4,256,1024]{2,1,0:T(8,128)(2,1)S(1)} %copy-done.7), custom_call_target="tpu_custom_call" | custom-call | tf_op jit(solution)/shard_map/pallas_call | solution.py:34
  35.2 3.5 %shard_map.89 = (bf16[4,256,512]{2,1,0:T(8,128)(2,1)S(1)}, f32[4,256,128]{2,1,0:T(8,128)S(1)}, f32[4,8,256]{2,1,0:T(8,128)S(1)}) custom-call(s32[7]{0:T(128)S(1)} %pad_add_fusion.2.info, s32[2,4,2,256]{3,2,1,0:T(2,128)S(1)} %pad_add_fusion.meta, s32[4,16,32]{2,1,0:T(8,128)S(1)} %copy-done.10), custom_call_target="tpu_custom_call" | custom-call | tf_op jit(solution)/shard_map/pallas_call | solution.py:34
  38.7 0.8 copy-done.8
  39.5 0.5 collective-permute-start.6
  40.6 0.6 collective-permute-done.6.refs_4_
  41.5 0.5 collective-permute-start.10
  42.3 8.7 %shard_map.90.weight = bf16[4,1024,512]{2,1,0:T(8,128)(2,1)S(1)} custom-call(s32[7]{0:T(128)S(1)} %pad_add_fusion.2.info, bf16[4,512,1024]{2,1,0:T(8,128)(2,1)S(1)} %copy-done.1, bf16[2,128,512]{2,1,0:T(8,128)(2,1)S(1)} %pad_maximum_fusion.refs_0_, bf16[2,128,512]{2,1,0:T(8,128)(2,1)S(1)} %collective-permute-done.1.refs_1_, ...), custom_call_target="tpu_custom_call" | custom-call | tf_op jit(solution)/shard_map/pallas_call | solution.py:34
  51.0 2.0 %copy-done.4 = bf16[4,1024,512]{2,1,0:T(8,128)(2,1)} copy-done((bf16[4,1024,512]{2,1,0:T(8,128)(2,1)}, bf16[4,1024,512]{2,1,0:T(8,128)(2,1)S(1)}, u32[]{:S(2)}) %copy-start.4) | copy-done | bytes 4194328
  53.0 2.1 %slice.17 = bf16[1,3,128,1024]{3,2,1,0:T(8,128)(2,1)} slice(bf16[2,3,128,1024]{3,2,1,0:T(8,128)(2,1)} %collective-permute-done.5.refs_0_), slice={[1:2], [0:3], [0:128], [0:1024]} | slice | bytes 1572864 | tf_op jit(solution)/shard_map/slice | solution.py:366
  55.4 1.0 collective-permute-start.14
  56.4 0.5 collective-permute-start.15
  56.9 3.5 %shard_map.92 = (bf16[4,256,512]{2,1,0:T(8,128)(2,1)S(1)}, f32[4,256,128]{2,1,0:T(8,128)S(1)}, f32[4,8,256]{2,1,0:T(8,128)S(1)}) custom-call(s32[7]{0:T(128)S(1)} %pad_add_fusion.2.info, s32[2,4,2,256]{3,2,1,0:T(2,128)S(1)} %collective-permute-done.10.meta, s32[4,16,32]{2,1,0:T(8,128)S(1)} %copy-done.10), custom_call_target="tpu_custom_call" | custom-call | tf_op jit(solution)/shard_map/pallas_call | solution.py:34
  60.4 2.2 %copy-done.2 = bf16[4,512,1024]{2,1,0:T(8,128)(2,1)S(1)} copy-done((bf16[4,512,1024]{2,1,0:T(8,128)(2,1)S(1)}, bf16[4,512,1024]{2,1,0:T(8,128)(2,1)}, u32[]{:S(2)}) %copy-start.2) | copy-done | bytes 4194328
  62.6 2.2 %copy-done.5 = bf16[4,1024,512]{2,1,0:T(8,128)(2,1)S(1)} copy-done((bf16[4,1024,512]{2,1,0:T(8,128)(2,1)S(1)}, bf16[4,1024,512]{2,1,0:T(8,128)(2,1)}, u32[]{:S(2)}) %copy-start.5) | copy-done | bytes 4194328
  64.8 1.0 copy-done.9
  65.9 7.7 %shard_map.91 = (f32[4,1024,256]{2,1,0:T(8,128)S(1)}, f32[4,2,256]{2,1,0:T(2,128)S(1)}) custom-call(s32[7]{0:T(128)S(1)} %pad_add_fusion.2.info, bf16[4,256,512]{2,1,0:T(8,128)(2,1)S(1)} %get-tuple-element.45.bias, f32[4,256,128]{2,1,0:T(8,128)S(1)} %copy-done.9, f32[4,8,256]{2,1,0:T(8,128)S(1)} %get-tuple-element.47.rank, ...), custom_call_target="tpu_custom_call" | custom-call | tf_op jit(solution)/shard_map/pallas_call | solution.py:34
  73.6 7.3 %shard_map.93 = (f32[4,1024,256]{2,1,0:T(8,128)S(1)}, f32[3,2,256]{2,1,0:T(2,128)S(1)}) custom-call(s32[7]{0:T(128)S(1)} %pad_add_fusion.2.info, bf16[4,256,512]{2,1,0:T(8,128)(2,1)S(1)} %get-tuple-element.58.bias, f32[4,256,128]{2,1,0:T(8,128)S(1)} %get-tuple-element.59.table, f32[4,8,256]{2,1,0:T(8,128)S(1)} %get-tuple-element.60.rank, ...), custom_call_target="tpu_custom_call" | custom-call | tf_op jit(solution)/shard_map/pallas_call | solution.py:34
  80.9 3.7 %shard_map.94 = (f32[2,2,4,64,256]{4,3,2,1,0:T(8,128)S(1)}, f32[2,2,4,64,256]{4,3,2,1,0:T(8,128)S(1)}, bf16[2,2,4,64,256]{4,3,2,1,0:T(8,128)(2,1)S(1)}, bf16[2,2...) custom-call(s32[7]{0:T(128)S(1)} %pad_add_fusion.2.info, bf16[4,256,512]{2,1,0:T(8,128)(2,1)S(1)} %get-tuple-element.58.bias, ...), custom_call_target="tpu_custom_call" | custom-call | tf_op jit(solution)/shard_map/pallas_call | solution.py:34
  84.6 0.7 collective-permute-start.18
  85.9 1.1 collective-permute-start.16
  87.4 1.1 collective-permute-start.19
  88.6 0.9 collective-permute-done.16
  89.5 0.5 collective-permute-done.17
  90.0 0.6 fusion.14
  90.7 0.6 collective-permute-start.22
  91.3 5.2 %collective-permute-done.19 = bf16[2,4,64,256]{3,2,1,0:T(8,128)(2,1)S(1)} collective-permute-done((bf16[2,4,64,256]{3,2,1,0:T(8,128)(2,1)S(1)}, bf16[2,4,64,256]{3,2,1,0:T(8,128)(2,1)S(1)}, u32[]{:S(2)}, u32[]{:S(2)}) %collective-permute-start.19) | collective-permute-done | bytes 262176 | tf_op jit(solution)/shard_map/ppermute | solution.py:305
  96.5 0.6 collective-permute-start.20
  97.2 1.9 %collective-permute-done.22 = bf16[2,4,64,256]{3,2,1,0:T(8,128)(2,1)S(1)} collective-permute-done((bf16[2,4,64,256]{3,2,1,0:T(8,128)(2,1)S(1)}, bf16[2,4,64,256]{3,2,1,0:T(8,128)(2,1)S(1)}, u32[]{:S(2)}, u32[]{:S(2)}) %collective-permute-start.22) | collective-permute-done | bytes 262176 | tf_op jit(solution)/shard_map/ppermute | solution.py:305
  99.2 1.1 collective-permute-start.23
  100.3 1.6 %collective-permute-done.20 = bf16[4,64,256]{2,1,0:T(8,128)(2,1)S(1)} collective-permute-done((bf16[4,64,256]{2,1,0:T(8,128)(2,1)S(1)}, bf16[4,64,256]{2,1,0:T(8,128)(2,1)S(1)}, u32[]{:S(2)}, u32[]{:S(2)}) %collective-permute-start.20) | collective-permute-done | bytes 131104 | tf_op jit(solution)/shard_map/ppermute | solution.py:305
  101.9 2.3 %collective-permute-done.23 = bf16[4,64,256]{2,1,0:T(8,128)(2,1)S(1)} collective-permute-done((bf16[4,64,256]{2,1,0:T(8,128)(2,1)S(1)}, bf16[4,64,256]{2,1,0:T(8,128)(2,1)S(1)}, u32[]{:S(2)}, u32[]{:S(2)}) %collective-permute-start.23) | collective-permute-done | bytes 131104 | tf_op jit(solution)/shard_map/ppermute | solution.py:305
  104.3 0.7 collective-permute-start.24
  105.0 3.4 %collective-permute-start.25 = (bf16[128,256]{1,0:T(8,128)(2,1)S(1)}, bf16[128,256]{1,0:T(8,128)(2,1)S(1)}, u32[]{:S(2)}, u32[]{:S(2)}) collective-permute-start(bf16[128,256]{1,0:T(8,128)(2,1)S(1)} %pad_maximum_fusion.2), channel_id=1, source_target_pairs={{0,16},{4,20},{8,24},{12,28},{16,0},{20,4},{24,8},{28,12},{1,17},{... | collective-permute-start | bytes 196616 | tf_op jit(solution)/shard_map/ppermute | solution.py:305
  108.8 3.3 %collective-permute-done.25 = bf16[128,256]{1,0:T(8,128)(2,1)S(1)} collective-permute-done((bf16[128,256]{1,0:T(8,128)(2,1)S(1)}, bf16[128,256]{1,0:T(8,128)(2,1)S(1)}, u32[]{:S(2)}, u32[]{:S(2)}) %collective-permute-start.25) | collective-permute-done | bytes 65568 | tf_op jit(solution)/shard_map/ppermute | solution.py:305
  112.1 2.4 %collective-permute-done.26 = bf16[128,256]{1,0:T(8,128)(2,1)S(1)} collective-permute-done((bf16[128,256]{1,0:T(8,128)(2,1)S(1)}, bf16[128,256]{1,0:T(8,128)(2,1)S(1)}, u32[]{:S(2)}, u32[]{:S(2)}) %collective-permute-start.26) | collective-permute-done | bytes 65568 | tf_op jit(solution)/shard_map/ppermute | solution.py:305
  114.5 0.7 fusion.5
  (74 shorter events, 3.6 us)
Async XLA Ops:
  0.6 9.2 %copy-start = (bf16[128,1024]{1,0:T(8,128)(2,1)S(1)}, bf16[128,1024]{1,0:T(8,128)(2,1)}, u32[]{:S(2)}) copy-start(bf16[128,1024]{1,0:T(8,128)(2,1)} %param.9) | copy-start | bytes 786436
  0.6 29.3 %copy-start.12 = (s32[4,256,1]{1,2,0:T(1,128)S(1)}, s32[4,256,1]{1,2,0:T(1,128)}, u32[]{:S(2)}) copy-start(s32[4,256,1]{1,2,0:T(1,128)} %param.10) | copy-start | bytes 12292
  0.7 29.3 %copy-start.13 = (s32[4,256]{1,0:T(4,128)S(1)}, s32[4,256]{1,0:T(4,128)}, u32[]{:S(2)}) copy-start(s32[4,256]{1,0:T(4,128)} %param.11) | copy-start | bytes 12292
  1.5 1.6 %copy-start.6 = (bf16[4,256,1024]{2,1,0:T(8,128)(2,1)S(1)}, bf16[4,256,1024]{2,1,0:T(8,128)(2,1)}, u32[]{:S(2)}) copy-start(bf16[4,256,1024]{2,1,0:T(8,128)(2,1)} %words.5) | copy-start | bytes 6291460
  3.0 0.7 copy-start.11
  3.7 26.3 %copy-start.7 = (bf16[4,256,1024]{2,1,0:T(8,128)(2,1)S(1)}, bf16[4,256,1024]{2,1,0:T(8,128)(2,1)}, u32[]{:S(2)}) copy-start(bf16[4,256,1024]{2,1,0:T(8,128)(2,1)} %words.5) | copy-start | bytes 6291460
  3.7 31.4 %copy-start.10 = (s32[4,16,32]{2,1,0:T(8,128)S(1)}, s32[4,16,32]{2,1,0:T(8,128)}, u32[]{:S(2)}) copy-start(s32[4,16,32]{2,1,0:T(8,128)} %flags.3) | copy-start | bytes 24580
  6.8 46.2 %collective-permute-start.5 = (bf16[2,3,128,1024]{3,2,1,0:T(8,128)(2,1)}, bf16[2,3,128,1024]{3,2,1,0:T(8,128)(2,1)}, u32[]{:S(2)}, u32[]{:S(2)}) collective-permute-start(bf16[2,3,128,1024]{3,2,1,0:T(8,128)(2,1)} %shard_map.86), channel_id=1, source_target_pairs={{0,2},{1,3},{2,0},{3,1},{4,6},{5,7},{6,4},{7,5},{8,10},{9,11},{10,... | collective-permute-start | bytes 4718600 | tf_op jit(solution)/shard_map/ppermute | solution.py:305
  9.8 32.5 %copy-start.1 = (bf16[4,512,1024]{2,1,0:T(8,128)(2,1)S(1)}, bf16[4,512,1024]{2,1,0:T(8,128)(2,1)}, u32[]{:S(2)}) copy-start(bf16[4,512,1024]{2,1,0:T(8,128)(2,1)} %patches.7) | copy-start | bytes 12582916
  9.8 5.0 %collective-permute-start = (bf16[1,128,512]{2,1,0:T(8,128)(2,1)S(1)}, bf16[1,128,512]{2,1,0:T(8,128)(2,1)S(1)}, u32[]{:S(2)}, u32[]{:S(2)}) collective-permute-start(bf16[1,128,512]{2,1,0:T(8,128)(2,1)S(1)} %dynamic-slice_bitcast_fusion), channel_id=1, source_target_pairs={{0,8},{4,12},{8,0},{12,4},{16,24},{20,28},{24,16},{28,20},{1,9},{5... | collective-permute-start | bytes 393224 | tf_op jit(solution)/shard_map/ppermute | solution.py:305
  14.9 13.6 %collective-permute-start.2 = (bf16[2,128,512]{2,1,0:T(8,128)(2,1)S(1)}, bf16[2,128,512]{2,1,0:T(8,128)(2,1)S(1)}, u32[]{:S(2)}, u32[]{:S(2)}) collective-permute-start(bf16[2,128,512]{2,1,0:T(8,128)(2,1)S(1)} %pad_maximum_fusion.refs_0_), channel_id=1, source_target_pairs={{0,16},{4,20},{8,24},{12,28},{16,0},{20,4},{24,8},{28,12},{1,17},{... | collective-permute-start | bytes 786440 | tf_op jit(solution)/shard_map/ppermute | solution.py:305
  17.5 22.0 %collective-permute-start.1 = (bf16[2,128,512]{2,1,0:T(8,128)(2,1)S(1)}, bf16[2,128,512]{2,1,0:T(8,128)(2,1)S(1)}, u32[]{:S(2)}, u32[]{:S(2)}) collective-permute-start(bf16[2,128,512]{2,1,0:T(8,128)(2,1)S(1)} %pad_maximum_fusion.refs_0_), channel_id=1, source_target_pairs={{0,4},{4,0},{8,12},{12,8},{16,20},{20,16},{24,28},{28,24},{1,5},{5... | collective-permute-start | bytes 786440 | tf_op jit(solution)/shard_map/ppermute | solution.py:305
  28.5 11.0 %collective-permute-start.3 = (bf16[2,128,512]{2,1,0:T(8,128)(2,1)S(1)}, bf16[2,128,512]{2,1,0:T(8,128)(2,1)S(1)}, u32[]{:S(2)}, u32[]{:S(2)}) collective-permute-start(bf16[2,128,512]{2,1,0:T(8,128)(2,1)S(1)} %collective-permute-done.2.refs_2_), channel_id=1, source_target_pairs={{0,4},{4,0},{8,12},{12,8},{16,20},{20,16},{24,28},{28,24},{1,5},{5... | collective-permute-start | bytes 786440 | tf_op jit(solution)/shard_map/ppermute | solution.py:305
  30.0 5.2 %collective-permute-start.4 = (s32[4,2,256]{2,1,0:T(2,128)S(1)}, s32[4,2,256]{2,1,0:T(2,128)S(1)}, u32[]{:S(2)}, u32[]{:S(2)}) collective-permute-start(s32[4,2,256]{2,1,0:T(2,128)S(1)} %get-tuple-element.81), channel_id=1, source_target_pairs={{0,1},{1,0},{2,3},{3,2},{4,5},{5,4},{6,7},{7,6},{8,9},{9,8},{10,11... | collective-permute-start | bytes 24584 | tf_op jit(solution)/shard_map/ppermute | solution.py:305
  38.7 0.8 copy-start.8
  39.5 1.6 %collective-permute-start.6 = (bf16[2,128,512]{2,1,0:T(8,128)(2,1)S(1)}, bf16[2,128,512]{2,1,0:T(8,128)(2,1)S(1)}, u32[]{:S(2)}, u32[]{:S(2)}) collective-permute-start(bf16[2,128,512]{2,1,0:T(8,128)(2,1)S(1)} %pad_maximum_fusion.refs_0_), channel_id=1, source_target_pairs={{0,1},{1,0},{2,3},{3,2},{4,5},{5,4},{6,7},{7,6},{8,9},{9,8},{10,11... | collective-permute-start | bytes 786440 | tf_op jit(solution)/shard_map/ppermute | solution.py:305
  40.0 1.5 %collective-permute-start.7 = (bf16[2,128,512]{2,1,0:T(8,128)(2,1)S(1)}, bf16[2,128,512]{2,1,0:T(8,128)(2,1)S(1)}, u32[]{:S(2)}, u32[]{:S(2)}) collective-permute-start(bf16[2,128,512]{2,1,0:T(8,128)(2,1)S(1)} %collective-permute-done.1.refs_1_), channel_id=1, source_target_pairs={{0,1},{1,0},{2,3},{3,2},{4,5},{5,4},{6,7},{7,6},{8,9},{9,8},{10,11... | collective-permute-start | bytes 786440 | tf_op jit(solution)/shard_map/ppermute | solution.py:305
  40.1 2.0 %collective-permute-start.8 = (bf16[2,128,512]{2,1,0:T(8,128)(2,1)S(1)}, bf16[2,128,512]{2,1,0:T(8,128)(2,1)S(1)}, u32[]{:S(2)}, u32[]{:S(2)}) collective-permute-start(bf16[2,128,512]{2,1,0:T(8,128)(2,1)S(1)} %collective-permute-done.2.refs_2_), channel_id=1, source_target_pairs={{0,1},{1,0},{2,3},{3,2},{4,5},{5,4},{6,7},{7,6},{8,9},{9,8},{10,11... | collective-permute-start | bytes 786440 | tf_op jit(solution)/shard_map/ppermute | solution.py:305
  40.5 1.8 %collective-permute-start.9 = (bf16[2,128,512]{2,1,0:T(8,128)(2,1)S(1)}, bf16[2,128,512]{2,1,0:T(8,128)(2,1)S(1)}, u32[]{:S(2)}, u32[]{:S(2)}) collective-permute-start(bf16[2,128,512]{2,1,0:T(8,128)(2,1)S(1)} %collective-permute-done.3.refs_3_), channel_id=1, source_target_pairs={{0,1},{1,0},{2,3},{3,2},{4,5},{5,4},{6,7},{7,6},{8,9},{9,8},{10,11... | collective-permute-start | bytes 786440 | tf_op jit(solution)/shard_map/ppermute | solution.py:305
  41.1 19.3 %collective-permute-start.11 = (bf16[1,4,128,1024]{3,2,1,0:T(8,128)(2,1)}, bf16[1,4,128,1024]{3,2,1,0:T(8,128)(2,1)S(1)}, u32[]{:S(2)}, u32[]{:S(2)}) collective-permute-start(bf16[1,4,128,1024]{3,2,1,0:T(8,128)(2,1)} %get-tuple-element.55), channel_id=1, source_target_pairs={{0,1},{1,0},{2,3},{3,2},{4,5},{5,4},{6,7},{7,6},{8,9},{9,8},{10,11... | collective-permute-start | bytes 3145736 | tf_op jit(solution)/shard_map/ppermute | solution.py:305
  41.5 11.5 %collective-permute-start.10 = (s32[2,4,2,256]{3,2,1,0:T(2,128)S(1)}, s32[2,4,2,256]{3,2,1,0:T(2,128)S(1)}, u32[]{:S(2)}, u32[]{:S(2)}) collective-permute-start(s32[2,4,2,256]{3,2,1,0:T(2,128)S(1)} %pad_add_fusion.meta), channel_id=1, source_target_pairs={{0,2},{1,3},{2,0},{3,1},{4,6},{5,7},{6,4},{7,5},{8,10},{9,11},{10,... | collective-permute-start | bytes 49160 | tf_op jit(solution)/shard_map/ppermute | solution.py:305
  51.0 2.0 %copy-start.4 = (bf16[4,1024,512]{2,1,0:T(8,128)(2,1)}, bf16[4,1024,512]{2,1,0:T(8,128)(2,1)S(1)}, u32[]{:S(2)}) copy-start(bf16[4,1024,512]{2,1,0:T(8,128)(2,1)S(1)} %shard_map.90.weight) | copy-start | bytes 12582916
  55.1 18.5 %collective-permute-start.13 = (bf16[1,3,128,1024]{3,2,1,0:T(8,128)(2,1)}, bf16[1,3,128,1024]{3,2,1,0:T(8,128)(2,1)}, u32[]{:S(2)}, u32[]{:S(2)}) collective-permute-start(bf16[1,3,128,1024]{3,2,1,0:T(8,128)(2,1)} %slice.17), channel_id=1, source_target_pairs={{0,1},{1,0},{2,3},{3,2},{4,5},{5,4},{6,7},{7,6},{8,9},{9,8},{10,11... | collective-permute-start | bytes 2359304 | tf_op jit(solution)/shard_map/ppermute | solution.py:305
  55.4 25.4 %collective-permute-start.14 = (bf16[1,1,128,1024]{3,2,1,0:T(8,128)(2,1)}, bf16[1,1,128,1024]{3,2,1,0:T(8,128)(2,1)}, u32[]{:S(2)}, u32[]{:S(2)}) collective-permute-start(bf16[1,1,128,1024]{3,2,1,0:T(8,128)(2,1)} %get-tuple-element.64), channel_id=1, source_target_pairs={{0,2},{1,3},{2,0},{3,1},{4,6},{5,7},{6,4},{7,5},{8,10},{9,11},{10,... | collective-permute-start | bytes 786440 | tf_op jit(solution)/shard_map/ppermute | solution.py:305
  56.4 24.4 %collective-permute-start.15 = (bf16[1,1,128,1024]{3,2,1,0:T(8,128)(2,1)}, bf16[1,1,128,1024]{3,2,1,0:T(8,128)(2,1)}, u32[]{:S(2)}, u32[]{:S(2)}) collective-permute-start(bf16[1,1,128,1024]{3,2,1,0:T(8,128)(2,1)} %get-tuple-element.65), channel_id=1, source_target_pairs={{0,3},{1,2},{2,1},{3,0},{4,7},{5,6},{6,5},{7,4},{8,11},{9,10},{10,... | collective-permute-start | bytes 786440 | tf_op jit(solution)/shard_map/ppermute | solution.py:305
  60.4 2.2 %copy-start.2 = (bf16[4,512,1024]{2,1,0:T(8,128)(2,1)S(1)}, bf16[4,512,1024]{2,1,0:T(8,128)(2,1)}, u32[]{:S(2)}) copy-start(bf16[4,512,1024]{2,1,0:T(8,128)(2,1)} %patches.7) | copy-start | bytes 12582916
  62.6 2.2 %copy-start.5 = (bf16[4,1024,512]{2,1,0:T(8,128)(2,1)S(1)}, bf16[4,1024,512]{2,1,0:T(8,128)(2,1)}, u32[]{:S(2)}) copy-start(bf16[4,1024,512]{2,1,0:T(8,128)(2,1)} %copy-done.4) | copy-start | bytes 12582916
  64.8 1.0 copy-start.9
  65.9 7.7 %copy-start.3 = (bf16[4,512,1024]{2,1,0:T(8,128)(2,1)S(1)}, bf16[4,512,1024]{2,1,0:T(8,128)(2,1)}, u32[]{:S(2)}) copy-start(bf16[4,512,1024]{2,1,0:T(8,128)(2,1)} %patches.7) | copy-start | bytes 12582916
  84.6 2.7 %collective-permute-start.18 = (bf16[2,2,4,64,256]{4,3,2,1,0:T(8,128)(2,1)S(1)}, bf16[2,2,4,64,256]{4,3,2,1,0:T(8,128)(2,1)S(1)}, u32[]{:S(2)}, u32[]{:S(2)}) collective-permute-start(bf16[2,2,4,64,256]{4,3,2,1,0:T(8,128)(2,1)S(1)} %get-tuple-element.69), channel_id=1, source_target_pairs={{0,1},{1,0},{2,3},{3,2},{4,5},{5,4},{6,7},{7,6},{8,9},{9,8},{10,11... | collective-permute-start | bytes 1572872 | tf_op jit(solution)/shard_map/ppermute | solution.py:305
  85.3 3.3 %collective-permute-start.12 = (f32[4,256]{1,0:T(4,128)S(1)}, f32[4,256]{1,0:T(4,128)S(1)}, u32[]{:S(2)}, u32[]{:S(2)}) collective-permute-start(f32[4,256]{1,0:T(4,128)S(1)} %slice_bitcast_fusion), channel_id=1, source_target_pairs={{0,1},{1,0},{2,3},{3,2},{4,5},{5,4},{6,7},{7,6},{8,9},{9,8},{10,11... | collective-permute-start | bytes 12296 | tf_op jit(solution)/shard_map/ppermute | solution.py:305
  85.4 5.2 %collective-permute-start.21 = (bf16[2,2,4,64,256]{4,3,2,1,0:T(8,128)(2,1)S(1)}, bf16[2,2,4,64,256]{4,3,2,1,0:T(8,128)(2,1)S(1)}, u32[]{:S(2)}, u32[]{:S(2)}) collective-permute-start(bf16[2,2,4,64,256]{4,3,2,1,0:T(8,128)(2,1)S(1)} %get-tuple-element.71), channel_id=1, source_target_pairs={{0,1},{1,0},{2,3},{3,2},{4,5},{5,4},{6,7},{7,6},{8,9},{9,8},{10,11... | collective-permute-start | bytes 1572872 | tf_op jit(solution)/shard_map/ppermute | solution.py:305
  85.9 3.7 %collective-permute-start.16 = (f32[4,256]{1,0:T(4,128)S(1)}, f32[4,256]{1,0:T(4,128)S(1)}, u32[]{:S(2)}, u32[]{:S(2)}) collective-permute-start(f32[4,256]{1,0:T(4,128)S(1)} %bitcast.64), channel_id=1, source_target_pairs={{0,2},{1,3},{2,0},{3,1},{4,6},{5,7},{6,4},{7,5},{8,10},{9,11},{10,... | collective-permute-start | bytes 12296 | tf_op jit(solution)/shard_map/ppermute | solution.py:305
  87.0 3.0 %collective-permute-start.17 = (f32[4,256]{1,0:T(4,128)S(1)}, f32[4,256]{1,0:T(4,128)S(1)}, u32[]{:S(2)}, u32[]{:S(2)}) collective-permute-start(f32[4,256]{1,0:T(4,128)S(1)} %bitcast.65), channel_id=1, source_target_pairs={{0,3},{1,2},{2,1},{3,0},{4,7},{5,6},{6,5},{7,4},{8,11},{9,10},{10,... | collective-permute-start | bytes 12296 | tf_op jit(solution)/shard_map/ppermute | solution.py:305
  87.4 9.0 %collective-permute-start.19 = (bf16[2,4,64,256]{3,2,1,0:T(8,128)(2,1)S(1)}, bf16[2,4,64,256]{3,2,1,0:T(8,128)(2,1)S(1)}, u32[]{:S(2)}, u32[]{:S(2)}) collective-permute-start(bf16[2,4,64,256]{3,2,1,0:T(8,128)(2,1)S(1)} %fusion), channel_id=1, source_target_pairs={{0,2},{1,3},{2,0},{3,1},{4,6},{5,7},{6,4},{7,5},{8,10},{9,11},{10,... | collective-permute-start | bytes 786440 | tf_op jit(solution)/shard_map/ppermute | solution.py:305
  90.7 8.4 %collective-permute-start.22 = (bf16[2,4,64,256]{3,2,1,0:T(8,128)(2,1)S(1)}, bf16[2,4,64,256]{3,2,1,0:T(8,128)(2,1)S(1)}, u32[]{:S(2)}, u32[]{:S(2)}) collective-permute-start(bf16[2,4,64,256]{3,2,1,0:T(8,128)(2,1)S(1)} %fusion.1), channel_id=1, source_target_pairs={{0,4},{4,0},{8,12},{12,8},{16,20},{20,16},{24,28},{28,24},{1,5},{5... | collective-permute-start | bytes 786440 | tf_op jit(solution)/shard_map/ppermute | solution.py:305
  96.5 5.3 %collective-permute-start.20 = (bf16[4,64,256]{2,1,0:T(8,128)(2,1)S(1)}, bf16[4,64,256]{2,1,0:T(8,128)(2,1)S(1)}, u32[]{:S(2)}, u32[]{:S(2)}) collective-permute-start(bf16[4,64,256]{2,1,0:T(8,128)(2,1)S(1)} %fusion.2), channel_id=1, source_target_pairs={{0,4},{4,0},{8,12},{12,8},{16,20},{20,16},{24,28},{28,24},{1,5},{5... | collective-permute-start | bytes 393224 | tf_op jit(solution)/shard_map/ppermute | solution.py:305
  99.2 5.0 %collective-permute-start.23 = (bf16[4,64,256]{2,1,0:T(8,128)(2,1)S(1)}, bf16[4,64,256]{2,1,0:T(8,128)(2,1)S(1)}, u32[]{:S(2)}, u32[]{:S(2)}) collective-permute-start(bf16[4,64,256]{2,1,0:T(8,128)(2,1)S(1)} %fusion.3), channel_id=1, source_target_pairs={{0,2},{1,3},{2,0},{3,1},{4,6},{5,7},{6,4},{7,5},{8,10},{9,11},{10,... | collective-permute-start | bytes 393224 | tf_op jit(solution)/shard_map/ppermute | solution.py:305
  104.3 4.5 %collective-permute-start.24 = (bf16[128,256]{1,0:T(8,128)(2,1)S(1)}, bf16[128,256]{1,0:T(8,128)(2,1)S(1)}, u32[]{:S(2)}, u32[]{:S(2)}) collective-permute-start(bf16[128,256]{1,0:T(8,128)(2,1)S(1)} %pad_maximum_fusion.1), channel_id=1, source_target_pairs={{0,8},{4,12},{8,0},{12,4},{16,24},{20,28},{24,16},{28,20},{1,9},{5... | collective-permute-start | bytes 196616 | tf_op jit(solution)/shard_map/ppermute | solution.py:305
  105.0 7.1 %collective-permute-start.25 = (bf16[128,256]{1,0:T(8,128)(2,1)S(1)}, bf16[128,256]{1,0:T(8,128)(2,1)S(1)}, u32[]{:S(2)}, u32[]{:S(2)}) collective-permute-start(bf16[128,256]{1,0:T(8,128)(2,1)S(1)} %pad_maximum_fusion.2), channel_id=1, source_target_pairs={{0,16},{4,20},{8,24},{12,28},{16,0},{20,4},{24,8},{28,12},{1,17},{... | collective-permute-start | bytes 196616 | tf_op jit(solution)/shard_map/ppermute | solution.py:305
  108.4 6.1 %collective-permute-start.26 = (bf16[128,256]{1,0:T(8,128)(2,1)S(1)}, bf16[128,256]{1,0:T(8,128)(2,1)S(1)}, u32[]{:S(2)}, u32[]{:S(2)}) collective-permute-start(bf16[128,256]{1,0:T(8,128)(2,1)S(1)} %pad_maximum_fusion.3), channel_id=1, source_target_pairs={{0,24},{4,28},{8,16},{12,20},{16,8},{20,12},{24,0},{28,4},{1,25},{... | collective-permute-start | bytes 196616 | tf_op jit(solution)/shard_map/ppermute | solution.py:305

commit v4 on v3

--- a/solution.py
+++ b/solution.py
@@ -9,10 +9,9 @@
 from jax.sharding import PartitionSpec as P
 
 MARGIN_BLOCK_SIZE = 64
-VMEM_LIMIT = 28 * 1024 * 1024
+VMEM_LIMIT = 16 * 1024 * 1024
 ME, CORE, DP, COUNTS = 0, 1, 2, 3
 TARGET, COEF = 0, 1
-FREE = pl.CostEstimate(flops=0, bytes_accessed=0, transcendentals=0)
 F32, BF16 = jnp.float32, jnp.bfloat16
 
 
@@ -30,7 +29,7 @@
     return jnp.where(hits > 0, dot(hits.astype(BF16), before), -1.0)
 
 
-def call(kernel, n_pages, in_specs, out_specs, out_shape, operands, scratch=(), cost=FREE):
+def call(kernel, n_pages, in_specs, out_specs, out_shape, operands, scratch=(), aliases={}, flops=0):
     return pl.pallas_call(
         kernel,
         grid_spec=pltpu.PrefetchScalarGridSpec(
@@ -42,7 +41,8 @@
         ),
         out_shape=out_shape,
         compiler_params=pltpu.CompilerParams(vmem_limit_bytes=VMEM_LIMIT),
-        cost_estimate=cost,
+        cost_estimate=pl.CostEstimate(flops=flops, bytes_accessed=0, transcendentals=0),
+        input_output_aliases=aliases,
     )(*operands)
 
 
@@ -144,7 +144,7 @@
 
 def weights_kernel(offsets, info, patches, *refs):
     *gathered, out, proj, sems = refs
-    half = proj.shape[2]
+    half = proj.shape[1] // 2
 
     def copies():
         for g, ref in enumerate(gathered):
@@ -152,9 +152,10 @@
             core = g // len(offsets)
             for i, offset in enumerate(offsets[g % len(offsets)]):
                 shard = jnp.bitwise_xor(info[DP], offset)
+                first = jnp.bitwise_xor(info[CORE], core) * half
                 to = proj.at[
-                    jnp.bitwise_xor(info[CORE], core),
                     pl.ds(pl.multiple_of(shard * rows, rows), rows),
+                    pl.ds(pl.multiple_of(first, half), half),
                 ]
                 yield ref.at[i], to
 
@@ -168,10 +169,7 @@
         for copy in started:
             copy.wait()
 
-    pat = patches[0]
-    out[0] = sum(
-        dot(proj[h], pat[:, h * half : (h + 1) * half], ((1,), (1,))) for h in range(2)
-    ).astype(BF16)
+    out[0] = dot(proj[...], patches[0], ((1,), (1,))).astype(BF16)
 
 
 def weights(info, patches, gathered, offsets):
@@ -185,39 +183,19 @@
         out,
         (info, patches, *gathered),
         [
-            pltpu.VMEM((2, width, width // 2), BF16),
+            pltpu.VMEM((width, width), BF16),
             pltpu.SemaphoreType.DMA((sum(g.shape[0] for g in gathered),)),
         ],
     )
 
 
-def page_kernel(n_homes, n_pages, has_acc, last, info, bias, table, rank, weight, patches, *refs):
-    refs = list(refs)
-    words, rest = refs[:n_homes], refs[n_homes:]
-    acc_in = rest.pop(0) if has_acc else None
-    n_outs = 4 if last else 1
-    outs, (loss, x_t, dqs, *rest) = rest[:n_outs], rest[n_outs:]
-    page = pl.program_id(0)
+def page_kernel(n_homes, cut, info, bias, table, rank, weight, patches, *refs):
+    words, (loss, x_t, dq) = refs[:n_homes], refs[-3:]
     pps, width = patches.shape[1:]
     cap = words[0].shape[2]
     n_rows = n_homes * cap
-    wcol = outs[0].shape[-1]
-    n_cols = width // wcol
     scale = 2.0 / math.sqrt(width)
-    if has_acc:
-        acc, sem = rest
-        acc_copy = pltpu.make_async_copy(acc_in, acc, sem)
-
-        @pl.when(page == 0)
-        def _():
-            acc_copy.start()
-
     x = jnp.concatenate([w[0, 0] for w in words], axis=0)
-    if x_t.shape[0] == n_pages:
-        x_t[page] = x.T
-    else:
-        x_t[0, :, pl.ds(pl.multiple_of(page * n_rows, n_rows), n_rows)] = x.T
-    pat = patches[0]
     scores = dot(x, weight[0]) * scale
     is_target = iota((n_rows, pps), 1) == table[0, :, TARGET : TARGET + 1].astype(jnp.int32)
     coef = table[0, :, COEF : COEF + 1]
@@ -229,74 +207,84 @@
     row_loss = jnp.where(coef > 0, top + jnp.log(total) - target_score, 0.0)
     share = expo * (1.0 / total)
     dscore = (coef * jnp.where(is_target, share - 1.0, share)).astype(BF16)
-    dqs[pl.ds(pl.multiple_of(page * n_rows, n_rows), n_rows), :] = (
-        dot(dscore, pat) * scale
-    ).astype(BF16)
+    dq[0] = (dot(dscore, patches[0]) * scale).astype(BF16)
     slots = iota((cap, rank.shape[2]), 0).astype(F32)
     for r in range(n_homes):
         picked = jnp.where(slots == rank[0, r : r + 1, :], row_loss[r * cap : (r + 1) * cap], 0.0)
         loss[0, r : r + 1, :] = jnp.sum(picked, axis=0, keepdims=True)
-
-    @pl.when(page == n_pages - 1)
-    def _():
-        if has_acc:
-            acc_copy.wait()
-
-        def gradient(j):
-            got = acc[j] if has_acc else 0.0
-            depth = x_t.shape[2]
-            for g in range(x_t.shape[0]):
-                some = pl.ds(pl.multiple_of(j * wcol, wcol), wcol)
-                got += dot(x_t[g], dqs[g * depth : (g + 1) * depth, some])
-            return got
-
-        def store(halves, y, got):
-            _, lows, highs, cut, _ = halves[0].shape
-            for part in range(2 * lows * highs):
-                rows = got[part * cut : (part + 1) * cut]
-                out = halves[part % 2]
-                out[y, part // 2 % lows, part // (2 * lows)] = rows.astype(out.dtype)
-
-        if last:
-            for y in range(n_cols // 2):
-                store(outs[2:], y, gradient(2 * y + 1 - info[CORE]))
-            for y in range(n_cols // 2):
-                store(outs[:2], y, gradient(2 * y + info[CORE]))
-        else:
-            for j in range(n_cols):
-                outs[0][j] = gradient(j)
-
-
-def run_pages(n_seq, n_high, info, weight, patches, table, words, acc, first_page, last):
-    _, n_pages, cap, width = words[0].shape
+    t = x.T
+    for part in range(width // cut):
+        x_t[0, part % 2, part // 2 * cut : (part // 2 + 1) * cut] = t[part * cut : (part + 1) * cut]
+
+
+def run_pages(cut, info, weight, patches, table, words, first_page, kept=None):
+    _, n_pages, cap, width = words[0][0].shape
+    pages, wdev = patches.shape[0], table[2].shape[2]
     n_homes = len(words)
     n_rows = n_homes * cap
-    wdev = table[2].shape[2]
-    wcol = width // n_seq
-    has_acc = acc is not None
-    if last:
-        form = (n_seq // 2, 2, n_high, width // (4 * n_high), wcol)
-        out = [jax.ShapeDtypeStruct(form, t) for t in (F32, F32, BF16, BF16)]
-    else:
-        out = [jax.ShapeDtypeStruct((n_seq, width, wcol), F32)]
-    loss = jax.ShapeDtypeStruct((n_pages, n_homes, wdev), F32)
-    groups = 1 if n_rows % 128 == 0 else n_pages
-    scratch = [
-        pltpu.VMEM((groups, width, n_pages * n_rows // groups), BF16),
-        pltpu.VMEM((n_pages * n_rows, width), BF16),
+    out = [
+        jax.ShapeDtypeStruct((n_pages, n_homes, wdev), F32),
+        jax.ShapeDtypeStruct((pages, 2, width // 2, n_rows), BF16),
+        jax.ShapeDtypeStruct((pages, n_rows, width), BF16),
     ]
-    if has_acc:
-        scratch += [pltpu.VMEM((n_seq, width, wcol), F32), pltpu.SemaphoreType.DMA(())]
+    inputs = (*table, weight, patches)
+    n = 1 + len(inputs) + n_homes
     return call(
-        functools.partial(page_kernel, n_homes, n_pages, has_acc, last),
+        functools.partial(page_kernel, n_homes, cut),
         n_pages,
-        [page_of(a, first_page) for a in (*table, weight, patches)]
-        + [pl.BlockSpec((1, 1, cap, width), lambda p, info: (0, p, 0, 0))] * n_homes
-        + [pl.BlockSpec(memory_space=pl.ANY)] * has_acc,
-        [all_of(o) for o in out] + [page_of(loss)],
-        out + [loss],
-        (info, *table, weight, patches, *words) + ((acc,) if has_acc else ()),
-        scratch,
+        [page_of(a, first_page) for a in inputs]
+        + [pl.BlockSpec((1, 1, cap, width), lambda p, info, i=i: (i, p, 0, 0)) for _, i in words]
+        + [pl.BlockSpec(memory_space=pl.ANY)] * (2 if kept else 0),
+        [page_of(out[0])] + [page_of(o, first_page) for o in out[1:]],
+        out,
+        (info, *inputs, *(w for w, _ in words), *(kept or ())),
+        aliases={n: 1, n + 1: 2} if kept else {},
+    )
+
+
+def gradient_kernel(info, *refs):
+    *pairs, keep, send, acc = refs
+    n_y, lows, highs, cut, wcol = keep.shape
+    page = pl.program_id(0)
+    got = sum(dot(pairs[i][0, 0], pairs[i + 1][0]) for i in range(0, len(pairs), 2))
+
+    @pl.when(page == 0)
+    def _():
+        acc[...] = got
+
+    @pl.when(page > 0)
+    def _():
+        acc[...] += got
+
+    @pl.when(page == pl.num_programs(0) - 1)
+    def _():
+        for out, core in ((send, 1 - info[CORE]), (keep, info[CORE])):
+            for y in range(n_y):
+                column = pl.multiple_of((2 * y + core) * wcol, wcol)
+                for part in range(lows * highs):
+                    rows = acc[part * cut : (part + 1) * cut, pl.ds(column, wcol)]
+                    out[y, part % lows, part // lows] = rows.astype(out.dtype)
+
+
+def gradient(info, half, n_y, n_high, pairs):
+    width = pairs[0][1].shape[-1]
+    form = (n_y, 2, n_high, width // (4 * n_high), width // (2 * n_y))
+    out = [jax.ShapeDtypeStruct(form, t) for t in (F32, BF16)]
+    specs = []
+    for x_t, dq in pairs:
+        specs.append(
+            pl.BlockSpec((1, 1) + x_t.shape[2:], lambda p, info: (p, half, 0, 0))
+        )
+        specs.append(page_of(dq))
+    return call(
+        gradient_kernel,
+        pairs[0][1].shape[0],
+        specs,
+        [all_of(o) for o in out],
+        out,
+        (info, *(x for pair in pairs for x in pair)),
+        [pltpu.VMEM((width // 2, width), F32)],
+        flops=2 * width * width * sum(dq.shape[0] * dq.shape[1] for _, dq in pairs),
     )
 
 
@@ -324,54 +312,61 @@
     n_y, n_high = n_seq // 2, n_dp // 2
     cap = 2 * wdev // n_seq
     half = width // 2
+    shard_rows = proj.shape[0]
     near, far = (0, 1), tuple(range(2, n_seq))
 
     info = jnp.concatenate([jnp.stack([me, core, my_dp]).astype(jnp.int32), counts])
     routes = routes.reshape(pages, 1, wdev)
 
-    cut = pages - 1
-    both = dispatch(info, routes, words, far, cap, 0, cut, 2)
-    held, proj, both = lax.optimization_barrier((info, proj, both))
-    rest = dispatch(held, routes, words, far, cap, cut, pages - cut)
+    piece, bit = lax.dynamic_slice_in_dim(proj, core * half, half, 1)[None], 1
+    other = exchange(piece, "dp", 2)
+    routes, other = lax.optimization_barrier((routes, other))
+    pieces = [(piece, 0), (other, bit)]
+    while 2 * bit < n_high:
+        piece, bit = jnp.concatenate([piece, other], axis=0), 2 * bit
+        other = exchange(piece, "dp", 2 * bit)
+        pieces = [(piece, 0), (other, bit)]
+
+    split = pages - 1
+    both = dispatch(info, routes, words, far, cap, 0, split, 2)
+    held, both = lax.optimization_barrier((info, both))
+    both = [exchange(rows, "seq", 2 * (k + 1)) for k, rows in enumerate(both)]
+    rest = dispatch(held, routes, words, far, cap, split, pages - split)
     stay, across = dispatch(held, routes, words, near, cap, 0, pages)
-    both = [exchange(rows, "seq", 2 * (k + 1)) for k, rows in enumerate(both)]
 
     pair = jnp.concatenate([routes, targets.reshape(pages, 1, wdev)], axis=1)
     meta_near = jnp.stack([pair, exchange(pair, "seq", 1)])
     table_near = tables(info, meta_near, flags, near, cap, pps)
     meta_far = jnp.concatenate([exchange(meta_near, "seq", 2 * k) for k in range(1, n_y)], axis=0)
 
-    piece, bit = lax.dynamic_slice_in_dim(proj, core * half, half, 1)[None], 1
-    pieces = [(piece, 0)]
-    while bit < n_high:
-        other = exchange(piece, "dp", 2 * bit)
-        pieces = [(piece, 0), (other, bit)]
-        bit *= 2
-        if bit < n_high:
-            piece = jnp.concatenate([piece, other], axis=0)
+    last, rest, stay, across, table_near = lax.optimization_barrier(
+        (pieces[-1][0], rest, stay, across, table_near)
+    )
+    pieces[-1] = (last, pieces[-1][1])
     gathered, offsets = [], []
     for piece, start in pieces:
         gathered += [piece, exchange(piece, "dp", 1)]
         offsets += [[2 * (start + i) + low for i in range(piece.shape[0])] for low in range(2)]
-    gathered, rest, across, table_near = lax.optimization_barrier(
-        (gathered, rest, across, table_near)
-    )
     gathered += [exchange(piece, "seq", 1) for piece in gathered]
+    across = exchange(across, "seq", 1)
     rest = [exchange(rows, "seq", r) for rows, r in zip(rest, far)]
-    across = exchange(across, "seq", 1)
-
     weight = weights(info, patches, gathered, offsets)
+
     both, weight, meta_far = lax.optimization_barrier((both, weight, meta_far))
+    first = [pair for rows in both for pair in ((rows, 0), (exchange(rows, "seq", 1), 1))]
     table_far = tables(info, meta_far, flags, far, cap, pps)
-    first = [x for rows in both for x in (rows, exchange(rows[1:], "seq", 1))]
-    run = functools.partial(run_pages, n_seq, n_high, info, weight, patches)
-    acc, loss = run(table_near, [stay, across], None, 0, False)
+    run = functools.partial(run_pages, shard_rows // 2, info, weight, patches)
+    loss, *pair_near = run(table_near, [(stay, 0), (across, 0)], 0)
     word_loss = [loss[:, 0], exchange(loss[:, 1], "seq", 1)]
-    acc, loss_a = run(table_far, first, acc, 0, False)
-    *out, loss_b = run(table_far, rest, acc, cut, True)
+    loss_a, *pair_far = run(table_far, first, 0)
+    loss_b, *pair_far = run(table_far, [(rows, 0) for rows in rest], split, pair_far)
     losses = jnp.concatenate([loss_a, loss_b], axis=0)
 
-    terms = [[out[h], exchange(out[2 + h], "seq", 1)] for h in range(2)]
+    terms = []
+    for h in range(2):
+        keep, send = gradient(info, h, n_y, n_high, [pair_near, pair_far])
+        info, keep, send = lax.optimization_barrier((info, keep, send))
+        terms.append([keep, exchange(send, "seq", 1)])
 
     def over_y(terms):
         total = pick_sum(terms, y)

time: 116 us -> 114 us (0.983)
  waiting for transfers between devices: 31.8 us -> 26.7 us
  local copies, waits for them, and re-layouts: 12.7 us -> 16 us
    unnamed x31 -> x35, local copies, waits for them, and re-layouts: 10.5 us -> 15.8 us
    ppermute x27, waiting for transfers between devices: 31.8 us -> 26.7 us  [exchange(): return lax.ppermute(x, axis, [(i, i ^ offset) for i in range(n)])]
    slice x1 -> x0, local copies, waits for them, and re-layouts: 2.07 us -> none  [local(): first = [x for rows in both for x in (rows, exchange(rows[1:], 'seq', 1))]]
    pallas_call x9 -> x11, Pallas kernels: 42.6 us -> 41.7 us  [call(): pl.pallas_call(kernel, grid_spec=pltpu.PrefetchScalarGridSpec(num_scalar_...]
  transfers between devices with their start and end apart: 27 -> 27, of which waited for: 12 -> 11; matrix products, arithmetic and copies ran while one was open for 3% -> 2% of each run, Pallas kernels for 31% -> 25%
where the time goes in v4:
time: 114 us; the launch traced here: 113 us
  Pallas kernels  41.7 us (37%)
  waiting for transfers between devices  26.7 us (23%)
  starting transfers between devices  25.4 us (22%)
  local copies, waits for them, and re-layouts  16 us (14%)
  other arithmetic  2.48 us (2%)
    pallas_call x11, Pallas kernels, call(): pl.pallas_call(kernel, grid_spec=pltpu.PrefetchScalarGridSpec(num_scalar_...  41.7 us
    ppermute x27, waiting for transfers between devices, exchange(): return lax.ppermute(x, axis, [(i, i ^ offset) for i in range(n)])  26.7 us
    ppermute x27, starting transfers between devices, exchange(): return lax.ppermute(x, axis, [(i, i ^ offset) for i in range(n)])  25.4 us
    unnamed x35, local copies, waits for them, and re-layouts  15.8 us
  transfers between devices with their start and end apart: 27, of which 11 were waited for; matrix products, arithmetic and copies ran while one was open for 2% of the time, Pallas kernels for 25%

profile of v4, /device:TPU:0, one launch (start us, length us, event | category | flops | bytes accessed | tf_op | source)
XLA Modules:
  0.0 113.2 jit_solution(8315732783708005299)
XLA Ops:
  0.7 0.9 copy-done
  1.6 3.1 %collective-permute-start = (bf16[1,128,512]{2,1,0:T(8,128)(2,1)S(1)}, bf16[1,128,512]{2,1,0:T(8,128)(2,1)S(1)}, u32[]{:S(2)}, u32[]{:S(2)}) collective-permute-start(bf16[1,128,512]{2,1,0:T(8,128)(2,1)S(1)} %dynamic-slice_bitcast_fusion), channel_id=1, source_target_pairs={{0,8},{4,12},{8,0},{12,4},{16,24},{20,28},{24,16},{28,20},{1,9},{5... | collective-permute-start | bytes 393224 | tf_op jit(solution)/shard_map/ppermute | solution.py:293
  4.7 0.7 pad_add_fusion.2.info
  5.4 2.8 %collective-permute-done = bf16[1,128,512]{2,1,0:T(8,128)(2,1)S(1)} collective-permute-done((bf16[1,128,512]{2,1,0:T(8,128)(2,1)S(1)}, bf16[1,128,512]{2,1,0:T(8,128)(2,1)S(1)}, u32[]{:S(2)}, u32[]{:S(2)}) %collective-permute-start) | collective-permute-done | bytes 131104 | tf_op jit(solution)/shard_map/ppermute | solution.py:293
  8.2 1.6 %copy-done.6 = bf16[4,256,1024]{2,1,0:T(8,128)(2,1)S(1)} copy-done((bf16[4,256,1024]{2,1,0:T(8,128)(2,1)S(1)}, bf16[4,256,1024]{2,1,0:T(8,128)(2,1)}, u32[]{:S(2)}) %copy-start.6) | copy-done | bytes 2097176
  9.8 0.7 copy-done.14
  10.5 1.9 %shard_map.86 = bf16[2,3,128,1024]{3,2,1,0:T(8,128)(2,1)S(1)} custom-call(s32[7]{0:T(128)S(1)} %pad_add_fusion.2.info, s32[4,1,256]{2,1,0:T(1,128)S(1)} %bitcast.59, bf16[4,256,1024]{2,1,0:T(8,128)(2,1)S(1)} %copy-done.6), custom_call_target="tpu_custom_call" | custom-call | tf_op jit(solution)/shard_map/pallas_call | solution.py:33
  12.4 1.7 %collective-permute-start.3 = (bf16[2,3,128,1024]{3,2,1,0:T(8,128)(2,1)S(1)}, bf16[2,3,128,1024]{3,2,1,0:T(8,128)(2,1)S(1)}, u32[]{:S(2)}, u32[]{:S(2)}) collective-permute-start(bf16[2,3,128,1024]{3,2,1,0:T(8,128)(2,1)S(1)} %shard_map.86), channel_id=1, source_target_pairs={{0,2},{1,3},{2,0},{3,1},{4,6},{5,7},{6,4},{7,5},{8,10},{9,11},{10,... | collective-permute-start | bytes 4718600 | tf_op jit(solution)/shard_map/ppermute | solution.py:293
  14.2 2.7 %collective-permute-start.1 = (bf16[2,128,512]{2,1,0:T(8,128)(2,1)S(1)}, bf16[2,128,512]{2,1,0:T(8,128)(2,1)S(1)}, u32[]{:S(2)}, u32[]{:S(2)}) collective-permute-start(bf16[2,128,512]{2,1,0:T(8,128)(2,1)S(1)} %pad_maximum_fusion.refs_0_), channel_id=1, source_target_pairs={{0,16},{4,20},{8,24},{12,28},{16,0},{20,4},{24,8},{28,12},{1,17},{... | collective-permute-start | bytes 786440 | tf_op jit(solution)/shard_map/ppermute | solution.py:293
  17.0 1.6 %collective-permute-start.4 = (bf16[2,128,512]{2,1,0:T(8,128)(2,1)S(1)}, bf16[2,128,512]{2,1,0:T(8,128)(2,1)S(1)}, u32[]{:S(2)}, u32[]{:S(2)}) collective-permute-start(bf16[2,128,512]{2,1,0:T(8,128)(2,1)S(1)} %pad_maximum_fusion.refs_0_), channel_id=1, source_target_pairs={{0,4},{4,0},{8,12},{12,8},{16,20},{20,16},{24,28},{28,24},{1,5},{5... | collective-permute-start | bytes 786440 | tf_op jit(solution)/shard_map/ppermute | solution.py:293
  18.5 1.7 %shard_map.87 = (bf16[1,1,128,1024]{3,2,1,0:T(8,128)(2,1)}, bf16[1,1,128,1024]{3,2,1,0:T(8,128)(2,1)}) custom-call(s32[7]{0:T(128)S(1)} %pad_add_fusion.2.info, s32[4,1,256]{2,1,0:T(1,128)S(1)} %bitcast.61, bf16[4,256,1024]{2,1,0:T(8,128)(2,1)S(1)} %copy-done.6), custom_call_target="tpu_custom_call" | custom-call | tf_op jit(solution)/shard_map/pallas_call | solution.py:33
  20.2 3.3 %shard_map.88 = (bf16[1,4,128,1024]{3,2,1,0:T(8,128)(2,1)S(1)}, bf16[1,4,128,1024]{3,2,1,0:T(8,128)(2,1)}) custom-call(s32[7]{0:T(128)S(1)} %pad_add_fusion.2.info, s32[4,1,256]{2,1,0:T(1,128)S(1)} %bitcast.62, bf16[4,256,1024]{2,1,0:T(8,128)(2,1)S(1)} %copy-done.6), custom_call_target="tpu_custom_call" | custom-call | tf_op jit(solution)/shard_map/pallas_call | solution.py:33
  23.5 1.0 copy-done.7
  24.5 3.5 %shard_map.89 = (bf16[4,256,512]{2,1,0:T(8,128)(2,1)S(1)}, f32[4,256,128]{2,1,0:T(8,128)S(1)}, f32[4,8,256]{2,1,0:T(8,128)S(1)}) custom-call(s32[7]{0:T(128)S(1)} %pad_add_fusion.2.info, s32[2,4,2,256]{3,2,1,0:T(2,128)S(1)} %pad_add_fusion.meta, s32[4,16,32]{2,1,0:T(8,128)S(1)} %copy-done.13), custom_call_target="tpu_custom_call" | custom-call | tf_op jit(solution)/shard_map/pallas_call | solution.py:33
  28.0 1.0 copy-done.9
  29.0 0.8 copy-done.11
  30.9 7.3 %collective-permute-done.5.refs_3_ = bf16[2,128,512]{2,1,0:T(8,128)(2,1)S(1)} collective-permute-done((bf16[2,128,512]{2,1,0:T(8,128)(2,1)S(1)}, bf16[2,128,512]{2,1,0:T(8,128)(2,1)S(1)}, u32[]{:S(2)}, u32[]{:S(2)}) %collective-permute-start.5) | collective-permute-done | bytes 262176 | tf_op jit(solution)/shard_map/ppermute | solution.py:293
  38.7 1.0 collective-permute-done.9.refs_7_
  39.7 6.2 %shard_map.90.weight = bf16[4,1024,512]{2,1,0:T(8,128)(2,1)S(1)} custom-call(s32[7]{0:T(128)S(1)} %pad_add_fusion.2.info, bf16[4,512,1024]{2,1,0:T(8,128)(2,1)S(1)} %copy-done.1, bf16[2,128,512]{2,1,0:T(8,128)(2,1)S(1)} %pad_maximum_fusion.refs_0_, bf16[2,128,512]{2,1,0:T(8,128)(2,1)S(1)} %collective-permute-done.4.refs_1_, ...), custom_call_target="tpu_custom_call" | custom-call | tf_op jit(solution)/shard_map/pallas_call | solution.py:33
  45.9 2.0 %copy-done.4 = bf16[4,1024,512]{2,1,0:T(8,128)(2,1)} copy-done((bf16[4,1024,512]{2,1,0:T(8,128)(2,1)}, bf16[4,1024,512]{2,1,0:T(8,128)(2,1)S(1)}, u32[]{:S(2)}) %copy-start.4) | copy-done | bytes 4194328
  48.9 1.4 %collective-permute-start.14 = (bf16[1,1,128,1024]{3,2,1,0:T(8,128)(2,1)}, bf16[1,1,128,1024]{3,2,1,0:T(8,128)(2,1)}, u32[]{:S(2)}, u32[]{:S(2)}) collective-permute-start(bf16[1,1,128,1024]{3,2,1,0:T(8,128)(2,1)} %get-tuple-element.70), channel_id=1, source_target_pairs={{0,2},{1,3},{2,0},{3,1},{4,6},{5,7},{6,4},{7,5},{8,10},{9,11},{10,... | collective-permute-start | bytes 786440 | tf_op jit(solution)/shard_map/ppermute | solution.py:293
  50.3 3.5 %shard_map.92 = (bf16[4,256,512]{2,1,0:T(8,128)(2,1)S(1)}, f32[4,256,128]{2,1,0:T(8,128)S(1)}, f32[4,8,256]{2,1,0:T(8,128)S(1)}) custom-call(s32[7]{0:T(128)S(1)} %pad_add_fusion.2.info, s32[2,4,2,256]{3,2,1,0:T(2,128)S(1)} %collective-permute-done.10.meta, s32[4,16,32]{2,1,0:T(8,128)S(1)} %copy-done.13), custom_call_target="tpu_custom_call" | custom-call | tf_op jit(solution)/shard_map/pallas_call | solution.py:33
  53.8 2.2 %copy-done.2 = bf16[4,512,1024]{2,1,0:T(8,128)(2,1)S(1)} copy-done((bf16[4,512,1024]{2,1,0:T(8,128)(2,1)S(1)}, bf16[4,512,1024]{2,1,0:T(8,128)(2,1)}, u32[]{:S(2)}) %copy-start.2) | copy-done | bytes 4194328
  56.0 2.2 %copy-done.5 = bf16[4,1024,512]{2,1,0:T(8,128)(2,1)S(1)} copy-done((bf16[4,1024,512]{2,1,0:T(8,128)(2,1)S(1)}, bf16[4,1024,512]{2,1,0:T(8,128)(2,1)}, u32[]{:S(2)}) %copy-start.5) | copy-done | bytes 4194328
  58.2 1.2 %copy-done.8 = bf16[1,4,128,1024]{3,2,1,0:T(8,128)(2,1)S(1)} copy-done((bf16[1,4,128,1024]{3,2,1,0:T(8,128)(2,1)S(1)}, bf16[1,4,128,1024]{3,2,1,0:T(8,128)(2,1)}, u32[]{:S(2)}) %copy-start.8) | copy-done | bytes 1048600
  59.4 1.2 %copy-done.10 = bf16[4,256,512]{2,1,0:T(8,128)(2,1)S(1)} copy-done((bf16[4,256,512]{2,1,0:T(8,128)(2,1)S(1)}, bf16[4,256,512]{2,1,0:T(8,128)(2,1)}, u32[]{:S(2)}) %copy-start.10) | copy-done | bytes 1048600
  60.6 1.0 copy-done.12
  61.7 6.3 %shard_map.91 = (f32[4,2,256]{2,1,0:T(2,128)S(1)}, bf16[4,2,512,256]{3,2,1,0:T(8,128)(2,1)S(1)}, bf16[4,256,1024]{2,1,0:T(8,128)(2,1)S(1)}) custom-call(s32[7]{0:T(128)S(1)} %pad_add_fusion.2.info, bf16[4,256,512]{2,1,0:T(8,128)(2,1)S(1)} %copy-done.10, f32[4,256,128]{2,1,0:T(8,128)S(1)} %copy-done.12, f32[4,8,256]{2,1,0:T(8,128)S(1)} %get-tuple-element.57.rank, ...), custom_call_target="tpu_custom_call" | custom-call | tf_op jit(solution)/shard_map/pallas_call | solution.py:33
  68.0 4.0 %shard_map.93 = (f32[3,2,256]{2,1,0:T(2,128)S(1)}, bf16[4,2,512,256]{3,2,1,0:T(8,128)(2,1)S(1)}, bf16[4,256,1024]{2,1,0:T(8,128)(2,1)S(1)}) custom-call(s32[7]{0:T(128)S(1)} %pad_add_fusion.2.info, bf16[4,256,512]{2,1,0:T(8,128)(2,1)S(1)} %get-tuple-element.65.bias, f32[4,256,128]{2,1,0:T(8,128)S(1)} %get-tuple-element.66.table, ...), custom_call_target="tpu_custom_call" | custom-call | tf_op jit(solution)/shard_map/pallas_call | solution.py:33
  72.0 2.7 %shard_map.94 = (f32[1,2,256]{2,1,0:T(2,128)S(1)}, bf16[4,2,512,256]{3,2,1,0:T(8,128)(2,1)S(1)}, bf16[4,256,1024]{2,1,0:T(8,128)(2,1)S(1)}) custom-call(s32[7]{0:T(128)S(1)} %pad_add_fusion.2.info, bf16[4,256,512]{2,1,0:T(8,128)(2,1)S(1)} %get-tuple-element.65.bias, ...), custom_call_target="tpu_custom_call", output_to_operand_aliasing={{1}: (8, {}), {2}: (9, {})} | custom-call | tf_op jit(solution)/shard_map/pallas_call | solution.py:33
  74.7 4.3 %shard_map.95 = (f32[2,2,4,64,256]{4,3,2,1,0:T(8,128)S(1)}, bf16[2,2,4,64,256]{4,3,2,1,0:T(8,128)(2,1)S(1)}) custom-call(s32[7]{0:T(128)S(1)} %pad_add_fusion.2.info, bf16[4,2,512,256]{3,2,1,0:T(8,128)(2,1)S(1)} %get-tuple-element.75.refs_0_, bf16[4,256,1024]{2,1,0:T(8,128)(2,1)S(1)} %get-tuple-element.76.refs_1_, ...), custom_call_target="tpu_custom_call" | custom-call | flops 4294967296 | tf_op jit(solution)/shard_map/pallas_call | solution.py:33
  79.1 4.3 %shard_map.96 = (f32[2,2,4,64,256]{4,3,2,1,0:T(8,128)S(1)}, bf16[2,2,4,64,256]{4,3,2,1,0:T(8,128)(2,1)S(1)}) custom-call(s32[7]{0:T(128)S(1)} %pad_add_fusion.2.info, bf16[4,2,512,256]{3,2,1,0:T(8,128)(2,1)S(1)} %get-tuple-element.75.refs_0_, bf16[4,256,1024]{2,1,0:T(8,128)(2,1)S(1)} %get-tuple-element.76.refs_1_, ...), custom_call_target="tpu_custom_call" | custom-call | flops 4294967296 | tf_op jit(solution)/shard_map/pallas_call | solution.py:33
  83.4 0.8 collective-permute-start.21
  84.8 1.1 %collective-permute-start.17 = (f32[4,256]{1,0:T(4,128)S(1)}, f32[4,256]{1,0:T(4,128)S(1)}, u32[]{:S(2)}, u32[]{:S(2)}) collective-permute-start(f32[4,256]{1,0:T(4,128)S(1)} %bitcast.64), channel_id=1, source_target_pairs={{0,3},{1,2},{2,1},{3,0},{4,7},{5,6},{6,5},{7,4},{8,11},{9,10},{10,... | collective-permute-start | bytes 12296 | tf_op jit(solution)/shard_map/ppermute | solution.py:293
  85.9 0.6 collective-permute-start.16
  86.6 1.4 %collective-permute-start.22 = (bf16[2,4,64,256]{3,2,1,0:T(8,128)(2,1)S(1)}, bf16[2,4,64,256]{3,2,1,0:T(8,128)(2,1)S(1)}, u32[]{:S(2)}, u32[]{:S(2)}) collective-permute-start(bf16[2,4,64,256]{3,2,1,0:T(8,128)(2,1)S(1)} %fusion.1), channel_id=1, source_target_pairs={{0,4},{4,0},{8,12},{12,8},{16,20},{20,16},{24,28},{28,24},{1,5},{5... | collective-permute-start | bytes 786440 | tf_op jit(solution)/shard_map/ppermute | solution.py:293
  88.0 1.5 %collective-permute-done.16 = f32[4,256]{1,0:T(4,128)S(1)} collective-permute-done((f32[4,256]{1,0:T(4,128)S(1)}, f32[4,256]{1,0:T(4,128)S(1)}, u32[]{:S(2)}, u32[]{:S(2)}) %collective-permute-start.16) | collective-permute-done | bytes 4128 | tf_op jit(solution)/shard_map/ppermute | solution.py:293
  90.2 0.7 collective-permute-start.19
  90.9 4.2 %collective-permute-done.22 = bf16[2,4,64,256]{3,2,1,0:T(8,128)(2,1)S(1)} collective-permute-done((bf16[2,4,64,256]{3,2,1,0:T(8,128)(2,1)S(1)}, bf16[2,4,64,256]{3,2,1,0:T(8,128)(2,1)S(1)}, u32[]{:S(2)}, u32[]{:S(2)}) %collective-permute-start.22) | collective-permute-done | bytes 262176 | tf_op jit(solution)/shard_map/ppermute | solution.py:293
  95.2 1.4 %collective-permute-start.23 = (bf16[4,64,256]{2,1,0:T(8,128)(2,1)S(1)}, bf16[4,64,256]{2,1,0:T(8,128)(2,1)S(1)}, u32[]{:S(2)}, u32[]{:S(2)}) collective-permute-start(bf16[4,64,256]{2,1,0:T(8,128)(2,1)S(1)} %fusion.3), channel_id=1, source_target_pairs={{0,2},{1,3},{2,0},{3,1},{4,6},{5,7},{6,4},{7,5},{8,10},{9,11},{10,... | collective-permute-start | bytes 393224 | tf_op jit(solution)/shard_map/ppermute | solution.py:293
  96.6 1.6 %collective-permute-done.19 = bf16[2,4,64,256]{3,2,1,0:T(8,128)(2,1)S(1)} collective-permute-done((bf16[2,4,64,256]{3,2,1,0:T(8,128)(2,1)S(1)}, bf16[2,4,64,256]{3,2,1,0:T(8,128)(2,1)S(1)}, u32[]{:S(2)}, u32[]{:S(2)}) %collective-permute-start.19) | collective-permute-done | bytes 262176 | tf_op jit(solution)/shard_map/ppermute | solution.py:293
  98.4 1.7 %collective-permute-start.20 = (bf16[4,64,256]{2,1,0:T(8,128)(2,1)S(1)}, bf16[4,64,256]{2,1,0:T(8,128)(2,1)S(1)}, u32[]{:S(2)}, u32[]{:S(2)}) collective-permute-start(bf16[4,64,256]{2,1,0:T(8,128)(2,1)S(1)} %fusion.2), channel_id=1, source_target_pairs={{0,4},{4,0},{8,12},{12,8},{16,20},{20,16},{24,28},{28,24},{1,5},{5... | collective-permute-start | bytes 393224 | tf_op jit(solution)/shard_map/ppermute | solution.py:293
  100.6 2.8 %collective-permute-done.20 = bf16[4,64,256]{2,1,0:T(8,128)(2,1)S(1)} collective-permute-done((bf16[4,64,256]{2,1,0:T(8,128)(2,1)S(1)}, bf16[4,64,256]{2,1,0:T(8,128)(2,1)S(1)}, u32[]{:S(2)}, u32[]{:S(2)}) %collective-permute-start.20) | collective-permute-done | bytes 131104 | tf_op jit(solution)/shard_map/ppermute | solution.py:293
  103.5 3.8 %collective-permute-start.26 = (bf16[128,256]{1,0:T(8,128)(2,1)S(1)}, bf16[128,256]{1,0:T(8,128)(2,1)S(1)}, u32[]{:S(2)}, u32[]{:S(2)}) collective-permute-start(bf16[128,256]{1,0:T(8,128)(2,1)S(1)} %pad_maximum_fusion.3), channel_id=1, source_target_pairs={{0,24},{4,28},{8,16},{12,20},{16,8},{20,12},{24,0},{28,4},{1,25},{... | collective-permute-start | bytes 196616 | tf_op jit(solution)/shard_map/ppermute | solution.py:293
  107.3 0.7 collective-permute-start.24
  108.0 2.0 %collective-permute-done.26 = bf16[128,256]{1,0:T(8,128)(2,1)S(1)} collective-permute-done((bf16[128,256]{1,0:T(8,128)(2,1)S(1)}, bf16[128,256]{1,0:T(8,128)(2,1)S(1)}, u32[]{:S(2)}, u32[]{:S(2)}) %collective-permute-start.26) | collective-permute-done | bytes 65568 | tf_op jit(solution)/shard_map/ppermute | solution.py:293
  110.0 2.5 %collective-permute-done.25 = bf16[128,256]{1,0:T(8,128)(2,1)S(1)} collective-permute-done((bf16[128,256]{1,0:T(8,128)(2,1)S(1)}, bf16[128,256]{1,0:T(8,128)(2,1)S(1)}, u32[]{:S(2)}, u32[]{:S(2)}) %collective-permute-start.25) | collective-permute-done | bytes 65568 | tf_op jit(solution)/shard_map/ppermute | solution.py:293
  112.5 0.7 fusion.5
  (79 shorter events, 5.0 us)
Async XLA Ops:
  0.6 1.0 copy-start
  1.6 6.6 %collective-permute-start = (bf16[1,128,512]{2,1,0:T(8,128)(2,1)S(1)}, bf16[1,128,512]{2,1,0:T(8,128)(2,1)S(1)}, u32[]{:S(2)}, u32[]{:S(2)}) collective-permute-start(bf16[1,128,512]{2,1,0:T(8,128)(2,1)S(1)} %dynamic-slice_bitcast_fusion), channel_id=1, source_target_pairs={{0,8},{4,12},{8,0},{12,4},{16,24},{20,28},{24,16},{28,20},{1,9},{5... | collective-permute-start | bytes 393224 | tf_op jit(solution)/shard_map/ppermute | solution.py:293
  8.2 1.6 %copy-start.6 = (bf16[4,256,1024]{2,1,0:T(8,128)(2,1)S(1)}, bf16[4,256,1024]{2,1,0:T(8,128)(2,1)}, u32[]{:S(2)}) copy-start(bf16[4,256,1024]{2,1,0:T(8,128)(2,1)} %words.5) | copy-start | bytes 6291460
  9.8 0.7 copy-start.14
  10.5 6.4 %copy-start.15 = (s32[4,256]{1,0:T(4,128)S(1)}, s32[4,256]{1,0:T(4,128)}, u32[]{:S(2)}) copy-start(s32[4,256]{1,0:T(4,128)} %param.11) | copy-start | bytes 12292
  12.4 36.0 %collective-permute-start.3 = (bf16[2,3,128,1024]{3,2,1,0:T(8,128)(2,1)S(1)}, bf16[2,3,128,1024]{3,2,1,0:T(8,128)(2,1)S(1)}, u32[]{:S(2)}, u32[]{:S(2)}) collective-permute-start(bf16[2,3,128,1024]{3,2,1,0:T(8,128)(2,1)S(1)} %shard_map.86), channel_id=1, source_target_pairs={{0,2},{1,3},{2,0},{3,1},{4,6},{5,7},{6,4},{7,5},{8,10},{9,11},{10,... | collective-permute-start | bytes 4718600 | tf_op jit(solution)/shard_map/ppermute | solution.py:293
  14.2 15.6 %collective-permute-start.1 = (bf16[2,128,512]{2,1,0:T(8,128)(2,1)S(1)}, bf16[2,128,512]{2,1,0:T(8,128)(2,1)S(1)}, u32[]{:S(2)}, u32[]{:S(2)}) collective-permute-start(bf16[2,128,512]{2,1,0:T(8,128)(2,1)S(1)} %pad_maximum_fusion.refs_0_), channel_id=1, source_target_pairs={{0,16},{4,20},{8,24},{12,28},{16,0},{20,4},{24,8},{28,12},{1,17},{... | collective-permute-start | bytes 786440 | tf_op jit(solution)/shard_map/ppermute | solution.py:293
  16.9 7.7 %copy-start.13 = (s32[4,16,32]{2,1,0:T(8,128)S(1)}, s32[4,16,32]{2,1,0:T(8,128)}, u32[]{:S(2)}) copy-start(s32[4,16,32]{2,1,0:T(8,128)} %flags.3) | copy-start | bytes 24580
  16.9 22.9 %copy-start.1 = (bf16[4,512,1024]{2,1,0:T(8,128)(2,1)S(1)}, bf16[4,512,1024]{2,1,0:T(8,128)(2,1)}, u32[]{:S(2)}) copy-start(bf16[4,512,1024]{2,1,0:T(8,128)(2,1)} %patches.7) | copy-start | bytes 12582916
  16.9 7.6 %collective-permute-start.2 = (s32[4,2,256]{2,1,0:T(2,128)S(1)}, s32[4,2,256]{2,1,0:T(2,128)S(1)}, u32[]{:S(2)}, u32[]{:S(2)}) collective-permute-start(s32[4,2,256]{2,1,0:T(2,128)S(1)} %get-tuple-element.97), channel_id=1, source_target_pairs={{0,1},{1,0},{2,3},{3,2},{4,5},{5,4},{6,7},{7,6},{8,9},{9,8},{10,11... | collective-permute-start | bytes 24584 | tf_op jit(solution)/shard_map/ppermute | solution.py:293
  17.0 13.9 %collective-permute-start.4 = (bf16[2,128,512]{2,1,0:T(8,128)(2,1)S(1)}, bf16[2,128,512]{2,1,0:T(8,128)(2,1)S(1)}, u32[]{:S(2)}, u32[]{:S(2)}) collective-permute-start(bf16[2,128,512]{2,1,0:T(8,128)(2,1)S(1)} %pad_maximum_fusion.refs_0_), channel_id=1, source_target_pairs={{0,4},{4,0},{8,12},{12,8},{16,20},{20,16},{24,28},{28,24},{1,5},{5... | collective-permute-start | bytes 786440 | tf_op jit(solution)/shard_map/ppermute | solution.py:293
  23.5 1.0 copy-start.7
  28.0 1.0 copy-start.9
  29.0 0.8 copy-start.11
  29.8 8.4 %collective-permute-start.5 = (bf16[2,128,512]{2,1,0:T(8,128)(2,1)S(1)}, bf16[2,128,512]{2,1,0:T(8,128)(2,1)S(1)}, u32[]{:S(2)}, u32[]{:S(2)}) collective-permute-start(bf16[2,128,512]{2,1,0:T(8,128)(2,1)S(1)} %collective-permute-done.1.refs_2_), channel_id=1, source_target_pairs={{0,4},{4,0},{8,12},{12,8},{16,20},{20,16},{24,28},{28,24},{1,5},{5... | collective-permute-start | bytes 786440 | tf_op jit(solution)/shard_map/ppermute | solution.py:293
  30.4 7.8 %collective-permute-start.6 = (bf16[2,128,512]{2,1,0:T(8,128)(2,1)S(1)}, bf16[2,128,512]{2,1,0:T(8,128)(2,1)S(1)}, u32[]{:S(2)}, u32[]{:S(2)}) collective-permute-start(bf16[2,128,512]{2,1,0:T(8,128)(2,1)S(1)} %pad_maximum_fusion.refs_0_), channel_id=1, source_target_pairs={{0,1},{1,0},{2,3},{3,2},{4,5},{5,4},{6,7},{7,6},{8,9},{9,8},{10,11... | collective-permute-start | bytes 786440 | tf_op jit(solution)/shard_map/ppermute | solution.py:293
  30.4 8.4 %collective-permute-start.8 = (bf16[2,128,512]{2,1,0:T(8,128)(2,1)S(1)}, bf16[2,128,512]{2,1,0:T(8,128)(2,1)S(1)}, u32[]{:S(2)}, u32[]{:S(2)}) collective-permute-start(bf16[2,128,512]{2,1,0:T(8,128)(2,1)S(1)} %collective-permute-done.1.refs_2_), channel_id=1, source_target_pairs={{0,1},{1,0},{2,3},{3,2},{4,5},{5,4},{6,7},{7,6},{8,9},{9,8},{10,11... | collective-permute-start | bytes 786440 | tf_op jit(solution)/shard_map/ppermute | solution.py:293
  30.9 7.8 %collective-permute-start.7 = (bf16[2,128,512]{2,1,0:T(8,128)(2,1)S(1)}, bf16[2,128,512]{2,1,0:T(8,128)(2,1)S(1)}, u32[]{:S(2)}, u32[]{:S(2)}) collective-permute-start(bf16[2,128,512]{2,1,0:T(8,128)(2,1)S(1)} %collective-permute-done.4.refs_1_), channel_id=1, source_target_pairs={{0,1},{1,0},{2,3},{3,2},{4,5},{5,4},{6,7},{7,6},{8,9},{9,8},{10,11... | collective-permute-start | bytes 786440 | tf_op jit(solution)/shard_map/ppermute | solution.py:293
  38.2 1.5 %collective-permute-start.9 = (bf16[2,128,512]{2,1,0:T(8,128)(2,1)S(1)}, bf16[2,128,512]{2,1,0:T(8,128)(2,1)S(1)}, u32[]{:S(2)}, u32[]{:S(2)}) collective-permute-start(bf16[2,128,512]{2,1,0:T(8,128)(2,1)S(1)} %collective-permute-done.5.refs_3_), channel_id=1, source_target_pairs={{0,1},{1,0},{2,3},{3,2},{4,5},{5,4},{6,7},{7,6},{8,9},{9,8},{10,11... | collective-permute-start | bytes 786440 | tf_op jit(solution)/shard_map/ppermute | solution.py:293
  38.2 10.2 %collective-permute-start.10 = (s32[2,4,2,256]{3,2,1,0:T(2,128)S(1)}, s32[2,4,2,256]{3,2,1,0:T(2,128)S(1)}, u32[]{:S(2)}, u32[]{:S(2)}) collective-permute-start(s32[2,4,2,256]{3,2,1,0:T(2,128)S(1)} %pad_add_fusion.meta), channel_id=1, source_target_pairs={{0,2},{1,3},{2,0},{3,1},{4,6},{5,7},{6,4},{7,5},{8,10},{9,11},{10,... | collective-permute-start | bytes 49160 | tf_op jit(solution)/shard_map/ppermute | solution.py:293
  45.9 2.0 %copy-start.4 = (bf16[4,1024,512]{2,1,0:T(8,128)(2,1)}, bf16[4,1024,512]{2,1,0:T(8,128)(2,1)S(1)}, u32[]{:S(2)}) copy-start(bf16[4,1024,512]{2,1,0:T(8,128)(2,1)S(1)} %shard_map.90.weight) | copy-start | bytes 12582916
  48.4 19.6 %collective-permute-start.13 = (bf16[2,3,128,1024]{3,2,1,0:T(8,128)(2,1)S(1)}, bf16[2,3,128,1024]{3,2,1,0:T(8,128)(2,1)S(1)}, u32[]{:S(2)}, u32[]{:S(2)}) collective-permute-start(bf16[2,3,128,1024]{3,2,1,0:T(8,128)(2,1)S(1)} %collective-permute-done.3.refs_0_), channel_id=1, source_target_pairs={{0,1},{1,0},{2,3},{3,2},{4,5},{5,4},{6,7},{7,6},{8,9},{9,8},{10,11... | collective-permute-start | bytes 4718600 | tf_op jit(solution)/shard_map/ppermute | solution.py:293
  48.4 5.4 %collective-permute-start.11 = (bf16[1,4,128,1024]{3,2,1,0:T(8,128)(2,1)}, bf16[1,4,128,1024]{3,2,1,0:T(8,128)(2,1)}, u32[]{:S(2)}, u32[]{:S(2)}) collective-permute-start(bf16[1,4,128,1024]{3,2,1,0:T(8,128)(2,1)} %get-tuple-element.62), channel_id=1, source_target_pairs={{0,1},{1,0},{2,3},{3,2},{4,5},{5,4},{6,7},{7,6},{8,9},{9,8},{10,11... | collective-permute-start | bytes 3145736 | tf_op jit(solution)/shard_map/ppermute | solution.py:293
  48.9 23.1 %collective-permute-start.14 = (bf16[1,1,128,1024]{3,2,1,0:T(8,128)(2,1)}, bf16[1,1,128,1024]{3,2,1,0:T(8,128)(2,1)}, u32[]{:S(2)}, u32[]{:S(2)}) collective-permute-start(bf16[1,1,128,1024]{3,2,1,0:T(8,128)(2,1)} %get-tuple-element.70), channel_id=1, source_target_pairs={{0,2},{1,3},{2,0},{3,1},{4,6},{5,7},{6,4},{7,5},{8,10},{9,11},{10,... | collective-permute-start | bytes 786440 | tf_op jit(solution)/shard_map/ppermute | solution.py:293
  50.3 21.7 %collective-permute-start.15 = (bf16[1,1,128,1024]{3,2,1,0:T(8,128)(2,1)}, bf16[1,1,128,1024]{3,2,1,0:T(8,128)(2,1)}, u32[]{:S(2)}, u32[]{:S(2)}) collective-permute-start(bf16[1,1,128,1024]{3,2,1,0:T(8,128)(2,1)} %get-tuple-element.71), channel_id=1, source_target_pairs={{0,3},{1,2},{2,1},{3,0},{4,7},{5,6},{6,5},{7,4},{8,11},{9,10},{10,... | collective-permute-start | bytes 786440 | tf_op jit(solution)/shard_map/ppermute | solution.py:293
  53.8 2.2 %copy-start.2 = (bf16[4,512,1024]{2,1,0:T(8,128)(2,1)S(1)}, bf16[4,512,1024]{2,1,0:T(8,128)(2,1)}, u32[]{:S(2)}) copy-start(bf16[4,512,1024]{2,1,0:T(8,128)(2,1)} %patches.7) | copy-start | bytes 12582916
  56.0 2.2 %copy-start.5 = (bf16[4,1024,512]{2,1,0:T(8,128)(2,1)S(1)}, bf16[4,1024,512]{2,1,0:T(8,128)(2,1)}, u32[]{:S(2)}) copy-start(bf16[4,1024,512]{2,1,0:T(8,128)(2,1)} %copy-done.4) | copy-start | bytes 12582916
  58.2 1.2 %copy-start.8 = (bf16[1,4,128,1024]{3,2,1,0:T(8,128)(2,1)S(1)}, bf16[1,4,128,1024]{3,2,1,0:T(8,128)(2,1)}, u32[]{:S(2)}) copy-start(bf16[1,4,128,1024]{3,2,1,0:T(8,128)(2,1)} %copy-done.7) | copy-start | bytes 3145732
  59.4 1.2 %copy-start.10 = (bf16[4,256,512]{2,1,0:T(8,128)(2,1)S(1)}, bf16[4,256,512]{2,1,0:T(8,128)(2,1)}, u32[]{:S(2)}) copy-start(bf16[4,256,512]{2,1,0:T(8,128)(2,1)} %copy-done.9) | copy-start | bytes 3145732
  60.6 1.0 copy-start.12
  61.7 6.3 %copy-start.3 = (bf16[4,512,1024]{2,1,0:T(8,128)(2,1)S(1)}, bf16[4,512,1024]{2,1,0:T(8,128)(2,1)}, u32[]{:S(2)}) copy-start(bf16[4,512,1024]{2,1,0:T(8,128)(2,1)} %patches.7) | copy-start | bytes 12582916
  83.4 3.1 %collective-permute-start.21 = (bf16[2,2,4,64,256]{4,3,2,1,0:T(8,128)(2,1)S(1)}, bf16[2,2,4,64,256]{4,3,2,1,0:T(8,128)(2,1)S(1)}, u32[]{:S(2)}, u32[]{:S(2)}) collective-permute-start(bf16[2,2,4,64,256]{4,3,2,1,0:T(8,128)(2,1)S(1)} %get-tuple-element.87), channel_id=1, source_target_pairs={{0,1},{1,0},{2,3},{3,2},{4,5},{5,4},{6,7},{7,6},{8,9},{9,8},{10,11... | collective-permute-start | bytes 1572872 | tf_op jit(solution)/shard_map/ppermute | solution.py:293
  84.2 3.8 %collective-permute-start.12 = (f32[4,256]{1,0:T(4,128)S(1)}, f32[4,256]{1,0:T(4,128)S(1)}, u32[]{:S(2)}, u32[]{:S(2)}) collective-permute-start(f32[4,256]{1,0:T(4,128)S(1)} %slice_bitcast_fusion), channel_id=1, source_target_pairs={{0,1},{1,0},{2,3},{3,2},{4,5},{5,4},{6,7},{7,6},{8,9},{9,8},{10,11... | collective-permute-start | bytes 12296 | tf_op jit(solution)/shard_map/ppermute | solution.py:293
  84.3 5.8 %collective-permute-start.18 = (bf16[2,2,4,64,256]{4,3,2,1,0:T(8,128)(2,1)S(1)}, bf16[2,2,4,64,256]{4,3,2,1,0:T(8,128)(2,1)S(1)}, u32[]{:S(2)}, u32[]{:S(2)}) collective-permute-start(bf16[2,2,4,64,256]{4,3,2,1,0:T(8,128)(2,1)S(1)} %get-tuple-element.82), channel_id=1, source_target_pairs={{0,1},{1,0},{2,3},{3,2},{4,5},{5,4},{6,7},{7,6},{8,9},{9,8},{10,11... | collective-permute-start | bytes 1572872 | tf_op jit(solution)/shard_map/ppermute | solution.py:293
  84.8 3.3 %collective-permute-start.17 = (f32[4,256]{1,0:T(4,128)S(1)}, f32[4,256]{1,0:T(4,128)S(1)}, u32[]{:S(2)}, u32[]{:S(2)}) collective-permute-start(f32[4,256]{1,0:T(4,128)S(1)} %bitcast.64), channel_id=1, source_target_pairs={{0,3},{1,2},{2,1},{3,0},{4,7},{5,6},{6,5},{7,4},{8,11},{9,10},{10,... | collective-permute-start | bytes 12296 | tf_op jit(solution)/shard_map/ppermute | solution.py:293
  85.9 3.6 %collective-permute-start.16 = (f32[4,256]{1,0:T(4,128)S(1)}, f32[4,256]{1,0:T(4,128)S(1)}, u32[]{:S(2)}, u32[]{:S(2)}) collective-permute-start(f32[4,256]{1,0:T(4,128)S(1)} %bitcast.65), channel_id=1, source_target_pairs={{0,2},{1,3},{2,0},{3,1},{4,6},{5,7},{6,4},{7,5},{8,10},{9,11},{10,... | collective-permute-start | bytes 12296 | tf_op jit(solution)/shard_map/ppermute | solution.py:293
  86.6 8.4 %collective-permute-start.22 = (bf16[2,4,64,256]{3,2,1,0:T(8,128)(2,1)S(1)}, bf16[2,4,64,256]{3,2,1,0:T(8,128)(2,1)S(1)}, u32[]{:S(2)}, u32[]{:S(2)}) collective-permute-start(bf16[2,4,64,256]{3,2,1,0:T(8,128)(2,1)S(1)} %fusion.1), channel_id=1, source_target_pairs={{0,4},{4,0},{8,12},{12,8},{16,20},{20,16},{24,28},{28,24},{1,5},{5... | collective-permute-start | bytes 786440 | tf_op jit(solution)/shard_map/ppermute | solution.py:293
  90.2 8.1 %collective-permute-start.19 = (bf16[2,4,64,256]{3,2,1,0:T(8,128)(2,1)S(1)}, bf16[2,4,64,256]{3,2,1,0:T(8,128)(2,1)S(1)}, u32[]{:S(2)}, u32[]{:S(2)}) collective-permute-start(bf16[2,4,64,256]{3,2,1,0:T(8,128)(2,1)S(1)} %fusion), channel_id=1, source_target_pairs={{0,2},{1,3},{2,0},{3,1},{4,6},{5,7},{6,4},{7,5},{8,10},{9,11},{10,... | collective-permute-start | bytes 786440 | tf_op jit(solution)/shard_map/ppermute | solution.py:293
  95.2 5.4 %collective-permute-start.23 = (bf16[4,64,256]{2,1,0:T(8,128)(2,1)S(1)}, bf16[4,64,256]{2,1,0:T(8,128)(2,1)S(1)}, u32[]{:S(2)}, u32[]{:S(2)}) collective-permute-start(bf16[4,64,256]{2,1,0:T(8,128)(2,1)S(1)} %fusion.3), channel_id=1, source_target_pairs={{0,2},{1,3},{2,0},{3,1},{4,6},{5,7},{6,4},{7,5},{8,10},{9,11},{10,... | collective-permute-start | bytes 393224 | tf_op jit(solution)/shard_map/ppermute | solution.py:293
  98.4 5.0 %collective-permute-start.20 = (bf16[4,64,256]{2,1,0:T(8,128)(2,1)S(1)}, bf16[4,64,256]{2,1,0:T(8,128)(2,1)S(1)}, u32[]{:S(2)}, u32[]{:S(2)}) collective-permute-start(bf16[4,64,256]{2,1,0:T(8,128)(2,1)S(1)} %fusion.2), channel_id=1, source_target_pairs={{0,4},{4,0},{8,12},{12,8},{16,20},{20,16},{24,28},{28,24},{1,5},{5... | collective-permute-start | bytes 393224 | tf_op jit(solution)/shard_map/ppermute | solution.py:293
  103.5 6.5 %collective-permute-start.26 = (bf16[128,256]{1,0:T(8,128)(2,1)S(1)}, bf16[128,256]{1,0:T(8,128)(2,1)S(1)}, u32[]{:S(2)}, u32[]{:S(2)}) collective-permute-start(bf16[128,256]{1,0:T(8,128)(2,1)S(1)} %pad_maximum_fusion.3), channel_id=1, source_target_pairs={{0,24},{4,28},{8,16},{12,20},{16,8},{20,12},{24,0},{28,4},{1,25},{... | collective-permute-start | bytes 196616 | tf_op jit(solution)/shard_map/ppermute | solution.py:293
  107.3 5.2 %collective-permute-start.25 = (bf16[128,256]{1,0:T(8,128)(2,1)S(1)}, bf16[128,256]{1,0:T(8,128)(2,1)S(1)}, u32[]{:S(2)}, u32[]{:S(2)}) collective-permute-start(bf16[128,256]{1,0:T(8,128)(2,1)S(1)} %pad_maximum_fusion.2), channel_id=1, source_target_pairs={{0,16},{4,20},{8,24},{12,28},{16,0},{20,4},{24,8},{28,12},{1,17},{... | collective-permute-start | bytes 196616 | tf_op jit(solution)/shard_map/ppermute | solution.py:293
  107.3 5.1 %collective-permute-start.24 = (bf16[128,256]{1,0:T(8,128)(2,1)S(1)}, bf16[128,256]{1,0:T(8,128)(2,1)S(1)}, u32[]{:S(2)}, u32[]{:S(2)}) collective-permute-start(bf16[128,256]{1,0:T(8,128)(2,1)S(1)} %pad_maximum_fusion.1), channel_id=1, source_target_pairs={{0,8},{4,12},{8,0},{12,4},{16,24},{20,28},{24,16},{28,20},{1,9},{5... | collective-permute-start | bytes 196616 | tf_op jit(solution)/shard_map/ppermute | solution.py:293

commit v5 on v4

v5 whole, which is shorter than its diff:
```python
import functools
import math

import jax
import jax.numpy as jnp
from jax import lax
from jax.experimental import pallas as pl
from jax.experimental.pallas import tpu as pltpu
from jax.sharding import PartitionSpec as P

MARGIN_BLOCK_SIZE = 64
VMEM_LIMIT = 20 * 1024 * 1024
ME, CORE, DP, COUNTS = 0, 1, 2, 3
TARGET, COEF = 0, 1
F32, BF16 = jnp.float32, jnp.bfloat16


def dot(a, b, contract=((1,), (0,))):
    return lax.dot_general(a, b, (contract, ((), ())), preferred_element_type=F32)


def iota(shape, axis):
    return lax.broadcasted_iota(jnp.int32, shape, axis)


def ranks(hits):
    n = hits.shape[1]
    before = (iota((n, n), 0) < iota((n, n), 1)).astype(BF16)
    return jnp.where(hits > 0, dot(hits.astype(BF16), before), -1.0)


def call(kernel, n_pages, in_specs, out_specs, out_shape, operands, scratch=(), aliases={}, flops=0):
    return pl.pallas_call(
        kernel,
        grid_spec=pltpu.PrefetchScalarGridSpec(
            num_scalar_prefetch=1,
            grid=(n_pages,),
            in_specs=in_specs,
            out_specs=out_specs,
            scratch_shapes=scratch,
        ),
        out_shape=out_shape,
        compiler_params=pltpu.CompilerParams(vmem_limit_bytes=VMEM_LIMIT),
        cost_estimate=pl.CostEstimate(flops=flops, bytes_accessed=0, transcendentals=0),
        input_output_aliases=aliases,
    )(*operands)


def page_of(array, first_page=0):
    rest = array.shape[1:]
    return pl.BlockSpec((1,) + rest, lambda p, info: (p + first_page,) + (0,) * len(rest))


def all_of(array):
    return pl.BlockSpec(array.shape, lambda p, info: (0,) * len(array.shape))


def pad_rows(n):
    return -(-n // 8) * 8


def stacked(rows):
    n, width = pad_rows(len(rows)), rows[0].shape[1]
    row = iota((n, width), 0)
    out = jnp.zeros((n, width), rows[0].dtype)
    for i, r in enumerate(rows):
        out = jnp.where(row == i, r, out)
    return out


def dispatch_kernel(plan, cap, info, routes, words, *outs):
    wdev = words.shape[1]
    slots = iota((cap, wdev), 0).astype(F32)
    by_page = {}
    for out, (offsets, first_page, n_pages) in zip(outs, plan):
        for p in range(n_pages):
            for i, offset in enumerate(offsets):
                by_page.setdefault(first_page + p, []).append((offset, out, i, p))
    tasks = [(page, *task) for page in by_page for task in by_page[page]]
    rank = ranks(
        stacked(
            [
                (routes[page] == jnp.bitwise_xor(info[ME], offset)).astype(F32)
                for page, offset, *_ in tasks
            ]
        )
    )
    n = 0
    for page, some in by_page.items():
        picks = [
            (slots == rank[n + i : n + i + 1]).astype(BF16) for i in range(len(some))
        ]
        rows = dot(jnp.concatenate(picks, axis=0), words[page]).astype(BF16)
        for i, (_, out, place, p) in enumerate(some):
            out[place, p] = rows[i * cap : (i + 1) * cap]
        n += len(some)


def dispatch(info, routes, words, plan, cap):
    width = words.shape[2]
    out = [
        jax.ShapeDtypeStruct((len(offsets), n_pages, cap, width), BF16)
        for offsets, _, n_pages in plan
    ]
    return call(
        functools.partial(dispatch_kernel, plan, cap),
        1,
        [all_of(routes), all_of(words)],
        [all_of(o) for o in out],
        out,
        (info, routes, words),
    )


def table_kernel(offsets, cap, info, meta, flags, bias, table, rank_out):
    me = info[ME]
    n_homes, pages, _, wdev = meta.shape
    nblk, all_blk = flags.shape[1:]
    n_rows, pps = bias.shape[1:]
    slots = iota((cap, wdev), 0).astype(F32)
    rank = ranks(
        stacked(
            [
                (meta[i, p, 0:1, :] == me).astype(F32)
                for p in range(pages)
                for i in range(n_homes)
            ]
        )
    )
    first = me * (pps // MARGIN_BLOCK_SIZE)
    block = iota((all_blk, pps), 1) // MARGIN_BLOCK_SIZE
    spread = (iota((all_blk, pps), 0) == first + block).astype(BF16)
    place = iota((1, wdev), 1) + 1
    for p in range(pages):
        t, idx = [], []
        for i, offset in enumerate(offsets):
            own = rank[p * n_homes + i : p * n_homes + i + 1]
            rank_out[p, i : i + 1] = own
            target = meta[i, p, 1:2, :]
            values = stacked([target // 64, target % 64, place // 64, place % 64]).astype(F32)
            got = dot((slots == own).astype(BF16), values.astype(BF16), ((1,), (1,)))
            got = got.astype(jnp.int32)
            t.append(got[:, 0:1] * 64 + got[:, 1:2])
            at = got[:, 2:3] * 64 + got[:, 3:4]
            idx.append(jnp.where(at > 0, at - 1 + jnp.bitwise_xor(me, offset) * wdev, -1))
        t, idx = jnp.concatenate(t, axis=0), jnp.concatenate(idx, axis=0)
        word_block = jnp.maximum(idx, 0) // MARGIN_BLOCK_SIZE == iota((n_rows, nblk), 1)
        margin = dot(word_block.astype(BF16), flags[p].astype(BF16)).astype(BF16)
        hit = dot(margin, spread)
        own = iota((n_rows, pps), 1) // MARGIN_BLOCK_SIZE == t // MARGIN_BLOCK_SIZE
        bias[p] = jnp.where((hit > 0.5) | own, 0.0, -jnp.inf).astype(BF16)
        count = info[COUNTS + p]
        valid = (idx >= 0) & (idx < count)
        coef = jnp.where(valid, 64.0 / count.astype(F32), 0.0)
        lane = iota((n_rows, 128), 1)
        table[p] = jnp.where(lane == TARGET, t.astype(F32), jnp.where(lane == COEF, coef, 0.0))


def tables(info, meta, flags, offsets, cap, pps):
    n_homes, pages, _, wdev = meta.shape
    out = [
        jax.ShapeDtypeStruct((pages, n_homes * cap, pps), BF16),
        jax.ShapeDtypeStruct((pages, n_homes * cap, 128), F32),
        jax.ShapeDtypeStruct((pages, pad_rows(n_homes), wdev), F32),
    ]
    return call(
        functools.partial(table_kernel, offsets, cap),
        1,
        [all_of(meta), all_of(flags)],
        [all_of(o) for o in out],
        out,
        (info, meta, flags),
    )


def weights_kernel(offsets, info, patches, *refs):
    *gathered, out, proj, sems = refs
    half = proj.shape[1] // 2

    def copies():
        for g, ref in enumerate(gathered):
            rows = ref.shape[1]
            core = g // len(offsets)
            for i, offset in enumerate(offsets[g % len(offsets)]):
                shard = jnp.bitwise_xor(info[DP], offset)
                first = jnp.bitwise_xor(info[CORE], core) * half
                to = proj.at[
                    pl.ds(pl.multiple_of(shard * rows, rows), rows),
                    pl.ds(pl.multiple_of(first, half), half),
                ]
                yield ref.at[i], to

    @pl.when(pl.program_id(0) == 0)
    def _():
        started = [
            pltpu.make_async_copy(a, b, sems.at[i]) for i, (a, b) in enumerate(copies())
        ]
        for copy in started:
            copy.start()
        for copy in started:
            copy.wait()

    out[0] = dot(proj[...], patches[0], ((1,), (1,))).astype(BF16)


def weights(info, patches, gathered, offsets):
    pages, pps, width = patches.shape
    out = jax.ShapeDtypeStruct((pages, width, pps), BF16)
    return call(
        functools.partial(weights_kernel, offsets),
        pages,
        [page_of(patches)] + [pl.BlockSpec(memory_space=pl.ANY)] * len(gathered),
        page_of(out),
        out,
        (info, patches, *gathered),
        [
            pltpu.VMEM((width, width), BF16),
            pltpu.SemaphoreType.DMA((sum(g.shape[0] for g in gathered),)),
        ],
    )


def page_kernel(n_homes, cut, info, bias, table, rank, weight, patches, *refs):
    words, (loss, x_t, dq) = refs[:n_homes], refs[-3:]
    pps, width = patches.shape[1:]
    cap = words[0].shape[2]
    n_rows = n_homes * cap
    scale = 2.0 / math.sqrt(width)
    x = jnp.concatenate([w[0, 0] for w in words], axis=0)
    scores = dot(x, weight[0]) * scale
    is_target = iota((n_rows, pps), 1) == table[0, :, TARGET : TARGET + 1].astype(jnp.int32)
    coef = table[0, :, COEF : COEF + 1]
    masked = scores + bias[0].astype(F32)
    top = jnp.max(masked, axis=1, keepdims=True)
    expo = jnp.exp(masked - top)
    total = jnp.sum(expo, axis=1, keepdims=True)
    target_score = jnp.sum(jnp.where(is_target, scores, 0.0), axis=1, keepdims=True)
    row_loss = jnp.where(coef > 0, top + jnp.log(total) - target_score, 0.0)
    share = expo * (1.0 / total)
    dscore = (coef * jnp.where(is_target, share - 1.0, share)).astype(BF16)
    back = (dot(dscore, patches[0]) * scale).astype(BF16)
    more = dq.shape[0] - n_rows
    if more:
        back = jnp.concatenate([back, jnp.zeros((more, width), BF16)], axis=0)
        x = jnp.concatenate([x, jnp.zeros((more, width), BF16)], axis=0)
    dq[...] = back
    slots = iota((cap, rank.shape[2]), 0).astype(F32)
    for r in range(n_homes):
        picked = jnp.where(slots == rank[0, r : r + 1, :], row_loss[r * cap : (r + 1) * cap], 0.0)
        loss[0, r : r + 1, :] = jnp.sum(picked, axis=0, keepdims=True)
    t = x.T
    for part in range(width // cut):
        to = part % 2 * (width // 2) + part // 2 * cut
        x_t[to : to + cut] = t[part * cut : (part + 1) * cut]


def run_pages(cut, info, weight, patches, table, words, first_page, kept=None):
    _, n_pages, cap, width = words[0][0].shape
    pages, wdev = patches.shape[0], table[2].shape[2]
    n_homes = len(words)
    n_rows = -(-n_homes * cap // 128) * 128
    out = [
        jax.ShapeDtypeStruct((n_pages, n_homes, wdev), F32),
        jax.ShapeDtypeStruct((width, pages * n_rows), BF16),
        jax.ShapeDtypeStruct((pages * n_rows, width), BF16),
    ]
    inputs = (*table, weight, patches)
    n = 1 + len(inputs) + n_homes
    return call(
        functools.partial(page_kernel, n_homes, cut),
        n_pages,
        [page_of(a, first_page) for a in inputs]
        + [pl.BlockSpec((1, 1, cap, width), lambda p, info, i=i: (i, p, 0, 0)) for _, i in words]
        + [pl.BlockSpec(memory_space=pl.ANY)] * (2 if kept else 0),
        [
            page_of(out[0]),
            pl.BlockSpec((width, n_rows), lambda p, info: (0, p + first_page)),
            pl.BlockSpec((n_rows, width), lambda p, info: (p + first_page, 0)),
        ],
        out,
        (info, *inputs, *(w for w, _ in words), *(kept or ())),
        aliases={n: 1, n + 1: 2} if kept else {},
    )


def gradient_kernel(info, *refs):
    *pairs, one, two = refs
    _, lows, highs, cut, _ = one.shape
    got = sum(dot(pairs[i][...], pairs[i + 1][...]) for i in range(0, len(pairs), 2))
    for part in range(2 * lows * highs):
        out, shard = (one, two)[part // (lows * highs)], part % (lows * highs)
        rows = got[part * cut : (part + 1) * cut]
        out[0, shard % lows, shard // lows] = rows.astype(out.dtype)


def gradient(info, other, dtype, n_y, n_high, pairs):
    width = pairs[0][0].shape[0]
    wcol = width // (2 * n_y)
    form = (n_y, 2, n_high, width // (4 * n_high), wcol)
    out = [jax.ShapeDtypeStruct(form, dtype)] * 2
    column = lambda y, info: (0, 2 * y + jnp.bitwise_xor(info[CORE], other))
    specs = []
    for x_t, dq in pairs:
        specs += [all_of(x_t), pl.BlockSpec((dq.shape[0], wcol), column)]
    return call(
        gradient_kernel,
        n_y,
        specs,
        [page_of(o) for o in out],
        out,
        (info, *(x for pair in pairs for x in pair)),
        flops=64 * width * width * sum(dq.shape[0] for _, dq in pairs),
    )


def exchange(x, axis, offset):
    n = lax.axis_size(axis)
    return lax.ppermute(x, axis, [(i, i ^ offset) for i in range(n)])


def pick(x, i, axis=0):
    start = [i if a == axis else 0 for a in range(x.ndim)]
    size = [1 if a == axis else n for a, n in enumerate(x.shape)]
    got = lax.dynamic_slice(x, start, size, allow_negative_indices=False)
    return got.reshape(x.shape[:axis] + x.shape[axis + 1 :])


def pick_sum(terms, i, axis=0):
    return sum(pick(t, i, axis).astype(F32) for t in terms)


def local(words, patches, proj, routes, targets, counts, flags):
    pages, wdev, width = words.shape
    pps = patches.shape[1]
    n_seq = lax.axis_size("seq")
    n_dp = lax.axis_size("dp")
    n_y, n_high = n_seq // 2, n_dp // 2
    cap = 2 * wdev // n_seq
    half = width // 2
    shard_rows = proj.shape[0]
    near, far = (0, 1), tuple(range(2, n_seq))

    me, my_dp = lax.axis_index("seq"), lax.axis_index("dp")
    core, y, low, high = me & 1, me >> 1, my_dp & 1, my_dp >> 1
    own = {
        "column": core * half,
        "low": low,
        "not_low": 1 - low,
        "y": [y ^ k for k in range(n_y)],
        "high": [high ^ k for k in range(n_high)],
    }
    info = jnp.concatenate([jnp.stack([me, core, my_dp]).astype(jnp.int32), counts])
    info, own, proj = lax.optimization_barrier((info, own, proj))
    routes = routes.reshape(pages, 1, wdev)

    piece = lax.dynamic_slice(
        proj, (0, own["column"]), (shard_rows, half), allow_negative_indices=False
    )
    piece, bit = piece[None], 1
    other = exchange(piece, "dp", 2)
    info, other = lax.optimization_barrier((info, other))
    pieces = [(piece, 0), (other, bit)]
    while 2 * bit < n_high:
        piece, bit = jnp.concatenate([piece, other], axis=0), 2 * bit
        other = exchange(piece, "dp", 2 * bit)
        pieces = [(piece, 0), (other, bit)]

    split = pages - 1
    both = dispatch(
        info, routes, words, [((2 * k, 2 * k + 1), 0, split) for k in range(1, n_y)], cap
    )
    held, both = lax.optimization_barrier((info, both))
    both = [exchange(rows, "seq", 2 * (k + 1)) for k, rows in enumerate(both)]
    stay, across, *rest = dispatch(
        held,
        routes,
        words,
        [((r,), 0, pages) for r in near] + [((r,), split, pages - split) for r in far],
        cap,
    )

    pair = jnp.concatenate([routes, targets.reshape(pages, 1, wdev)], axis=1)
    meta_near = jnp.stack([pair, exchange(pair, "seq", 1)])
    table_near = tables(info, meta_near, flags, near, cap, pps)
    meta_far = jnp.concatenate([exchange(meta_near, "seq", 2 * k) for k in range(1, n_y)], axis=0)

    gathered, offsets = [], []
    for piece, start in pieces:
        gathered += [piece, exchange(piece, "dp", 1)]
        offsets += [[2 * (start + i) + low for i in range(piece.shape[0])] for low in range(2)]
    gathered, rest, stay, across, table_near = lax.optimization_barrier(
        (gathered, rest, stay, across, table_near)
    )
    gathered += [exchange(piece, "seq", 1) for piece in gathered]
    across = exchange(across, "seq", 1)
    rest = [exchange(rows, "seq", r) for rows, r in zip(rest, far)]
    weight = weights(info, patches, gathered, offsets)

    both, weight, meta_far = lax.optimization_barrier((both, weight, meta_far))
    first = [pair for rows in both for pair in ((rows, 0), (exchange(rows, "seq", 1), 1))]
    table_far = tables(info, meta_far, flags, far, cap, pps)
    run = functools.partial(run_pages, shard_rows // 2, info, weight, patches)
    loss, *pair_near = run(table_near, [(stay, 0), (across, 0)], 0)
    word_loss = [loss[:, 0], exchange(loss[:, 1], "seq", 1)]
    loss_a, *pair_far = run(table_far, first, 0)
    loss_b, *pair_far = run(table_far, [(rows, 0) for rows in rest], split, pair_far)
    losses = jnp.concatenate([loss_a, loss_b], axis=0)
    for i, r in enumerate(far):
        word_loss.append(exchange(losses[:, i], "seq", r))
    word_loss = sum(word_loss)

    sent = gradient(info, 1, BF16, n_y, n_high, [pair_near, pair_far])
    held, word_loss, sent = lax.optimization_barrier((info, word_loss, sent))
    kept = gradient(held, 0, F32, n_y, n_high, [pair_near, pair_far])
    terms = [[keep, exchange(send, "seq", 1)] for keep, send in zip(kept, sent)]

    def over_y(terms):
        total = pick_sum(terms, own["y"][0])
        for k in range(1, n_y):
            total = total + exchange(pick_sum(terms, own["y"][k]).astype(BF16), "seq", 2 * k)
        return total

    def over_low(terms, axis):
        other = pick_sum(terms, own["not_low"], axis).astype(BF16)
        return pick_sum(terms, own["low"], axis) + exchange(other, "dp", 1)

    one = over_low([over_y(terms[0])], 0)
    two = over_y([over_low(terms[1], 1)])
    part = lambda k: jnp.concatenate([pick(x, own["high"][k]) for x in (one, two)], axis=0)
    grad = part(0)
    for k in range(1, n_high):
        grad = grad + exchange(part(k).astype(BF16), "dp", 2 * k)
    return (word_loss, grad)


def solution(mesh):
    in_specs = (
        P("dp", "seq", None),
        P("dp", "seq", None),
        P("dp", None),
        P("dp", "seq", None),
        P("dp", "seq"),
        P("dp"),
        P("dp", None, None),
    )
    out_specs = (P("dp", "seq"), P("dp", "seq"))
    return jax.shard_map(local, mesh=mesh, in_specs=in_specs, out_specs=out_specs, check_vma=False)
```

time: 114 us -> 101 us (0.89)
  local copies, waits for them, and re-layouts: 16 us -> 3.37 us
  Pallas kernels: 41.7 us -> 32.9 us
  waiting for transfers between devices: 26.7 us -> 32.6 us
  starting transfers between devices: 25.4 us -> 27.6 us
    unnamed x35 -> x19, local copies, waits for them, and re-layouts: 15.8 us -> 2.49 us
    pallas_call x11 -> x10, Pallas kernels: 41.7 us -> 32.9 us  [call(): pl.pallas_call(kernel, grid_spec=pltpu.PrefetchScalarGridSpec(num_scalar_...]
    ppermute x27, waiting for transfers between devices: 26.7 us -> 32.6 us  [exchange(): return lax.ppermute(x, axis, [(i, i ^ offset) for i in range(n)])]
    ppermute x27, starting transfers between devices: 25.4 us -> 27.6 us  [exchange(): return lax.ppermute(x, axis, [(i, i ^ offset) for i in range(n)])]
  transfers between devices with their start and end apart: 27 -> 27, of which waited for: 11 -> 12; matrix products, arithmetic and copies ran while one was open for 2% -> 1% of each run, Pallas kernels for 25% -> 31%
where the time goes in v5:
time: 101 us
  Pallas kernels  32.9 us (33%)
  waiting for transfers between devices  32.6 us (32%)
  starting transfers between devices  27.6 us (27%)
  local copies, waits for them, and re-layouts  3.37 us (3%)
  other arithmetic  3.14 us (3%)
  between operations  1.02 us (1%)
    pallas_call x10, Pallas kernels, call(): pl.pallas_call(kernel, grid_spec=pltpu.PrefetchScalarGridSpec(num_scalar_...  32.9 us
    ppermute x27, waiting for transfers between devices, exchange(): return lax.ppermute(x, axis, [(i, i ^ offset) for i in range(n)])  32.6 us
    ppermute x27, starting transfers between devices, exchange(): return lax.ppermute(x, axis, [(i, i ^ offset) for i in range(n)])  27.6 us
    unnamed x19, local copies, waits for them, and re-layouts  2.49 us
  transfers between devices with their start and end apart: 27, of which 12 were waited for; matrix products, arithmetic and copies ran while one was open for 1% of the time, Pallas kernels for 31%

profile of v5, /device:TPU:0, one launch (start us, length us, event | category | flops | bytes accessed | tf_op | source)
XLA Modules:
  0.0 100.6 jit_solution(368684654856981971)
XLA Ops:
  0.7 0.8 pad_add_fusion.2.info
  1.7 3.1 %collective-permute-start = (bf16[1,128,512]{2,1,0:T(8,128)(2,1)S(1)}, bf16[1,128,512]{2,1,0:T(8,128)(2,1)S(1)}, u32[]{:S(2)}, u32[]{:S(2)}) collective-permute-start(bf16[1,128,512]{2,1,0:T(8,128)(2,1)S(1)} %dynamic-slice_bitcast_fusion), channel_id=1, source_target_pairs={{0,8},{4,12},{8,0},{12,4},{16,24},{20,28},{24,16},{28,20},{1,9},{5... | collective-permute-start | bytes 393224 | tf_op jit(solution)/shard_map/ppermute | solution.py:318
  4.8 3.5 %collective-permute-done = bf16[1,128,512]{2,1,0:T(8,128)(2,1)S(1)} collective-permute-done((bf16[1,128,512]{2,1,0:T(8,128)(2,1)S(1)}, bf16[1,128,512]{2,1,0:T(8,128)(2,1)S(1)}, u32[]{:S(2)}, u32[]{:S(2)}) %collective-permute-start) | collective-permute-done | bytes 131104 | tf_op jit(solution)/shard_map/ppermute | solution.py:318
  8.3 1.6 %copy-done.2 = bf16[4,256,1024]{2,1,0:T(8,128)(2,1)S(1)} copy-done((bf16[4,256,1024]{2,1,0:T(8,128)(2,1)S(1)}, bf16[4,256,1024]{2,1,0:T(8,128)(2,1)}, u32[]{:S(2)}) %copy-start.2) | copy-done | bytes 2097176
  9.9 0.7 copy-done.4
  10.6 1.3 %shard_map.86 = bf16[2,3,128,1024]{3,2,1,0:T(8,128)(2,1)S(1)} custom-call(s32[7]{0:T(128)S(1)} %pad_add_fusion.2.info, s32[4,1,256]{2,1,0:T(1,128)S(1)} %bitcast.60, bf16[4,256,1024]{2,1,0:T(8,128)(2,1)S(1)} %copy-done.2), custom_call_target="tpu_custom_call" | custom-call | tf_op jit(solution)/shard_map/pallas_call | solution.py:33
  11.9 1.7 %collective-permute-start.5 = (bf16[2,3,128,1024]{3,2,1,0:T(8,128)(2,1)S(1)}, bf16[2,3,128,1024]{3,2,1,0:T(8,128)(2,1)S(1)}, u32[]{:S(2)}, u32[]{:S(2)}) collective-permute-start(bf16[2,3,128,1024]{3,2,1,0:T(8,128)(2,1)S(1)} %shard_map.86), channel_id=1, source_target_pairs={{0,2},{1,3},{2,0},{3,1},{4,6},{5,7},{6,4},{7,5},{8,10},{9,11},{10,... | collective-permute-start | bytes 4718600 | tf_op jit(solution)/shard_map/ppermute | solution.py:318
  13.7 2.6 %collective-permute-start.2 = (bf16[2,128,512]{2,1,0:T(8,128)(2,1)S(1)}, bf16[2,128,512]{2,1,0:T(8,128)(2,1)S(1)}, u32[]{:S(2)}, u32[]{:S(2)}) collective-permute-start(bf16[2,128,512]{2,1,0:T(8,128)(2,1)S(1)} %pad_maximum_fusion.refs_0_), channel_id=1, source_target_pairs={{0,16},{4,20},{8,24},{12,28},{16,0},{20,4},{24,8},{28,12},{1,17},{... | collective-permute-start | bytes 786440 | tf_op jit(solution)/shard_map/ppermute | solution.py:318
  16.3 1.5 %collective-permute-start.1 = (bf16[2,128,512]{2,1,0:T(8,128)(2,1)S(1)}, bf16[2,128,512]{2,1,0:T(8,128)(2,1)S(1)}, u32[]{:S(2)}, u32[]{:S(2)}) collective-permute-start(bf16[2,128,512]{2,1,0:T(8,128)(2,1)S(1)} %pad_maximum_fusion.refs_0_), channel_id=1, source_target_pairs={{0,4},{4,0},{8,12},{12,8},{16,20},{20,16},{24,28},{28,24},{1,5},{5... | collective-permute-start | bytes 786440 | tf_op jit(solution)/shard_map/ppermute | solution.py:318
  17.8 9.3 %collective-permute-done.2.refs_2_ = bf16[2,128,512]{2,1,0:T(8,128)(2,1)S(1)} collective-permute-done((bf16[2,128,512]{2,1,0:T(8,128)(2,1)S(1)}, bf16[2,128,512]{2,1,0:T(8,128)(2,1)S(1)}, u32[]{:S(2)}, u32[]{:S(2)}) %collective-permute-start.2) | collective-permute-done | bytes 262176 | tf_op jit(solution)/shard_map/ppermute | solution.py:318
  27.1 1.5 %collective-permute-start.3 = (bf16[2,128,512]{2,1,0:T(8,128)(2,1)S(1)}, bf16[2,128,512]{2,1,0:T(8,128)(2,1)S(1)}, u32[]{:S(2)}, u32[]{:S(2)}) collective-permute-start(bf16[2,128,512]{2,1,0:T(8,128)(2,1)S(1)} %collective-permute-done.2.refs_2_), channel_id=1, source_target_pairs={{0,4},{4,0},{8,12},{12,8},{16,20},{20,16},{24,28},{28,24},{1,5},{5... | collective-permute-start | bytes 786440 | tf_op jit(solution)/shard_map/ppermute | solution.py:318
  28.7 1.2 %collective-permute-done.4 = s32[4,2,256]{2,1,0:T(2,128)S(1)} collective-permute-done((s32[4,2,256]{2,1,0:T(2,128)S(1)}, s32[4,2,256]{2,1,0:T(2,128)S(1)}, u32[]{:S(2)}, u32[]{:S(2)}) %collective-permute-start.4) | collective-permute-done | bytes 8224 | tf_op jit(solution)/shard_map/ppermute | solution.py:318
  29.9 1.5 %shard_map.87 = (bf16[1,4,128,1024]{3,2,1,0:T(8,128)(2,1)S(1)}, bf16[1,4,128,1024]{3,2,1,0:T(8,128)(2,1)S(1)}, bf16[1,1,128,1024]{3,2,1,0:T(8,128)(2,1)S(1)}, bf16[1,1,128,1024]{3,2,1,0:T(8,128)(2,1)S(1)}) custom-call(s32[7]{0:T(128)S(1)} %pad_add_fusion.2.info, s32[4,1,256]{2,1,0:T(1,128)S(1)} %bitcast.62, bf16[4,256,1024]{2,1,0:T(8,128)(2,1)S(1)} %copy-done.2), custom_call_target="tpu_custom_call" | custom-call | tf_op jit(solution)/shard_map/pallas_call | solution.py:33
  31.4 3.0 %shard_map.88 = (bf16[4,256,512]{2,1,0:T(8,128)(2,1)S(1)}, f32[4,256,128]{2,1,0:T(8,128)S(1)}, f32[4,8,256]{2,1,0:T(8,128)S(1)}) custom-call(s32[7]{0:T(128)S(1)} %pad_add_fusion.2.info, s32[2,4,2,256]{3,2,1,0:T(2,128)S(1)} %pad_add_fusion.meta, s32[4,16,32]{2,1,0:T(8,128)S(1)} %copy-done.3), custom_call_target="tpu_custom_call" | custom-call | tf_op jit(solution)/shard_map/pallas_call | solution.py:33
  34.7 0.3 collective-permute-start.7
  35.2 0.3 collective-permute-start.9
  35.5 0.5 collective-permute-done.6.refs_4_
  36.0 0.6 collective-permute-start.10
  36.8 0.4 collective-permute-done.9.refs_7_
  37.2 6.4 %shard_map.89.weight = bf16[4,1024,512]{2,1,0:T(8,128)(2,1)S(1)} custom-call(s32[7]{0:T(128)S(1)} %pad_add_fusion.2.info, bf16[4,512,1024]{2,1,0:T(8,128)(2,1)S(1)} %copy-done.1, bf16[2,128,512]{2,1,0:T(8,128)(2,1)S(1)} %pad_maximum_fusion.refs_0_, bf16[2,128,512]{2,1,0:T(8,128)(2,1)S(1)} %collective-permute-done.1.refs_1_, ...), custom_call_target="tpu_custom_call" | custom-call | tf_op jit(solution)/shard_map/pallas_call | solution.py:33
  43.6 4.3 %collective-permute-done.10.meta = s32[2,4,2,256]{3,2,1,0:T(2,128)S(1)} collective-permute-done((s32[2,4,2,256]{3,2,1,0:T(2,128)S(1)}, s32[2,4,2,256]{3,2,1,0:T(2,128)S(1)}, u32[]{:S(2)}, u32[]{:S(2)}) %collective-permute-start.10) | collective-permute-done | bytes 16416 | tf_op jit(solution)/shard_map/ppermute | solution.py:318
  47.9 0.5 collective-permute-start.11
  48.4 1.4 %collective-permute-start.14 = (bf16[1,1,128,1024]{3,2,1,0:T(8,128)(2,1)S(1)}, bf16[1,1,128,1024]{3,2,1,0:T(8,128)(2,1)S(1)}, u32[]{:S(2)}, u32[]{:S(2)}) collective-permute-start(bf16[1,1,128,1024]{3,2,1,0:T(8,128)(2,1)S(1)} %get-tuple-element.89), channel_id=1, source_target_pairs={{0,2},{1,3},{2,0},{3,1},{4,6},{5,7},{6,4},{7,5},{8,10},{9,11},{10,... | collective-permute-start | bytes 786440 | tf_op jit(solution)/shard_map/ppermute | solution.py:318
  49.8 3.0 %shard_map.91 = (bf16[4,256,512]{2,1,0:T(8,128)(2,1)S(1)}, f32[4,256,128]{2,1,0:T(8,128)S(1)}, f32[4,8,256]{2,1,0:T(8,128)S(1)}) custom-call(s32[7]{0:T(128)S(1)} %pad_add_fusion.2.info, s32[2,4,2,256]{3,2,1,0:T(2,128)S(1)} %collective-permute-done.10.meta, s32[4,16,32]{2,1,0:T(8,128)S(1)} %copy-done.3), custom_call_target="tpu_custom_call" | custom-call | tf_op jit(solution)/shard_map/pallas_call | solution.py:33
  52.8 5.3 %shard_map.90 = (f32[4,2,256]{2,1,0:T(2,128)S(1)}, bf16[1024,1024]{1,0:T(8,128)(2,1)S(1)}, bf16[1024,1024]{1,0:T(8,128)(2,1)S(1)}) custom-call(s32[7]{0:T(128)S(1)} %pad_add_fusion.2.info, bf16[4,256,512]{2,1,0:T(8,128)(2,1)S(1)} %get-tuple-element.71.bias, f32[4,256,128]{2,1,0:T(8,128)S(1)} %get-tuple-element.72.table, ...), custom_call_target="tpu_custom_call" | custom-call | tf_op jit(solution)/shard_map/pallas_call | solution.py:33
  58.1 0.6 slice_bitcast_fusion
  58.7 0.7 collective-permute-start.12
  59.4 4.1 %shard_map.92 = (f32[3,2,256]{2,1,0:T(2,128)S(1)}, bf16[1024,1024]{1,0:T(8,128)(2,1)S(1)}, bf16[1024,1024]{1,0:T(8,128)(2,1)S(1)}) custom-call(s32[7]{0:T(128)S(1)} %pad_add_fusion.2.info, bf16[4,256,512]{2,1,0:T(8,128)(2,1)S(1)} %get-tuple-element.84.bias, f32[4,256,128]{2,1,0:T(8,128)S(1)} %get-tuple-element.85.table, ...), custom_call_target="tpu_custom_call" | custom-call | tf_op jit(solution)/shard_map/pallas_call | solution.py:33
  63.6 1.7 %shard_map.93 = (f32[1,2,256]{2,1,0:T(2,128)S(1)}, bf16[1024,1024]{1,0:T(8,128)(2,1)S(1)}, bf16[1024,1024]{1,0:T(8,128)(2,1)S(1)}) custom-call(s32[7]{0:T(128)S(1)} %pad_add_fusion.2.info, bf16[4,256,512]{2,1,0:T(8,128)(2,1)S(1)} %get-tuple-element.84.bias, ...), custom_call_target="tpu_custom_call", output_to_operand_aliasing={{1}: (8, {}), {2}: (9, {})} | custom-call | tf_op jit(solution)/shard_map/pallas_call | solution.py:33
  65.3 1.1 %collective-permute-start.17 = (f32[4,256]{1,0:T(4,128)S(1)}, f32[4,256]{1,0:T(4,128)S(1)}, u32[]{:S(2)}, u32[]{:S(2)}) collective-permute-start(f32[4,256]{1,0:T(4,128)S(1)} %bitcast.64), channel_id=1, source_target_pairs={{0,3},{1,2},{2,1},{3,0},{4,7},{5,6},{6,5},{7,4},{8,11},{9,10},{10,... | collective-permute-start | bytes 12296 | tf_op jit(solution)/shard_map/ppermute | solution.py:318
  66.3 0.6 collective-permute-start.16
  67.0 3.4 %shard_map.94 = (bf16[2,2,4,64,256]{4,3,2,1,0:T(8,128)(2,1)S(1)}, bf16[2,2,4,64,256]{4,3,2,1,0:T(8,128)(2,1)S(1)}) custom-call(s32[7]{0:T(128)S(1)} %pad_add_fusion.2.info, bf16[1024,1024]{1,0:T(8,128)(2,1)S(1)} %get-tuple-element.94.refs_0_, bf16[1024,1024]{1,0:T(8,128)(2,1)S(1)} %get-tuple-element.95.refs_1_, ...), custom_call_target="tpu_custom_call" | custom-call | flops 137438953472 | tf_op jit(solution)/shard_map/pallas_call | solution.py:33
  70.4 1.3 %fusion.15 = f32[4,256]{1,0:T(4,128)} fusion(f32[4,256]{1,0:T(4,128)S(1)} %collective-permute-done.17, f32[4,256]{1,0:T(4,128)S(1)} %collective-permute-done.16, f32[4,256]{1,0:T(4,128)} %collective-permute-done.12, f32[4,2,256]{2,0,1:T(4,128)S(1)} %copy-done.6), kind=kLoop, calls=%fused_computation.43 | loop fusion | flops 3072 | bytes 20480 | tf_op jit(solution)/shard_map/add | solution.py:410
  71.7 0.3 collective-permute-start.21
  72.0 0.3 collective-permute-start.18
  72.3 3.4 %shard_map.95 = (f32[2,2,4,64,256]{4,3,2,1,0:T(8,128)S(1)}, f32[2,2,4,64,256]{4,3,2,1,0:T(8,128)S(1)}) custom-call(s32[7]{0:T(128)S(1)} %pad_add_fusion.2.info, bf16[1024,1024]{1,0:T(8,128)(2,1)S(1)} %get-tuple-element.94.refs_0_, bf16[1024,1024]{1,0:T(8,128)(2,1)S(1)} %get-tuple-element.95.refs_1_, bf16[1024,1024]{1,0:T(8,128)(2,1)S(1)} %get-tuple-element.96.refs_2_, ...), custom_call_target="tpu_custom_call" | custom-call | flops 137438953472 | tf_op jit(solution)/shard_map/pallas_call | solution.py:33
  75.8 1.4 %collective-permute-start.22 = (bf16[2,4,64,256]{3,2,1,0:T(8,128)(2,1)S(1)}, bf16[2,4,64,256]{3,2,1,0:T(8,128)(2,1)S(1)}, u32[]{:S(2)}, u32[]{:S(2)}) collective-permute-start(bf16[2,4,64,256]{3,2,1,0:T(8,128)(2,1)S(1)} %fusion.2), channel_id=1, source_target_pairs={{0,4},{4,0},{8,12},{12,8},{16,20},{20,16},{24,28},{28,24},{1,5},{5... | collective-permute-start | bytes 786440 | tf_op jit(solution)/shard_map/ppermute | solution.py:318
  77.3 1.6 %collective-permute-start.19 = (bf16[2,4,64,256]{3,2,1,0:T(8,128)(2,1)S(1)}, bf16[2,4,64,256]{3,2,1,0:T(8,128)(2,1)S(1)}, u32[]{:S(2)}, u32[]{:S(2)}) collective-permute-start(bf16[2,4,64,256]{3,2,1,0:T(8,128)(2,1)S(1)} %fusion.1), channel_id=1, source_target_pairs={{0,2},{1,3},{2,0},{3,1},{4,6},{5,7},{6,4},{7,5},{8,10},{9,11},{10,... | collective-permute-start | bytes 786440 | tf_op jit(solution)/shard_map/ppermute | solution.py:318
  78.9 5.4 %collective-permute-done.22 = bf16[2,4,64,256]{3,2,1,0:T(8,128)(2,1)S(1)} collective-permute-done((bf16[2,4,64,256]{3,2,1,0:T(8,128)(2,1)S(1)}, bf16[2,4,64,256]{3,2,1,0:T(8,128)(2,1)S(1)}, u32[]{:S(2)}, u32[]{:S(2)}) %collective-permute-start.22) | collective-permute-done | bytes 262176 | tf_op jit(solution)/shard_map/ppermute | solution.py:318
  84.4 1.5 %collective-permute-start.23 = (bf16[4,64,256]{2,1,0:T(8,128)(2,1)S(1)}, bf16[4,64,256]{2,1,0:T(8,128)(2,1)S(1)}, u32[]{:S(2)}, u32[]{:S(2)}) collective-permute-start(bf16[4,64,256]{2,1,0:T(8,128)(2,1)S(1)} %fusion.4), channel_id=1, source_target_pairs={{0,2},{1,3},{2,0},{3,1},{4,6},{5,7},{6,4},{7,5},{8,10},{9,11},{10,... | collective-permute-start | bytes 393224 | tf_op jit(solution)/shard_map/ppermute | solution.py:318
  86.0 1.5 %collective-permute-start.20 = (bf16[4,64,256]{2,1,0:T(8,128)(2,1)S(1)}, bf16[4,64,256]{2,1,0:T(8,128)(2,1)S(1)}, u32[]{:S(2)}, u32[]{:S(2)}) collective-permute-start(bf16[4,64,256]{2,1,0:T(8,128)(2,1)S(1)} %fusion.3), channel_id=1, source_target_pairs={{0,4},{4,0},{8,12},{12,8},{16,20},{20,16},{24,28},{28,24},{1,5},{5... | collective-permute-start | bytes 393224 | tf_op jit(solution)/shard_map/ppermute | solution.py:318
  87.5 1.9 %collective-permute-done.23 = bf16[4,64,256]{2,1,0:T(8,128)(2,1)S(1)} collective-permute-done((bf16[4,64,256]{2,1,0:T(8,128)(2,1)S(1)}, bf16[4,64,256]{2,1,0:T(8,128)(2,1)S(1)}, u32[]{:S(2)}, u32[]{:S(2)}) %collective-permute-start.23) | collective-permute-done | bytes 131104 | tf_op jit(solution)/shard_map/ppermute | solution.py:318
  89.5 1.5 %collective-permute-done.20 = bf16[4,64,256]{2,1,0:T(8,128)(2,1)S(1)} collective-permute-done((bf16[4,64,256]{2,1,0:T(8,128)(2,1)S(1)}, bf16[4,64,256]{2,1,0:T(8,128)(2,1)S(1)}, u32[]{:S(2)}, u32[]{:S(2)}) %collective-permute-start.20) | collective-permute-done | bytes 131104 | tf_op jit(solution)/shard_map/ppermute | solution.py:318
  91.1 3.6 %collective-permute-start.26 = (bf16[128,256]{1,0:T(8,128)(2,1)S(1)}, bf16[128,256]{1,0:T(8,128)(2,1)S(1)}, u32[]{:S(2)}, u32[]{:S(2)}) collective-permute-start(bf16[128,256]{1,0:T(8,128)(2,1)S(1)} %pad_maximum_fusion.3), channel_id=1, source_target_pairs={{0,24},{4,28},{8,16},{12,20},{16,8},{20,12},{24,0},{28,4},{1,25},{... | collective-permute-start | bytes 196616 | tf_op jit(solution)/shard_map/ppermute | solution.py:318
  94.8 0.8 collective-permute-start.24
  95.6 1.8 %collective-permute-done.26 = bf16[128,256]{1,0:T(8,128)(2,1)S(1)} collective-permute-done((bf16[128,256]{1,0:T(8,128)(2,1)S(1)}, bf16[128,256]{1,0:T(8,128)(2,1)S(1)}, u32[]{:S(2)}, u32[]{:S(2)}) %collective-permute-start.26) | collective-permute-done | bytes 65568 | tf_op jit(solution)/shard_map/ppermute | solution.py:318
  97.3 2.6 %collective-permute-done.25 = bf16[128,256]{1,0:T(8,128)(2,1)S(1)} collective-permute-done((bf16[128,256]{1,0:T(8,128)(2,1)S(1)}, bf16[128,256]{1,0:T(8,128)(2,1)S(1)}, u32[]{:S(2)}, u32[]{:S(2)}) %collective-permute-start.25) | collective-permute-done | bytes 65568 | tf_op jit(solution)/shard_map/ppermute | solution.py:318
  99.9 0.7 fusion.6
  (63 shorter events, 1.6 us)
Async XLA Ops:
  0.6 1.0 copy-start
  1.7 6.6 %collective-permute-start = (bf16[1,128,512]{2,1,0:T(8,128)(2,1)S(1)}, bf16[1,128,512]{2,1,0:T(8,128)(2,1)S(1)}, u32[]{:S(2)}, u32[]{:S(2)}) collective-permute-start(bf16[1,128,512]{2,1,0:T(8,128)(2,1)S(1)} %dynamic-slice_bitcast_fusion), channel_id=1, source_target_pairs={{0,8},{4,12},{8,0},{12,4},{16,24},{20,28},{24,16},{28,20},{1,9},{5... | collective-permute-start | bytes 393224 | tf_op jit(solution)/shard_map/ppermute | solution.py:318
  8.3 1.6 %copy-start.2 = (bf16[4,256,1024]{2,1,0:T(8,128)(2,1)S(1)}, bf16[4,256,1024]{2,1,0:T(8,128)(2,1)}, u32[]{:S(2)}) copy-start(bf16[4,256,1024]{2,1,0:T(8,128)(2,1)} %words.3) | copy-start | bytes 6291460
  9.9 0.7 copy-start.4
  10.6 18.1 %copy-start.7 = (s32[4,256]{1,0:T(4,128)S(1)}, s32[4,256]{1,0:T(4,128)}, u32[]{:S(2)}) copy-start(s32[4,256]{1,0:T(4,128)} %param.11) | copy-start | bytes 12292
  10.6 26.6 %copy-start.1 = (bf16[4,512,1024]{2,1,0:T(8,128)(2,1)S(1)}, bf16[4,512,1024]{2,1,0:T(8,128)(2,1)}, u32[]{:S(2)}) copy-start(bf16[4,512,1024]{2,1,0:T(8,128)(2,1)} %patches.7) | copy-start | bytes 12582916
  11.9 19.5 %copy-start.3 = (s32[4,16,32]{2,1,0:T(8,128)S(1)}, s32[4,16,32]{2,1,0:T(8,128)}, u32[]{:S(2)}) copy-start(s32[4,16,32]{2,1,0:T(8,128)} %flags.3) | copy-start | bytes 24580
  11.9 36.0 %collective-permute-start.5 = (bf16[2,3,128,1024]{3,2,1,0:T(8,128)(2,1)S(1)}, bf16[2,3,128,1024]{3,2,1,0:T(8,128)(2,1)S(1)}, u32[]{:S(2)}, u32[]{:S(2)}) collective-permute-start(bf16[2,3,128,1024]{3,2,1,0:T(8,128)(2,1)S(1)} %shard_map.86), channel_id=1, source_target_pairs={{0,2},{1,3},{2,0},{3,1},{4,6},{5,7},{6,4},{7,5},{8,10},{9,11},{10,... | collective-permute-start | bytes 4718600 | tf_op jit(solution)/shard_map/ppermute | solution.py:318
  13.7 13.5 %collective-permute-start.2 = (bf16[2,128,512]{2,1,0:T(8,128)(2,1)S(1)}, bf16[2,128,512]{2,1,0:T(8,128)(2,1)S(1)}, u32[]{:S(2)}, u32[]{:S(2)}) collective-permute-start(bf16[2,128,512]{2,1,0:T(8,128)(2,1)S(1)} %pad_maximum_fusion.refs_0_), channel_id=1, source_target_pairs={{0,16},{4,20},{8,24},{12,28},{16,0},{20,4},{24,8},{28,12},{1,17},{... | collective-permute-start | bytes 786440 | tf_op jit(solution)/shard_map/ppermute | solution.py:318
  16.3 18.1 %collective-permute-start.1 = (bf16[2,128,512]{2,1,0:T(8,128)(2,1)S(1)}, bf16[2,128,512]{2,1,0:T(8,128)(2,1)S(1)}, u32[]{:S(2)}, u32[]{:S(2)}) collective-permute-start(bf16[2,128,512]{2,1,0:T(8,128)(2,1)S(1)} %pad_maximum_fusion.refs_0_), channel_id=1, source_target_pairs={{0,4},{4,0},{8,12},{12,8},{16,20},{20,16},{24,28},{28,24},{1,5},{5... | collective-permute-start | bytes 786440 | tf_op jit(solution)/shard_map/ppermute | solution.py:318
  27.1 7.3 %collective-permute-start.3 = (bf16[2,128,512]{2,1,0:T(8,128)(2,1)S(1)}, bf16[2,128,512]{2,1,0:T(8,128)(2,1)S(1)}, u32[]{:S(2)}, u32[]{:S(2)}) collective-permute-start(bf16[2,128,512]{2,1,0:T(8,128)(2,1)S(1)} %collective-permute-done.2.refs_2_), channel_id=1, source_target_pairs={{0,4},{4,0},{8,12},{12,8},{16,20},{20,16},{24,28},{28,24},{1,5},{5... | collective-permute-start | bytes 786440 | tf_op jit(solution)/shard_map/ppermute | solution.py:318
  28.7 1.2 %collective-permute-start.4 = (s32[4,2,256]{2,1,0:T(2,128)S(1)}, s32[4,2,256]{2,1,0:T(2,128)S(1)}, u32[]{:S(2)}, u32[]{:S(2)}) collective-permute-start(s32[4,2,256]{2,1,0:T(2,128)S(1)} %get-tuple-element.123), channel_id=1, source_target_pairs={{0,1},{1,0},{2,3},{3,2},{4,5},{5,4},{6,7},{7,6},{8,9},{9,8},{10,11... | collective-permute-start | bytes 24584 | tf_op jit(solution)/shard_map/ppermute | solution.py:318
  34.4 1.6 %collective-permute-start.6 = (bf16[2,128,512]{2,1,0:T(8,128)(2,1)S(1)}, bf16[2,128,512]{2,1,0:T(8,128)(2,1)S(1)}, u32[]{:S(2)}, u32[]{:S(2)}) collective-permute-start(bf16[2,128,512]{2,1,0:T(8,128)(2,1)S(1)} %pad_maximum_fusion.refs_0_), channel_id=1, source_target_pairs={{0,1},{1,0},{2,3},{3,2},{4,5},{5,4},{6,7},{7,6},{8,9},{9,8},{10,11... | collective-permute-start | bytes 786440 | tf_op jit(solution)/shard_map/ppermute | solution.py:318
  34.7 2.0 %collective-permute-start.7 = (bf16[2,128,512]{2,1,0:T(8,128)(2,1)S(1)}, bf16[2,128,512]{2,1,0:T(8,128)(2,1)S(1)}, u32[]{:S(2)}, u32[]{:S(2)}) collective-permute-start(bf16[2,128,512]{2,1,0:T(8,128)(2,1)S(1)} %collective-permute-done.1.refs_1_), channel_id=1, source_target_pairs={{0,1},{1,0},{2,3},{3,2},{4,5},{5,4},{6,7},{7,6},{8,9},{9,8},{10,11... | collective-permute-start | bytes 786440 | tf_op jit(solution)/shard_map/ppermute | solution.py:318
  35.0 1.8 %collective-permute-start.8 = (bf16[2,128,512]{2,1,0:T(8,128)(2,1)S(1)}, bf16[2,128,512]{2,1,0:T(8,128)(2,1)S(1)}, u32[]{:S(2)}, u32[]{:S(2)}) collective-permute-start(bf16[2,128,512]{2,1,0:T(8,128)(2,1)S(1)} %collective-permute-done.2.refs_2_), channel_id=1, source_target_pairs={{0,1},{1,0},{2,3},{3,2},{4,5},{5,4},{6,7},{7,6},{8,9},{9,8},{10,11... | collective-permute-start | bytes 786440 | tf_op jit(solution)/shard_map/ppermute | solution.py:318
  35.2 2.0 %collective-permute-start.9 = (bf16[2,128,512]{2,1,0:T(8,128)(2,1)S(1)}, bf16[2,128,512]{2,1,0:T(8,128)(2,1)S(1)}, u32[]{:S(2)}, u32[]{:S(2)}) collective-permute-start(bf16[2,128,512]{2,1,0:T(8,128)(2,1)S(1)} %collective-permute-done.3.refs_3_), channel_id=1, source_target_pairs={{0,1},{1,0},{2,3},{3,2},{4,5},{5,4},{6,7},{7,6},{8,9},{9,8},{10,11... | collective-permute-start | bytes 786440 | tf_op jit(solution)/shard_map/ppermute | solution.py:318
  36.0 11.9 %collective-permute-start.10 = (s32[2,4,2,256]{3,2,1,0:T(2,128)S(1)}, s32[2,4,2,256]{3,2,1,0:T(2,128)S(1)}, u32[]{:S(2)}, u32[]{:S(2)}) collective-permute-start(s32[2,4,2,256]{3,2,1,0:T(2,128)S(1)} %pad_add_fusion.meta), channel_id=1, source_target_pairs={{0,2},{1,3},{2,0},{3,1},{4,6},{5,7},{6,4},{7,5},{8,10},{9,11},{10,... | collective-permute-start | bytes 49160 | tf_op jit(solution)/shard_map/ppermute | solution.py:318
  47.9 11.5 %collective-permute-start.13 = (bf16[2,3,128,1024]{3,2,1,0:T(8,128)(2,1)S(1)}, bf16[2,3,128,1024]{3,2,1,0:T(8,128)(2,1)S(1)}, u32[]{:S(2)}, u32[]{:S(2)}) collective-permute-start(bf16[2,3,128,1024]{3,2,1,0:T(8,128)(2,1)S(1)} %collective-permute-done.5.refs_0_), channel_id=1, source_target_pairs={{0,1},{1,0},{2,3},{3,2},{4,5},{5,4},{6,7},{7,6},{8,9},{9,8},{10,11... | collective-permute-start | bytes 4718600 | tf_op jit(solution)/shard_map/ppermute | solution.py:318
  47.9 4.9 %collective-permute-start.11 = (bf16[1,4,128,1024]{3,2,1,0:T(8,128)(2,1)S(1)}, bf16[1,4,128,1024]{3,2,1,0:T(8,128)(2,1)S(1)}, u32[]{:S(2)}, u32[]{:S(2)}) collective-permute-start(bf16[1,4,128,1024]{3,2,1,0:T(8,128)(2,1)S(1)} %get-tuple-element.81), channel_id=1, source_target_pairs={{0,1},{1,0},{2,3},{3,2},{4,5},{5,4},{6,7},{7,6},{8,9},{9,8},{10,11... | collective-permute-start | bytes 3145736 | tf_op jit(solution)/shard_map/ppermute | solution.py:318
  48.4 15.1 %collective-permute-start.14 = (bf16[1,1,128,1024]{3,2,1,0:T(8,128)(2,1)S(1)}, bf16[1,1,128,1024]{3,2,1,0:T(8,128)(2,1)S(1)}, u32[]{:S(2)}, u32[]{:S(2)}) collective-permute-start(bf16[1,1,128,1024]{3,2,1,0:T(8,128)(2,1)S(1)} %get-tuple-element.89), channel_id=1, source_target_pairs={{0,2},{1,3},{2,0},{3,1},{4,6},{5,7},{6,4},{7,5},{8,10},{9,11},{10,... | collective-permute-start | bytes 786440 | tf_op jit(solution)/shard_map/ppermute | solution.py:318
  49.8 13.8 %collective-permute-start.15 = (bf16[1,1,128,1024]{3,2,1,0:T(8,128)(2,1)S(1)}, bf16[1,1,128,1024]{3,2,1,0:T(8,128)(2,1)S(1)}, u32[]{:S(2)}, u32[]{:S(2)}) collective-permute-start(bf16[1,1,128,1024]{3,2,1,0:T(8,128)(2,1)S(1)} %get-tuple-element.90), channel_id=1, source_target_pairs={{0,3},{1,2},{2,1},{3,0},{4,7},{5,6},{6,5},{7,4},{8,11},{9,10},{10,... | collective-permute-start | bytes 786440 | tf_op jit(solution)/shard_map/ppermute | solution.py:318
  58.1 5.4 %copy-start.5 = (f32[4,2,256]{2,0,1:T(4,128)}, f32[4,2,256]{2,0,1:T(4,128)S(1)}, u32[]{:S(2)}) copy-start(f32[4,2,256]{2,0,1:T(4,128)S(1)} %copy.11) | copy-start | bytes 24580
  58.7 11.7 %collective-permute-start.12 = (f32[4,256]{1,0:T(4,128)}, f32[4,256]{1,0:T(4,128)}, u32[]{:S(2)}, u32[]{:S(2)}) collective-permute-start(f32[4,256]{1,0:T(4,128)} %slice_bitcast_fusion), channel_id=1, source_target_pairs={{0,1},{1,0},{2,3},{3,2},{4,5},{5,4},{6,7},{7,6},{8,9},{9,8},{10,11... | collective-permute-start | bytes 12296 | tf_op jit(solution)/shard_map/ppermute | solution.py:318
  65.3 5.1 %collective-permute-start.17 = (f32[4,256]{1,0:T(4,128)S(1)}, f32[4,256]{1,0:T(4,128)S(1)}, u32[]{:S(2)}, u32[]{:S(2)}) collective-permute-start(f32[4,256]{1,0:T(4,128)S(1)} %bitcast.64), channel_id=1, source_target_pairs={{0,3},{1,2},{2,1},{3,0},{4,7},{5,6},{6,5},{7,4},{8,11},{9,10},{10,... | collective-permute-start | bytes 12296 | tf_op jit(solution)/shard_map/ppermute | solution.py:318
  66.3 4.1 %collective-permute-start.16 = (f32[4,256]{1,0:T(4,128)S(1)}, f32[4,256]{1,0:T(4,128)S(1)}, u32[]{:S(2)}, u32[]{:S(2)}) collective-permute-start(f32[4,256]{1,0:T(4,128)S(1)} %bitcast.65), channel_id=1, source_target_pairs={{0,2},{1,3},{2,0},{3,1},{4,6},{5,7},{6,4},{7,5},{8,10},{9,11},{10,... | collective-permute-start | bytes 12296 | tf_op jit(solution)/shard_map/ppermute | solution.py:318
  67.0 3.4 %copy-start.6 = (f32[4,2,256]{2,0,1:T(4,128)S(1)}, f32[4,2,256]{2,0,1:T(4,128)}, u32[]{:S(2)}) copy-start(f32[4,2,256]{2,0,1:T(4,128)} %copy-done.5) | copy-start | bytes 24580
  71.7 4.0 %collective-permute-start.21 = (bf16[2,2,4,64,256]{4,3,2,0,1:T(8,128)(2,1)S(1)}, bf16[2,2,4,64,256]{4,3,2,0,1:T(8,128)(2,1)S(1)}, u32[]{:S(2)}, u32[]{:S(2)}) collective-permute-start(bf16[2,2,4,64,256]{4,3,2,0,1:T(8,128)(2,1)S(1)} %copy.15), channel_id=1, source_target_pairs={{0,1},{1,0},{2,3},{3,2},{4,5},{5,4},{6,7},{7,6},{8,9},{9,8},{10,11... | collective-permute-start | bytes 1572872 | tf_op jit(solution)/shard_map/ppermute | solution.py:318
  72.0 5.2 %collective-permute-start.18 = (bf16[2,2,4,64,256]{4,3,2,1,0:T(8,128)(2,1)S(1)}, bf16[2,2,4,64,256]{4,3,2,1,0:T(8,128)(2,1)S(1)}, u32[]{:S(2)}, u32[]{:S(2)}) collective-permute-start(bf16[2,2,4,64,256]{4,3,2,1,0:T(8,128)(2,1)S(1)} %get-tuple-element.104), channel_id=1, source_target_pairs={{0,1},{1,0},{2,3},{3,2},{4,5},{5,4},{6,7},{7,6},{8,9},{9,8},{10,11... | collective-permute-start | bytes 1572872 | tf_op jit(solution)/shard_map/ppermute | solution.py:318
  75.8 8.5 %collective-permute-start.22 = (bf16[2,4,64,256]{3,2,1,0:T(8,128)(2,1)S(1)}, bf16[2,4,64,256]{3,2,1,0:T(8,128)(2,1)S(1)}, u32[]{:S(2)}, u32[]{:S(2)}) collective-permute-start(bf16[2,4,64,256]{3,2,1,0:T(8,128)(2,1)S(1)} %fusion.2), channel_id=1, source_target_pairs={{0,4},{4,0},{8,12},{12,8},{16,20},{20,16},{24,28},{28,24},{1,5},{5... | collective-permute-start | bytes 786440 | tf_op jit(solution)/shard_map/ppermute | solution.py:318
  77.3 8.6 %collective-permute-start.19 = (bf16[2,4,64,256]{3,2,1,0:T(8,128)(2,1)S(1)}, bf16[2,4,64,256]{3,2,1,0:T(8,128)(2,1)S(1)}, u32[]{:S(2)}, u32[]{:S(2)}) collective-permute-start(bf16[2,4,64,256]{3,2,1,0:T(8,128)(2,1)S(1)} %fusion.1), channel_id=1, source_target_pairs={{0,2},{1,3},{2,0},{3,1},{4,6},{5,7},{6,4},{7,5},{8,10},{9,11},{10,... | collective-permute-start | bytes 786440 | tf_op jit(solution)/shard_map/ppermute | solution.py:318
  84.4 5.0 %collective-permute-start.23 = (bf16[4,64,256]{2,1,0:T(8,128)(2,1)S(1)}, bf16[4,64,256]{2,1,0:T(8,128)(2,1)S(1)}, u32[]{:S(2)}, u32[]{:S(2)}) collective-permute-start(bf16[4,64,256]{2,1,0:T(8,128)(2,1)S(1)} %fusion.4), channel_id=1, source_target_pairs={{0,2},{1,3},{2,0},{3,1},{4,6},{5,7},{6,4},{7,5},{8,10},{9,11},{10,... | collective-permute-start | bytes 393224 | tf_op jit(solution)/shard_map/ppermute | solution.py:318
  86.0 5.0 %collective-permute-start.20 = (bf16[4,64,256]{2,1,0:T(8,128)(2,1)S(1)}, bf16[4,64,256]{2,1,0:T(8,128)(2,1)S(1)}, u32[]{:S(2)}, u32[]{:S(2)}) collective-permute-start(bf16[4,64,256]{2,1,0:T(8,128)(2,1)S(1)} %fusion.3), channel_id=1, source_target_pairs={{0,4},{4,0},{8,12},{12,8},{16,20},{20,16},{24,28},{28,24},{1,5},{5... | collective-permute-start | bytes 393224 | tf_op jit(solution)/shard_map/ppermute | solution.py:318
  91.1 6.2 %collective-permute-start.26 = (bf16[128,256]{1,0:T(8,128)(2,1)S(1)}, bf16[128,256]{1,0:T(8,128)(2,1)S(1)}, u32[]{:S(2)}, u32[]{:S(2)}) collective-permute-start(bf16[128,256]{1,0:T(8,128)(2,1)S(1)} %pad_maximum_fusion.3), channel_id=1, source_target_pairs={{0,24},{4,28},{8,16},{12,20},{16,8},{20,12},{24,0},{28,4},{1,25},{... | collective-permute-start | bytes 196616 | tf_op jit(solution)/shard_map/ppermute | solution.py:318
  94.8 5.2 %collective-permute-start.25 = (bf16[128,256]{1,0:T(8,128)(2,1)S(1)}, bf16[128,256]{1,0:T(8,128)(2,1)S(1)}, u32[]{:S(2)}, u32[]{:S(2)}) collective-permute-start(bf16[128,256]{1,0:T(8,128)(2,1)S(1)} %pad_maximum_fusion.2), channel_id=1, source_target_pairs={{0,16},{4,20},{8,24},{12,28},{16,0},{20,4},{24,8},{28,12},{1,17},{... | collective-permute-start | bytes 196616 | tf_op jit(solution)/shard_map/ppermute | solution.py:318
  94.8 5.1 %collective-permute-start.24 = (bf16[128,256]{1,0:T(8,128)(2,1)S(1)}, bf16[128,256]{1,0:T(8,128)(2,1)S(1)}, u32[]{:S(2)}, u32[]{:S(2)}) collective-permute-start(bf16[128,256]{1,0:T(8,128)(2,1)S(1)} %pad_maximum_fusion.1), channel_id=1, source_target_pairs={{0,8},{4,12},{8,0},{12,4},{16,24},{20,28},{24,16},{28,20},{1,9},{5... | collective-permute-start | bytes 196616 | tf_op jit(solution)/shard_map/ppermute | solution.py:318

commit v6 on v5

--- a/solution.py
+++ b/solution.py
@@ -9,7 +9,8 @@
 from jax.sharding import PartitionSpec as P
 
 MARGIN_BLOCK_SIZE = 64
-VMEM_LIMIT = 20 * 1024 * 1024
+SHIFT = 6
+VMEM_LIMIT = 16 * 1024 * 1024
 ME, CORE, DP, COUNTS = 0, 1, 2, 3
 TARGET, COEF = 0, 1
 F32, BF16 = jnp.float32, jnp.bfloat16
@@ -128,7 +129,7 @@
         )
     )
     first = me * (pps // MARGIN_BLOCK_SIZE)
-    block = iota((all_blk, pps), 1) // MARGIN_BLOCK_SIZE
+    block = iota((all_blk, pps), 1) >> SHIFT
     spread = (iota((all_blk, pps), 0) == first + block).astype(BF16)
     place = iota((1, wdev), 1) + 1
     for p in range(pages):
@@ -137,17 +138,17 @@
             own = rank[p * n_homes + i : p * n_homes + i + 1]
             rank_out[p, i : i + 1] = own
             target = meta[i, p, 1:2, :]
-            values = stacked([target // 64, target % 64, place // 64, place % 64]).astype(F32)
+            values = stacked([target >> 6, target & 63, place >> 6, place & 63]).astype(F32)
             got = dot((slots == own).astype(BF16), values.astype(BF16), ((1,), (1,)))
             got = got.astype(jnp.int32)
             t.append(got[:, 0:1] * 64 + got[:, 1:2])
             at = got[:, 2:3] * 64 + got[:, 3:4]
             idx.append(jnp.where(at > 0, at - 1 + jnp.bitwise_xor(me, offset) * wdev, -1))
         t, idx = jnp.concatenate(t, axis=0), jnp.concatenate(idx, axis=0)
-        word_block = jnp.maximum(idx, 0) // MARGIN_BLOCK_SIZE == iota((n_rows, nblk), 1)
+        word_block = jnp.maximum(idx, 0) >> SHIFT == iota((n_rows, nblk), 1)
         margin = dot(word_block.astype(BF16), flags[p].astype(BF16)).astype(BF16)
         hit = dot(margin, spread)
-        own = iota((n_rows, pps), 1) // MARGIN_BLOCK_SIZE == t // MARGIN_BLOCK_SIZE
+        own = iota((n_rows, pps), 1) >> SHIFT == t >> SHIFT
         bias[p] = jnp.where((hit > 0.5) | own, 0.0, -jnp.inf).astype(BF16)
         count = info[COUNTS + p]
         valid = (idx >= 0) & (idx < count)
@@ -220,8 +221,8 @@
     )
 
 
-def page_kernel(n_homes, cut, info, bias, table, rank, weight, patches, *refs):
-    words, (loss, x_t, dq) = refs[:n_homes], refs[-3:]
+def page_kernel(n_homes, info, bias, table, rank, weight, patches, *refs):
+    *words, loss, x_t, dq = refs
     pps, width = patches.shape[1:]
     cap = words[0].shape[2]
     n_rows = n_homes * cap
@@ -248,67 +249,58 @@
     for r in range(n_homes):
         picked = jnp.where(slots == rank[0, r : r + 1, :], row_loss[r * cap : (r + 1) * cap], 0.0)
         loss[0, r : r + 1, :] = jnp.sum(picked, axis=0, keepdims=True)
-    t = x.T
-    for part in range(width // cut):
-        to = part % 2 * (width // 2) + part // 2 * cut
-        x_t[to : to + cut] = t[part * cut : (part + 1) * cut]
-
-
-def run_pages(cut, info, weight, patches, table, words, first_page, kept=None):
+    x_t[...] = x.T
+
+
+def run_pages(info, weight, patches, table, words, first_page):
     _, n_pages, cap, width = words[0][0].shape
-    pages, wdev = patches.shape[0], table[2].shape[2]
+    wdev = table[2].shape[2]
     n_homes = len(words)
     n_rows = -(-n_homes * cap // 128) * 128
     out = [
         jax.ShapeDtypeStruct((n_pages, n_homes, wdev), F32),
-        jax.ShapeDtypeStruct((width, pages * n_rows), BF16),
-        jax.ShapeDtypeStruct((pages * n_rows, width), BF16),
+        jax.ShapeDtypeStruct((width, n_pages * n_rows), BF16),
+        jax.ShapeDtypeStruct((n_pages * n_rows, width), BF16),
     ]
     inputs = (*table, weight, patches)
-    n = 1 + len(inputs) + n_homes
     return call(
-        functools.partial(page_kernel, n_homes, cut),
+        functools.partial(page_kernel, n_homes),
         n_pages,
         [page_of(a, first_page) for a in inputs]
-        + [pl.BlockSpec((1, 1, cap, width), lambda p, info, i=i: (i, p, 0, 0)) for _, i in words]
-        + [pl.BlockSpec(memory_space=pl.ANY)] * (2 if kept else 0),
+        + [pl.BlockSpec((1, 1, cap, width), lambda p, info, i=i: (i, p, 0, 0)) for _, i in words],
         [
             page_of(out[0]),
-            pl.BlockSpec((width, n_rows), lambda p, info: (0, p + first_page)),
-            pl.BlockSpec((n_rows, width), lambda p, info: (p + first_page, 0)),
+            pl.BlockSpec((width, n_rows), lambda p, info: (0, p)),
+            pl.BlockSpec((n_rows, width), lambda p, info: (p, 0)),
         ],
         out,
-        (info, *inputs, *(w for w, _ in words), *(kept or ())),
-        aliases={n: 1, n + 1: 2} if kept else {},
-    )
-
-
-def gradient_kernel(info, *refs):
-    *pairs, one, two = refs
-    _, lows, highs, cut, _ = one.shape
+        (info, *inputs, *(w for w, _ in words)),
+    )
+
+
+def gradient_kernel(n_pairs, info, *refs):
+    pairs, (*before, out) = refs[: 2 * n_pairs], refs[2 * n_pairs :]
     got = sum(dot(pairs[i][...], pairs[i + 1][...]) for i in range(0, len(pairs), 2))
-    for part in range(2 * lows * highs):
-        out, shard = (one, two)[part // (lows * highs)], part % (lows * highs)
-        rows = got[part * cut : (part + 1) * cut]
-        out[0, shard % lows, shard // lows] = rows.astype(out.dtype)
-
-
-def gradient(info, other, dtype, n_y, n_high, pairs):
+    for part in before:
+        got = got + part[0]
+    out[0] = got.astype(out.dtype)
+
+
+def gradient(info, other, dtype, n_y, pairs, before=()):
     width = pairs[0][0].shape[0]
     wcol = width // (2 * n_y)
-    form = (n_y, 2, n_high, width // (4 * n_high), wcol)
-    out = [jax.ShapeDtypeStruct(form, dtype)] * 2
+    out = jax.ShapeDtypeStruct((n_y, width, wcol), dtype)
     column = lambda y, info: (0, 2 * y + jnp.bitwise_xor(info[CORE], other))
     specs = []
     for x_t, dq in pairs:
         specs += [all_of(x_t), pl.BlockSpec((dq.shape[0], wcol), column)]
     return call(
-        gradient_kernel,
+        functools.partial(gradient_kernel, len(pairs)),
         n_y,
-        specs,
-        [page_of(o) for o in out],
+        specs + [page_of(b) for b in before],
+        page_of(out),
         out,
-        (info, *(x for pair in pairs for x in pair)),
+        (info, *(x for pair in pairs for x in pair), *before),
         flops=64 * width * width * sum(dq.shape[0] for _, dq in pairs),
     )
 
@@ -318,15 +310,18 @@
     return lax.ppermute(x, axis, [(i, i ^ offset) for i in range(n)])
 
 
-def pick(x, i, axis=0):
-    start = [i if a == axis else 0 for a in range(x.ndim)]
-    size = [1 if a == axis else n for a, n in enumerate(x.shape)]
+def exchange_both(x, dp, seq):
+    n_seq = lax.axis_size("seq")
+    n = lax.axis_size("dp") * n_seq
+    return lax.ppermute(x, ("dp", "seq"), [(i, i ^ (dp * n_seq + seq)) for i in range(n)])
+
+
+def pick(x, places):
+    places = list(places) + [None] * (x.ndim - len(places))
+    start = [0 if i is None else i for i in places]
+    size = [n if i is None else 1 for i, n in zip(places, x.shape)]
     got = lax.dynamic_slice(x, start, size, allow_negative_indices=False)
-    return got.reshape(x.shape[:axis] + x.shape[axis + 1 :])
-
-
-def pick_sum(terms, i, axis=0):
-    return sum(pick(t, i, axis).astype(F32) for t in terms)
+    return got.reshape([n for i, n in zip(places, x.shape) if i is None])
 
 
 def local(words, patches, proj, routes, targets, counts, flags):
@@ -344,8 +339,7 @@
     core, y, low, high = me & 1, me >> 1, my_dp & 1, my_dp >> 1
     own = {
         "column": core * half,
-        "low": low,
-        "not_low": 1 - low,
+        "low": [low ^ k for k in range(2)],
         "y": [y ^ k for k in range(n_y)],
         "high": [high ^ k for k in range(n_high)],
     }
@@ -353,84 +347,73 @@
     info, own, proj = lax.optimization_barrier((info, own, proj))
     routes = routes.reshape(pages, 1, wdev)
 
-    piece = lax.dynamic_slice(
-        proj, (0, own["column"]), (shard_rows, half), allow_negative_indices=False
-    )
-    piece, bit = piece[None], 1
-    other = exchange(piece, "dp", 2)
-    info, other = lax.optimization_barrier((info, other))
-    pieces = [(piece, 0), (other, bit)]
-    while 2 * bit < n_high:
-        piece, bit = jnp.concatenate([piece, other], axis=0), 2 * bit
-        other = exchange(piece, "dp", 2 * bit)
-        pieces = [(piece, 0), (other, bit)]
-
     split = pages - 1
     both = dispatch(
         info, routes, words, [((2 * k, 2 * k + 1), 0, split) for k in range(1, n_y)], cap
     )
-    held, both = lax.optimization_barrier((info, both))
+    info, proj, both = lax.optimization_barrier((info, proj, both))
     both = [exchange(rows, "seq", 2 * (k + 1)) for k, rows in enumerate(both)]
     stay, across, *rest = dispatch(
-        held,
+        info,
         routes,
         words,
         [((r,), 0, pages) for r in near] + [((r,), split, pages - split) for r in far],
         cap,
     )
 
+    piece = lax.dynamic_slice(
+        proj, (0, own["column"]), (shard_rows, half), allow_negative_indices=False
+    )
+    pieces = [piece] + [exchange(piece, "dp", 2 * k) for k in range(1, n_high)]
+    group = n_high // 2
+    groups = [jnp.stack(pieces[i : i + group]) for i in range(0, n_high, group)]
+
     pair = jnp.concatenate([routes, targets.reshape(pages, 1, wdev)], axis=1)
     meta_near = jnp.stack([pair, exchange(pair, "seq", 1)])
     table_near = tables(info, meta_near, flags, near, cap, pps)
     meta_far = jnp.concatenate([exchange(meta_near, "seq", 2 * k) for k in range(1, n_y)], axis=0)
 
-    gathered, offsets = [], []
-    for piece, start in pieces:
-        gathered += [piece, exchange(piece, "dp", 1)]
-        offsets += [[2 * (start + i) + low for i in range(piece.shape[0])] for low in range(2)]
-    gathered, rest, stay, across, table_near = lax.optimization_barrier(
-        (gathered, rest, stay, across, table_near)
-    )
-    gathered += [exchange(piece, "seq", 1) for piece in gathered]
+    crossed = exchange(groups[0], "dp", 1)
+    crossed, groups[1], rest, stay, across, table_near = lax.optimization_barrier(
+        (crossed, groups[1], rest, stay, across, table_near)
+    )
+    gathered = [groups[0], crossed, groups[1], exchange(groups[1], "dp", 1)]
+    offsets = [[2 * (i + k) + bit for k in range(group)] for i in (0, group) for bit in range(2)]
+    gathered += [exchange(some, "seq", 1) for some in gathered]
     across = exchange(across, "seq", 1)
     rest = [exchange(rows, "seq", r) for rows, r in zip(rest, far)]
     weight = weights(info, patches, gathered, offsets)
-
-    both, weight, meta_far = lax.optimization_barrier((both, weight, meta_far))
+    run = functools.partial(run_pages, info, weight, patches)
+    loss, *pair_near = run(table_near, [(stay, 0), (across, 0)], 0)
+    word_loss = [loss[:, 0], exchange(loss[:, 1], "seq", 1)]
+
+    both, meta_far, pair_near = lax.optimization_barrier((both, meta_far, pair_near))
     first = [pair for rows in both for pair in ((rows, 0), (exchange(rows, "seq", 1), 1))]
     table_far = tables(info, meta_far, flags, far, cap, pps)
-    run = functools.partial(run_pages, shard_rows // 2, info, weight, patches)
-    loss, *pair_near = run(table_near, [(stay, 0), (across, 0)], 0)
-    word_loss = [loss[:, 0], exchange(loss[:, 1], "seq", 1)]
-    loss_a, *pair_far = run(table_far, first, 0)
-    loss_b, *pair_far = run(table_far, [(rows, 0) for rows in rest], split, pair_far)
+    loss_a, *pair_a = run(table_far, first, 0)
+    before = [gradient(info, other, F32, n_y, [pair_near, pair_a]) for other in range(2)]
+    before, rest = lax.optimization_barrier((before, rest))
+    loss_b, *pair_b = run(table_far, [(rows, 0) for rows in rest], split)
     losses = jnp.concatenate([loss_a, loss_b], axis=0)
     for i, r in enumerate(far):
         word_loss.append(exchange(losses[:, i], "seq", r))
-    word_loss = sum(word_loss)
-
-    sent = gradient(info, 1, BF16, n_y, n_high, [pair_near, pair_far])
-    held, word_loss, sent = lax.optimization_barrier((info, word_loss, sent))
-    kept = gradient(held, 0, F32, n_y, n_high, [pair_near, pair_far])
-    terms = [[keep, exchange(send, "seq", 1)] for keep, send in zip(kept, sent)]
-
-    def over_y(terms):
-        total = pick_sum(terms, own["y"][0])
-        for k in range(1, n_y):
-            total = total + exchange(pick_sum(terms, own["y"][k]).astype(BF16), "seq", 2 * k)
-        return total
-
-    def over_low(terms, axis):
-        other = pick_sum(terms, own["not_low"], axis).astype(BF16)
-        return pick_sum(terms, own["low"], axis) + exchange(other, "dp", 1)
-
-    one = over_low([over_y(terms[0])], 0)
-    two = over_y([over_low(terms[1], 1)])
-    part = lambda k: jnp.concatenate([pick(x, own["high"][k]) for x in (one, two)], axis=0)
-    grad = part(0)
+
+    sent = gradient(info, 1, BF16, n_y, [pair_b], [before[1]])
+    kept = gradient(info, 0, F32, n_y, [pair_b], [before[0]])
+    form = (n_y, n_high, 2, shard_rows, width // n_seq)
+    terms = [kept.reshape(form), exchange(sent, "seq", 1).reshape(form)]
+    part = lambda i, j: sum(
+        pick(t, (own["y"][i], None, own["low"][j])).astype(F32) for t in terms
+    )
+    total = part(0, 0)
+    for i in range(n_y):
+        for j in range(2):
+            if i or j:
+                total = total + exchange_both(part(i, j).astype(BF16), j, 2 * i)
+    grad = pick(total, (own["high"][0],))
     for k in range(1, n_high):
-        grad = grad + exchange(part(k).astype(BF16), "dp", 2 * k)
-    return (word_loss, grad)
+        grad = grad + exchange(pick(total, (own["high"][k],)).astype(BF16), "dp", 2 * k)
+    return (sum(word_loss), grad)
 
 
 def solution(mesh):

time: 101 us -> 96.6 us (0.956)
  waiting for transfers between devices: 32.6 us -> 27.3 us
  Pallas kernels: 32.9 us -> 36.5 us
  starting transfers between devices: 27.6 us -> 25.1 us
    ppermute x27 -> x23, waiting for transfers between devices: 32.6 us -> 17.1 us  [exchange(): return lax.ppermute(x, axis, [(i, i ^ offset) for i in range(n)])]
    ppermute x0 -> x3, waiting for transfers between devices: none -> 10.3 us  [exchange_both(): lax.ppermute(x, ('dp', 'seq'), [(i, i ^ dp * n_seq + seq) for i in range(...]
    ppermute x27 -> x23, starting transfers between devices: 27.6 us -> 21.5 us  [exchange(): return lax.ppermute(x, axis, [(i, i ^ offset) for i in range(n)])]
    ppermute x0 -> x3, starting transfers between devices: none -> 3.55 us  [exchange_both(): lax.ppermute(x, ('dp', 'seq'), [(i, i ^ dp * n_seq + seq) for i in range(...]
    pallas_call x10 -> x12, Pallas kernels: 32.9 us -> 36.5 us  [call(): pl.pallas_call(kernel, grid_spec=pltpu.PrefetchScalarGridSpec(num_scalar_...]
    unnamed x19 -> x31, local copies, waits for them, and re-layouts: 2.49 us -> 2.35 us
    add x6 -> x3, other arithmetic: 2.17 us -> 2.14 us  [the longest x1 1.28 us: local(): return (sum(word_loss), grad)]
  transfers between devices with their start and end apart: 27 -> 26, of which waited for: 12 -> 10; matrix products, arithmetic and copies ran while one was open for 1% -> 3% of each run, Pallas kernels for 31% -> 37%
where the time goes in v6:
time: 96.6 us; the launch traced here: 96.3 us
  Pallas kernels  36.5 us (38%)
  waiting for transfers between devices  27.3 us (28%)
  starting transfers between devices  25.1 us (26%)
  other arithmetic  3.24 us (3%)
  local copies, waits for them, and re-layouts  3.21 us (3%)
  between operations  1 us (1%)
    pallas_call x12, Pallas kernels, call(): pl.pallas_call(kernel, grid_spec=pltpu.PrefetchScalarGridSpec(num_scalar_...  36.5 us
    ppermute x23, starting transfers between devices, exchange(): return lax.ppermute(x, axis, [(i, i ^ offset) for i in range(n)])  21.5 us
    ppermute x23, waiting for transfers between devices, exchange(): return lax.ppermute(x, axis, [(i, i ^ offset) for i in range(n)])  17.1 us
    ppermute x3, waiting for transfers between devices, exchange_both(): lax.ppermute(x, ('dp', 'seq'), [(i, i ^ dp * n_seq + seq) for i in range(...  10.3 us
    ppermute x3, starting transfers between devices, exchange_both(): lax.ppermute(x, ('dp', 'seq'), [(i, i ^ dp * n_seq + seq) for i in range(...  3.55 us
    unnamed x31, local copies, waits for them, and re-layouts  2.35 us
  transfers between devices with their start and end apart: 26, of which 10 were waited for; matrix products, arithmetic and copies ran while one was open for 3% of the time, Pallas kernels for 37%

profile of v6, /device:TPU:0, one launch (start us, length us, event | category | flops | bytes accessed | tf_op | source)
XLA Modules:
  0.0 96.3 jit_solution(7770434442446860367)
XLA Ops:
  0.7 0.8 pad_add_fusion.2.info
  1.4 1.6 %copy-done.2 = bf16[4,256,1024]{2,1,0:T(8,128)(2,1)S(1)} copy-done((bf16[4,256,1024]{2,1,0:T(8,128)(2,1)S(1)}, bf16[4,256,1024]{2,1,0:T(8,128)(2,1)}, u32[]{:S(2)}) %copy-start.2) | copy-done | bytes 2097176
  3.0 0.7 copy-done.10
  3.7 1.3 %shard_map.86 = bf16[2,3,128,1024]{3,2,1,0:T(8,128)(2,1)S(1)} custom-call(s32[7]{0:T(128)S(1)} %pad_add_fusion.2.info, s32[4,1,256]{2,1,0:T(1,128)S(1)} %bitcast.94, bf16[4,256,1024]{2,1,0:T(8,128)(2,1)S(1)} %copy-done.2), custom_call_target="tpu_custom_call" | custom-call | tf_op jit(solution)/shard_map/pallas_call | solution.py:34
  5.1 3.1 %collective-permute-start = (bf16[128,512]{1,0:T(8,128)(2,1)S(1)}, bf16[128,512]{1,0:T(8,128)(2,1)S(1)}, u32[]{:S(2)}, u32[]{:S(2)}) collective-permute-start(bf16[128,512]{1,0:T(8,128)(2,1)S(1)} %constant_dynamic-slice_fusion), channel_id=1, source_target_pairs={{0,8},{4,12},{8,0},{12,4},{16,24},{20,28},{24,16},{28,20},{1,9},{5... | collective-permute-start | bytes 393224 | tf_op jit(solution)/shard_map/ppermute | solution.py:310
  8.2 2.6 %collective-permute-start.2 = (bf16[128,512]{1,0:T(8,128)(2,1)S(1)}, bf16[128,512]{1,0:T(8,128)(2,1)S(1)}, u32[]{:S(2)}, u32[]{:S(2)}) collective-permute-start(bf16[128,512]{1,0:T(8,128)(2,1)S(1)} %constant_dynamic-slice_fusion), channel_id=1, source_target_pairs={{0,16},{4,20},{8,24},{12,28},{16,0},{20,4},{24,8},{28,12},{1,17},{... | collective-permute-start | bytes 393224 | tf_op jit(solution)/shard_map/ppermute | solution.py:310
  10.8 1.7 %collective-permute-start.12 = (bf16[2,3,128,1024]{3,2,1,0:T(8,128)(2,1)S(1)}, bf16[2,3,128,1024]{3,2,1,0:T(8,128)(2,1)S(1)}, u32[]{:S(2)}, u32[]{:S(2)}) collective-permute-start(bf16[2,3,128,1024]{3,2,1,0:T(8,128)(2,1)S(1)} %shard_map.86), channel_id=1, source_target_pairs={{0,2},{1,3},{2,0},{3,1},{4,6},{5,7},{6,4},{7,5},{8,10},{9,11},{10,... | collective-permute-start | bytes 4718600 | tf_op jit(solution)/shard_map/ppermute | solution.py:310
  12.7 0.6 collective-permute-done
  13.3 1.8 %collective-permute-start.1 = (bf16[2,128,512]{2,1,0:T(8,128)(2,1)S(1)}, bf16[2,128,512]{2,1,0:T(8,128)(2,1)S(1)}, u32[]{:S(2)}, u32[]{:S(2)}) collective-permute-start(bf16[2,128,512]{2,1,0:T(8,128)(2,1)S(1)} %pad_maximum_fusion.refs_0_), channel_id=1, source_target_pairs={{0,4},{4,0},{8,12},{12,8},{16,20},{20,16},{24,28},{28,24},{1,5},{5... | collective-permute-start | bytes 786440 | tf_op jit(solution)/shard_map/ppermute | solution.py:310
  15.2 2.3 %shard_map.87 = (bf16[1,4,128,1024]{3,2,1,0:T(8,128)(2,1)S(1)}, bf16[1,4,128,1024]{3,2,1,0:T(8,128)(2,1)S(1)}, bf16[1,1,128,1024]{3,2,1,0:T(8,128)(2,1)}, bf16[1,1,128,1024]{3,2,1,0:T(8,128)(2,1)}) custom-call(s32[7]{0:T(128)S(1)} %pad_add_fusion.2.info, s32[4,1,256]{2,1,0:T(1,128)S(1)} %bitcast.96, bf16[4,256,1024]{2,1,0:T(8,128)(2,1)S(1)} %copy-done.2), custom_call_target="tpu_custom_call" | custom-call | tf_op jit(solution)/shard_map/pallas_call | solution.py:34
  17.5 2.9 %shard_map.88 = (bf16[4,256,512]{2,1,0:T(8,128)(2,1)S(1)}, f32[4,256,128]{2,1,0:T(8,128)S(1)}, f32[4,8,256]{2,1,0:T(8,128)S(1)}) custom-call(s32[7]{0:T(128)S(1)} %pad_add_fusion.2.info, s32[2,4,2,256]{3,2,1,0:T(2,128)S(1)} %pad_add_fusion.meta, s32[4,16,32]{2,1,0:T(8,128)S(1)} %copy-done.9), custom_call_target="tpu_custom_call" | custom-call | tf_op jit(solution)/shard_map/pallas_call | solution.py:34
  20.4 0.8 collective-permute-done.2
  21.3 0.5 collective-permute-start.6
  21.8 1.5 %collective-permute-start.5 = (bf16[2,128,512]{2,1,0:T(8,128)(2,1)S(1)}, bf16[2,128,512]{2,1,0:T(8,128)(2,1)S(1)}, u32[]{:S(2)}, u32[]{:S(2)}) collective-permute-start(bf16[2,128,512]{2,1,0:T(8,128)(2,1)S(1)} %pad_maximum_fusion.1.refs_2_), channel_id=1, source_target_pairs={{0,4},{4,0},{8,12},{12,8},{16,20},{20,16},{24,28},{28,24},{1,5},{5... | collective-permute-start | bytes 786440 | tf_op jit(solution)/shard_map/ppermute | solution.py:310
  23.3 1.0 %collective-permute-done.6.refs_4_ = bf16[2,128,512]{2,1,0:T(8,128)(2,1)S(1)} collective-permute-done((bf16[2,128,512]{2,1,0:T(8,128)(2,1)S(1)}, bf16[2,128,512]{2,1,0:T(8,128)(2,1)S(1)}, u32[]{:S(2)}, u32[]{:S(2)}) %collective-permute-start.6) | collective-permute-done | bytes 262176 | tf_op jit(solution)/shard_map/ppermute | solution.py:310
  24.4 5.6 %collective-permute-done.5.refs_3_ = bf16[2,128,512]{2,1,0:T(8,128)(2,1)S(1)} collective-permute-done((bf16[2,128,512]{2,1,0:T(8,128)(2,1)S(1)}, bf16[2,128,512]{2,1,0:T(8,128)(2,1)S(1)}, u32[]{:S(2)}, u32[]{:S(2)}) %collective-permute-start.5) | collective-permute-done | bytes 262176 | tf_op jit(solution)/shard_map/ppermute | solution.py:310
  30.1 1.5 %collective-permute-start.13 = (s32[2,4,2,256]{3,2,1,0:T(2,128)S(1)}, s32[2,4,2,256]{3,2,1,0:T(2,128)S(1)}, u32[]{:S(2)}, u32[]{:S(2)}) collective-permute-start(s32[2,4,2,256]{3,2,1,0:T(2,128)S(1)} %pad_add_fusion.meta), channel_id=1, source_target_pairs={{0,2},{1,3},{2,0},{3,1},{4,6},{5,7},{6,4},{7,5},{8,10},{9,11},{10,... | collective-permute-start | bytes 49160 | tf_op jit(solution)/shard_map/ppermute | solution.py:310
  31.6 6.4 %shard_map.89.weight = bf16[4,1024,512]{2,1,0:T(8,128)(2,1)S(1)} custom-call(s32[7]{0:T(128)S(1)} %pad_add_fusion.2.info, bf16[4,512,1024]{2,1,0:T(8,128)(2,1)S(1)} %copy-done.1, bf16[2,128,512]{2,1,0:T(8,128)(2,1)S(1)} %pad_maximum_fusion.refs_0_, bf16[2,128,512]{2,1,0:T(8,128)(2,1)S(1)} %collective-permute-done.1.refs_1_, ...), custom_call_target="tpu_custom_call" | custom-call | tf_op jit(solution)/shard_map/pallas_call | solution.py:34
  38.0 5.3 %shard_map.90 = (f32[4,2,256]{2,1,0:T(2,128)S(1)}, bf16[1024,1024]{1,0:T(8,128)(2,1)S(1)}, bf16[1024,1024]{1,0:T(8,128)(2,1)S(1)}) custom-call(s32[7]{0:T(128)S(1)} %pad_add_fusion.2.info, bf16[4,256,512]{2,1,0:T(8,128)(2,1)S(1)} %get-tuple-element.64.bias, f32[4,256,128]{2,1,0:T(8,128)S(1)} %get-tuple-element.65.table, ...), custom_call_target="tpu_custom_call" | custom-call | tf_op jit(solution)/shard_map/pallas_call | solution.py:34
  43.4 3.4 %collective-permute-done.13.meta = s32[2,4,2,256]{3,2,1,0:T(2,128)S(1)} collective-permute-done((s32[2,4,2,256]{3,2,1,0:T(2,128)S(1)}, s32[2,4,2,256]{3,2,1,0:T(2,128)S(1)}, u32[]{:S(2)}, u32[]{:S(2)}) %collective-permute-start.13) | collective-permute-done | bytes 16416 | tf_op jit(solution)/shard_map/ppermute | solution.py:310
  46.7 1.5 %collective-permute-start.15 = (bf16[1,1,128,1024]{3,2,1,0:T(8,128)(2,1)}, bf16[1,1,128,1024]{3,2,1,0:T(8,128)(2,1)}, u32[]{:S(2)}, u32[]{:S(2)}) collective-permute-start(bf16[1,1,128,1024]{3,2,1,0:T(8,128)(2,1)} %get-tuple-element.85), channel_id=1, source_target_pairs={{0,2},{1,3},{2,0},{3,1},{4,6},{5,7},{6,4},{7,5},{8,10},{9,11},{10,... | collective-permute-start | bytes 786440 | tf_op jit(solution)/shard_map/ppermute | solution.py:310
  48.3 0.3 collective-permute-start.16
  48.6 0.6 slice_bitcast_fusion
  49.2 0.3 collective-permute-start.11
  49.5 2.9 %shard_map.91 = (bf16[4,256,512]{2,1,0:T(8,128)(2,1)S(1)}, f32[4,256,128]{2,1,0:T(8,128)S(1)}, f32[4,8,256]{2,1,0:T(8,128)S(1)}) custom-call(s32[7]{0:T(128)S(1)} %pad_add_fusion.2.info, s32[2,4,2,256]{3,2,1,0:T(2,128)S(1)} %collective-permute-done.13.meta, s32[4,16,32]{2,1,0:T(8,128)S(1)} %copy-done.9), custom_call_target="tpu_custom_call" | custom-call | tf_op jit(solution)/shard_map/pallas_call | solution.py:34
  52.5 4.0 %shard_map.92 = (f32[3,2,256]{2,1,0:T(2,128)S(1)}, bf16[1024,768]{1,0:T(8,128)(2,1)S(1)}, bf16[768,1024]{1,0:T(8,128)(2,1)S(1)}) custom-call(s32[7]{0:T(128)S(1)} %pad_add_fusion.2.info, bf16[4,256,512]{2,1,0:T(8,128)(2,1)S(1)} %get-tuple-element.76.bias, f32[4,256,128]{2,1,0:T(8,128)S(1)} %get-tuple-element.77.table, ...), custom_call_target="tpu_custom_call" | custom-call | tf_op jit(solution)/shard_map/pallas_call | solution.py:34
  56.5 3.1 %shard_map.94.refs_2_ = f32[2,1024,256]{2,1,0:T(8,128)S(1)} custom-call(s32[7]{0:T(128)S(1)} %pad_add_fusion.2.info, bf16[1024,1024]{1,0:T(8,128)(2,1)S(1)} %get-tuple-element.81.refs_0_, bf16[1024,1024]{1,0:T(8,128)(2,1)S(1)} %get-tuple-element.82.refs_1_, bf16[1024,768]{1,0:T(8,128)(2,1)S(1)} %get-tuple-element.83.refs_2_, ...), custom_call_target="tpu_custom_call" | custom-call | flops 120259084288 | tf_op jit(solution)/shard_map/pallas_call | solution.py:34
  59.6 3.1 %shard_map.93.refs_2_ = f32[2,1024,256]{2,1,0:T(8,128)S(1)} custom-call(s32[7]{0:T(128)S(1)} %pad_add_fusion.2.info, bf16[1024,1024]{1,0:T(8,128)(2,1)S(1)} %get-tuple-element.81.refs_0_, bf16[1024,1024]{1,0:T(8,128)(2,1)S(1)} %get-tuple-element.82.refs_1_, bf16[1024,768]{1,0:T(8,128)(2,1)S(1)} %get-tuple-element.83.refs_2_, ...), custom_call_target="tpu_custom_call" | custom-call | flops 120259084288 | tf_op jit(solution)/shard_map/pallas_call | solution.py:34
  62.8 2.7 %shard_map.95 = (f32[1,2,256]{2,1,0:T(2,128)S(1)}, bf16[1024,256]{1,0:T(8,128)(2,1)S(1)}, bf16[256,1024]{1,0:T(8,128)(2,1)S(1)}) custom-call(s32[7]{0:T(128)S(1)} %pad_add_fusion.2.info, bf16[4,256,512]{2,1,0:T(8,128)(2,1)S(1)} %copy-done.4, f32[4,256,128]{2,1,0:T(8,128)S(1)} %copy-done.6, f32[4,8,256]{2,1,0:T(8,128)S(1)} %copy-done.8, ...), custom_call_target="tpu_custom_call" | custom-call | tf_op jit(solution)/shard_map/pallas_call | solution.py:34
  65.5 1.2 %shard_map.97 = bf16[2,1024,256]{2,1,0:T(8,128)(2,1)S(1)} custom-call(s32[7]{0:T(128)S(1)} %pad_add_fusion.2.info, bf16[1024,256]{1,0:T(8,128)(2,1)S(1)} %get-tuple-element.90.refs_0_, bf16[256,1024]{1,0:T(8,128)(2,1)S(1)} %get-tuple-element.91.refs_1_, f32[2,1024,256]{2,1,0:T(8,128)S(1)} %shard_map.94.refs_2_), custom_call_target="tpu_custom_call" | custom-call | flops 17179869184 | tf_op jit(solution)/shard_map/pallas_call | solution.py:34
  66.7 0.3 collective-permute-start.19
  67.1 1.2 %shard_map.96 = f32[2,1024,256]{2,1,0:T(8,128)S(1)} custom-call(s32[7]{0:T(128)S(1)} %pad_add_fusion.2.info, bf16[1024,256]{1,0:T(8,128)(2,1)S(1)} %get-tuple-element.90.refs_0_, bf16[256,1024]{1,0:T(8,128)(2,1)S(1)} %get-tuple-element.91.refs_1_, f32[2,1024,256]{2,1,0:T(8,128)S(1)} %shard_map.93.refs_2_), custom_call_target="tpu_custom_call" | custom-call | flops 17179869184 | tf_op jit(solution)/shard_map/pallas_call | solution.py:34
  68.3 1.2 %collective-permute-done.19 = bf16[2,1024,256]{2,1,0:T(8,128)(2,1)S(1)} collective-permute-done((bf16[2,1024,256]{2,1,0:T(8,128)(2,1)S(1)}, bf16[2,1024,256]{2,1,0:T(8,128)(2,1)S(1)}, u32[]{:S(2)}, u32[]{:S(2)}) %collective-permute-start.19) | collective-permute-done | bytes 1048608 | tf_op jit(solution)/shard_map/ppermute | solution.py:310
  69.5 0.3 fusion.7
  69.7 1.6 %collective-permute-start.20 = (bf16[4,128,256]{2,1,0:T(8,128)(2,1)S(1)}, bf16[4,128,256]{2,1,0:T(8,128)(2,1)S(1)}, u32[]{:S(2)}, u32[]{:S(2)}) collective-permute-start(bf16[4,128,256]{2,1,0:T(8,128)(2,1)S(1)} %get-tuple-element.102), channel_id=1, source_target_pairs={{0,4},{1,5},{2,6},{3,7},{4,0},{5,1},{6,2},{7,3},{8,12},{9,13},{10,... | collective-permute-start | bytes 786440 | tf_op jit(solution)/shard_map/ppermute | solution.py:316
  71.3 1.5 %collective-permute-start.21 = (bf16[4,128,256]{2,1,0:T(8,128)(2,1)S(1)}, bf16[4,128,256]{2,1,0:T(8,128)(2,1)S(1)}, u32[]{:S(2)}, u32[]{:S(2)}) collective-permute-start(bf16[4,128,256]{2,1,0:T(8,128)(2,1)S(1)} %get-tuple-element.103), channel_id=1, source_target_pairs={{0,2},{1,3},{2,0},{3,1},{4,6},{5,7},{6,4},{7,5},{8,10},{9,11},{10,... | collective-permute-start | bytes 786440 | tf_op jit(solution)/shard_map/ppermute | solution.py:316
  72.8 0.5 collective-permute-start.22
  73.3 1.6 %collective-permute-start.17 = (f32[4,256]{1,0:T(4,128)S(1)}, f32[4,256]{1,0:T(4,128)S(1)}, u32[]{:S(2)}, u32[]{:S(2)}) collective-permute-start(f32[4,256]{1,0:T(4,128)S(1)} %bitcast.103), channel_id=1, source_target_pairs={{0,2},{1,3},{2,0},{3,1},{4,6},{5,7},{6,4},{7,5},{8,10},{9,11},{10,... | collective-permute-start | bytes 12296 | tf_op jit(solution)/shard_map/ppermute | solution.py:310
  74.9 4.0 %collective-permute-done.20 = bf16[4,128,256]{2,1,0:T(8,128)(2,1)S(1)} collective-permute-done((bf16[4,128,256]{2,1,0:T(8,128)(2,1)S(1)}, bf16[4,128,256]{2,1,0:T(8,128)(2,1)S(1)}, u32[]{:S(2)}, u32[]{:S(2)}) %collective-permute-start.20) | collective-permute-done | bytes 262176 | tf_op jit(solution)/shard_map/ppermute | solution.py:316
  78.9 6.2 %collective-permute-done.21 = bf16[4,128,256]{2,1,0:T(8,128)(2,1)S(1)} collective-permute-done((bf16[4,128,256]{2,1,0:T(8,128)(2,1)S(1)}, bf16[4,128,256]{2,1,0:T(8,128)(2,1)S(1)}, u32[]{:S(2)}, u32[]{:S(2)}) %collective-permute-start.21) | collective-permute-done | bytes 262176 | tf_op jit(solution)/shard_map/ppermute | solution.py:316
  85.2 0.2 fusion.6
  85.4 0.7 collective-permute-start.23
  86.1 3.5 %collective-permute-start.24 = (bf16[128,256]{1,0:T(8,128)(2,1)S(1)}, bf16[128,256]{1,0:T(8,128)(2,1)S(1)}, u32[]{:S(2)}, u32[]{:S(2)}) collective-permute-start(bf16[128,256]{1,0:T(8,128)(2,1)S(1)} %get-tuple-element.107), channel_id=1, source_target_pairs={{0,16},{4,20},{8,24},{12,28},{16,0},{20,4},{24,8},{28,12},{1,17},{... | collective-permute-start | bytes 196616 | tf_op jit(solution)/shard_map/ppermute | solution.py:310
  89.6 0.3 collective-permute-start.25
  89.9 1.3 %fusion.17 = f32[4,256]{1,0:T(4,128)} fusion(f32[4,256]{1,0:T(4,128)S(1)} %collective-permute-done.18, f32[4,256]{1,0:T(4,128)S(1)} %collective-permute-done.17, f32[4,256]{1,0:T(4,128)} %collective-permute-done.11, f32[4,2,256]{2,0,1:T(4,128)S(1)} %copy-done.12), kind=kLoop, calls=%fused_computation.33 | loop fusion | flops 3072 | bytes 20480 | tf_op jit(solution)/shard_map/add | solution.py:416
  91.2 2.3 %collective-permute-done.24 = bf16[128,256]{1,0:T(8,128)(2,1)S(1)} collective-permute-done((bf16[128,256]{1,0:T(8,128)(2,1)S(1)}, bf16[128,256]{1,0:T(8,128)(2,1)S(1)}, u32[]{:S(2)}, u32[]{:S(2)}) %collective-permute-start.24) | collective-permute-done | bytes 65568 | tf_op jit(solution)/shard_map/ppermute | solution.py:310
  93.5 2.2 %collective-permute-done.25 = bf16[128,256]{1,0:T(8,128)(2,1)S(1)} collective-permute-done((bf16[128,256]{1,0:T(8,128)(2,1)S(1)}, bf16[128,256]{1,0:T(8,128)(2,1)S(1)}, u32[]{:S(2)}, u32[]{:S(2)}) %collective-permute-start.25) | collective-permute-done | bytes 65568 | tf_op jit(solution)/shard_map/ppermute | solution.py:310
  95.6 0.7 fusion.11
  (64 shorter events, 0.7 us)
Async XLA Ops:
  0.6 4.4 %copy-start = (bf16[128,1024]{1,0:T(8,128)(2,1)S(1)}, bf16[128,1024]{1,0:T(8,128)(2,1)}, u32[]{:S(2)}) copy-start(bf16[128,1024]{1,0:T(8,128)(2,1)} %param.9) | copy-start | bytes 786436
  1.4 1.6 %copy-start.2 = (bf16[4,256,1024]{2,1,0:T(8,128)(2,1)S(1)}, bf16[4,256,1024]{2,1,0:T(8,128)(2,1)}, u32[]{:S(2)}) copy-start(bf16[4,256,1024]{2,1,0:T(8,128)(2,1)} %words.3) | copy-start | bytes 6291460
  3.0 0.7 copy-start.10
  3.7 9.0 %copy-start.13 = (s32[4,256]{1,0:T(4,128)S(1)}, s32[4,256]{1,0:T(4,128)}, u32[]{:S(2)}) copy-start(s32[4,256]{1,0:T(4,128)} %param.11) | copy-start | bytes 12292
  3.7 27.9 %copy-start.1 = (bf16[4,512,1024]{2,1,0:T(8,128)(2,1)S(1)}, bf16[4,512,1024]{2,1,0:T(8,128)(2,1)}, u32[]{:S(2)}) copy-start(bf16[4,512,1024]{2,1,0:T(8,128)(2,1)} %patches.7) | copy-start | bytes 12582916
  5.0 12.5 %copy-start.9 = (s32[4,16,32]{2,1,0:T(8,128)S(1)}, s32[4,16,32]{2,1,0:T(8,128)}, u32[]{:S(2)}) copy-start(s32[4,16,32]{2,1,0:T(8,128)} %flags.3) | copy-start | bytes 24580
  5.1 8.1 %collective-permute-start = (bf16[128,512]{1,0:T(8,128)(2,1)S(1)}, bf16[128,512]{1,0:T(8,128)(2,1)S(1)}, u32[]{:S(2)}, u32[]{:S(2)}) collective-permute-start(bf16[128,512]{1,0:T(8,128)(2,1)S(1)} %constant_dynamic-slice_fusion), channel_id=1, source_target_pairs={{0,8},{4,12},{8,0},{12,4},{16,24},{20,28},{24,16},{28,20},{1,9},{5... | collective-permute-start | bytes 393224 | tf_op jit(solution)/shard_map/ppermute | solution.py:310
  8.2 12.9 %collective-permute-start.2 = (bf16[128,512]{1,0:T(8,128)(2,1)S(1)}, bf16[128,512]{1,0:T(8,128)(2,1)S(1)}, u32[]{:S(2)}, u32[]{:S(2)}) collective-permute-start(bf16[128,512]{1,0:T(8,128)(2,1)S(1)} %constant_dynamic-slice_fusion), channel_id=1, source_target_pairs={{0,16},{4,20},{8,24},{12,28},{16,0},{20,4},{24,8},{28,12},{1,17},{... | collective-permute-start | bytes 393224 | tf_op jit(solution)/shard_map/ppermute | solution.py:310
  10.8 10.3 %collective-permute-start.3 = (bf16[128,512]{1,0:T(8,128)(2,1)S(1)}, bf16[128,512]{1,0:T(8,128)(2,1)S(1)}, u32[]{:S(2)}, u32[]{:S(2)}) collective-permute-start(bf16[128,512]{1,0:T(8,128)(2,1)S(1)} %constant_dynamic-slice_fusion), channel_id=1, source_target_pairs={{0,24},{4,28},{8,16},{12,20},{16,8},{20,12},{24,0},{28,4},{1,25},{... | collective-permute-start | bytes 393224 | tf_op jit(solution)/shard_map/ppermute | solution.py:310
  10.8 35.9 %collective-permute-start.12 = (bf16[2,3,128,1024]{3,2,1,0:T(8,128)(2,1)S(1)}, bf16[2,3,128,1024]{3,2,1,0:T(8,128)(2,1)S(1)}, u32[]{:S(2)}, u32[]{:S(2)}) collective-permute-start(bf16[2,3,128,1024]{3,2,1,0:T(8,128)(2,1)S(1)} %shard_map.86), channel_id=1, source_target_pairs={{0,2},{1,3},{2,0},{3,1},{4,6},{5,7},{6,4},{7,5},{8,10},{9,11},{10,... | collective-permute-start | bytes 4718600 | tf_op jit(solution)/shard_map/ppermute | solution.py:310
  13.3 7.9 %collective-permute-start.1 = (bf16[2,128,512]{2,1,0:T(8,128)(2,1)S(1)}, bf16[2,128,512]{2,1,0:T(8,128)(2,1)S(1)}, u32[]{:S(2)}, u32[]{:S(2)}) collective-permute-start(bf16[2,128,512]{2,1,0:T(8,128)(2,1)S(1)} %pad_maximum_fusion.refs_0_), channel_id=1, source_target_pairs={{0,4},{4,0},{8,12},{12,8},{16,20},{20,16},{24,28},{28,24},{1,5},{5... | collective-permute-start | bytes 786440 | tf_op jit(solution)/shard_map/ppermute | solution.py:310
  15.1 2.4 %collective-permute-start.4 = (s32[4,2,256]{2,1,0:T(2,128)S(1)}, s32[4,2,256]{2,1,0:T(2,128)S(1)}, u32[]{:S(2)}, u32[]{:S(2)}) collective-permute-start(s32[4,2,256]{2,1,0:T(2,128)S(1)} %get-tuple-element.111), channel_id=1, source_target_pairs={{0,1},{1,0},{2,3},{3,2},{4,5},{5,4},{6,7},{7,6},{8,9},{9,8},{10,11... | collective-permute-start | bytes 24584 | tf_op jit(solution)/shard_map/ppermute | solution.py:310
  21.2 16.8 %collective-permute-start.10 = (bf16[1,4,128,1024]{3,2,1,0:T(8,128)(2,1)S(1)}, bf16[1,4,128,1024]{3,2,1,0:T(8,128)(2,1)S(1)}, u32[]{:S(2)}, u32[]{:S(2)}) collective-permute-start(bf16[1,4,128,1024]{3,2,1,0:T(8,128)(2,1)S(1)} %get-tuple-element.70), channel_id=1, source_target_pairs={{0,1},{1,0},{2,3},{3,2},{4,5},{5,4},{6,7},{7,6},{8,9},{9,8},{10,11... | collective-permute-start | bytes 3145736 | tf_op jit(solution)/shard_map/ppermute | solution.py:310
  21.3 3.0 %collective-permute-start.6 = (bf16[2,128,512]{2,1,0:T(8,128)(2,1)S(1)}, bf16[2,128,512]{2,1,0:T(8,128)(2,1)S(1)}, u32[]{:S(2)}, u32[]{:S(2)}) collective-permute-start(bf16[2,128,512]{2,1,0:T(8,128)(2,1)S(1)} %pad_maximum_fusion.refs_0_), channel_id=1, source_target_pairs={{0,1},{1,0},{2,3},{3,2},{4,5},{5,4},{6,7},{7,6},{8,9},{9,8},{10,11... | collective-permute-start | bytes 786440 | tf_op jit(solution)/shard_map/ppermute | solution.py:310
  21.8 8.3 %collective-permute-start.5 = (bf16[2,128,512]{2,1,0:T(8,128)(2,1)S(1)}, bf16[2,128,512]{2,1,0:T(8,128)(2,1)S(1)}, u32[]{:S(2)}, u32[]{:S(2)}) collective-permute-start(bf16[2,128,512]{2,1,0:T(8,128)(2,1)S(1)} %pad_maximum_fusion.1.refs_2_), channel_id=1, source_target_pairs={{0,4},{4,0},{8,12},{12,8},{16,20},{20,16},{24,28},{28,24},{1,5},{5... | collective-permute-start | bytes 786440 | tf_op jit(solution)/shard_map/ppermute | solution.py:310
  23.3 6.8 %collective-permute-start.7 = (bf16[2,128,512]{2,1,0:T(8,128)(2,1)S(1)}, bf16[2,128,512]{2,1,0:T(8,128)(2,1)S(1)}, u32[]{:S(2)}, u32[]{:S(2)}) collective-permute-start(bf16[2,128,512]{2,1,0:T(8,128)(2,1)S(1)} %collective-permute-done.1.refs_1_), channel_id=1, source_target_pairs={{0,1},{1,0},{2,3},{3,2},{4,5},{5,4},{6,7},{7,6},{8,9},{9,8},{10,11... | collective-permute-start | bytes 786440 | tf_op jit(solution)/shard_map/ppermute | solution.py:310
  24.3 7.3 %collective-permute-start.8 = (bf16[2,128,512]{2,1,0:T(8,128)(2,1)S(1)}, bf16[2,128,512]{2,1,0:T(8,128)(2,1)S(1)}, u32[]{:S(2)}, u32[]{:S(2)}) collective-permute-start(bf16[2,128,512]{2,1,0:T(8,128)(2,1)S(1)} %pad_maximum_fusion.1.refs_2_), channel_id=1, source_target_pairs={{0,1},{1,0},{2,3},{3,2},{4,5},{5,4},{6,7},{7,6},{8,9},{9,8},{10,11... | collective-permute-start | bytes 786440 | tf_op jit(solution)/shard_map/ppermute | solution.py:310
  30.1 1.5 %collective-permute-start.9 = (bf16[2,128,512]{2,1,0:T(8,128)(2,1)S(1)}, bf16[2,128,512]{2,1,0:T(8,128)(2,1)S(1)}, u32[]{:S(2)}, u32[]{:S(2)}) collective-permute-start(bf16[2,128,512]{2,1,0:T(8,128)(2,1)S(1)} %collective-permute-done.5.refs_3_), channel_id=1, source_target_pairs={{0,1},{1,0},{2,3},{3,2},{4,5},{5,4},{6,7},{7,6},{8,9},{9,8},{10,11... | collective-permute-start | bytes 786440 | tf_op jit(solution)/shard_map/ppermute | solution.py:310
  30.1 16.7 %collective-permute-start.13 = (s32[2,4,2,256]{3,2,1,0:T(2,128)S(1)}, s32[2,4,2,256]{3,2,1,0:T(2,128)S(1)}, u32[]{:S(2)}, u32[]{:S(2)}) collective-permute-start(s32[2,4,2,256]{3,2,1,0:T(2,128)S(1)} %pad_add_fusion.meta), channel_id=1, source_target_pairs={{0,2},{1,3},{2,0},{3,1},{4,6},{5,7},{6,4},{7,5},{8,10},{9,11},{10,... | collective-permute-start | bytes 49160 | tf_op jit(solution)/shard_map/ppermute | solution.py:310
  46.7 5.7 %collective-permute-start.14 = (bf16[2,3,128,1024]{3,2,1,0:T(8,128)(2,1)S(1)}, bf16[2,3,128,1024]{3,2,1,0:T(8,128)(2,1)S(1)}, u32[]{:S(2)}, u32[]{:S(2)}) collective-permute-start(bf16[2,3,128,1024]{3,2,1,0:T(8,128)(2,1)S(1)} %collective-permute-done.12.refs_0_), channel_id=1, source_target_pairs={{0,1},{1,0},{2,3},{3,2},{4,5},{5,4},{6,7},{7,6},{8,9},{9,8},{10,11... | collective-permute-start | bytes 4718600 | tf_op jit(solution)/shard_map/ppermute | solution.py:310
  46.7 16.0 %collective-permute-start.15 = (bf16[1,1,128,1024]{3,2,1,0:T(8,128)(2,1)}, bf16[1,1,128,1024]{3,2,1,0:T(8,128)(2,1)}, u32[]{:S(2)}, u32[]{:S(2)}) collective-permute-start(bf16[1,1,128,1024]{3,2,1,0:T(8,128)(2,1)} %get-tuple-element.85), channel_id=1, source_target_pairs={{0,2},{1,3},{2,0},{3,1},{4,6},{5,7},{6,4},{7,5},{8,10},{9,11},{10,... | collective-permute-start | bytes 786440 | tf_op jit(solution)/shard_map/ppermute | solution.py:310
  48.3 14.5 %collective-permute-start.16 = (bf16[1,1,128,1024]{3,2,1,0:T(8,128)(2,1)}, bf16[1,1,128,1024]{3,2,1,0:T(8,128)(2,1)}, u32[]{:S(2)}, u32[]{:S(2)}) collective-permute-start(bf16[1,1,128,1024]{3,2,1,0:T(8,128)(2,1)} %get-tuple-element.86), channel_id=1, source_target_pairs={{0,3},{1,2},{2,1},{3,0},{4,7},{5,6},{6,5},{7,4},{8,11},{9,10},{10,... | collective-permute-start | bytes 786440 | tf_op jit(solution)/shard_map/ppermute | solution.py:310
  48.6 7.8 %copy-start.11 = (f32[4,2,256]{2,0,1:T(4,128)}, f32[4,2,256]{2,0,1:T(4,128)S(1)}, u32[]{:S(2)}) copy-start(f32[4,2,256]{2,0,1:T(4,128)S(1)} %copy.9) | copy-start | bytes 24580
  49.2 40.4 %collective-permute-start.11 = (f32[4,256]{1,0:T(4,128)}, f32[4,256]{1,0:T(4,128)}, u32[]{:S(2)}, u32[]{:S(2)}) collective-permute-start(f32[4,256]{1,0:T(4,128)} %slice_bitcast_fusion), channel_id=1, source_target_pairs={{0,1},{1,0},{2,3},{3,2},{4,5},{5,4},{6,7},{7,6},{8,9},{9,8},{10,11... | collective-permute-start | bytes 12296 | tf_op jit(solution)/shard_map/ppermute | solution.py:310
  52.4 4.0 %copy-start.3 = (bf16[4,256,512]{2,1,0:T(8,128)(2,1)}, bf16[4,256,512]{2,1,0:T(8,128)(2,1)S(1)}, u32[]{:S(2)}) copy-start(bf16[4,256,512]{2,1,0:T(8,128)(2,1)S(1)} %get-tuple-element.76.bias) | copy-start | bytes 3145732
  52.4 4.0 %copy-start.5 = (f32[4,256,128]{2,1,0:T(8,128)}, f32[4,256,128]{2,1,0:T(8,128)S(1)}, u32[]{:S(2)}) copy-start(f32[4,256,128]{2,1,0:T(8,128)S(1)} %get-tuple-element.77.table) | copy-start | bytes 1572868
  52.4 4.0 %copy-start.7 = (f32[4,8,256]{2,1,0:T(8,128)}, f32[4,8,256]{2,1,0:T(8,128)S(1)}, u32[]{:S(2)}) copy-start(f32[4,8,256]{2,1,0:T(8,128)S(1)} %get-tuple-element.78.rank) | copy-start | bytes 98308
  59.6 3.2 %copy-start.4 = (bf16[4,256,512]{2,1,0:T(8,128)(2,1)S(1)}, bf16[4,256,512]{2,1,0:T(8,128)(2,1)}, u32[]{:S(2)}) copy-start(bf16[4,256,512]{2,1,0:T(8,128)(2,1)} %copy-done.3) | copy-start | bytes 3145732
  59.6 3.2 %copy-start.6 = (f32[4,256,128]{2,1,0:T(8,128)S(1)}, f32[4,256,128]{2,1,0:T(8,128)}, u32[]{:S(2)}) copy-start(f32[4,256,128]{2,1,0:T(8,128)} %copy-done.5) | copy-start | bytes 1572868
  59.6 3.2 %copy-start.8 = (f32[4,8,256]{2,1,0:T(8,128)S(1)}, f32[4,8,256]{2,1,0:T(8,128)}, u32[]{:S(2)}) copy-start(f32[4,8,256]{2,1,0:T(8,128)} %copy-done.7) | copy-start | bytes 98308
  66.7 2.7 %collective-permute-start.19 = (bf16[2,1024,256]{2,1,0:T(8,128)(2,1)S(1)}, bf16[2,1024,256]{2,1,0:T(8,128)(2,1)S(1)}, u32[]{:S(2)}, u32[]{:S(2)}) collective-permute-start(bf16[2,1024,256]{2,1,0:T(8,128)(2,1)S(1)} %shard_map.97), channel_id=1, source_target_pairs={{0,1},{1,0},{2,3},{3,2},{4,5},{5,4},{6,7},{7,6},{8,9},{9,8},{10,11... | collective-permute-start | bytes 3145736 | tf_op jit(solution)/shard_map/ppermute | solution.py:310
  69.5 20.4 %copy-start.12 = (f32[4,2,256]{2,0,1:T(4,128)S(1)}, f32[4,2,256]{2,0,1:T(4,128)}, u32[]{:S(2)}) copy-start(f32[4,2,256]{2,0,1:T(4,128)} %copy-done.11) | copy-start | bytes 24580
  69.7 9.2 %collective-permute-start.20 = (bf16[4,128,256]{2,1,0:T(8,128)(2,1)S(1)}, bf16[4,128,256]{2,1,0:T(8,128)(2,1)S(1)}, u32[]{:S(2)}, u32[]{:S(2)}) collective-permute-start(bf16[4,128,256]{2,1,0:T(8,128)(2,1)S(1)} %get-tuple-element.102), channel_id=1, source_target_pairs={{0,4},{1,5},{2,6},{3,7},{4,0},{5,1},{6,2},{7,3},{8,12},{9,13},{10,... | collective-permute-start | bytes 786440 | tf_op jit(solution)/shard_map/ppermute | solution.py:316
  71.3 13.9 %collective-permute-start.21 = (bf16[4,128,256]{2,1,0:T(8,128)(2,1)S(1)}, bf16[4,128,256]{2,1,0:T(8,128)(2,1)S(1)}, u32[]{:S(2)}, u32[]{:S(2)}) collective-permute-start(bf16[4,128,256]{2,1,0:T(8,128)(2,1)S(1)} %get-tuple-element.103), channel_id=1, source_target_pairs={{0,2},{1,3},{2,0},{3,1},{4,6},{5,7},{6,4},{7,5},{8,10},{9,11},{10,... | collective-permute-start | bytes 786440 | tf_op jit(solution)/shard_map/ppermute | solution.py:316
  72.8 12.3 %collective-permute-start.22 = (bf16[4,128,256]{2,1,0:T(8,128)(2,1)S(1)}, bf16[4,128,256]{2,1,0:T(8,128)(2,1)S(1)}, u32[]{:S(2)}, u32[]{:S(2)}) collective-permute-start(bf16[4,128,256]{2,1,0:T(8,128)(2,1)S(1)} %get-tuple-element.104), channel_id=1, source_target_pairs={{0,6},{1,7},{2,4},{3,5},{4,2},{5,3},{6,0},{7,1},{8,14},{9,15},{10,... | collective-permute-start | bytes 786440 | tf_op jit(solution)/shard_map/ppermute | solution.py:316
  73.3 16.5 %collective-permute-start.17 = (f32[4,256]{1,0:T(4,128)S(1)}, f32[4,256]{1,0:T(4,128)S(1)}, u32[]{:S(2)}, u32[]{:S(2)}) collective-permute-start(f32[4,256]{1,0:T(4,128)S(1)} %bitcast.103), channel_id=1, source_target_pairs={{0,2},{1,3},{2,0},{3,1},{4,6},{5,7},{6,4},{7,5},{8,10},{9,11},{10,... | collective-permute-start | bytes 12296 | tf_op jit(solution)/shard_map/ppermute | solution.py:310
  78.9 10.9 %collective-permute-start.18 = (f32[4,256]{1,0:T(4,128)S(1)}, f32[4,256]{1,0:T(4,128)S(1)}, u32[]{:S(2)}, u32[]{:S(2)}) collective-permute-start(f32[4,256]{1,0:T(4,128)S(1)} %bitcast.104), channel_id=1, source_target_pairs={{0,3},{1,2},{2,1},{3,0},{4,7},{5,6},{6,5},{7,4},{8,11},{9,10},{10,... | collective-permute-start | bytes 12296 | tf_op jit(solution)/shard_map/ppermute | solution.py:310
  85.4 5.8 %collective-permute-start.23 = (bf16[128,256]{1,0:T(8,128)(2,1)S(1)}, bf16[128,256]{1,0:T(8,128)(2,1)S(1)}, u32[]{:S(2)}, u32[]{:S(2)}) collective-permute-start(bf16[128,256]{1,0:T(8,128)(2,1)S(1)} %get-tuple-element.105), channel_id=1, source_target_pairs={{0,8},{4,12},{8,0},{12,4},{16,24},{20,28},{24,16},{28,20},{1,9},{5... | collective-permute-start | bytes 196616 | tf_op jit(solution)/shard_map/ppermute | solution.py:310
  86.1 7.4 %collective-permute-start.24 = (bf16[128,256]{1,0:T(8,128)(2,1)S(1)}, bf16[128,256]{1,0:T(8,128)(2,1)S(1)}, u32[]{:S(2)}, u32[]{:S(2)}) collective-permute-start(bf16[128,256]{1,0:T(8,128)(2,1)S(1)} %get-tuple-element.107), channel_id=1, source_target_pairs={{0,16},{4,20},{8,24},{12,28},{16,0},{20,4},{24,8},{28,12},{1,17},{... | collective-permute-start | bytes 196616 | tf_op jit(solution)/shard_map/ppermute | solution.py:310
  89.6 6.1 %collective-permute-start.25 = (bf16[128,256]{1,0:T(8,128)(2,1)S(1)}, bf16[128,256]{1,0:T(8,128)(2,1)S(1)}, u32[]{:S(2)}, u32[]{:S(2)}) collective-permute-start(bf16[128,256]{1,0:T(8,128)(2,1)S(1)} %get-tuple-element.106), channel_id=1, source_target_pairs={{0,24},{4,28},{8,16},{12,20},{16,8},{20,12},{24,0},{28,4},{1,25},{... | collective-permute-start | bytes 196616 | tf_op jit(solution)/shard_map/ppermute | solution.py:310

commit v7 on v6

--- a/solution.py
+++ b/solution.py
@@ -11,6 +11,7 @@
 MARGIN_BLOCK_SIZE = 64
 SHIFT = 6
 VMEM_LIMIT = 16 * 1024 * 1024
+WORK = 1<<31
 ME, CORE, DP, COUNTS = 0, 1, 2, 3
 TARGET, COEF = 0, 1
 F32, BF16 = jnp.float32, jnp.bfloat16
@@ -97,7 +98,7 @@
         n += len(some)
 
 
-def dispatch(info, routes, words, plan, cap):
+def dispatch(info, routes, words, plan, cap, flops=0):
     width = words.shape[2]
     out = [
         jax.ShapeDtypeStruct((len(offsets), n_pages, cap, width), BF16)
@@ -110,6 +111,7 @@
         [all_of(o) for o in out],
         out,
         (info, routes, words),
+        flops=flops,
     )
 
 
@@ -157,7 +159,7 @@
         table[p] = jnp.where(lane == TARGET, t.astype(F32), jnp.where(lane == COEF, coef, 0.0))
 
 
-def tables(info, meta, flags, offsets, cap, pps):
+def tables(info, meta, flags, offsets, cap, pps, flops=0):
     n_homes, pages, _, wdev = meta.shape
     out = [
         jax.ShapeDtypeStruct((pages, n_homes * cap, pps), BF16),
@@ -171,53 +173,79 @@
         [all_of(o) for o in out],
         out,
         (info, meta, flags),
+        flops=flops,
+    )
+
+
+def half_kernel(info, proj, out):
+    out[...] = proj[...]
+
+
+def half_of(info, proj):
+    rows, width = proj.shape
+    out = jax.ShapeDtypeStruct((rows, width // 2), BF16)
+    return call(
+        half_kernel,
+        1,
+        [pl.BlockSpec((rows, width // 2), lambda p, info: (0, info[CORE]))],
+        all_of(out),
+        out,
+        (info, proj),
+        flops=1 << 35,
     )
 
 
 def weights_kernel(offsets, info, patches, *refs):
-    *gathered, out, proj, sems = refs
+    gathered, (*before, out, proj, sems) = refs[: 2 * len(offsets)], refs[2 * len(offsets) :]
     half = proj.shape[1] // 2
+    rows = gathered[0].shape[1]
+    shards = [offset for some in offsets for offset in some]
 
     def copies():
-        for g, ref in enumerate(gathered):
-            rows = ref.shape[1]
-            core = g // len(offsets)
-            for i, offset in enumerate(offsets[g % len(offsets)]):
-                shard = jnp.bitwise_xor(info[DP], offset)
-                first = jnp.bitwise_xor(info[CORE], core) * half
-                to = proj.at[
-                    pl.ds(pl.multiple_of(shard * rows, rows), rows),
-                    pl.ds(pl.multiple_of(first, half), half),
-                ]
-                yield ref.at[i], to
+        n = 0
+        for core in range(2):
+            at = 0
+            for some, ref in zip(offsets, gathered[core * len(offsets) :]):
+                for i in range(len(some)):
+                    first = jnp.bitwise_xor(info[CORE], core) * half
+                    to = proj.at[pl.ds(at * rows, rows), pl.ds(pl.multiple_of(first, half), half)]
+                    yield pltpu.make_async_copy(ref.at[i], to, sems.at[n])
+                    at, n = at + 1, n + 1
 
     @pl.when(pl.program_id(0) == 0)
     def _():
-        started = [
-            pltpu.make_async_copy(a, b, sems.at[i]) for i, (a, b) in enumerate(copies())
-        ]
+        started = list(copies())
         for copy in started:
             copy.start()
         for copy in started:
             copy.wait()
 
-    out[0] = dot(proj[...], patches[0], ((1,), (1,))).astype(BF16)
-
-
-def weights(info, patches, gathered, offsets):
+    for other in before:
+        out[...] = other[...]
+    got = dot(proj[...], patches[0], ((1,), (1,))).astype(BF16)
+    for i, offset in enumerate(shards):
+        to = pl.multiple_of(jnp.bitwise_xor(info[DP], offset) * rows, rows)
+        out[0, pl.ds(to, rows)] = got[i * rows : (i + 1) * rows]
+
+
+def weights(info, patches, gathered, offsets, before=(), flops=0):
     pages, pps, width = patches.shape
+    n_shards = sum(len(some) for some in offsets)
     out = jax.ShapeDtypeStruct((pages, width, pps), BF16)
     return call(
         functools.partial(weights_kernel, offsets),
         pages,
-        [page_of(patches)] + [pl.BlockSpec(memory_space=pl.ANY)] * len(gathered),
+        [page_of(patches)]
+        + [pl.BlockSpec(memory_space=pl.ANY)] * len(gathered)
+        + [page_of(b) for b in before],
         page_of(out),
         out,
-        (info, patches, *gathered),
+        (info, patches, *gathered, *before),
         [
-            pltpu.VMEM((width, width), BF16),
-            pltpu.SemaphoreType.DMA((sum(g.shape[0] for g in gathered),)),
+            pltpu.VMEM((n_shards * gathered[0].shape[1], width), BF16),
+            pltpu.SemaphoreType.DMA((2 * n_shards,)),
         ],
+        flops=flops,
     )
 
 
@@ -301,7 +329,7 @@
         page_of(out),
         out,
         (info, *(x for pair in pairs for x in pair), *before),
-        flops=64 * width * width * sum(dq.shape[0] for _, dq in pairs),
+        flops=64 * width * width * sum(dq.shape[0] for _, dq in pairs) if before else 0,
     )
 
 
@@ -331,14 +359,12 @@
     n_dp = lax.axis_size("dp")
     n_y, n_high = n_seq // 2, n_dp // 2
     cap = 2 * wdev // n_seq
-    half = width // 2
     shard_rows = proj.shape[0]
     near, far = (0, 1), tuple(range(2, n_seq))
 
     me, my_dp = lax.axis_index("seq"), lax.axis_index("dp")
     core, y, low, high = me & 1, me >> 1, my_dp & 1, my_dp >> 1
     own = {
-        "column": core * half,
         "low": [low ^ k for k in range(2)],
         "y": [y ^ k for k in range(n_y)],
         "high": [high ^ k for k in range(n_high)],
@@ -353,53 +379,63 @@
     )
     info, proj, both = lax.optimization_barrier((info, proj, both))
     both = [exchange(rows, "seq", 2 * (k + 1)) for k, rows in enumerate(both)]
+    piece = half_of(info, proj)
+    pieces = [piece] + [exchange(piece, "dp", 2 * k) for k in range(1, n_high)]
+    group = n_high // 2
     stay, across, *rest = dispatch(
         info,
         routes,
         words,
         [((r,), 0, pages) for r in near] + [((r,), split, pages - split) for r in far],
         cap,
-    )
-
-    piece = lax.dynamic_slice(
-        proj, (0, own["column"]), (shard_rows, half), allow_negative_indices=False
-    )
-    pieces = [piece] + [exchange(piece, "dp", 2 * k) for k in range(1, n_high)]
-    group = n_high // 2
-    groups = [jnp.stack(pieces[i : i + group]) for i in range(0, n_high, group)]
+        WORK,
+    )
+    pieces[1:group], rest, stay, across = lax.optimization_barrier(
+        (pieces[1:group], rest, stay, across)
+    )
+    early = jnp.stack(pieces[:group])
+    early = [early, exchange(early, "dp", 1)]
+    late_offsets = [[2 * k + bit] for k in range(group, n_high) for bit in range(2)]
 
     pair = jnp.concatenate([routes, targets.reshape(pages, 1, wdev)], axis=1)
     meta_near = jnp.stack([pair, exchange(pair, "seq", 1)])
-    table_near = tables(info, meta_near, flags, near, cap, pps)
+    table_near = tables(info, meta_near, flags, near, cap, pps, WORK)
     meta_far = jnp.concatenate([exchange(meta_near, "seq", 2 * k) for k in range(1, n_y)], axis=0)
 
-    crossed = exchange(groups[0], "dp", 1)
-    crossed, groups[1], rest, stay, across, table_near = lax.optimization_barrier(
-        (crossed, groups[1], rest, stay, across, table_near)
-    )
-    gathered = [groups[0], crossed, groups[1], exchange(groups[1], "dp", 1)]
-    offsets = [[2 * (i + k) + bit for k in range(group)] for i in (0, group) for bit in range(2)]
-    gathered += [exchange(some, "seq", 1) for some in gathered]
+    early, pieces[group:], table_near = lax.optimization_barrier(
+        (early, pieces[group:], table_near)
+    )
+    late = [jnp.stack([piece]) for piece in pieces[group:]]
+
+    early += [exchange(some, "seq", 1) for some in early]
+    early, late[-1] = lax.optimization_barrier((early, late[-1]))
+    weight = weights(
+        info, patches, early, [[2 * k + bit for k in range(group)] for bit in range(2)], (), WORK
+    )
+    late = [x for piece in late for x in (piece, exchange(piece, "dp", 1))]
+    late, weight = lax.optimization_barrier((late, weight))
     across = exchange(across, "seq", 1)
+    late += [exchange(piece, "seq", 1) for piece in late]
     rest = [exchange(rows, "seq", r) for rows, r in zip(rest, far)]
-    weight = weights(info, patches, gathered, offsets)
+    weight = weights(info, patches, late, late_offsets, [weight])
     run = functools.partial(run_pages, info, weight, patches)
     loss, *pair_near = run(table_near, [(stay, 0), (across, 0)], 0)
     word_loss = [loss[:, 0], exchange(loss[:, 1], "seq", 1)]
 
     both, meta_far, pair_near = lax.optimization_barrier((both, meta_far, pair_near))
     first = [pair for rows in both for pair in ((rows, 0), (exchange(rows, "seq", 1), 1))]
+    before = [gradient(info, other, F32, n_y, [pair_near]) for other in range(2)]
+    info, before = lax.optimization_barrier((info, before))
     table_far = tables(info, meta_far, flags, far, cap, pps)
     loss_a, *pair_a = run(table_far, first, 0)
-    before = [gradient(info, other, F32, n_y, [pair_near, pair_a]) for other in range(2)]
-    before, rest = lax.optimization_barrier((before, rest))
+    rest, pair_a = lax.optimization_barrier((rest, pair_a))
     loss_b, *pair_b = run(table_far, [(rows, 0) for rows in rest], split)
     losses = jnp.concatenate([loss_a, loss_b], axis=0)
     for i, r in enumerate(far):
         word_loss.append(exchange(losses[:, i], "seq", r))
 
-    sent = gradient(info, 1, BF16, n_y, [pair_b], [before[1]])
-    kept = gradient(info, 0, F32, n_y, [pair_b], [before[0]])
+    sent = gradient(info, 1, BF16, n_y, [pair_a, pair_b], [before[1]])
+    kept = gradient(info, 0, F32, n_y, [pair_a, pair_b], [before[0]])
     form = (n_y, n_high, 2, shard_rows, width // n_seq)
     terms = [kept.reshape(form), exchange(sent, "seq", 1).reshape(form)]
     part = lambda i, j: sum(

time: 96.6 us -> 92.4 us (0.957)
  waiting for transfers between devices: 27.3 us -> 23.6 us
    ppermute x23 -> x26, waiting for transfers between devices: 17.1 us -> 12.7 us  [exchange(): return lax.ppermute(x, axis, [(i, i ^ offset) for i in range(n)])]
    pallas_call x12 -> x14, Pallas kernels: 36.5 us -> 36.6 us  [call(): pl.pallas_call(kernel, grid_spec=pltpu.PrefetchScalarGridSpec(num_scalar_...]
    ppermute x23 -> x26, starting transfers between devices: 21.5 us -> 21.4 us  [exchange(): return lax.ppermute(x, axis, [(i, i ^ offset) for i in range(n)])]
    unnamed x31 -> x21, local copies, waits for them, and re-layouts: 2.35 us -> 2.32 us
  transfers between devices with their start and end apart: 26 -> 29, of which waited for: 10 -> 11; matrix products, arithmetic and copies ran while one was open for 3% -> 3% of each run, Pallas kernels for 37% -> 38%
where the time goes in v7:
time: 92.4 us; the launch traced here: 92.2 us
  Pallas kernels  36.6 us (40%)
  starting transfers between devices  25 us (27%)
  waiting for transfers between devices  23.6 us (26%)
  other arithmetic  3.11 us (3%)
  local copies, waits for them, and re-layouts  2.97 us (3%)
  between operations  0.93 us (1%)
    pallas_call x14, Pallas kernels, call(): pl.pallas_call(kernel, grid_spec=pltpu.PrefetchScalarGridSpec(num_scalar_...  36.6 us
    ppermute x26, starting transfers between devices, exchange(): return lax.ppermute(x, axis, [(i, i ^ offset) for i in range(n)])  21.4 us
    ppermute x26, waiting for transfers between devices, exchange(): return lax.ppermute(x, axis, [(i, i ^ offset) for i in range(n)])  12.7 us
    ppermute x3, waiting for transfers between devices, exchange_both(): lax.ppermute(x, ('dp', 'seq'), [(i, i ^ dp * n_seq + seq) for i in range(...  10.9 us
    ppermute x3, starting transfers between devices, exchange_both(): lax.ppermute(x, ('dp', 'seq'), [(i, i ^ dp * n_seq + seq) for i in range(...  3.55 us
    unnamed x21, local copies, waits for them, and re-layouts  2.32 us
  transfers between devices with their start and end apart: 29, of which 11 were waited for; matrix products, arithmetic and copies ran while one was open for 3% of the time, Pallas kernels for 38%

profile of v7, /device:TPU:0, one launch (start us, length us, event | category | flops | bytes accessed | tf_op | source)
XLA Modules:
  0.0 92.2 jit_solution(12469457309324194071)
XLA Ops:
  0.6 0.7 pad_add_fusion.2.info
  1.4 1.6 %copy-done.1 = bf16[4,256,1024]{2,1,0:T(8,128)(2,1)S(1)} copy-done((bf16[4,256,1024]{2,1,0:T(8,128)(2,1)S(1)}, bf16[4,256,1024]{2,1,0:T(8,128)(2,1)}, u32[]{:S(2)}) %copy-start.1) | copy-done | bytes 2097176
  3.0 0.7 copy-done.4
  3.7 1.3 %shard_map.86 = bf16[2,3,128,1024]{3,2,1,0:T(8,128)(2,1)S(1)} custom-call(s32[7]{0:T(128)S(1)} %pad_add_fusion.2.info, s32[4,1,256]{2,1,0:T(1,128)S(1)} %bitcast.100, bf16[4,256,1024]{2,1,0:T(8,128)(2,1)S(1)} %copy-done.1), custom_call_target="tpu_custom_call" | custom-call | tf_op jit(solution)/shard_map/pallas_call | solution.py:35
  5.0 3.0 %collective-permute-start.15 = (bf16[2,3,128,1024]{3,2,1,0:T(8,128)(2,1)S(1)}, bf16[2,3,128,1024]{3,2,1,0:T(8,128)(2,1)S(1)}, u32[]{:S(2)}, u32[]{:S(2)}) collective-permute-start(bf16[2,3,128,1024]{3,2,1,0:T(8,128)(2,1)S(1)} %shard_map.86), channel_id=1, source_target_pairs={{0,2},{1,3},{2,0},{3,1},{4,6},{5,7},{6,4},{7,5},{8,10},{9,11},{10,... | collective-permute-start | bytes 4718600 | tf_op jit(solution)/shard_map/ppermute | solution.py:338
  8.0 0.6 shard_map.87
  8.6 1.6 %collective-permute-start = (bf16[128,512]{1,0:T(8,128)(2,1)S(1)}, bf16[128,512]{1,0:T(8,128)(2,1)S(1)}, u32[]{:S(2)}, u32[]{:S(2)}) collective-permute-start(bf16[128,512]{1,0:T(8,128)(2,1)S(1)} %shard_map.87), channel_id=1, source_target_pairs={{0,8},{4,12},{8,0},{12,4},{16,24},{20,28},{24,16},{28,20},{1,9},{5... | collective-permute-start | bytes 393224 | tf_op jit(solution)/shard_map/ppermute | solution.py:338
  10.2 2.6 %collective-permute-start.2 = (bf16[128,512]{1,0:T(8,128)(2,1)S(1)}, bf16[128,512]{1,0:T(8,128)(2,1)S(1)}, u32[]{:S(2)}, u32[]{:S(2)}) collective-permute-start(bf16[128,512]{1,0:T(8,128)(2,1)S(1)} %shard_map.87), channel_id=1, source_target_pairs={{0,16},{4,20},{8,24},{12,28},{16,0},{20,4},{24,8},{28,12},{1,17},{... | collective-permute-start | bytes 393224 | tf_op jit(solution)/shard_map/ppermute | solution.py:338
  13.1 1.5 %shard_map.88 = (bf16[1,4,128,1024]{3,2,1,0:T(8,128)(2,1)S(1)}, bf16[1,4,128,1024]{3,2,1,0:T(8,128)(2,1)S(1)}, bf16[1,1,128,1024]{3,2,1,0:T(8,128)(2,1)S(1)}, bf16[1,1,128,1024]{3,2,1,0:T(8,128)(2,1)S(1)}) custom-call(s32[7]{0:T(128)S(1)} %pad_add_fusion.2.info, s32[4,1,256]{2,1,0:T(1,128)S(1)} %bitcast.102, bf16[4,256,1024]{2,1,0:T(8,128)(2,1)S(1)} %copy-done.2), custom_call_target="tpu_custom_call" | custom-call | flops 2147483648 | tf_op jit(solution)/shard_map/pallas_call | solution.py:35
  14.7 0.4 collective-permute-done
  15.3 1.5 %collective-permute-start.1 = (bf16[2,128,512]{2,1,0:T(8,128)(2,1)S(1)}, bf16[2,128,512]{2,1,0:T(8,128)(2,1)S(1)}, u32[]{:S(2)}, u32[]{:S(2)}) collective-permute-start(bf16[2,128,512]{2,1,0:T(8,128)(2,1)S(1)} %pad_maximum_fusion.refs_0_), channel_id=1, source_target_pairs={{0,4},{4,0},{8,12},{12,8},{16,20},{20,16},{24,28},{28,24},{1,5},{5... | collective-permute-start | bytes 786440 | tf_op jit(solution)/shard_map/ppermute | solution.py:338
  16.8 2.9 %shard_map.89 = (bf16[4,256,512]{2,1,0:T(8,128)(2,1)S(1)}, f32[4,256,128]{2,1,0:T(8,128)S(1)}, f32[4,8,256]{2,1,0:T(8,128)S(1)}) custom-call(s32[7]{0:T(128)S(1)} %pad_add_fusion.2.info, s32[2,4,2,256]{3,2,1,0:T(2,128)S(1)} %pad_add_fusion.meta, s32[4,16,32]{2,1,0:T(8,128)S(1)} %copy-done.3), custom_call_target="tpu_custom_call" | custom-call | flops 2147483648 | tf_op jit(solution)/shard_map/pallas_call | solution.py:35
  19.8 3.1 %collective-permute-done.2 = bf16[128,512]{1,0:T(8,128)(2,1)S(1)} collective-permute-done((bf16[128,512]{1,0:T(8,128)(2,1)S(1)}, bf16[128,512]{1,0:T(8,128)(2,1)S(1)}, u32[]{:S(2)}, u32[]{:S(2)}) %collective-permute-start.2) | collective-permute-done | bytes 131104 | tf_op jit(solution)/shard_map/ppermute | solution.py:338
  22.9 1.0 %collective-permute-done.1.refs_1_ = bf16[2,128,512]{2,1,0:T(8,128)(2,1)S(1)} collective-permute-done((bf16[2,128,512]{2,1,0:T(8,128)(2,1)S(1)}, bf16[2,128,512]{2,1,0:T(8,128)(2,1)S(1)}, u32[]{:S(2)}, u32[]{:S(2)}) %collective-permute-start.1) | collective-permute-done | bytes 262176 | tf_op jit(solution)/shard_map/ppermute | solution.py:338
  23.9 0.5 collective-permute-start.7
  24.4 1.5 %collective-permute-start.5 = (bf16[1,128,512]{2,1,0:T(8,128)(2,1)S(1)}, bf16[1,128,512]{2,1,0:T(8,128)(2,1)S(1)}, u32[]{:S(2)}, u32[]{:S(2)}) collective-permute-start(bf16[1,128,512]{2,1,0:T(8,128)(2,1)S(1)} %bitcast.93), channel_id=1, source_target_pairs={{0,4},{4,0},{8,12},{12,8},{16,20},{20,16},{24,28},{28,24},{1,5},{5... | collective-permute-start | bytes 393224 | tf_op jit(solution)/shard_map/ppermute | solution.py:338
  25.9 1.4 %collective-permute-start.8 = (bf16[1,128,512]{2,1,0:T(8,128)(2,1)S(1)}, bf16[1,128,512]{2,1,0:T(8,128)(2,1)S(1)}, u32[]{:S(2)}, u32[]{:S(2)}) collective-permute-start(bf16[1,128,512]{2,1,0:T(8,128)(2,1)S(1)} %bitcast.96), channel_id=1, source_target_pairs={{0,4},{4,0},{8,12},{12,8},{16,20},{20,16},{24,28},{28,24},{1,5},{5... | collective-permute-start | bytes 393224 | tf_op jit(solution)/shard_map/ppermute | solution.py:338
  27.3 4.0 %shard_map.90.refs_8_ = bf16[4,1024,512]{2,1,0:T(8,128)(2,1)S(1)} custom-call(s32[7]{0:T(128)S(1)} %pad_add_fusion.2.info, bf16[4,512,1024]{2,1,0:T(8,128)(2,1)S(1)} %copy-done, bf16[2,128,512]{2,1,0:T(8,128)(2,1)S(1)} %pad_maximum_fusion.refs_0_, bf16[2,128,512]{2,1,0:T(8,128)(2,1)S(1)} %collective-permute-done.1.refs_1_, ...), custom_call_target="tpu_custom_call" | custom-call | flops 2147483648 | tf_op jit(solution)/shard_map/pallas_call | solution.py:35
  31.3 1.3 %collective-permute-done.8.refs_3_ = bf16[1,128,512]{2,1,0:T(8,128)(2,1)S(1)} collective-permute-done((bf16[1,128,512]{2,1,0:T(8,128)(2,1)S(1)}, bf16[1,128,512]{2,1,0:T(8,128)(2,1)S(1)}, u32[]{:S(2)}, u32[]{:S(2)}) %collective-permute-start.8) | collective-permute-done | bytes 131104 | tf_op jit(solution)/shard_map/ppermute | solution.py:338
  32.6 0.5 collective-permute-start.11
  33.1 0.8 collective-permute-done.10.refs_5_
  34.5 0.8 collective-permute-done.9.refs_4_
  35.3 3.8 %shard_map.91.weight = bf16[4,1024,512]{2,1,0:T(8,128)(2,1)S(1)} custom-call(s32[7]{0:T(128)S(1)} %pad_add_fusion.2.info, bf16[4,512,1024]{2,1,0:T(8,128)(2,1)S(1)} %copy-done, bf16[1,128,512]{2,1,0:T(8,128)(2,1)S(1)} %bitcast.95, bf16[1,128,512]{2,1,0:T(8,128)(2,1)S(1)} %collective-permute-done.5.refs_1_, bf16[1,128,512]{2,1,0:T(8,128)(2,1)S(1)} %bitcast.98, ...), custom_call_target="tpu_custom_call" | custom-call | tf_op jit(solution)/shard_map/pallas_call | solution.py:35
  39.1 5.3 %shard_map.92 = (f32[4,2,256]{2,1,0:T(2,128)S(1)}, bf16[1024,1024]{1,0:T(8,128)(2,1)S(1)}, bf16[1024,1024]{1,0:T(8,128)(2,1)S(1)}) custom-call(s32[7]{0:T(128)S(1)} %pad_add_fusion.2.info, bf16[4,256,512]{2,1,0:T(8,128)(2,1)S(1)} %get-tuple-element.79.bias, f32[4,256,128]{2,1,0:T(8,128)S(1)} %get-tuple-element.80.table, ...), custom_call_target="tpu_custom_call" | custom-call | tf_op jit(solution)/shard_map/pallas_call | solution.py:35
  44.7 0.8 collective-permute-start.18
  45.5 0.9 collective-permute-start.19
  46.4 0.6 slice_bitcast_fusion
  47.0 0.4 collective-permute-start.14
  47.4 2.2 %shard_map.94.refs_4_ = f32[2,1024,256]{2,1,0:T(8,128)S(1)} custom-call(s32[7]{0:T(128)S(1)} %pad_add_fusion.2.info, bf16[1024,1024]{1,0:T(8,128)(2,1)S(1)} %get-tuple-element.102.refs_0_, bf16[1024,1024]{1,0:T(8,128)(2,1)S(1)} %get-tuple-element.103.refs_1_), custom_call_target="tpu_custom_call" | custom-call | tf_op jit(solution)/shard_map/pallas_call | solution.py:35
  49.6 2.2 %shard_map.93.refs_4_ = f32[2,1024,256]{2,1,0:T(8,128)S(1)} custom-call(s32[7]{0:T(128)S(1)} %pad_add_fusion.2.info, bf16[1024,1024]{1,0:T(8,128)(2,1)S(1)} %get-tuple-element.102.refs_0_, bf16[1024,1024]{1,0:T(8,128)(2,1)S(1)} %get-tuple-element.103.refs_1_), custom_call_target="tpu_custom_call" | custom-call | tf_op jit(solution)/shard_map/pallas_call | solution.py:35
  51.7 2.9 %shard_map.95 = (bf16[4,256,512]{2,1,0:T(8,128)(2,1)S(1)}, f32[4,256,128]{2,1,0:T(8,128)S(1)}, f32[4,8,256]{2,1,0:T(8,128)S(1)}) custom-call(s32[7]{0:T(128)S(1)} %pad_add_fusion.2.info, s32[2,4,2,256]{3,2,1,0:T(2,128)S(1)} %collective-permute-done.16.meta, s32[4,16,32]{2,1,0:T(8,128)S(1)} %copy-done.3), custom_call_target="tpu_custom_call" | custom-call | tf_op jit(solution)/shard_map/pallas_call | solution.py:35
  54.7 4.0 %shard_map.96 = (f32[3,2,256]{2,1,0:T(2,128)S(1)}, bf16[1024,768]{1,0:T(8,128)(2,1)S(1)}, bf16[768,1024]{1,0:T(8,128)(2,1)S(1)}) custom-call(s32[7]{0:T(128)S(1)} %pad_add_fusion.2.info, bf16[4,256,512]{2,1,0:T(8,128)(2,1)S(1)} %get-tuple-element.106.bias, f32[4,256,128]{2,1,0:T(8,128)S(1)} %get-tuple-element.107.table, ...), custom_call_target="tpu_custom_call" | custom-call | tf_op jit(solution)/shard_map/pallas_call | solution.py:35
  58.7 1.6 %shard_map.97 = (f32[1,2,256]{2,1,0:T(2,128)S(1)}, bf16[1024,256]{1,0:T(8,128)(2,1)S(1)}, bf16[256,1024]{1,0:T(8,128)(2,1)S(1)}) custom-call(s32[7]{0:T(128)S(1)} %pad_add_fusion.2.info, bf16[4,256,512]{2,1,0:T(8,128)(2,1)S(1)} %get-tuple-element.106.bias, f32[4,256,128]{2,1,0:T(8,128)S(1)} %get-tuple-element.107.table, ...), custom_call_target="tpu_custom_call" | custom-call | tf_op jit(solution)/shard_map/pallas_call | solution.py:35
  60.4 2.2 %shard_map.99 = bf16[2,1024,256]{2,1,0:T(8,128)(2,1)S(1)} custom-call(s32[7]{0:T(128)S(1)} %pad_add_fusion.2.info, bf16[1024,768]{1,0:T(8,128)(2,1)S(1)} %get-tuple-element.118.refs_0_, bf16[768,1024]{1,0:T(8,128)(2,1)S(1)} %get-tuple-element.119.refs_1_, bf16[1024,256]{1,0:T(8,128)(2,1)S(1)} %get-tuple-element.120.refs_2_, ...), custom_call_target="tpu_custom_call" | custom-call | flops 68719476736 | tf_op jit(solution)/shard_map/pallas_call | solution.py:35
  62.7 2.2 %shard_map.98 = f32[2,1024,256]{2,1,0:T(8,128)S(1)} custom-call(s32[7]{0:T(128)S(1)} %pad_add_fusion.2.info, bf16[1024,768]{1,0:T(8,128)(2,1)S(1)} %get-tuple-element.118.refs_0_, bf16[768,1024]{1,0:T(8,128)(2,1)S(1)} %get-tuple-element.119.refs_1_, bf16[1024,256]{1,0:T(8,128)(2,1)S(1)} %get-tuple-element.120.refs_2_, ...), custom_call_target="tpu_custom_call" | custom-call | flops 68719476736 | tf_op jit(solution)/shard_map/pallas_call | solution.py:35
  64.9 0.4 collective-permute-done.22
  65.6 1.6 %collective-permute-start.23 = (bf16[4,128,256]{2,1,0:T(8,128)(2,1)S(1)}, bf16[4,128,256]{2,1,0:T(8,128)(2,1)S(1)}, u32[]{:S(2)}, u32[]{:S(2)}) collective-permute-start(bf16[4,128,256]{2,1,0:T(8,128)(2,1)S(1)} %get-tuple-element.132), channel_id=1, source_target_pairs={{0,4},{1,5},{2,6},{3,7},{4,0},{5,1},{6,2},{7,3},{8,12},{9,13},{10,... | collective-permute-start | bytes 786440 | tf_op jit(solution)/shard_map/ppermute | solution.py:344
  67.1 0.8 collective-permute-start.24
  67.9 1.2 %collective-permute-start.25 = (bf16[4,128,256]{2,1,0:T(8,128)(2,1)S(1)}, bf16[4,128,256]{2,1,0:T(8,128)(2,1)S(1)}, u32[]{:S(2)}, u32[]{:S(2)}) collective-permute-start(bf16[4,128,256]{2,1,0:T(8,128)(2,1)S(1)} %get-tuple-element.134), channel_id=1, source_target_pairs={{0,6},{1,7},{2,4},{3,5},{4,2},{5,3},{6,0},{7,1},{8,14},{9,15},{10,... | collective-permute-start | bytes 786440 | tf_op jit(solution)/shard_map/ppermute | solution.py:344
  69.1 0.9 collective-permute-start.20
  70.0 4.8 %collective-permute-done.23 = bf16[4,128,256]{2,1,0:T(8,128)(2,1)S(1)} collective-permute-done((bf16[4,128,256]{2,1,0:T(8,128)(2,1)S(1)}, bf16[4,128,256]{2,1,0:T(8,128)(2,1)S(1)}, u32[]{:S(2)}, u32[]{:S(2)}) %collective-permute-start.23) | collective-permute-done | bytes 262176 | tf_op jit(solution)/shard_map/ppermute | solution.py:344
  74.8 6.1 %collective-permute-done.24 = bf16[4,128,256]{2,1,0:T(8,128)(2,1)S(1)} collective-permute-done((bf16[4,128,256]{2,1,0:T(8,128)(2,1)S(1)}, bf16[4,128,256]{2,1,0:T(8,128)(2,1)S(1)}, u32[]{:S(2)}, u32[]{:S(2)}) %collective-permute-start.24) | collective-permute-done | bytes 262176 | tf_op jit(solution)/shard_map/ppermute | solution.py:344
  81.1 1.0 %collective-permute-start.26 = (bf16[128,256]{1,0:T(8,128)(2,1)S(1)}, bf16[128,256]{1,0:T(8,128)(2,1)S(1)}, u32[]{:S(2)}, u32[]{:S(2)}) collective-permute-start(bf16[128,256]{1,0:T(8,128)(2,1)S(1)} %get-tuple-element.135), channel_id=1, source_target_pairs={{0,8},{4,12},{8,0},{12,4},{16,24},{20,28},{24,16},{28,20},{1,9},{5... | collective-permute-start | bytes 196616 | tf_op jit(solution)/shard_map/ppermute | solution.py:338
  82.1 3.3 %collective-permute-start.27 = (bf16[128,256]{1,0:T(8,128)(2,1)S(1)}, bf16[128,256]{1,0:T(8,128)(2,1)S(1)}, u32[]{:S(2)}, u32[]{:S(2)}) collective-permute-start(bf16[128,256]{1,0:T(8,128)(2,1)S(1)} %get-tuple-element.137), channel_id=1, source_target_pairs={{0,16},{4,20},{8,24},{12,28},{16,0},{20,4},{24,8},{28,12},{1,17},{... | collective-permute-start | bytes 196616 | tf_op jit(solution)/shard_map/ppermute | solution.py:338
  85.6 1.3 %fusion.17 = f32[4,256]{1,0:T(4,128)} fusion(f32[4,256]{1,0:T(4,128)S(1)} %collective-permute-done.21, f32[4,256]{1,0:T(4,128)S(1)} %collective-permute-done.20, f32[4,256]{1,0:T(4,128)} %collective-permute-done.14, f32[4,2,256]{2,0,1:T(4,128)S(1)} %copy-done.7), kind=kLoop, calls=%fused_computation.32 | loop fusion | flops 3072 | bytes 20480 | tf_op jit(solution)/shard_map/add | solution.py:452
  86.8 2.2 %collective-permute-done.27 = bf16[128,256]{1,0:T(8,128)(2,1)S(1)} collective-permute-done((bf16[128,256]{1,0:T(8,128)(2,1)S(1)}, bf16[128,256]{1,0:T(8,128)(2,1)S(1)}, u32[]{:S(2)}, u32[]{:S(2)}) %collective-permute-start.27) | collective-permute-done | bytes 65568 | tf_op jit(solution)/shard_map/ppermute | solution.py:338
  89.1 2.4 %collective-permute-done.28 = bf16[128,256]{1,0:T(8,128)(2,1)S(1)} collective-permute-done((bf16[128,256]{1,0:T(8,128)(2,1)S(1)}, bf16[128,256]{1,0:T(8,128)(2,1)S(1)}, u32[]{:S(2)}, u32[]{:S(2)}) %collective-permute-start.28) | collective-permute-done | bytes 65568 | tf_op jit(solution)/shard_map/ppermute | solution.py:338
  91.5 0.7 fusion.11
  (59 shorter events, 2.0 us)
Async XLA Ops:
  1.4 1.6 %copy-start.1 = (bf16[4,256,1024]{2,1,0:T(8,128)(2,1)S(1)}, bf16[4,256,1024]{2,1,0:T(8,128)(2,1)}, u32[]{:S(2)}) copy-start(bf16[4,256,1024]{2,1,0:T(8,128)(2,1)} %words.3) | copy-start | bytes 6291460
  3.0 0.7 copy-start.4
  3.7 4.3 %copy-start.5 = (bf16[128,1024]{1,0:T(8,128)(2,1)S(1)}, bf16[128,1024]{1,0:T(8,128)(2,1)}, u32[]{:S(2)}) copy-start(bf16[128,1024]{1,0:T(8,128)(2,1)} %proj) | copy-start | bytes 786436
  4.9 8.1 %copy-start.8 = (s32[4,256]{1,0:T(4,128)S(1)}, s32[4,256]{1,0:T(4,128)}, u32[]{:S(2)}) copy-start(s32[4,256]{1,0:T(4,128)} %param.11) | copy-start | bytes 12292
  5.0 8.2 %copy-start.2 = (bf16[4,256,1024]{2,1,0:T(8,128)(2,1)S(1)}, bf16[4,256,1024]{2,1,0:T(8,128)(2,1)}, u32[]{:S(2)}) copy-start(bf16[4,256,1024]{2,1,0:T(8,128)(2,1)} %words.3) | copy-start | bytes 6291460
  5.0 39.5 %collective-permute-start.15 = (bf16[2,3,128,1024]{3,2,1,0:T(8,128)(2,1)S(1)}, bf16[2,3,128,1024]{3,2,1,0:T(8,128)(2,1)S(1)}, u32[]{:S(2)}, u32[]{:S(2)}) collective-permute-start(bf16[2,3,128,1024]{3,2,1,0:T(8,128)(2,1)S(1)} %shard_map.86), channel_id=1, source_target_pairs={{0,2},{1,3},{2,0},{3,1},{4,6},{5,7},{6,4},{7,5},{8,10},{9,11},{10,... | collective-permute-start | bytes 4718600 | tf_op jit(solution)/shard_map/ppermute | solution.py:338
  8.6 6.5 %collective-permute-start = (bf16[128,512]{1,0:T(8,128)(2,1)S(1)}, bf16[128,512]{1,0:T(8,128)(2,1)S(1)}, u32[]{:S(2)}, u32[]{:S(2)}) collective-permute-start(bf16[128,512]{1,0:T(8,128)(2,1)S(1)} %shard_map.87), channel_id=1, source_target_pairs={{0,8},{4,12},{8,0},{12,4},{16,24},{20,28},{24,16},{28,20},{1,9},{5... | collective-permute-start | bytes 393224 | tf_op jit(solution)/shard_map/ppermute | solution.py:338
  10.2 12.6 %collective-permute-start.2 = (bf16[128,512]{1,0:T(8,128)(2,1)S(1)}, bf16[128,512]{1,0:T(8,128)(2,1)S(1)}, u32[]{:S(2)}, u32[]{:S(2)}) collective-permute-start(bf16[128,512]{1,0:T(8,128)(2,1)S(1)} %shard_map.87), channel_id=1, source_target_pairs={{0,16},{4,20},{8,24},{12,28},{16,0},{20,4},{24,8},{28,12},{1,17},{... | collective-permute-start | bytes 393224 | tf_op jit(solution)/shard_map/ppermute | solution.py:338
  12.8 10.1 %collective-permute-start.3 = (bf16[128,512]{1,0:T(8,128)(2,1)S(1)}, bf16[128,512]{1,0:T(8,128)(2,1)S(1)}, u32[]{:S(2)}, u32[]{:S(2)}) collective-permute-start(bf16[128,512]{1,0:T(8,128)(2,1)S(1)} %shard_map.87), channel_id=1, source_target_pairs={{0,24},{4,28},{8,16},{12,20},{16,8},{20,12},{24,0},{28,4},{1,25},{... | collective-permute-start | bytes 393224 | tf_op jit(solution)/shard_map/ppermute | solution.py:338
  13.0 3.8 %copy-start.3 = (s32[4,16,32]{2,1,0:T(8,128)S(1)}, s32[4,16,32]{2,1,0:T(8,128)}, u32[]{:S(2)}) copy-start(s32[4,16,32]{2,1,0:T(8,128)} %flags.3) | copy-start | bytes 24580
  13.1 2.2 %collective-permute-start.4 = (s32[4,2,256]{2,1,0:T(2,128)S(1)}, s32[4,2,256]{2,1,0:T(2,128)S(1)}, u32[]{:S(2)}, u32[]{:S(2)}) collective-permute-start(s32[4,2,256]{2,1,0:T(2,128)S(1)} %get-tuple-element.141), channel_id=1, source_target_pairs={{0,1},{1,0},{2,3},{3,2},{4,5},{5,4},{6,7},{7,6},{8,9},{9,8},{10,11... | collective-permute-start | bytes 24584 | tf_op jit(solution)/shard_map/ppermute | solution.py:338
  15.1 24.1 %collective-permute-start.13 = (bf16[1,4,128,1024]{3,2,1,0:T(8,128)(2,1)S(1)}, bf16[1,4,128,1024]{3,2,1,0:T(8,128)(2,1)S(1)}, u32[]{:S(2)}, u32[]{:S(2)}) collective-permute-start(bf16[1,4,128,1024]{3,2,1,0:T(8,128)(2,1)S(1)} %get-tuple-element.97), channel_id=1, source_target_pairs={{0,1},{1,0},{2,3},{3,2},{4,5},{5,4},{6,7},{7,6},{8,9},{9,8},{10,11... | collective-permute-start | bytes 3145736 | tf_op jit(solution)/shard_map/ppermute | solution.py:338
  15.3 8.6 %collective-permute-start.1 = (bf16[2,128,512]{2,1,0:T(8,128)(2,1)S(1)}, bf16[2,128,512]{2,1,0:T(8,128)(2,1)S(1)}, u32[]{:S(2)}, u32[]{:S(2)}) collective-permute-start(bf16[2,128,512]{2,1,0:T(8,128)(2,1)S(1)} %pad_maximum_fusion.refs_0_), channel_id=1, source_target_pairs={{0,4},{4,0},{8,12},{12,8},{16,20},{20,16},{24,28},{28,24},{1,5},{5... | collective-permute-start | bytes 786440 | tf_op jit(solution)/shard_map/ppermute | solution.py:338
  16.8 10.5 %copy-start = (bf16[4,512,1024]{2,1,0:T(8,128)(2,1)S(1)}, bf16[4,512,1024]{2,1,0:T(8,128)(2,1)}, u32[]{:S(2)}) copy-start(bf16[4,512,1024]{2,1,0:T(8,128)(2,1)} %patches.9) | copy-start | bytes 12582916
  23.9 2.0 %collective-permute-start.6 = (bf16[2,128,512]{2,1,0:T(8,128)(2,1)S(1)}, bf16[2,128,512]{2,1,0:T(8,128)(2,1)S(1)}, u32[]{:S(2)}, u32[]{:S(2)}) collective-permute-start(bf16[2,128,512]{2,1,0:T(8,128)(2,1)S(1)} %pad_maximum_fusion.refs_0_), channel_id=1, source_target_pairs={{0,1},{1,0},{2,3},{3,2},{4,5},{5,4},{6,7},{7,6},{8,9},{9,8},{10,11... | collective-permute-start | bytes 786440 | tf_op jit(solution)/shard_map/ppermute | solution.py:338
  23.9 2.0 %collective-permute-start.7 = (bf16[2,128,512]{2,1,0:T(8,128)(2,1)S(1)}, bf16[2,128,512]{2,1,0:T(8,128)(2,1)S(1)}, u32[]{:S(2)}, u32[]{:S(2)}) collective-permute-start(bf16[2,128,512]{2,1,0:T(8,128)(2,1)S(1)} %collective-permute-done.1.refs_1_), channel_id=1, source_target_pairs={{0,1},{1,0},{2,3},{3,2},{4,5},{5,4},{6,7},{7,6},{8,9},{9,8},{10,11... | collective-permute-start | bytes 786440 | tf_op jit(solution)/shard_map/ppermute | solution.py:338
  24.4 6.9 %collective-permute-start.5 = (bf16[1,128,512]{2,1,0:T(8,128)(2,1)S(1)}, bf16[1,128,512]{2,1,0:T(8,128)(2,1)S(1)}, u32[]{:S(2)}, u32[]{:S(2)}) collective-permute-start(bf16[1,128,512]{2,1,0:T(8,128)(2,1)S(1)} %bitcast.93), channel_id=1, source_target_pairs={{0,4},{4,0},{8,12},{12,8},{16,20},{20,16},{24,28},{28,24},{1,5},{5... | collective-permute-start | bytes 393224 | tf_op jit(solution)/shard_map/ppermute | solution.py:338
  25.9 6.7 %collective-permute-start.8 = (bf16[1,128,512]{2,1,0:T(8,128)(2,1)S(1)}, bf16[1,128,512]{2,1,0:T(8,128)(2,1)S(1)}, u32[]{:S(2)}, u32[]{:S(2)}) collective-permute-start(bf16[1,128,512]{2,1,0:T(8,128)(2,1)S(1)} %bitcast.96), channel_id=1, source_target_pairs={{0,4},{4,0},{8,12},{12,8},{16,20},{20,16},{24,28},{28,24},{1,5},{5... | collective-permute-start | bytes 393224 | tf_op jit(solution)/shard_map/ppermute | solution.py:338
  32.6 1.3 %collective-permute-start.10 = (bf16[1,128,512]{2,1,0:T(8,128)(2,1)S(1)}, bf16[1,128,512]{2,1,0:T(8,128)(2,1)S(1)}, u32[]{:S(2)}, u32[]{:S(2)}) collective-permute-start(bf16[1,128,512]{2,1,0:T(8,128)(2,1)S(1)} %collective-permute-done.5.refs_1_), channel_id=1, source_target_pairs={{0,1},{1,0},{2,3},{3,2},{4,5},{5,4},{6,7},{7,6},{8,9},{9,8},{10,11... | collective-permute-start | bytes 393224 | tf_op jit(solution)/shard_map/ppermute | solution.py:338
  32.6 1.5 %collective-permute-start.11 = (bf16[1,128,512]{2,1,0:T(8,128)(2,1)S(1)}, bf16[1,128,512]{2,1,0:T(8,128)(2,1)S(1)}, u32[]{:S(2)}, u32[]{:S(2)}) collective-permute-start(bf16[1,128,512]{2,1,0:T(8,128)(2,1)S(1)} %bitcast.97), channel_id=1, source_target_pairs={{0,1},{1,0},{2,3},{3,2},{4,5},{5,4},{6,7},{7,6},{8,9},{9,8},{10,11... | collective-permute-start | bytes 393224 | tf_op jit(solution)/shard_map/ppermute | solution.py:338
  33.1 1.3 %collective-permute-start.12 = (bf16[1,128,512]{2,1,0:T(8,128)(2,1)S(1)}, bf16[1,128,512]{2,1,0:T(8,128)(2,1)S(1)}, u32[]{:S(2)}, u32[]{:S(2)}) collective-permute-start(bf16[1,128,512]{2,1,0:T(8,128)(2,1)S(1)} %collective-permute-done.8.refs_3_), channel_id=1, source_target_pairs={{0,1},{1,0},{2,3},{3,2},{4,5},{5,4},{6,7},{7,6},{8,9},{9,8},{10,11... | collective-permute-start | bytes 393224 | tf_op jit(solution)/shard_map/ppermute | solution.py:338
  34.0 1.3 %collective-permute-start.9 = (bf16[1,128,512]{2,1,0:T(8,128)(2,1)S(1)}, bf16[1,128,512]{2,1,0:T(8,128)(2,1)S(1)}, u32[]{:S(2)}, u32[]{:S(2)}) collective-permute-start(bf16[1,128,512]{2,1,0:T(8,128)(2,1)S(1)} %bitcast.94), channel_id=1, source_target_pairs={{0,1},{1,0},{2,3},{3,2},{4,5},{5,4},{6,7},{7,6},{8,9},{9,8},{10,11... | collective-permute-start | bytes 393224 | tf_op jit(solution)/shard_map/ppermute | solution.py:338
  34.2 10.3 %collective-permute-start.16 = (s32[2,4,2,256]{3,2,1,0:T(2,128)S(1)}, s32[2,4,2,256]{3,2,1,0:T(2,128)S(1)}, u32[]{:S(2)}, u32[]{:S(2)}) collective-permute-start(s32[2,4,2,256]{3,2,1,0:T(2,128)S(1)} %pad_add_fusion.meta), channel_id=1, source_target_pairs={{0,2},{1,3},{2,0},{3,1},{4,6},{5,7},{6,4},{7,5},{8,10},{9,11},{10,... | collective-permute-start | bytes 49160 | tf_op jit(solution)/shard_map/ppermute | solution.py:338
  44.4 10.2 %collective-permute-start.17 = (bf16[2,3,128,1024]{3,2,1,0:T(8,128)(2,1)S(1)}, bf16[2,3,128,1024]{3,2,1,0:T(8,128)(2,1)S(1)}, u32[]{:S(2)}, u32[]{:S(2)}) collective-permute-start(bf16[2,3,128,1024]{3,2,1,0:T(8,128)(2,1)S(1)} %collective-permute-done.15.refs_0_), channel_id=1, source_target_pairs={{0,1},{1,0},{2,3},{3,2},{4,5},{5,4},{6,7},{7,6},{8,9},{9,8},{10,11... | collective-permute-start | bytes 4718600 | tf_op jit(solution)/shard_map/ppermute | solution.py:338
  44.7 14.0 %collective-permute-start.18 = (bf16[1,1,128,1024]{3,2,1,0:T(8,128)(2,1)S(1)}, bf16[1,1,128,1024]{3,2,1,0:T(8,128)(2,1)S(1)}, u32[]{:S(2)}, u32[]{:S(2)}) collective-permute-start(bf16[1,1,128,1024]{3,2,1,0:T(8,128)(2,1)S(1)} %get-tuple-element.111), channel_id=1, source_target_pairs={{0,2},{1,3},{2,0},{3,1},{4,6},{5,7},{6,4},{7,5},{8,10},{9,11},{10,... | collective-permute-start | bytes 786440 | tf_op jit(solution)/shard_map/ppermute | solution.py:338
  45.5 13.2 %collective-permute-start.19 = (bf16[1,1,128,1024]{3,2,1,0:T(8,128)(2,1)S(1)}, bf16[1,1,128,1024]{3,2,1,0:T(8,128)(2,1)S(1)}, u32[]{:S(2)}, u32[]{:S(2)}) collective-permute-start(bf16[1,1,128,1024]{3,2,1,0:T(8,128)(2,1)S(1)} %get-tuple-element.112), channel_id=1, source_target_pairs={{0,3},{1,2},{2,1},{3,0},{4,7},{5,6},{6,5},{7,4},{8,11},{9,10},{10,... | collective-permute-start | bytes 786440 | tf_op jit(solution)/shard_map/ppermute | solution.py:338
  46.4 3.2 %copy-start.6 = (f32[4,2,256]{2,0,1:T(4,128)}, f32[4,2,256]{2,0,1:T(4,128)S(1)}, u32[]{:S(2)}) copy-start(f32[4,2,256]{2,0,1:T(4,128)S(1)} %copy.9) | copy-start | bytes 24580
  47.0 38.5 %collective-permute-start.14 = (f32[4,256]{1,0:T(4,128)}, f32[4,256]{1,0:T(4,128)}, u32[]{:S(2)}, u32[]{:S(2)}) collective-permute-start(f32[4,256]{1,0:T(4,128)} %slice_bitcast_fusion), channel_id=1, source_target_pairs={{0,1},{1,0},{2,3},{3,2},{4,5},{5,4},{6,7},{7,6},{8,9},{9,8},{10,11... | collective-permute-start | bytes 12296 | tf_op jit(solution)/shard_map/ppermute | solution.py:338
  62.6 2.7 %collective-permute-start.22 = (bf16[2,1024,256]{2,1,0:T(8,128)(2,1)S(1)}, bf16[2,1024,256]{2,1,0:T(8,128)(2,1)S(1)}, u32[]{:S(2)}, u32[]{:S(2)}) collective-permute-start(bf16[2,1024,256]{2,1,0:T(8,128)(2,1)S(1)} %shard_map.99), channel_id=1, source_target_pairs={{0,1},{1,0},{2,3},{3,2},{4,5},{5,4},{6,7},{7,6},{8,9},{9,8},{10,11... | collective-permute-start | bytes 3145736 | tf_op jit(solution)/shard_map/ppermute | solution.py:338
  65.3 20.2 %copy-start.7 = (f32[4,2,256]{2,0,1:T(4,128)S(1)}, f32[4,2,256]{2,0,1:T(4,128)}, u32[]{:S(2)}) copy-start(f32[4,2,256]{2,0,1:T(4,128)} %copy-done.6) | copy-start | bytes 24580
  65.6 9.2 %collective-permute-start.23 = (bf16[4,128,256]{2,1,0:T(8,128)(2,1)S(1)}, bf16[4,128,256]{2,1,0:T(8,128)(2,1)S(1)}, u32[]{:S(2)}, u32[]{:S(2)}) collective-permute-start(bf16[4,128,256]{2,1,0:T(8,128)(2,1)S(1)} %get-tuple-element.132), channel_id=1, source_target_pairs={{0,4},{1,5},{2,6},{3,7},{4,0},{5,1},{6,2},{7,3},{8,12},{9,13},{10,... | collective-permute-start | bytes 786440 | tf_op jit(solution)/shard_map/ppermute | solution.py:344
  67.1 13.8 %collective-permute-start.24 = (bf16[4,128,256]{2,1,0:T(8,128)(2,1)S(1)}, bf16[4,128,256]{2,1,0:T(8,128)(2,1)S(1)}, u32[]{:S(2)}, u32[]{:S(2)}) collective-permute-start(bf16[4,128,256]{2,1,0:T(8,128)(2,1)S(1)} %get-tuple-element.133), channel_id=1, source_target_pairs={{0,2},{1,3},{2,0},{3,1},{4,6},{5,7},{6,4},{7,5},{8,10},{9,11},{10,... | collective-permute-start | bytes 786440 | tf_op jit(solution)/shard_map/ppermute | solution.py:344
  67.9 13.0 %collective-permute-start.25 = (bf16[4,128,256]{2,1,0:T(8,128)(2,1)S(1)}, bf16[4,128,256]{2,1,0:T(8,128)(2,1)S(1)}, u32[]{:S(2)}, u32[]{:S(2)}) collective-permute-start(bf16[4,128,256]{2,1,0:T(8,128)(2,1)S(1)} %get-tuple-element.134), channel_id=1, source_target_pairs={{0,6},{1,7},{2,4},{3,5},{4,2},{5,3},{6,0},{7,1},{8,14},{9,15},{10,... | collective-permute-start | bytes 786440 | tf_op jit(solution)/shard_map/ppermute | solution.py:344
  69.1 16.4 %collective-permute-start.20 = (f32[4,256]{1,0:T(4,128)S(1)}, f32[4,256]{1,0:T(4,128)S(1)}, u32[]{:S(2)}, u32[]{:S(2)}) collective-permute-start(f32[4,256]{1,0:T(4,128)S(1)} %bitcast.107), channel_id=1, source_target_pairs={{0,2},{1,3},{2,0},{3,1},{4,6},{5,7},{6,4},{7,5},{8,10},{9,11},{10,... | collective-permute-start | bytes 12296 | tf_op jit(solution)/shard_map/ppermute | solution.py:338
  74.8 10.8 %collective-permute-start.21 = (f32[4,256]{1,0:T(4,128)S(1)}, f32[4,256]{1,0:T(4,128)S(1)}, u32[]{:S(2)}, u32[]{:S(2)}) collective-permute-start(f32[4,256]{1,0:T(4,128)S(1)} %bitcast.108), channel_id=1, source_target_pairs={{0,3},{1,2},{2,1},{3,0},{4,7},{5,6},{6,5},{7,4},{8,11},{9,10},{10,... | collective-permute-start | bytes 12296 | tf_op jit(solution)/shard_map/ppermute | solution.py:338
  81.1 5.7 %collective-permute-start.26 = (bf16[128,256]{1,0:T(8,128)(2,1)S(1)}, bf16[128,256]{1,0:T(8,128)(2,1)S(1)}, u32[]{:S(2)}, u32[]{:S(2)}) collective-permute-start(bf16[128,256]{1,0:T(8,128)(2,1)S(1)} %get-tuple-element.135), channel_id=1, source_target_pairs={{0,8},{4,12},{8,0},{12,4},{16,24},{20,28},{24,16},{28,20},{1,9},{5... | collective-permute-start | bytes 196616 | tf_op jit(solution)/shard_map/ppermute | solution.py:338
  82.1 7.0 %collective-permute-start.27 = (bf16[128,256]{1,0:T(8,128)(2,1)S(1)}, bf16[128,256]{1,0:T(8,128)(2,1)S(1)}, u32[]{:S(2)}, u32[]{:S(2)}) collective-permute-start(bf16[128,256]{1,0:T(8,128)(2,1)S(1)} %get-tuple-element.137), channel_id=1, source_target_pairs={{0,16},{4,20},{8,24},{12,28},{16,0},{20,4},{24,8},{28,12},{1,17},{... | collective-permute-start | bytes 196616 | tf_op jit(solution)/shard_map/ppermute | solution.py:338
  85.4 6.1 %collective-permute-start.28 = (bf16[128,256]{1,0:T(8,128)(2,1)S(1)}, bf16[128,256]{1,0:T(8,128)(2,1)S(1)}, u32[]{:S(2)}, u32[]{:S(2)}) collective-permute-start(bf16[128,256]{1,0:T(8,128)(2,1)S(1)} %get-tuple-element.136), channel_id=1, source_target_pairs={{0,24},{4,28},{8,16},{12,20},{16,8},{20,12},{24,0},{28,4},{1,25},{... | collective-permute-start | bytes 196616 | tf_op jit(solution)/shard_map/ppermute | solution.py:338

commit v8 on v7

--- a/solution.py
+++ b/solution.py
@@ -12,6 +12,7 @@
 SHIFT = 6
 VMEM_LIMIT = 16 * 1024 * 1024
 WORK = 1<<31
+MUCH = 1 << 35
 ME, CORE, DP, COUNTS = 0, 1, 2, 3
 TARGET, COEF = 0, 1
 F32, BF16 = jnp.float32, jnp.bfloat16
@@ -191,7 +192,7 @@
         all_of(out),
         out,
         (info, proj),
-        flops=1 << 35,
+        flops=MUCH,
     )
 
 
@@ -249,7 +250,7 @@
     )
 
 
-def page_kernel(n_homes, info, bias, table, rank, weight, patches, *refs):
+def page_kernel(n_homes, cut, info, bias, table, rank, weight, patches, *refs):
     *words, loss, x_t, dq = refs
     pps, width = patches.shape[1:]
     cap = words[0].shape[2]
@@ -277,10 +278,13 @@
     for r in range(n_homes):
         picked = jnp.where(slots == rank[0, r : r + 1, :], row_loss[r * cap : (r + 1) * cap], 0.0)
         loss[0, r : r + 1, :] = jnp.sum(picked, axis=0, keepdims=True)
-    x_t[...] = x.T
-
-
-def run_pages(info, weight, patches, table, words, first_page):
+    t = x.T
+    for part in range(width // cut):
+        to = part % 2 * (width // 2) + part // 2 * cut
+        x_t[to : to + cut] = t[part * cut : (part + 1) * cut]
+
+
+def run_pages(cut, info, weight, patches, table, words, first_page):
     _, n_pages, cap, width = words[0][0].shape
     wdev = table[2].shape[2]
     n_homes = len(words)
@@ -292,7 +296,7 @@
     ]
     inputs = (*table, weight, patches)
     return call(
-        functools.partial(page_kernel, n_homes),
+        functools.partial(page_kernel, n_homes, cut),
         n_pages,
         [page_of(a, first_page) for a in inputs]
         + [pl.BlockSpec((1, 1, cap, width), lambda p, info, i=i: (i, p, 0, 0)) for _, i in words],
@@ -314,22 +318,31 @@
     out[0] = got.astype(out.dtype)
 
 
-def gradient(info, other, dtype, n_y, pairs, before=()):
+def gradient(info, dtype, n_y, pairs, cores, half=None, before=(), flops=0):
     width = pairs[0][0].shape[0]
     wcol = width // (2 * n_y)
-    out = jax.ShapeDtypeStruct((n_y, width, wcol), dtype)
-    column = lambda y, info: (0, 2 * y + jnp.bitwise_xor(info[CORE], other))
+    rows, at = (width, 0) if half is None else (width // 2, half)
+    out = jax.ShapeDtypeStruct((len(cores) * n_y, rows, wcol), dtype)
+
+    def column(i, info):
+        core = cores[0] if len(cores) == 1 else jnp.where(i < n_y, cores[0], cores[1])
+        return 0, 2 * (i % n_y) + jnp.bitwise_xor(info[CORE], core)
+
     specs = []
     for x_t, dq in pairs:
-        specs += [all_of(x_t), pl.BlockSpec((dq.shape[0], wcol), column)]
+        specs.append(pl.BlockSpec((rows, x_t.shape[1]), lambda i, info: (at, 0)))
+        specs.append(pl.BlockSpec((dq.shape[0], wcol), column))
+    if before:
+        total, first = before
+        specs.append(pl.BlockSpec((1, rows, wcol), lambda i, info: (first + i, at, 0)))
     return call(
         functools.partial(gradient_kernel, len(pairs)),
-        n_y,
-        specs + [page_of(b) for b in before],
+        len(cores) * n_y,
+        specs,
         page_of(out),
         out,
-        (info, *(x for pair in pairs for x in pair), *before),
-        flops=64 * width * width * sum(dq.shape[0] for _, dq in pairs) if before else 0,
+        (info, *(x for pair in pairs for x in pair), *before[:1]),
+        flops=flops,
     )
 
 
@@ -418,38 +431,46 @@
     late += [exchange(piece, "seq", 1) for piece in late]
     rest = [exchange(rows, "seq", r) for rows, r in zip(rest, far)]
     weight = weights(info, patches, late, late_offsets, [weight])
-    run = functools.partial(run_pages, info, weight, patches)
+    run = functools.partial(run_pages, shard_rows // 2, info, weight, patches)
     loss, *pair_near = run(table_near, [(stay, 0), (across, 0)], 0)
-    word_loss = [loss[:, 0], exchange(loss[:, 1], "seq", 1)]
+    near_loss = loss[:, 0] + exchange(loss[:, 1], "seq", 1)
 
     both, meta_far, pair_near = lax.optimization_barrier((both, meta_far, pair_near))
     first = [pair for rows in both for pair in ((rows, 0), (exchange(rows, "seq", 1), 1))]
-    before = [gradient(info, other, F32, n_y, [pair_near]) for other in range(2)]
+    before = gradient(info, F32, n_y, [pair_near], (1, 0))
     info, before = lax.optimization_barrier((info, before))
     table_far = tables(info, meta_far, flags, far, cap, pps)
     loss_a, *pair_a = run(table_far, first, 0)
-    rest, pair_a = lax.optimization_barrier((rest, pair_a))
+    rest, pair_a, near_loss = lax.optimization_barrier((rest, pair_a, near_loss))
     loss_b, *pair_b = run(table_far, [(rows, 0) for rows in rest], split)
     losses = jnp.concatenate([loss_a, loss_b], axis=0)
-    for i, r in enumerate(far):
-        word_loss.append(exchange(losses[:, i], "seq", r))
-
-    sent = gradient(info, 1, BF16, n_y, [pair_a, pair_b], [before[1]])
-    kept = gradient(info, 0, F32, n_y, [pair_a, pair_b], [before[0]])
-    form = (n_y, n_high, 2, shard_rows, width // n_seq)
-    terms = [kept.reshape(form), exchange(sent, "seq", 1).reshape(form)]
-    part = lambda i, j: sum(
-        pick(t, (own["y"][i], None, own["low"][j])).astype(F32) for t in terms
-    )
-    total = part(0, 0)
-    for i in range(n_y):
-        for j in range(2):
-            if i or j:
-                total = total + exchange_both(part(i, j).astype(BF16), j, 2 * i)
-    grad = pick(total, (own["high"][0],))
-    for k in range(1, n_high):
-        grad = grad + exchange(pick(total, (own["high"][k],)).astype(BF16), "dp", 2 * k)
-    return (sum(word_loss), grad)
+    far_loss = [exchange(losses[:, i], "seq", r) for i, r in enumerate(far)]
+
+    form = (n_y, n_high, 2, shard_rows // 2, width // n_seq)
+    pairs = [pair_a, pair_b]
+    grads = []
+    for half in range(2):
+        sent = gradient(info, BF16, n_y, pairs, (1,), half, (before, 0), half * MUCH)
+        info, sent = lax.optimization_barrier((info, sent))
+        if half:
+            far_loss, sent = lax.optimization_barrier((far_loss, sent))
+        kept = gradient(info, F32, n_y, pairs, (0,), half, (before, n_y), MUCH)
+        terms = [kept.reshape(form), exchange(sent, "seq", 1).reshape(form)]
+        parts = {
+            (i, j): sum(pick(t, (own["y"][i], None, own["low"][j])).astype(F32) for t in terms)
+            for i in range(n_y)
+            for j in range(2)
+        }
+        leaving = {key: part.astype(BF16) for key, part in parts.items() if key != (0, 0)}
+        info, leaving = lax.optimization_barrier((info, leaving))
+        total = parts[0, 0]
+        for (i, j), part in leaving.items():
+            total = total + exchange_both(part, j, 2 * i)
+        grad = pick(total, (own["high"][0],))
+        for k in range(1, n_high):
+            grad = grad + exchange(pick(total, (own["high"][k],)).astype(BF16), "dp", 2 * k)
+        grads.append(grad)
+    return (near_loss + sum(far_loss), jnp.concatenate(grads, axis=0))
 
 
 def solution(mesh):

time: 92.4 us -> 98.5 us (1.066)
  starting transfers between devices: 25 us -> 33.6 us
  waiting for transfers between devices: 23.6 us -> 20.4 us
  Pallas kernels: 36.6 us -> 38.4 us
    ppermute x3 -> x6, waiting for transfers between devices: 10.9 us -> 2.21 us  [exchange_both(): lax.ppermute(x, ('dp', 'seq'), [(i, i ^ dp * n_seq + seq) for i in range(...]
    ppermute x26 -> x30, waiting for transfers between devices: 12.7 us -> 18.2 us  [exchange(): return lax.ppermute(x, axis, [(i, i ^ offset) for i in range(n)])]
    ppermute x26 -> x30, starting transfers between devices: 21.4 us -> 26.5 us  [exchange(): return lax.ppermute(x, axis, [(i, i ^ offset) for i in range(n)])]
    ppermute x3 -> x6, starting transfers between devices: 3.55 us -> 7.11 us  [exchange_both(): lax.ppermute(x, ('dp', 'seq'), [(i, i ^ dp * n_seq + seq) for i in range(...]
    pallas_call x14 -> x15, Pallas kernels: 36.6 us -> 38.4 us  [call(): pl.pallas_call(kernel, grid_spec=pltpu.PrefetchScalarGridSpec(num_scalar_...]
    unnamed x21 -> x17, local copies, waits for them, and re-layouts: 2.32 us -> 2.31 us
  transfers between devices with their start and end apart: 29 -> 36, of which waited for: 11 -> 9; matrix products, arithmetic and copies ran while one was open for 3% -> 1% of each run, Pallas kernels for 38% -> 36%
where the time goes in v8:
time: 98.5 us; the launch traced here: 98.3 us
  Pallas kernels  38.4 us (39%)
  starting transfers between devices  33.6 us (34%)
  waiting for transfers between devices  20.4 us (21%)
  other arithmetic  2.51 us (3%)
  local copies, waits for them, and re-layouts  2.39 us (2%)
  between operations  1.03 us (1%)
    pallas_call x15, Pallas kernels, call(): pl.pallas_call(kernel, grid_spec=pltpu.PrefetchScalarGridSpec(num_scalar_...  38.4 us
    ppermute x30, starting transfers between devices, exchange(): return lax.ppermute(x, axis, [(i, i ^ offset) for i in range(n)])  26.5 us
    ppermute x30, waiting for transfers between devices, exchange(): return lax.ppermute(x, axis, [(i, i ^ offset) for i in range(n)])  18.2 us
    ppermute x6, starting transfers between devices, exchange_both(): lax.ppermute(x, ('dp', 'seq'), [(i, i ^ dp * n_seq + seq) for i in range(...  7.11 us
    unnamed x17, local copies, waits for them, and re-layouts  2.31 us
    ppermute x6, waiting for transfers between devices, exchange_both(): lax.ppermute(x, ('dp', 'seq'), [(i, i ^ dp * n_seq + seq) for i in range(...  2.21 us
  transfers between devices with their start and end apart: 36, of which 9 were waited for; matrix products, arithmetic and copies ran while one was open for 1% of the time, Pallas kernels for 36%

profile of v8, /device:TPU:0, one launch (start us, length us, event | category | flops | bytes accessed | tf_op | source)
XLA Modules:
  0.0 98.3 jit_solution(11931656908922030654)
XLA Ops:
  0.6 0.7 pad_add_fusion.2.info
  1.4 1.6 %copy-done.1 = bf16[4,256,1024]{2,1,0:T(8,128)(2,1)S(1)} copy-done((bf16[4,256,1024]{2,1,0:T(8,128)(2,1)S(1)}, bf16[4,256,1024]{2,1,0:T(8,128)(2,1)}, u32[]{:S(2)}) %copy-start.1) | copy-done | bytes 2097176
  3.0 0.7 copy-done.4
  3.7 1.3 %shard_map.86 = bf16[2,3,128,1024]{3,2,1,0:T(8,128)(2,1)S(1)} custom-call(s32[7]{0:T(128)S(1)} %pad_add_fusion.2.info, s32[4,1,256]{2,1,0:T(1,128)S(1)} %bitcast.162, bf16[4,256,1024]{2,1,0:T(8,128)(2,1)S(1)} %copy-done.1), custom_call_target="tpu_custom_call" | custom-call | tf_op jit(solution)/shard_map/pallas_call | solution.py:36
  5.0 3.0 %collective-permute-start.3 = (bf16[2,3,128,1024]{3,2,1,0:T(8,128)(2,1)S(1)}, bf16[2,3,128,1024]{3,2,1,0:T(8,128)(2,1)S(1)}, u32[]{:S(2)}, u32[]{:S(2)}) collective-permute-start(bf16[2,3,128,1024]{3,2,1,0:T(8,128)(2,1)S(1)} %shard_map.86), channel_id=1, source_target_pairs={{0,2},{1,3},{2,0},{3,1},{4,6},{5,7},{6,4},{7,5},{8,10},{9,11},{10,... | collective-permute-start | bytes 4718600 | tf_op jit(solution)/shard_map/ppermute | solution.py:351
  8.6 3.7 %collective-permute-start.8 = (bf16[128,512]{1,0:T(8,128)(2,1)S(1)}, bf16[128,512]{1,0:T(8,128)(2,1)S(1)}, u32[]{:S(2)}, u32[]{:S(2)}) collective-permute-start(bf16[128,512]{1,0:T(8,128)(2,1)S(1)} %shard_map.87), channel_id=1, source_target_pairs={{0,24},{4,28},{8,16},{12,20},{16,8},{20,12},{24,0},{28,4},{1,25},{... | collective-permute-start | bytes 393224 | tf_op jit(solution)/shard_map/ppermute | solution.py:351
  12.2 0.8 collective-permute-start
  13.1 1.5 %shard_map.88 = (bf16[1,4,128,1024]{3,2,1,0:T(8,128)(2,1)S(1)}, bf16[1,4,128,1024]{3,2,1,0:T(8,128)(2,1)S(1)}, bf16[1,1,128,1024]{3,2,1,0:T(8,128)(2,1)S(1)}, bf16[1,1,128,1024]{3,2,1,0:T(8,128)(2,1)S(1)}) custom-call(s32[7]{0:T(128)S(1)} %pad_add_fusion.2.info, s32[4,1,256]{2,1,0:T(1,128)S(1)} %bitcast.164, bf16[4,256,1024]{2,1,0:T(8,128)(2,1)S(1)} %copy-done.2), custom_call_target="tpu_custom_call" | custom-call | flops 2147483648 | tf_op jit(solution)/shard_map/pallas_call | solution.py:36
  14.7 5.7 %collective-permute-done = bf16[128,512]{1,0:T(8,128)(2,1)S(1)} collective-permute-done((bf16[128,512]{1,0:T(8,128)(2,1)S(1)}, bf16[128,512]{1,0:T(8,128)(2,1)S(1)}, u32[]{:S(2)}, u32[]{:S(2)}) %collective-permute-start) | collective-permute-done | bytes 131104 | tf_op jit(solution)/shard_map/ppermute | solution.py:351
  20.4 1.6 %collective-permute-start.6 = (bf16[2,128,512]{2,1,0:T(8,128)(2,1)S(1)}, bf16[2,128,512]{2,1,0:T(8,128)(2,1)S(1)}, u32[]{:S(2)}, u32[]{:S(2)}) collective-permute-start(bf16[2,128,512]{2,1,0:T(8,128)(2,1)S(1)} %pad_maximum_fusion.refs_0_), channel_id=1, source_target_pairs={{0,4},{4,0},{8,12},{12,8},{16,20},{20,16},{24,28},{28,24},{1,5},{5... | collective-permute-start | bytes 786440 | tf_op jit(solution)/shard_map/ppermute | solution.py:351
  22.0 2.9 %shard_map.89 = (bf16[4,256,512]{2,1,0:T(8,128)(2,1)S(1)}, f32[4,256,128]{2,1,0:T(8,128)S(1)}, f32[4,8,256]{2,1,0:T(8,128)S(1)}) custom-call(s32[7]{0:T(128)S(1)} %pad_add_fusion.2.info, s32[2,4,2,256]{3,2,1,0:T(2,128)S(1)} %pad_add_fusion.meta, s32[4,16,32]{2,1,0:T(8,128)S(1)} %copy-done.3), custom_call_target="tpu_custom_call" | custom-call | flops 2147483648 | tf_op jit(solution)/shard_map/pallas_call | solution.py:36
  24.9 4.3 %collective-permute-done.6.refs_1_ = bf16[2,128,512]{2,1,0:T(8,128)(2,1)S(1)} collective-permute-done((bf16[2,128,512]{2,1,0:T(8,128)(2,1)S(1)}, bf16[2,128,512]{2,1,0:T(8,128)(2,1)S(1)}, u32[]{:S(2)}, u32[]{:S(2)}) %collective-permute-start.6) | collective-permute-done | bytes 262176 | tf_op jit(solution)/shard_map/ppermute | solution.py:351
  29.7 1.5 %collective-permute-start.9 = (bf16[1,128,512]{2,1,0:T(8,128)(2,1)S(1)}, bf16[1,128,512]{2,1,0:T(8,128)(2,1)S(1)}, u32[]{:S(2)}, u32[]{:S(2)}) collective-permute-start(bf16[1,128,512]{2,1,0:T(8,128)(2,1)S(1)} %bitcast.158), channel_id=1, source_target_pairs={{0,4},{4,0},{8,12},{12,8},{16,20},{20,16},{24,28},{28,24},{1,5},{5... | collective-permute-start | bytes 393224 | tf_op jit(solution)/shard_map/ppermute | solution.py:351
  31.2 1.4 %collective-permute-start.12 = (bf16[1,128,512]{2,1,0:T(8,128)(2,1)S(1)}, bf16[1,128,512]{2,1,0:T(8,128)(2,1)S(1)}, u32[]{:S(2)}, u32[]{:S(2)}) collective-permute-start(bf16[1,128,512]{2,1,0:T(8,128)(2,1)S(1)} %bitcast.155), channel_id=1, source_target_pairs={{0,4},{4,0},{8,12},{12,8},{16,20},{20,16},{24,28},{28,24},{1,5},{5... | collective-permute-start | bytes 393224 | tf_op jit(solution)/shard_map/ppermute | solution.py:351
  32.6 4.0 %shard_map.90.refs_8_ = bf16[4,1024,512]{2,1,0:T(8,128)(2,1)S(1)} custom-call(s32[7]{0:T(128)S(1)} %pad_add_fusion.2.info, bf16[4,512,1024]{2,1,0:T(8,128)(2,1)S(1)} %copy-done, bf16[2,128,512]{2,1,0:T(8,128)(2,1)S(1)} %pad_maximum_fusion.refs_0_, bf16[2,128,512]{2,1,0:T(8,128)(2,1)S(1)} %collective-permute-done.6.refs_1_, ...), custom_call_target="tpu_custom_call" | custom-call | flops 2147483648 | tf_op jit(solution)/shard_map/pallas_call | solution.py:36
  36.6 1.3 %collective-permute-done.12.refs_3_ = bf16[1,128,512]{2,1,0:T(8,128)(2,1)S(1)} collective-permute-done((bf16[1,128,512]{2,1,0:T(8,128)(2,1)S(1)}, bf16[1,128,512]{2,1,0:T(8,128)(2,1)S(1)}, u32[]{:S(2)}, u32[]{:S(2)}) %collective-permute-start.12) | collective-permute-done | bytes 131104 | tf_op jit(solution)/shard_map/ppermute | solution.py:351
  38.4 0.8 collective-permute-done.13.refs_4_
  40.0 0.7 collective-permute-done.16.refs_7_
  40.6 3.8 %shard_map.91.weight = bf16[4,1024,512]{2,1,0:T(8,128)(2,1)S(1)} custom-call(s32[7]{0:T(128)S(1)} %pad_add_fusion.2.info, bf16[4,512,1024]{2,1,0:T(8,128)(2,1)S(1)} %copy-done, bf16[1,128,512]{2,1,0:T(8,128)(2,1)S(1)} %bitcast.160, bf16[1,128,512]{2,1,0:T(8,128)(2,1)S(1)} %collective-permute-done.9.refs_1_, bf16[1,128,512]{2,1,0:T(8,128)(2,1)S(1)} %bitcast.157, ...), custom_call_target="tpu_custom_call" | custom-call | tf_op jit(solution)/shard_map/pallas_call | solution.py:36
  44.4 5.3 %shard_map.92 = (f32[4,2,256]{2,1,0:T(2,128)S(1)}, bf16[1024,1024]{1,0:T(8,128)(2,1)S(1)}, bf16[1024,1024]{1,0:T(8,128)(2,1)S(1)}) custom-call(s32[7]{0:T(128)S(1)} %pad_add_fusion.2.info, bf16[4,256,512]{2,1,0:T(8,128)(2,1)S(1)} %get-tuple-element.96.bias, f32[4,256,128]{2,1,0:T(8,128)S(1)} %get-tuple-element.97.table, ...), custom_call_target="tpu_custom_call" | custom-call | tf_op jit(solution)/shard_map/pallas_call | solution.py:36
  50.0 0.8 collective-permute-start.1
  50.8 0.9 collective-permute-start.2
  52.1 1.1 %collective-permute-done.19 = f32[4,256]{1,0:T(4,128)S(1)} collective-permute-done((f32[4,256]{1,0:T(4,128)S(1)}, f32[4,256]{1,0:T(4,128)S(1)}, u32[]{:S(2)}, u32[]{:S(2)}) %collective-permute-start.19) | collective-permute-done | bytes 4128 | tf_op jit(solution)/shard_map/ppermute | solution.py:351
  53.3 3.8 %shard_map.93.refs_4_ = f32[4,1024,256]{2,1,0:T(8,128)S(1)} custom-call(s32[7]{0:T(128)S(1)} %pad_add_fusion.2.info, bf16[1024,1024]{1,0:T(8,128)(2,1)S(1)} %get-tuple-element.117.refs_0_, bf16[1024,1024]{1,0:T(8,128)(2,1)S(1)} %get-tuple-element.118.refs_1_), custom_call_target="tpu_custom_call" | custom-call | tf_op jit(solution)/shard_map/pallas_call | solution.py:36
  57.1 2.9 %shard_map.94 = (bf16[4,256,512]{2,1,0:T(8,128)(2,1)S(1)}, f32[4,256,128]{2,1,0:T(8,128)S(1)}, f32[4,8,256]{2,1,0:T(8,128)S(1)}) custom-call(s32[7]{0:T(128)S(1)} %pad_add_fusion.2.info, s32[2,4,2,256]{3,2,1,0:T(2,128)S(1)} %collective-permute-done.5.meta, s32[4,16,32]{2,1,0:T(8,128)S(1)} %copy-done.3), custom_call_target="tpu_custom_call" | custom-call | tf_op jit(solution)/shard_map/pallas_call | solution.py:36
  60.0 4.0 %shard_map.95 = (f32[3,2,256]{2,1,0:T(2,128)S(1)}, bf16[1024,768]{1,0:T(8,128)(2,1)S(1)}, bf16[768,1024]{1,0:T(8,128)(2,1)S(1)}) custom-call(s32[7]{0:T(128)S(1)} %pad_add_fusion.2.info, bf16[4,256,512]{2,1,0:T(8,128)(2,1)S(1)} %get-tuple-element.121.bias, f32[4,256,128]{2,1,0:T(8,128)S(1)} %get-tuple-element.122.table, ...), custom_call_target="tpu_custom_call" | custom-call | tf_op jit(solution)/shard_map/pallas_call | solution.py:36
  64.0 1.6 %shard_map.96 = (f32[1,2,256]{2,1,0:T(2,128)S(1)}, bf16[1024,256]{1,0:T(8,128)(2,1)S(1)}, bf16[256,1024]{1,0:T(8,128)(2,1)S(1)}) custom-call(s32[7]{0:T(128)S(1)} %pad_add_fusion.2.info, bf16[4,256,512]{2,1,0:T(8,128)(2,1)S(1)} %get-tuple-element.121.bias, f32[4,256,128]{2,1,0:T(8,128)S(1)} %get-tuple-element.122.table, ...), custom_call_target="tpu_custom_call" | custom-call | tf_op jit(solution)/shard_map/pallas_call | solution.py:36
  65.7 0.9 collective-permute-start.20
  66.7 0.6 collective-permute-start.21
  67.3 1.7 %shard_map.97 = bf16[2,512,256]{2,1,0:T(8,128)(2,1)S(1)} custom-call(s32[7]{0:T(128)S(1)} %pad_add_fusion.2.info, bf16[1024,768]{1,0:T(8,128)(2,1)S(1)} %get-tuple-element.133.refs_0_, bf16[768,1024]{1,0:T(8,128)(2,1)S(1)} %get-tuple-element.134.refs_1_, bf16[1024,256]{1,0:T(8,128)(2,1)S(1)} %get-tuple-element.135.refs_2_, ...), custom_call_target="tpu_custom_call" | custom-call | tf_op jit(solution)/shard_map/pallas_call | solution.py:36
  69.0 0.7 collective-permute-start.22
  69.7 1.7 %shard_map.98 = f32[2,512,256]{2,1,0:T(8,128)S(1)} custom-call(s32[7]{0:T(128)S(1)} %pad_add_fusion.2.info, bf16[1024,768]{1,0:T(8,128)(2,1)S(1)} %get-tuple-element.133.refs_0_, bf16[768,1024]{1,0:T(8,128)(2,1)S(1)} %get-tuple-element.134.refs_1_, bf16[1024,256]{1,0:T(8,128)(2,1)S(1)} %get-tuple-element.135.refs_2_, ...), custom_call_target="tpu_custom_call" | custom-call | flops 34359738368 | tf_op jit(solution)/shard_map/pallas_call | solution.py:36
  71.5 1.5 %collective-permute-start.23 = (bf16[4,64,256]{2,1,0:T(8,128)(2,1)S(1)}, bf16[4,64,256]{2,1,0:T(8,128)(2,1)S(1)}, u32[]{:S(2)}, u32[]{:S(2)}) collective-permute-start(bf16[4,64,256]{2,1,0:T(8,128)(2,1)S(1)} %get-tuple-element.148), channel_id=1, source_target_pairs={{0,4},{1,5},{2,6},{3,7},{4,0},{5,1},{6,2},{7,3},{8,12},{9,13},{10,... | collective-permute-start | bytes 393224 | tf_op jit(solution)/shard_map/ppermute | solution.py:357
  73.1 0.9 collective-permute-start.24
  73.9 1.1 %collective-permute-start.25 = (bf16[4,64,256]{2,1,0:T(8,128)(2,1)S(1)}, bf16[4,64,256]{2,1,0:T(8,128)(2,1)S(1)}, u32[]{:S(2)}, u32[]{:S(2)}) collective-permute-start(bf16[4,64,256]{2,1,0:T(8,128)(2,1)S(1)} %get-tuple-element.150), channel_id=1, source_target_pairs={{0,6},{1,7},{2,4},{3,5},{4,2},{5,3},{6,0},{7,1},{8,14},{9,15},{10,... | collective-permute-start | bytes 393224 | tf_op jit(solution)/shard_map/ppermute | solution.py:357
  75.1 1.7 %shard_map.99 = bf16[2,512,256]{2,1,0:T(8,128)(2,1)S(1)} custom-call(s32[7]{0:T(128)S(1)} %pad_add_fusion.2.info, bf16[1024,768]{1,0:T(8,128)(2,1)S(1)} %get-tuple-element.133.refs_0_, bf16[768,1024]{1,0:T(8,128)(2,1)S(1)} %get-tuple-element.134.refs_1_, bf16[1024,256]{1,0:T(8,128)(2,1)S(1)} %get-tuple-element.135.refs_2_, ...), custom_call_target="tpu_custom_call" | custom-call | flops 34359738368 | tf_op jit(solution)/shard_map/pallas_call | solution.py:36
  76.9 1.7 %shard_map.100 = f32[2,512,256]{2,1,0:T(8,128)S(1)} custom-call(s32[7]{0:T(128)S(1)} %pad_add_fusion.2.info, bf16[1024,768]{1,0:T(8,128)(2,1)S(1)} %get-tuple-element.133.refs_0_, bf16[768,1024]{1,0:T(8,128)(2,1)S(1)} %get-tuple-element.134.refs_1_, bf16[1024,256]{1,0:T(8,128)(2,1)S(1)} %get-tuple-element.135.refs_2_, ...), custom_call_target="tpu_custom_call" | custom-call | flops 34359738368 | tf_op jit(solution)/shard_map/pallas_call | solution.py:36
  78.6 0.6 add_add_fusion
  79.3 1.5 %collective-permute-start.30 = (bf16[4,64,256]{2,1,0:T(8,128)(2,1)S(1)}, bf16[4,64,256]{2,1,0:T(8,128)(2,1)S(1)}, u32[]{:S(2)}, u32[]{:S(2)}) collective-permute-start(bf16[4,64,256]{2,1,0:T(8,128)(2,1)S(1)} %get-tuple-element.157), channel_id=1, source_target_pairs={{0,4},{1,5},{2,6},{3,7},{4,0},{5,1},{6,2},{7,3},{8,12},{9,13},{10,... | collective-permute-start | bytes 393224 | tf_op jit(solution)/shard_map/ppermute | solution.py:357
  80.8 0.9 collective-permute-start.31
  81.7 1.1 %collective-permute-start.32 = (bf16[4,64,256]{2,1,0:T(8,128)(2,1)S(1)}, bf16[4,64,256]{2,1,0:T(8,128)(2,1)S(1)}, u32[]{:S(2)}, u32[]{:S(2)}) collective-permute-start(bf16[4,64,256]{2,1,0:T(8,128)(2,1)S(1)} %get-tuple-element.159), channel_id=1, source_target_pairs={{0,6},{1,7},{2,4},{3,5},{4,2},{5,3},{6,0},{7,1},{8,14},{9,15},{10,... | collective-permute-start | bytes 393224 | tf_op jit(solution)/shard_map/ppermute | solution.py:357
  83.0 2.5 %collective-permute-start.26 = (bf16[64,256]{1,0:T(8,128)(2,1)S(1)}, bf16[64,256]{1,0:T(8,128)(2,1)S(1)}, u32[]{:S(2)}, u32[]{:S(2)}) collective-permute-start(bf16[64,256]{1,0:T(8,128)(2,1)S(1)} %get-tuple-element.166), channel_id=1, source_target_pairs={{0,8},{4,12},{8,0},{12,4},{16,24},{20,28},{24,16},{28,20},{1,9},{5... | collective-permute-start | bytes 98312 | tf_op jit(solution)/shard_map/ppermute | solution.py:351
  85.8 1.3 %collective-permute-start.27 = (bf16[64,256]{1,0:T(8,128)(2,1)S(1)}, bf16[64,256]{1,0:T(8,128)(2,1)S(1)}, u32[]{:S(2)}, u32[]{:S(2)}) collective-permute-start(bf16[64,256]{1,0:T(8,128)(2,1)S(1)} %get-tuple-element.168), channel_id=1, source_target_pairs={{0,16},{4,20},{8,24},{12,28},{16,0},{20,4},{24,8},{28,12},{1,17},{... | collective-permute-start | bytes 98312 | tf_op jit(solution)/shard_map/ppermute | solution.py:351
  87.1 2.2 %collective-permute-done.31 = bf16[4,64,256]{2,1,0:T(8,128)(2,1)S(1)} collective-permute-done((bf16[4,64,256]{2,1,0:T(8,128)(2,1)S(1)}, bf16[4,64,256]{2,1,0:T(8,128)(2,1)S(1)}, u32[]{:S(2)}, u32[]{:S(2)}) %collective-permute-start.31) | collective-permute-done | bytes 131104 | tf_op jit(solution)/shard_map/ppermute | solution.py:357
  89.4 2.6 %collective-permute-start.33 = (bf16[64,256]{1,0:T(8,128)(2,1)S(1)}, bf16[64,256]{1,0:T(8,128)(2,1)S(1)}, u32[]{:S(2)}, u32[]{:S(2)}) collective-permute-start(bf16[64,256]{1,0:T(8,128)(2,1)S(1)} %get-tuple-element.169), channel_id=1, source_target_pairs={{0,8},{4,12},{8,0},{12,4},{16,24},{20,28},{24,16},{28,20},{1,9},{5... | collective-permute-start | bytes 98312 | tf_op jit(solution)/shard_map/ppermute | solution.py:351
  92.2 1.3 %collective-permute-start.34 = (bf16[64,256]{1,0:T(8,128)(2,1)S(1)}, bf16[64,256]{1,0:T(8,128)(2,1)S(1)}, u32[]{:S(2)}, u32[]{:S(2)}) collective-permute-start(bf16[64,256]{1,0:T(8,128)(2,1)S(1)} %get-tuple-element.171), channel_id=1, source_target_pairs={{0,16},{4,20},{8,24},{12,28},{16,0},{20,4},{24,8},{28,12},{1,17},{... | collective-permute-start | bytes 98312 | tf_op jit(solution)/shard_map/ppermute | solution.py:351
  93.8 3.8 %collective-permute-done.35 = bf16[64,256]{1,0:T(8,128)(2,1)S(1)} collective-permute-done((bf16[64,256]{1,0:T(8,128)(2,1)S(1)}, bf16[64,256]{1,0:T(8,128)(2,1)S(1)}, u32[]{:S(2)}, u32[]{:S(2)}) %collective-permute-start.35) | collective-permute-done | bytes 32800 | tf_op jit(solution)/shard_map/ppermute | solution.py:351
  97.7 0.7 pad_maximum_fusion.1
  (76 shorter events, 4.6 us)
Async XLA Ops:
  1.4 1.6 %copy-start.1 = (bf16[4,256,1024]{2,1,0:T(8,128)(2,1)S(1)}, bf16[4,256,1024]{2,1,0:T(8,128)(2,1)}, u32[]{:S(2)}) copy-start(bf16[4,256,1024]{2,1,0:T(8,128)(2,1)} %words.3) | copy-start | bytes 6291460
  3.0 0.7 copy-start.4
  3.7 4.3 %copy-start.5 = (bf16[128,1024]{1,0:T(8,128)(2,1)S(1)}, bf16[128,1024]{1,0:T(8,128)(2,1)}, u32[]{:S(2)}) copy-start(bf16[128,1024]{1,0:T(8,128)(2,1)} %proj) | copy-start | bytes 786436
  4.9 8.1 %copy-start.6 = (s32[4,256]{1,0:T(4,128)S(1)}, s32[4,256]{1,0:T(4,128)}, u32[]{:S(2)}) copy-start(s32[4,256]{1,0:T(4,128)} %param.11) | copy-start | bytes 12292
  5.0 8.2 %copy-start.2 = (bf16[4,256,1024]{2,1,0:T(8,128)(2,1)S(1)}, bf16[4,256,1024]{2,1,0:T(8,128)(2,1)}, u32[]{:S(2)}) copy-start(bf16[4,256,1024]{2,1,0:T(8,128)(2,1)} %words.3) | copy-start | bytes 6291460
  5.0 44.8 %collective-permute-start.3 = (bf16[2,3,128,1024]{3,2,1,0:T(8,128)(2,1)S(1)}, bf16[2,3,128,1024]{3,2,1,0:T(8,128)(2,1)S(1)}, u32[]{:S(2)}, u32[]{:S(2)}) collective-permute-start(bf16[2,3,128,1024]{3,2,1,0:T(8,128)(2,1)S(1)} %shard_map.86), channel_id=1, source_target_pairs={{0,2},{1,3},{2,0},{3,1},{4,6},{5,7},{6,4},{7,5},{8,10},{9,11},{10,... | collective-permute-start | bytes 4718600 | tf_op jit(solution)/shard_map/ppermute | solution.py:351
  8.6 16.3 %collective-permute-start.8 = (bf16[128,512]{1,0:T(8,128)(2,1)S(1)}, bf16[128,512]{1,0:T(8,128)(2,1)S(1)}, u32[]{:S(2)}, u32[]{:S(2)}) collective-permute-start(bf16[128,512]{1,0:T(8,128)(2,1)S(1)} %shard_map.87), channel_id=1, source_target_pairs={{0,24},{4,28},{8,16},{12,20},{16,8},{20,12},{24,0},{28,4},{1,25},{... | collective-permute-start | bytes 393224 | tf_op jit(solution)/shard_map/ppermute | solution.py:351
  12.2 12.7 %collective-permute-start.7 = (bf16[128,512]{1,0:T(8,128)(2,1)S(1)}, bf16[128,512]{1,0:T(8,128)(2,1)S(1)}, u32[]{:S(2)}, u32[]{:S(2)}) collective-permute-start(bf16[128,512]{1,0:T(8,128)(2,1)S(1)} %shard_map.87), channel_id=1, source_target_pairs={{0,16},{4,20},{8,24},{12,28},{16,0},{20,4},{24,8},{28,12},{1,17},{... | collective-permute-start | bytes 393224 | tf_op jit(solution)/shard_map/ppermute | solution.py:351
  12.2 8.1 %collective-permute-start = (bf16[128,512]{1,0:T(8,128)(2,1)S(1)}, bf16[128,512]{1,0:T(8,128)(2,1)S(1)}, u32[]{:S(2)}, u32[]{:S(2)}) collective-permute-start(bf16[128,512]{1,0:T(8,128)(2,1)S(1)} %shard_map.87), channel_id=1, source_target_pairs={{0,8},{4,12},{8,0},{12,4},{16,24},{20,28},{24,16},{28,20},{1,9},{5... | collective-permute-start | bytes 393224 | tf_op jit(solution)/shard_map/ppermute | solution.py:351
  13.0 8.9 %copy-start.3 = (s32[4,16,32]{2,1,0:T(8,128)S(1)}, s32[4,16,32]{2,1,0:T(8,128)}, u32[]{:S(2)}) copy-start(s32[4,16,32]{2,1,0:T(8,128)} %flags.3) | copy-start | bytes 24580
  13.1 7.4 %collective-permute-start.4 = (s32[4,2,256]{2,1,0:T(2,128)S(1)}, s32[4,2,256]{2,1,0:T(2,128)S(1)}, u32[]{:S(2)}, u32[]{:S(2)}) collective-permute-start(s32[4,2,256]{2,1,0:T(2,128)S(1)} %get-tuple-element.175), channel_id=1, source_target_pairs={{0,1},{1,0},{2,3},{3,2},{4,5},{5,4},{6,7},{7,6},{8,9},{9,8},{10,11... | collective-permute-start | bytes 24584 | tf_op jit(solution)/shard_map/ppermute | solution.py:351
  20.4 24.1 %collective-permute-start.17 = (bf16[1,4,128,1024]{3,2,1,0:T(8,128)(2,1)S(1)}, bf16[1,4,128,1024]{3,2,1,0:T(8,128)(2,1)S(1)}, u32[]{:S(2)}, u32[]{:S(2)}) collective-permute-start(bf16[1,4,128,1024]{3,2,1,0:T(8,128)(2,1)S(1)} %get-tuple-element.114), channel_id=1, source_target_pairs={{0,1},{1,0},{2,3},{3,2},{4,5},{5,4},{6,7},{7,6},{8,9},{9,8},{10,11... | collective-permute-start | bytes 3145736 | tf_op jit(solution)/shard_map/ppermute | solution.py:351
  20.4 8.8 %collective-permute-start.6 = (bf16[2,128,512]{2,1,0:T(8,128)(2,1)S(1)}, bf16[2,128,512]{2,1,0:T(8,128)(2,1)S(1)}, u32[]{:S(2)}, u32[]{:S(2)}) collective-permute-start(bf16[2,128,512]{2,1,0:T(8,128)(2,1)S(1)} %pad_maximum_fusion.refs_0_), channel_id=1, source_target_pairs={{0,4},{4,0},{8,12},{12,8},{16,20},{20,16},{24,28},{28,24},{1,5},{5... | collective-permute-start | bytes 786440 | tf_op jit(solution)/shard_map/ppermute | solution.py:351
  22.0 10.6 %copy-start = (bf16[4,512,1024]{2,1,0:T(8,128)(2,1)S(1)}, bf16[4,512,1024]{2,1,0:T(8,128)(2,1)}, u32[]{:S(2)}) copy-start(bf16[4,512,1024]{2,1,0:T(8,128)(2,1)} %patches.9) | copy-start | bytes 12582916
  29.2 2.0 %collective-permute-start.10 = (bf16[2,128,512]{2,1,0:T(8,128)(2,1)S(1)}, bf16[2,128,512]{2,1,0:T(8,128)(2,1)S(1)}, u32[]{:S(2)}, u32[]{:S(2)}) collective-permute-start(bf16[2,128,512]{2,1,0:T(8,128)(2,1)S(1)} %pad_maximum_fusion.refs_0_), channel_id=1, source_target_pairs={{0,1},{1,0},{2,3},{3,2},{4,5},{5,4},{6,7},{7,6},{8,9},{9,8},{10,11... | collective-permute-start | bytes 786440 | tf_op jit(solution)/shard_map/ppermute | solution.py:351
  29.2 2.0 %collective-permute-start.11 = (bf16[2,128,512]{2,1,0:T(8,128)(2,1)S(1)}, bf16[2,128,512]{2,1,0:T(8,128)(2,1)S(1)}, u32[]{:S(2)}, u32[]{:S(2)}) collective-permute-start(bf16[2,128,512]{2,1,0:T(8,128)(2,1)S(1)} %collective-permute-done.6.refs_1_), channel_id=1, source_target_pairs={{0,1},{1,0},{2,3},{3,2},{4,5},{5,4},{6,7},{7,6},{8,9},{9,8},{10,11... | collective-permute-start | bytes 786440 | tf_op jit(solution)/shard_map/ppermute | solution.py:351
  29.7 6.9 %collective-permute-start.9 = (bf16[1,128,512]{2,1,0:T(8,128)(2,1)S(1)}, bf16[1,128,512]{2,1,0:T(8,128)(2,1)S(1)}, u32[]{:S(2)}, u32[]{:S(2)}) collective-permute-start(bf16[1,128,512]{2,1,0:T(8,128)(2,1)S(1)} %bitcast.158), channel_id=1, source_target_pairs={{0,4},{4,0},{8,12},{12,8},{16,20},{20,16},{24,28},{28,24},{1,5},{5... | collective-permute-start | bytes 393224 | tf_op jit(solution)/shard_map/ppermute | solution.py:351
  31.2 6.7 %collective-permute-start.12 = (bf16[1,128,512]{2,1,0:T(8,128)(2,1)S(1)}, bf16[1,128,512]{2,1,0:T(8,128)(2,1)S(1)}, u32[]{:S(2)}, u32[]{:S(2)}) collective-permute-start(bf16[1,128,512]{2,1,0:T(8,128)(2,1)S(1)} %bitcast.155), channel_id=1, source_target_pairs={{0,4},{4,0},{8,12},{12,8},{16,20},{20,16},{24,28},{28,24},{1,5},{5... | collective-permute-start | bytes 393224 | tf_op jit(solution)/shard_map/ppermute | solution.py:351
  37.9 1.3 %collective-permute-start.13 = (bf16[1,128,512]{2,1,0:T(8,128)(2,1)S(1)}, bf16[1,128,512]{2,1,0:T(8,128)(2,1)S(1)}, u32[]{:S(2)}, u32[]{:S(2)}) collective-permute-start(bf16[1,128,512]{2,1,0:T(8,128)(2,1)S(1)} %bitcast.159), channel_id=1, source_target_pairs={{0,1},{1,0},{2,3},{3,2},{4,5},{5,4},{6,7},{7,6},{8,9},{9,8},{10,11... | collective-permute-start | bytes 393224 | tf_op jit(solution)/shard_map/ppermute | solution.py:351
  37.9 1.5 %collective-permute-start.14 = (bf16[1,128,512]{2,1,0:T(8,128)(2,1)S(1)}, bf16[1,128,512]{2,1,0:T(8,128)(2,1)S(1)}, u32[]{:S(2)}, u32[]{:S(2)}) collective-permute-start(bf16[1,128,512]{2,1,0:T(8,128)(2,1)S(1)} %collective-permute-done.9.refs_1_), channel_id=1, source_target_pairs={{0,1},{1,0},{2,3},{3,2},{4,5},{5,4},{6,7},{7,6},{8,9},{9,8},{10,11... | collective-permute-start | bytes 393224 | tf_op jit(solution)/shard_map/ppermute | solution.py:351
  38.4 1.5 %collective-permute-start.15 = (bf16[1,128,512]{2,1,0:T(8,128)(2,1)S(1)}, bf16[1,128,512]{2,1,0:T(8,128)(2,1)S(1)}, u32[]{:S(2)}, u32[]{:S(2)}) collective-permute-start(bf16[1,128,512]{2,1,0:T(8,128)(2,1)S(1)} %bitcast.156), channel_id=1, source_target_pairs={{0,1},{1,0},{2,3},{3,2},{4,5},{5,4},{6,7},{7,6},{8,9},{9,8},{10,11... | collective-permute-start | bytes 393224 | tf_op jit(solution)/shard_map/ppermute | solution.py:351
  39.3 1.3 %collective-permute-start.16 = (bf16[1,128,512]{2,1,0:T(8,128)(2,1)S(1)}, bf16[1,128,512]{2,1,0:T(8,128)(2,1)S(1)}, u32[]{:S(2)}, u32[]{:S(2)}) collective-permute-start(bf16[1,128,512]{2,1,0:T(8,128)(2,1)S(1)} %collective-permute-done.12.refs_3_), channel_id=1, source_target_pairs={{0,1},{1,0},{2,3},{3,2},{4,5},{5,4},{6,7},{7,6},{8,9},{9,8},{10,11... | collective-permute-start | bytes 393224 | tf_op jit(solution)/shard_map/ppermute | solution.py:351
  39.5 10.3 %collective-permute-start.5 = (s32[2,4,2,256]{3,2,1,0:T(2,128)S(1)}, s32[2,4,2,256]{3,2,1,0:T(2,128)S(1)}, u32[]{:S(2)}, u32[]{:S(2)}) collective-permute-start(s32[2,4,2,256]{3,2,1,0:T(2,128)S(1)} %pad_add_fusion.meta), channel_id=1, source_target_pairs={{0,2},{1,3},{2,0},{3,1},{4,6},{5,7},{6,4},{7,5},{8,10},{9,11},{10,... | collective-permute-start | bytes 49160 | tf_op jit(solution)/shard_map/ppermute | solution.py:351
  49.8 10.2 %collective-permute-start.18 = (bf16[2,3,128,1024]{3,2,1,0:T(8,128)(2,1)S(1)}, bf16[2,3,128,1024]{3,2,1,0:T(8,128)(2,1)S(1)}, u32[]{:S(2)}, u32[]{:S(2)}) collective-permute-start(bf16[2,3,128,1024]{3,2,1,0:T(8,128)(2,1)S(1)} %collective-permute-done.3.refs_0_), channel_id=1, source_target_pairs={{0,1},{1,0},{2,3},{3,2},{4,5},{5,4},{6,7},{7,6},{8,9},{9,8},{10,11... | collective-permute-start | bytes 4718600 | tf_op jit(solution)/shard_map/ppermute | solution.py:351
  50.0 14.0 %collective-permute-start.1 = (bf16[1,1,128,1024]{3,2,1,0:T(8,128)(2,1)S(1)}, bf16[1,1,128,1024]{3,2,1,0:T(8,128)(2,1)S(1)}, u32[]{:S(2)}, u32[]{:S(2)}) collective-permute-start(bf16[1,1,128,1024]{3,2,1,0:T(8,128)(2,1)S(1)} %get-tuple-element.89), channel_id=1, source_target_pairs={{0,2},{1,3},{2,0},{3,1},{4,6},{5,7},{6,4},{7,5},{8,10},{9,11},{10,... | collective-permute-start | bytes 786440 | tf_op jit(solution)/shard_map/ppermute | solution.py:351
  50.8 13.2 %collective-permute-start.2 = (bf16[1,1,128,1024]{3,2,1,0:T(8,128)(2,1)S(1)}, bf16[1,1,128,1024]{3,2,1,0:T(8,128)(2,1)S(1)}, u32[]{:S(2)}, u32[]{:S(2)}) collective-permute-start(bf16[1,1,128,1024]{3,2,1,0:T(8,128)(2,1)S(1)} %get-tuple-element.90), channel_id=1, source_target_pairs={{0,3},{1,2},{2,1},{3,0},{4,7},{5,6},{6,5},{7,4},{8,11},{9,10},{10,... | collective-permute-start | bytes 786440 | tf_op jit(solution)/shard_map/ppermute | solution.py:351
  51.7 1.5 %collective-permute-start.19 = (f32[4,256]{1,0:T(4,128)S(1)}, f32[4,256]{1,0:T(4,128)S(1)}, u32[]{:S(2)}, u32[]{:S(2)}) collective-permute-start(f32[4,256]{1,0:T(4,128)S(1)} %slice_bitcast_fusion), channel_id=1, source_target_pairs={{0,1},{1,0},{2,3},{3,2},{4,5},{5,4},{6,7},{7,6},{8,9},{9,8},{10,11... | collective-permute-start | bytes 12296 | tf_op jit(solution)/shard_map/ppermute | solution.py:351
  65.7 11.0 %collective-permute-start.20 = (f32[4,256]{1,0:T(4,128)S(1)}, f32[4,256]{1,0:T(4,128)S(1)}, u32[]{:S(2)}, u32[]{:S(2)}) collective-permute-start(f32[4,256]{1,0:T(4,128)S(1)} %bitcast.172), channel_id=1, source_target_pairs={{0,2},{1,3},{2,0},{3,1},{4,6},{5,7},{6,4},{7,5},{8,10},{9,11},{10,... | collective-permute-start | bytes 12296 | tf_op jit(solution)/shard_map/ppermute | solution.py:351
  66.7 10.1 %collective-permute-start.21 = (f32[4,256]{1,0:T(4,128)S(1)}, f32[4,256]{1,0:T(4,128)S(1)}, u32[]{:S(2)}, u32[]{:S(2)}) collective-permute-start(f32[4,256]{1,0:T(4,128)S(1)} %bitcast.171), channel_id=1, source_target_pairs={{0,3},{1,2},{2,1},{3,0},{4,7},{5,6},{6,5},{7,4},{8,11},{9,10},{10,... | collective-permute-start | bytes 12296 | tf_op jit(solution)/shard_map/ppermute | solution.py:351
  69.0 2.4 %collective-permute-start.22 = (bf16[2,512,256]{2,1,0:T(8,128)(2,1)S(1)}, bf16[2,512,256]{2,1,0:T(8,128)(2,1)S(1)}, u32[]{:S(2)}, u32[]{:S(2)}) collective-permute-start(bf16[2,512,256]{2,1,0:T(8,128)(2,1)S(1)} %shard_map.97), channel_id=1, source_target_pairs={{0,1},{1,0},{2,3},{3,2},{4,5},{5,4},{6,7},{7,6},{8,9},{9,8},{10,11... | collective-permute-start | bytes 1572872 | tf_op jit(solution)/shard_map/ppermute | solution.py:351
  71.5 10.2 %collective-permute-start.23 = (bf16[4,64,256]{2,1,0:T(8,128)(2,1)S(1)}, bf16[4,64,256]{2,1,0:T(8,128)(2,1)S(1)}, u32[]{:S(2)}, u32[]{:S(2)}) collective-permute-start(bf16[4,64,256]{2,1,0:T(8,128)(2,1)S(1)} %get-tuple-element.148), channel_id=1, source_target_pairs={{0,4},{1,5},{2,6},{3,7},{4,0},{5,1},{6,2},{7,3},{8,12},{9,13},{10,... | collective-permute-start | bytes 393224 | tf_op jit(solution)/shard_map/ppermute | solution.py:357
  73.1 9.8 %collective-permute-start.24 = (bf16[4,64,256]{2,1,0:T(8,128)(2,1)S(1)}, bf16[4,64,256]{2,1,0:T(8,128)(2,1)S(1)}, u32[]{:S(2)}, u32[]{:S(2)}) collective-permute-start(bf16[4,64,256]{2,1,0:T(8,128)(2,1)S(1)} %get-tuple-element.149), channel_id=1, source_target_pairs={{0,2},{1,3},{2,0},{3,1},{4,6},{5,7},{6,4},{7,5},{8,10},{9,11},{10,... | collective-permute-start | bytes 393224 | tf_op jit(solution)/shard_map/ppermute | solution.py:357
  73.9 8.9 %collective-permute-start.25 = (bf16[4,64,256]{2,1,0:T(8,128)(2,1)S(1)}, bf16[4,64,256]{2,1,0:T(8,128)(2,1)S(1)}, u32[]{:S(2)}, u32[]{:S(2)}) collective-permute-start(bf16[4,64,256]{2,1,0:T(8,128)(2,1)S(1)} %get-tuple-element.150), channel_id=1, source_target_pairs={{0,6},{1,7},{2,4},{3,5},{4,2},{5,3},{6,0},{7,1},{8,14},{9,15},{10,... | collective-permute-start | bytes 393224 | tf_op jit(solution)/shard_map/ppermute | solution.py:357
  76.8 2.4 %collective-permute-start.29 = (bf16[2,512,256]{2,1,0:T(8,128)(2,1)S(1)}, bf16[2,512,256]{2,1,0:T(8,128)(2,1)S(1)}, u32[]{:S(2)}, u32[]{:S(2)}) collective-permute-start(bf16[2,512,256]{2,1,0:T(8,128)(2,1)S(1)} %shard_map.99), channel_id=1, source_target_pairs={{0,1},{1,0},{2,3},{3,2},{4,5},{5,4},{6,7},{7,6},{8,9},{9,8},{10,11... | collective-permute-start | bytes 1572872 | tf_op jit(solution)/shard_map/ppermute | solution.py:351
  79.3 6.5 %collective-permute-start.30 = (bf16[4,64,256]{2,1,0:T(8,128)(2,1)S(1)}, bf16[4,64,256]{2,1,0:T(8,128)(2,1)S(1)}, u32[]{:S(2)}, u32[]{:S(2)}) collective-permute-start(bf16[4,64,256]{2,1,0:T(8,128)(2,1)S(1)} %get-tuple-element.157), channel_id=1, source_target_pairs={{0,4},{1,5},{2,6},{3,7},{4,0},{5,1},{6,2},{7,3},{8,12},{9,13},{10,... | collective-permute-start | bytes 393224 | tf_op jit(solution)/shard_map/ppermute | solution.py:357
  80.8 8.4 %collective-permute-start.31 = (bf16[4,64,256]{2,1,0:T(8,128)(2,1)S(1)}, bf16[4,64,256]{2,1,0:T(8,128)(2,1)S(1)}, u32[]{:S(2)}, u32[]{:S(2)}) collective-permute-start(bf16[4,64,256]{2,1,0:T(8,128)(2,1)S(1)} %get-tuple-element.158), channel_id=1, source_target_pairs={{0,2},{1,3},{2,0},{3,1},{4,6},{5,7},{6,4},{7,5},{8,10},{9,11},{10,... | collective-permute-start | bytes 393224 | tf_op jit(solution)/shard_map/ppermute | solution.py:357
  81.7 7.6 %collective-permute-start.32 = (bf16[4,64,256]{2,1,0:T(8,128)(2,1)S(1)}, bf16[4,64,256]{2,1,0:T(8,128)(2,1)S(1)}, u32[]{:S(2)}, u32[]{:S(2)}) collective-permute-start(bf16[4,64,256]{2,1,0:T(8,128)(2,1)S(1)} %get-tuple-element.159), channel_id=1, source_target_pairs={{0,6},{1,7},{2,4},{3,5},{4,2},{5,3},{6,0},{7,1},{8,14},{9,15},{10,... | collective-permute-start | bytes 393224 | tf_op jit(solution)/shard_map/ppermute | solution.py:357
  83.0 9.3 %collective-permute-start.26 = (bf16[64,256]{1,0:T(8,128)(2,1)S(1)}, bf16[64,256]{1,0:T(8,128)(2,1)S(1)}, u32[]{:S(2)}, u32[]{:S(2)}) collective-permute-start(bf16[64,256]{1,0:T(8,128)(2,1)S(1)} %get-tuple-element.166), channel_id=1, source_target_pairs={{0,8},{4,12},{8,0},{12,4},{16,24},{20,28},{24,16},{28,20},{1,9},{5... | collective-permute-start | bytes 98312 | tf_op jit(solution)/shard_map/ppermute | solution.py:351
  85.5 8.0 %collective-permute-start.28 = (bf16[64,256]{1,0:T(8,128)(2,1)S(1)}, bf16[64,256]{1,0:T(8,128)(2,1)S(1)}, u32[]{:S(2)}, u32[]{:S(2)}) collective-permute-start(bf16[64,256]{1,0:T(8,128)(2,1)S(1)} %get-tuple-element.167), channel_id=1, source_target_pairs={{0,24},{4,28},{8,16},{12,20},{16,8},{20,12},{24,0},{28,4},{1,25},{... | collective-permute-start | bytes 98312 | tf_op jit(solution)/shard_map/ppermute | solution.py:351
  85.8 7.7 %collective-permute-start.27 = (bf16[64,256]{1,0:T(8,128)(2,1)S(1)}, bf16[64,256]{1,0:T(8,128)(2,1)S(1)}, u32[]{:S(2)}, u32[]{:S(2)}) collective-permute-start(bf16[64,256]{1,0:T(8,128)(2,1)S(1)} %get-tuple-element.168), channel_id=1, source_target_pairs={{0,16},{4,20},{8,24},{12,28},{16,0},{20,4},{24,8},{28,12},{1,17},{... | collective-permute-start | bytes 98312 | tf_op jit(solution)/shard_map/ppermute | solution.py:351
  89.4 4.4 %collective-permute-start.33 = (bf16[64,256]{1,0:T(8,128)(2,1)S(1)}, bf16[64,256]{1,0:T(8,128)(2,1)S(1)}, u32[]{:S(2)}, u32[]{:S(2)}) collective-permute-start(bf16[64,256]{1,0:T(8,128)(2,1)S(1)} %get-tuple-element.169), channel_id=1, source_target_pairs={{0,8},{4,12},{8,0},{12,4},{16,24},{20,28},{24,16},{28,20},{1,9},{5... | collective-permute-start | bytes 98312 | tf_op jit(solution)/shard_map/ppermute | solution.py:351
  91.9 5.7 %collective-permute-start.35 = (bf16[64,256]{1,0:T(8,128)(2,1)S(1)}, bf16[64,256]{1,0:T(8,128)(2,1)S(1)}, u32[]{:S(2)}, u32[]{:S(2)}) collective-permute-start(bf16[64,256]{1,0:T(8,128)(2,1)S(1)} %get-tuple-element.170), channel_id=1, source_target_pairs={{0,24},{4,28},{8,16},{12,20},{16,8},{20,12},{24,0},{28,4},{1,25},{... | collective-permute-start | bytes 98312 | tf_op jit(solution)/shard_map/ppermute | solution.py:351
  92.2 5.4 %collective-permute-start.34 = (bf16[64,256]{1,0:T(8,128)(2,1)S(1)}, bf16[64,256]{1,0:T(8,128)(2,1)S(1)}, u32[]{:S(2)}, u32[]{:S(2)}) collective-permute-start(bf16[64,256]{1,0:T(8,128)(2,1)S(1)} %get-tuple-element.171), channel_id=1, source_target_pairs={{0,16},{4,20},{8,24},{12,28},{16,0},{20,4},{24,8},{28,12},{1,17},{... | collective-permute-start | bytes 98312 | tf_op jit(solution)/shard_map/ppermute | solution.py:351

commit v9 on v7

--- a/solution.py
+++ b/solution.py
@@ -11,7 +11,8 @@
 MARGIN_BLOCK_SIZE = 64
 SHIFT = 6
 VMEM_LIMIT = 16 * 1024 * 1024
-WORK = 1<<31
+WORK = 1 << 28
+MUCH = 1 << 35
 ME, CORE, DP, COUNTS = 0, 1, 2, 3
 TARGET, COEF = 0, 1
 F32, BF16 = jnp.float32, jnp.bfloat16
@@ -181,17 +182,17 @@
     out[...] = proj[...]
 
 
-def half_of(info, proj):
+def half_of(info, proj, half):
     rows, width = proj.shape
-    out = jax.ShapeDtypeStruct((rows, width // 2), BF16)
+    out = jax.ShapeDtypeStruct((rows, half), BF16)
     return call(
         half_kernel,
         1,
-        [pl.BlockSpec((rows, width // 2), lambda p, info: (0, info[CORE]))],
+        [pl.BlockSpec((rows, half), lambda p, info: (0, info[CORE] if width > half else 0))],
         all_of(out),
         out,
         (info, proj),
-        flops=1 << 35,
+        flops=MUCH,
     )
 
 
@@ -307,14 +308,12 @@
 
 
 def gradient_kernel(n_pairs, info, *refs):
-    pairs, (*before, out) = refs[: 2 * n_pairs], refs[2 * n_pairs :]
-    got = sum(dot(pairs[i][...], pairs[i + 1][...]) for i in range(0, len(pairs), 2))
-    for part in before:
-        got = got + part[0]
+    *pairs, out = refs
+    got = sum(dot(pairs[i][...], pairs[i + 1][...]) for i in range(0, 2 * n_pairs, 2))
     out[0] = got.astype(out.dtype)
 
 
-def gradient(info, other, dtype, n_y, pairs, before=()):
+def gradient(info, other, dtype, n_y, pairs, flops=0):
     width = pairs[0][0].shape[0]
     wcol = width // (2 * n_y)
     out = jax.ShapeDtypeStruct((n_y, width, wcol), dtype)
@@ -325,11 +324,11 @@
     return call(
         functools.partial(gradient_kernel, len(pairs)),
         n_y,
-        specs + [page_of(b) for b in before],
+        specs,
         page_of(out),
         out,
-        (info, *(x for pair in pairs for x in pair), *before),
-        flops=64 * width * width * sum(dq.shape[0] for _, dq in pairs) if before else 0,
+        (info, *(x for pair in pairs for x in pair)),
+        flops=flops,
     )
 
 
@@ -373,15 +372,21 @@
     info, own, proj = lax.optimization_barrier((info, own, proj))
     routes = routes.reshape(pages, 1, wdev)
 
+    pair = jnp.concatenate([routes, targets.reshape(pages, 1, wdev)], axis=1)
+    metas = [pair] + [exchange(pair, "seq", r) for r in range(1, n_seq)]
+    info, metas = lax.optimization_barrier((info, metas))
+    meta_near, meta_far = jnp.stack(metas[:2]), jnp.stack(metas[2:])
+
     split = pages - 1
-    both = dispatch(
-        info, routes, words, [((2 * k, 2 * k + 1), 0, split) for k in range(1, n_y)], cap
-    )
-    info, proj, both = lax.optimization_barrier((info, proj, both))
-    both = [exchange(rows, "seq", 2 * (k + 1)) for k, rows in enumerate(both)]
-    piece = half_of(info, proj)
-    pieces = [piece] + [exchange(piece, "dp", 2 * k) for k in range(1, n_high)]
+    first = dispatch(info, routes, words, [((r,), 0, split) for r in far], cap)
+    info, proj, first = lax.optimization_barrier((info, proj, first))
+    first = [exchange(rows, "seq", r) for rows, r in zip(first, far)]
+
+    piece = half_of(info, proj, width // 2)
+    again = half_of(info, piece, width // 2)
+    pieces = [piece] + [exchange(piece if k == 1 else again, "dp", 2 * k) for k in range(1, n_high)]
     group = n_high // 2
+
     stay, across, *rest = dispatch(
         info,
         routes,
@@ -396,19 +401,15 @@
     early = jnp.stack(pieces[:group])
     early = [early, exchange(early, "dp", 1)]
     late_offsets = [[2 * k + bit] for k in range(group, n_high) for bit in range(2)]
-
-    pair = jnp.concatenate([routes, targets.reshape(pages, 1, wdev)], axis=1)
-    meta_near = jnp.stack([pair, exchange(pair, "seq", 1)])
     table_near = tables(info, meta_near, flags, near, cap, pps, WORK)
-    meta_far = jnp.concatenate([exchange(meta_near, "seq", 2 * k) for k in range(1, n_y)], axis=0)
-
-    early, pieces[group:], table_near = lax.optimization_barrier(
-        (early, pieces[group:], table_near)
+    table_far = tables(info, meta_far, flags, far, cap, pps, WORK)
+    early, pieces[group:], table_near, table_far = lax.optimization_barrier(
+        (early, pieces[group:], table_near, table_far)
     )
     late = [jnp.stack([piece]) for piece in pieces[group:]]
 
     early += [exchange(some, "seq", 1) for some in early]
-    early, late[-1] = lax.optimization_barrier((early, late[-1]))
+    early, late[-1], first[0] = lax.optimization_barrier((early, late[-1], first[0]))
     weight = weights(
         info, patches, early, [[2 * k + bit for k in range(group)] for bit in range(2)], (), WORK
     )
@@ -418,24 +419,20 @@
     late += [exchange(piece, "seq", 1) for piece in late]
     rest = [exchange(rows, "seq", r) for rows, r in zip(rest, far)]
     weight = weights(info, patches, late, late_offsets, [weight])
+
     run = functools.partial(run_pages, info, weight, patches)
     loss, *pair_near = run(table_near, [(stay, 0), (across, 0)], 0)
-    word_loss = [loss[:, 0], exchange(loss[:, 1], "seq", 1)]
-
-    both, meta_far, pair_near = lax.optimization_barrier((both, meta_far, pair_near))
-    first = [pair for rows in both for pair in ((rows, 0), (exchange(rows, "seq", 1), 1))]
-    before = [gradient(info, other, F32, n_y, [pair_near]) for other in range(2)]
-    info, before = lax.optimization_barrier((info, before))
-    table_far = tables(info, meta_far, flags, far, cap, pps)
-    loss_a, *pair_a = run(table_far, first, 0)
-    rest, pair_a = lax.optimization_barrier((rest, pair_a))
+    near_loss = loss[:, 0] + exchange(loss[:, 1], "seq", 1)
+    first, pair_near = lax.optimization_barrier((first, pair_near))
+    loss_a, *pair_a = run(table_far, [(rows, 0) for rows in first], 0)
+    rest, pair_a, near_loss = lax.optimization_barrier((rest, pair_a, near_loss))
     loss_b, *pair_b = run(table_far, [(rows, 0) for rows in rest], split)
     losses = jnp.concatenate([loss_a, loss_b], axis=0)
-    for i, r in enumerate(far):
-        word_loss.append(exchange(losses[:, i], "seq", r))
-
-    sent = gradient(info, 1, BF16, n_y, [pair_a, pair_b], [before[1]])
-    kept = gradient(info, 0, F32, n_y, [pair_a, pair_b], [before[0]])
+    far_loss = [exchange(losses[:, i], "seq", r) for i, r in enumerate(far)]
+
+    pairs = [pair_near, pair_a, pair_b]
+    sent = gradient(info, 1, BF16, n_y, pairs)
+    kept = gradient(info, 0, F32, n_y, pairs, MUCH)
     form = (n_y, n_high, 2, shard_rows, width // n_seq)
     terms = [kept.reshape(form), exchange(sent, "seq", 1).reshape(form)]
     part = lambda i, j: sum(
@@ -449,7 +446,7 @@
     grad = pick(total, (own["high"][0],))
     for k in range(1, n_high):
         grad = grad + exchange(pick(total, (own["high"][k],)).astype(BF16), "dp", 2 * k)
-    return (sum(word_loss), grad)
+    return (near_loss + sum(far_loss), grad)
 
 
 def solution(mesh):

time: 92.4 us -> 95.1 us (1.029)
  starting transfers between devices: 25 us -> 27.6 us
  Pallas kernels: 36.6 us -> 35.3 us
  waiting for transfers between devices: 23.6 us -> 24.7 us
    ppermute x26 -> x27, starting transfers between devices: 21.4 us -> 24.1 us  [exchange(): return lax.ppermute(x, axis, [(i, i ^ offset) for i in range(n)])]
    pallas_call x14 -> x13, Pallas kernels: 36.6 us -> 35.3 us  [call(): pl.pallas_call(kernel, grid_spec=pltpu.PrefetchScalarGridSpec(num_scalar_...]
    ppermute x26 -> x27, waiting for transfers between devices: 12.7 us -> 13.8 us  [exchange(): return lax.ppermute(x, axis, [(i, i ^ offset) for i in range(n)])]
    unnamed x21 -> x15, local copies, waits for them, and re-layouts: 2.32 us -> 2.31 us
  transfers between devices with their start and end apart: 29 -> 30, of which waited for: 11 -> 10; matrix products, arithmetic and copies ran while one was open for 3% -> 2% of each run, Pallas kernels for 38% -> 30%
where the time goes in v9:
time: 95.1 us; the launch traced here: 94.8 us
  Pallas kernels  35.3 us (37%)
  starting transfers between devices  27.6 us (29%)
  waiting for transfers between devices  24.7 us (26%)
  other arithmetic  3.22 us (3%)
  local copies, waits for them, and re-layouts  3.06 us (3%)
    pallas_call x13, Pallas kernels, call(): pl.pallas_call(kernel, grid_spec=pltpu.PrefetchScalarGridSpec(num_scalar_...  35.3 us
    ppermute x27, starting transfers between devices, exchange(): return lax.ppermute(x, axis, [(i, i ^ offset) for i in range(n)])  24.1 us
    ppermute x27, waiting for transfers between devices, exchange(): return lax.ppermute(x, axis, [(i, i ^ offset) for i in range(n)])  13.8 us
    ppermute x3, waiting for transfers between devices, exchange_both(): lax.ppermute(x, ('dp', 'seq'), [(i, i ^ dp * n_seq + seq) for i in range(...  10.9 us
    ppermute x3, starting transfers between devices, exchange_both(): lax.ppermute(x, ('dp', 'seq'), [(i, i ^ dp * n_seq + seq) for i in range(...  3.55 us
    unnamed x15, local copies, waits for them, and re-layouts  2.31 us
  transfers between devices with their start and end apart: 30, of which 10 were waited for; matrix products, arithmetic and copies ran while one was open for 2% of the time, Pallas kernels for 30%

profile of v9, /device:TPU:0, one launch (start us, length us, event | category | flops | bytes accessed | tf_op | source)
XLA Modules:
  0.0 94.8 jit_solution(16230675155866033072)
XLA Ops:
  0.6 0.7 reshape.45
  1.3 0.7 pad_add_fusion.2
  2.0 2.5 %collective-permute-start.2 = (s32[4,2,256]{2,1,0:T(2,128)S(1)}, s32[4,2,256]{2,1,0:T(2,128)S(1)}, u32[]{:S(2)}, u32[]{:S(2)}) collective-permute-start(s32[4,2,256]{2,1,0:T(2,128)S(1)} %pad_add_fusion.2), channel_id=1, source_target_pairs={{0,3},{1,2},{2,1},{3,0},{4,7},{5,6},{6,5},{7,4},{8,11},{9,10},{10,... | collective-permute-start | bytes 24584 | tf_op jit(solution)/shard_map/ppermute | solution.py:337
  4.5 0.6 collective-permute-start.1
  5.2 0.7 pad_add_fusion.3.info
  5.9 2.2 %collective-permute-done.1 = s32[4,2,256]{2,1,0:T(2,128)S(1)} collective-permute-done((s32[4,2,256]{2,1,0:T(2,128)S(1)}, s32[4,2,256]{2,1,0:T(2,128)S(1)}, u32[]{:S(2)}, u32[]{:S(2)}) %collective-permute-start.1) | collective-permute-done | bytes 8224 | tf_op jit(solution)/shard_map/ppermute | solution.py:337
  8.1 1.6 %copy-done.1 = bf16[4,256,1024]{2,1,0:T(8,128)(2,1)S(1)} copy-done((bf16[4,256,1024]{2,1,0:T(8,128)(2,1)S(1)}, bf16[4,256,1024]{2,1,0:T(8,128)(2,1)}, u32[]{:S(2)}) %copy-start.1) | copy-done | bytes 2097176
  9.7 0.7 copy-done.3
  10.4 1.3 %shard_map.86 = (bf16[1,3,128,1024]{3,2,1,0:T(8,128)(2,1)S(1)}, bf16[1,3,128,1024]{3,2,1,0:T(8,128)(2,1)S(1)}) custom-call(s32[7]{0:T(128)S(1)} %pad_add_fusion.3.info, s32[4,1,256]{2,1,0:T(1,128)S(1)} %bitcast.98, bf16[4,256,1024]{2,1,0:T(8,128)(2,1)S(1)} %copy-done.1), custom_call_target="tpu_custom_call" | custom-call | tf_op jit(solution)/shard_map/pallas_call | solution.py:36
  11.7 0.6 shard_map.87.proj
  12.3 1.6 %collective-permute-start.3 = (bf16[128,512]{1,0:T(8,128)(2,1)S(1)}, bf16[128,512]{1,0:T(8,128)(2,1)S(1)}, u32[]{:S(2)}, u32[]{:S(2)}) collective-permute-start(bf16[128,512]{1,0:T(8,128)(2,1)S(1)} %shard_map.87.proj), channel_id=1, source_target_pairs={{0,8},{4,12},{8,0},{12,4},{16,24},{20,28},{24,16},{28,20},{1,9},{5... | collective-permute-start | bytes 393224 | tf_op jit(solution)/shard_map/ppermute | solution.py:337
  14.0 0.6 collective-permute-start.12
  14.6 0.5 shard_map.89
  15.2 2.5 %collective-permute-start.8 = (bf16[128,512]{1,0:T(8,128)(2,1)S(1)}, bf16[128,512]{1,0:T(8,128)(2,1)S(1)}, u32[]{:S(2)}, u32[]{:S(2)}) collective-permute-start(bf16[128,512]{1,0:T(8,128)(2,1)S(1)} %shard_map.89), channel_id=1, source_target_pairs={{0,24},{4,28},{8,16},{12,20},{16,8},{20,12},{24,0},{28,4},{1,25},{... | collective-permute-start | bytes 393224 | tf_op jit(solution)/shard_map/ppermute | solution.py:337
  17.9 1.5 %shard_map.88 = (bf16[1,4,128,1024]{3,2,1,0:T(8,128)(2,1)S(1)}, bf16[1,4,128,1024]{3,2,1,0:T(8,128)(2,1)S(1)}, bf16[1,1,128,1024]{3,2,1,0:T(8,128)(2,1)S(1)}, bf16[1,1,128,1024]{3,2,1,0:T(8,128)(2,1)S(1)}) custom-call(s32[7]{0:T(128)S(1)} %pad_add_fusion.3.info, s32[4,1,256]{2,1,0:T(1,128)S(1)} %bitcast.99, bf16[4,256,1024]{2,1,0:T(8,128)(2,1)S(1)} %copy-done.2), custom_call_target="tpu_custom_call" | custom-call | flops 268435456 | tf_op jit(solution)/shard_map/pallas_call | solution.py:36
  19.5 1.6 %collective-permute-start.6 = (bf16[2,128,512]{2,1,0:T(8,128)(2,1)S(1)}, bf16[2,128,512]{2,1,0:T(8,128)(2,1)S(1)}, u32[]{:S(2)}, u32[]{:S(2)}) collective-permute-start(bf16[2,128,512]{2,1,0:T(8,128)(2,1)S(1)} %pad_maximum_fusion.refs_0_), channel_id=1, source_target_pairs={{0,4},{4,0},{8,12},{12,8},{16,20},{20,16},{24,28},{28,24},{1,5},{5... | collective-permute-start | bytes 786440 | tf_op jit(solution)/shard_map/ppermute | solution.py:337
  21.1 2.9 %shard_map.91 = (bf16[4,256,512]{2,1,0:T(8,128)(2,1)S(1)}, f32[4,256,128]{2,1,0:T(8,128)S(1)}, f32[4,8,256]{2,1,0:T(8,128)S(1)}) custom-call(s32[7]{0:T(128)S(1)} %pad_add_fusion.3.info, s32[2,4,2,256]{3,2,1,0:T(2,128)S(1)} %pad_add_fusion.1.meta, s32[4,16,32]{2,1,0:T(8,128)S(1)} %copy-done.5), custom_call_target="tpu_custom_call" | custom-call | flops 268435456 | tf_op jit(solution)/shard_map/pallas_call | solution.py:36
  24.0 1.3 %collective-permute-start.18 = (bf16[1,3,128,1024]{3,2,1,0:T(8,128)(2,1)S(1)}, bf16[1,3,128,1024]{3,2,1,0:T(8,128)(2,1)S(1)}, u32[]{:S(2)}, u32[]{:S(2)}) collective-permute-start(bf16[1,3,128,1024]{3,2,1,0:T(8,128)(2,1)S(1)} %get-tuple-element.120), channel_id=1, source_target_pairs={{0,3},{1,2},{2,1},{3,0},{4,7},{5,6},{6,5},{7,4},{8,11},{9,10},{10,... | collective-permute-start | bytes 2359304 | tf_op jit(solution)/shard_map/ppermute | solution.py:337
  25.3 2.9 %shard_map.90 = (bf16[4,256,512]{2,1,0:T(8,128)(2,1)S(1)}, f32[4,256,128]{2,1,0:T(8,128)S(1)}, f32[4,8,256]{2,1,0:T(8,128)S(1)}) custom-call(s32[7]{0:T(128)S(1)} %pad_add_fusion.3.info, s32[2,4,2,256]{3,2,1,0:T(2,128)S(1)} %pad_add_fusion.meta, s32[4,16,32]{2,1,0:T(8,128)S(1)} %copy-done.5), custom_call_target="tpu_custom_call" | custom-call | flops 268435456 | tf_op jit(solution)/shard_map/pallas_call | solution.py:36
  28.2 0.6 collective-permute-done.7
  29.4 1.0 %collective-permute-done.10.refs_2_ = bf16[2,128,512]{2,1,0:T(8,128)(2,1)S(1)} collective-permute-done((bf16[2,128,512]{2,1,0:T(8,128)(2,1)S(1)}, bf16[2,128,512]{2,1,0:T(8,128)(2,1)S(1)}, u32[]{:S(2)}, u32[]{:S(2)}) %collective-permute-start.10) | collective-permute-done | bytes 262176 | tf_op jit(solution)/shard_map/ppermute | solution.py:337
  30.4 1.5 %collective-permute-start.9 = (bf16[1,128,512]{2,1,0:T(8,128)(2,1)S(1)}, bf16[1,128,512]{2,1,0:T(8,128)(2,1)S(1)}, u32[]{:S(2)}, u32[]{:S(2)}) collective-permute-start(bf16[1,128,512]{2,1,0:T(8,128)(2,1)S(1)} %bitcast.93), channel_id=1, source_target_pairs={{0,4},{4,0},{8,12},{12,8},{16,20},{20,16},{24,28},{28,24},{1,5},{5... | collective-permute-start | bytes 393224 | tf_op jit(solution)/shard_map/ppermute | solution.py:337
  31.9 2.5 %collective-permute-done.12.refs_0_ = bf16[1,3,128,1024]{3,2,1,0:T(8,128)(2,1)S(1)} collective-permute-done((bf16[1,3,128,1024]{3,2,1,0:T(8,128)(2,1)S(1)}, bf16[1,3,128,1024]{3,2,1,0:T(8,128)(2,1)S(1)}, u32[]{:S(2)}, u32[]{:S(2)}) %collective-permute-start.12) | collective-permute-done | bytes 786464 | tf_op jit(solution)/shard_map/ppermute | solution.py:337
  34.4 1.5 %collective-permute-start.13 = (bf16[1,128,512]{2,1,0:T(8,128)(2,1)S(1)}, bf16[1,128,512]{2,1,0:T(8,128)(2,1)S(1)}, u32[]{:S(2)}, u32[]{:S(2)}) collective-permute-start(bf16[1,128,512]{2,1,0:T(8,128)(2,1)S(1)} %bitcast.90), channel_id=1, source_target_pairs={{0,4},{4,0},{8,12},{12,8},{16,20},{20,16},{24,28},{28,24},{1,5},{5... | collective-permute-start | bytes 393224 | tf_op jit(solution)/shard_map/ppermute | solution.py:337
  35.9 4.0 %shard_map.92.refs_8_ = bf16[4,1024,512]{2,1,0:T(8,128)(2,1)S(1)} custom-call(s32[7]{0:T(128)S(1)} %pad_add_fusion.3.info, bf16[4,512,1024]{2,1,0:T(8,128)(2,1)S(1)} %copy-done, bf16[2,128,512]{2,1,0:T(8,128)(2,1)S(1)} %pad_maximum_fusion.refs_0_, bf16[2,128,512]{2,1,0:T(8,128)(2,1)S(1)} %collective-permute-done.6.refs_1_, ...), custom_call_target="tpu_custom_call" | custom-call | flops 268435456 | tf_op jit(solution)/shard_map/pallas_call | solution.py:36
  40.6 0.8 collective-permute-done.14.refs_4_
  41.5 0.6 collective-permute-start.4
  42.2 1.0 %collective-permute-start.5 = (bf16[1,1,128,1024]{3,2,1,0:T(8,128)(2,1)S(1)}, bf16[1,1,128,1024]{3,2,1,0:T(8,128)(2,1)S(1)}, u32[]{:S(2)}, u32[]{:S(2)}) collective-permute-start(bf16[1,1,128,1024]{3,2,1,0:T(8,128)(2,1)S(1)} %get-tuple-element.89), channel_id=1, source_target_pairs={{0,3},{1,2},{2,1},{3,0},{4,7},{5,6},{6,5},{7,4},{8,11},{9,10},{10,... | collective-permute-start | bytes 786440 | tf_op jit(solution)/shard_map/ppermute | solution.py:337
  43.2 3.8 %shard_map.93.weight = bf16[4,1024,512]{2,1,0:T(8,128)(2,1)S(1)} custom-call(s32[7]{0:T(128)S(1)} %pad_add_fusion.3.info, bf16[4,512,1024]{2,1,0:T(8,128)(2,1)S(1)} %copy-done, bf16[1,128,512]{2,1,0:T(8,128)(2,1)S(1)} %bitcast.95, bf16[1,128,512]{2,1,0:T(8,128)(2,1)S(1)} %collective-permute-done.9.refs_1_, bf16[1,128,512]{2,1,0:T(8,128)(2,1)S(1)} %bitcast.92, ...), custom_call_target="tpu_custom_call" | custom-call | tf_op jit(solution)/shard_map/pallas_call | solution.py:36
  47.0 5.3 %shard_map.94 = (f32[4,2,256]{2,1,0:T(2,128)S(1)}, bf16[1024,1024]{1,0:T(8,128)(2,1)S(1)}, bf16[1024,1024]{1,0:T(8,128)(2,1)S(1)}) custom-call(s32[7]{0:T(128)S(1)} %pad_add_fusion.3.info, bf16[4,256,512]{2,1,0:T(8,128)(2,1)S(1)} %get-tuple-element.121.bias, f32[4,256,128]{2,1,0:T(8,128)S(1)} %get-tuple-element.122.table, ...), custom_call_target="tpu_custom_call" | custom-call | tf_op jit(solution)/shard_map/pallas_call | solution.py:36
  52.3 0.5 collective-permute-start.20
  52.9 4.0 %shard_map.95 = (f32[3,2,256]{2,1,0:T(2,128)S(1)}, bf16[1024,768]{1,0:T(8,128)(2,1)S(1)}, bf16[768,1024]{1,0:T(8,128)(2,1)S(1)}) custom-call(s32[7]{0:T(128)S(1)} %pad_add_fusion.3.info, bf16[4,256,512]{2,1,0:T(8,128)(2,1)S(1)} %get-tuple-element.101.bias, f32[4,256,128]{2,1,0:T(8,128)S(1)} %get-tuple-element.102.table, ...), custom_call_target="tpu_custom_call" | custom-call | tf_op jit(solution)/shard_map/pallas_call | solution.py:36
  56.9 2.0 %collective-permute-done.5.refs_1_ = bf16[1,1,128,1024]{3,2,1,0:T(8,128)(2,1)S(1)} collective-permute-done((bf16[1,1,128,1024]{3,2,1,0:T(8,128)(2,1)S(1)}, bf16[1,1,128,1024]{3,2,1,0:T(8,128)(2,1)S(1)}, u32[]{:S(2)}, u32[]{:S(2)}) %collective-permute-start.5) | collective-permute-done | bytes 262176 | tf_op jit(solution)/shard_map/ppermute | solution.py:337
  58.9 1.6 %shard_map.96 = (f32[1,2,256]{2,1,0:T(2,128)S(1)}, bf16[1024,256]{1,0:T(8,128)(2,1)S(1)}, bf16[256,1024]{1,0:T(8,128)(2,1)S(1)}) custom-call(s32[7]{0:T(128)S(1)} %pad_add_fusion.3.info, bf16[4,256,512]{2,1,0:T(8,128)(2,1)S(1)} %get-tuple-element.101.bias, f32[4,256,128]{2,1,0:T(8,128)S(1)} %get-tuple-element.102.table, ...), custom_call_target="tpu_custom_call" | custom-call | tf_op jit(solution)/shard_map/pallas_call | solution.py:36
  60.6 3.4 %shard_map.98 = bf16[2,1024,256]{2,1,0:T(8,128)(2,1)S(1)} custom-call(s32[7]{0:T(128)S(1)} %pad_add_fusion.3.info, bf16[1024,1024]{1,0:T(8,128)(2,1)S(1)} %get-tuple-element.138.refs_0_, bf16[1024,1024]{1,0:T(8,128)(2,1)S(1)} %get-tuple-element.139.refs_1_, bf16[1024,768]{1,0:T(8,128)(2,1)S(1)} %get-tuple-element.140.refs_2_, ...), custom_call_target="tpu_custom_call" | custom-call | tf_op jit(solution)/shard_map/pallas_call | solution.py:36
  64.0 1.7 %collective-permute-start.23 = (bf16[2,1024,256]{2,1,0:T(8,128)(2,1)S(1)}, bf16[2,1024,256]{2,1,0:T(8,128)(2,1)S(1)}, u32[]{:S(2)}, u32[]{:S(2)}) collective-permute-start(bf16[2,1024,256]{2,1,0:T(8,128)(2,1)S(1)} %shard_map.98), channel_id=1, source_target_pairs={{0,1},{1,0},{2,3},{3,2},{4,5},{5,4},{6,7},{7,6},{8,9},{9,8},{10,11... | collective-permute-start | bytes 3145736 | tf_op jit(solution)/shard_map/ppermute | solution.py:337
  65.7 3.4 %shard_map.97 = f32[2,1024,256]{2,1,0:T(8,128)S(1)} custom-call(s32[7]{0:T(128)S(1)} %pad_add_fusion.3.info, bf16[1024,1024]{1,0:T(8,128)(2,1)S(1)} %get-tuple-element.138.refs_0_, bf16[1024,1024]{1,0:T(8,128)(2,1)S(1)} %get-tuple-element.139.refs_1_, bf16[1024,768]{1,0:T(8,128)(2,1)S(1)} %get-tuple-element.140.refs_2_, ...), custom_call_target="tpu_custom_call" | custom-call | flops 34359738368 | tf_op jit(solution)/shard_map/pallas_call | solution.py:36
  69.4 1.6 %collective-permute-start.24 = (bf16[4,128,256]{2,1,0:T(8,128)(2,1)S(1)}, bf16[4,128,256]{2,1,0:T(8,128)(2,1)S(1)}, u32[]{:S(2)}, u32[]{:S(2)}) collective-permute-start(bf16[4,128,256]{2,1,0:T(8,128)(2,1)S(1)} %get-tuple-element.152), channel_id=1, source_target_pairs={{0,4},{1,5},{2,6},{3,7},{4,0},{5,1},{6,2},{7,3},{8,12},{9,13},{10,... | collective-permute-start | bytes 786440 | tf_op jit(solution)/shard_map/ppermute | solution.py:343
  71.0 0.6 collective-permute-start.25
  71.6 1.3 %collective-permute-start.26 = (bf16[4,128,256]{2,1,0:T(8,128)(2,1)S(1)}, bf16[4,128,256]{2,1,0:T(8,128)(2,1)S(1)}, u32[]{:S(2)}, u32[]{:S(2)}) collective-permute-start(bf16[4,128,256]{2,1,0:T(8,128)(2,1)S(1)} %get-tuple-element.154), channel_id=1, source_target_pairs={{0,6},{1,7},{2,4},{3,5},{4,2},{5,3},{6,0},{7,1},{8,14},{9,15},{10,... | collective-permute-start | bytes 786440 | tf_op jit(solution)/shard_map/ppermute | solution.py:343
  73.0 0.7 collective-permute-start.21
  73.7 4.9 %collective-permute-done.24 = bf16[4,128,256]{2,1,0:T(8,128)(2,1)S(1)} collective-permute-done((bf16[4,128,256]{2,1,0:T(8,128)(2,1)S(1)}, bf16[4,128,256]{2,1,0:T(8,128)(2,1)S(1)}, u32[]{:S(2)}, u32[]{:S(2)}) %collective-permute-start.24) | collective-permute-done | bytes 262176 | tf_op jit(solution)/shard_map/ppermute | solution.py:343
  78.7 6.0 %collective-permute-done.25 = bf16[4,128,256]{2,1,0:T(8,128)(2,1)S(1)} collective-permute-done((bf16[4,128,256]{2,1,0:T(8,128)(2,1)S(1)}, bf16[4,128,256]{2,1,0:T(8,128)(2,1)S(1)}, u32[]{:S(2)}, u32[]{:S(2)}) %collective-permute-start.25) | collective-permute-done | bytes 262176 | tf_op jit(solution)/shard_map/ppermute | solution.py:343
  85.4 3.6 %collective-permute-start.29 = (bf16[128,256]{1,0:T(8,128)(2,1)S(1)}, bf16[128,256]{1,0:T(8,128)(2,1)S(1)}, u32[]{:S(2)}, u32[]{:S(2)}) collective-permute-start(bf16[128,256]{1,0:T(8,128)(2,1)S(1)} %get-tuple-element.156), channel_id=1, source_target_pairs={{0,24},{4,28},{8,16},{12,20},{16,8},{20,12},{24,0},{28,4},{1,25},{... | collective-permute-start | bytes 196616 | tf_op jit(solution)/shard_map/ppermute | solution.py:337
  89.0 0.6 add_add_fusion
  89.6 2.4 %collective-permute-done.29 = bf16[128,256]{1,0:T(8,128)(2,1)S(1)} collective-permute-done((bf16[128,256]{1,0:T(8,128)(2,1)S(1)}, bf16[128,256]{1,0:T(8,128)(2,1)S(1)}, u32[]{:S(2)}, u32[]{:S(2)}) %collective-permute-start.29) | collective-permute-done | bytes 65568 | tf_op jit(solution)/shard_map/ppermute | solution.py:337
  92.0 2.1 %collective-permute-done.28 = bf16[128,256]{1,0:T(8,128)(2,1)S(1)} collective-permute-done((bf16[128,256]{1,0:T(8,128)(2,1)S(1)}, bf16[128,256]{1,0:T(8,128)(2,1)S(1)}, u32[]{:S(2)}, u32[]{:S(2)}) %collective-permute-start.28) | collective-permute-done | bytes 65568 | tf_op jit(solution)/shard_map/ppermute | solution.py:337
  94.2 0.7 fusion.11
  (56 shorter events, 2.9 us)
Async XLA Ops:
  2.0 3.9 %collective-permute-start.2 = (s32[4,2,256]{2,1,0:T(2,128)S(1)}, s32[4,2,256]{2,1,0:T(2,128)S(1)}, u32[]{:S(2)}, u32[]{:S(2)}) collective-permute-start(s32[4,2,256]{2,1,0:T(2,128)S(1)} %pad_add_fusion.2), channel_id=1, source_target_pairs={{0,3},{1,2},{2,1},{3,0},{4,7},{5,6},{6,5},{7,4},{8,11},{9,10},{10,... | collective-permute-start | bytes 24584 | tf_op jit(solution)/shard_map/ppermute | solution.py:337
  4.5 3.7 %collective-permute-start.1 = (s32[4,2,256]{2,1,0:T(2,128)S(1)}, s32[4,2,256]{2,1,0:T(2,128)S(1)}, u32[]{:S(2)}, u32[]{:S(2)}) collective-permute-start(s32[4,2,256]{2,1,0:T(2,128)S(1)} %pad_add_fusion.2), channel_id=1, source_target_pairs={{0,2},{1,3},{2,0},{3,1},{4,6},{5,7},{6,4},{7,5},{8,10},{9,11},{10,... | collective-permute-start | bytes 24584 | tf_op jit(solution)/shard_map/ppermute | solution.py:337
  5.1 3.0 %collective-permute-start = (s32[4,2,256]{2,1,0:T(2,128)S(1)}, s32[4,2,256]{2,1,0:T(2,128)S(1)}, u32[]{:S(2)}, u32[]{:S(2)}) collective-permute-start(s32[4,2,256]{2,1,0:T(2,128)S(1)} %pad_add_fusion.2), channel_id=1, source_target_pairs={{0,1},{1,0},{2,3},{3,2},{4,5},{5,4},{6,7},{7,6},{8,9},{9,8},{10,11... | collective-permute-start | bytes 24584 | tf_op jit(solution)/shard_map/ppermute | solution.py:337
  8.1 1.6 %copy-start.1 = (bf16[4,256,1024]{2,1,0:T(8,128)(2,1)S(1)}, bf16[4,256,1024]{2,1,0:T(8,128)(2,1)}, u32[]{:S(2)}) copy-start(bf16[4,256,1024]{2,1,0:T(8,128)(2,1)} %words.3) | copy-start | bytes 6291460
  9.7 0.7 copy-start.3
  10.4 1.3 %copy-start.4 = (bf16[128,1024]{1,0:T(8,128)(2,1)S(1)}, bf16[128,1024]{1,0:T(8,128)(2,1)}, u32[]{:S(2)}) copy-start(bf16[128,1024]{1,0:T(8,128)(2,1)} %proj) | copy-start | bytes 786436
  12.3 5.6 %copy-start.2 = (bf16[4,256,1024]{2,1,0:T(8,128)(2,1)S(1)}, bf16[4,256,1024]{2,1,0:T(8,128)(2,1)}, u32[]{:S(2)}) copy-start(bf16[4,256,1024]{2,1,0:T(8,128)(2,1)} %words.3) | copy-start | bytes 6291460
  12.3 7.1 %collective-permute-start.3 = (bf16[128,512]{1,0:T(8,128)(2,1)S(1)}, bf16[128,512]{1,0:T(8,128)(2,1)S(1)}, u32[]{:S(2)}, u32[]{:S(2)}) collective-permute-start(bf16[128,512]{1,0:T(8,128)(2,1)S(1)} %shard_map.87.proj), channel_id=1, source_target_pairs={{0,8},{4,12},{8,0},{12,4},{16,24},{20,28},{24,16},{28,20},{1,9},{5... | collective-permute-start | bytes 393224 | tf_op jit(solution)/shard_map/ppermute | solution.py:337
  14.0 20.5 %collective-permute-start.12 = (bf16[1,3,128,1024]{3,2,1,0:T(8,128)(2,1)S(1)}, bf16[1,3,128,1024]{3,2,1,0:T(8,128)(2,1)S(1)}, u32[]{:S(2)}, u32[]{:S(2)}) collective-permute-start(bf16[1,3,128,1024]{3,2,1,0:T(8,128)(2,1)S(1)} %get-tuple-element.108), channel_id=1, source_target_pairs={{0,2},{1,3},{2,0},{3,1},{4,6},{5,7},{6,4},{7,5},{8,10},{9,11},{10,... | collective-permute-start | bytes 2359304 | tf_op jit(solution)/shard_map/ppermute | solution.py:337
  14.6 6.5 %copy-start.5 = (s32[4,16,32]{2,1,0:T(8,128)S(1)}, s32[4,16,32]{2,1,0:T(8,128)}, u32[]{:S(2)}) copy-start(s32[4,16,32]{2,1,0:T(8,128)} %flags.3) | copy-start | bytes 24580
  15.1 20.8 %copy-start = (bf16[4,512,1024]{2,1,0:T(8,128)(2,1)S(1)}, bf16[4,512,1024]{2,1,0:T(8,128)(2,1)}, u32[]{:S(2)}) copy-start(bf16[4,512,1024]{2,1,0:T(8,128)(2,1)} %patches.9) | copy-start | bytes 12582916
  15.2 8.9 %collective-permute-start.8 = (bf16[128,512]{1,0:T(8,128)(2,1)S(1)}, bf16[128,512]{1,0:T(8,128)(2,1)S(1)}, u32[]{:S(2)}, u32[]{:S(2)}) collective-permute-start(bf16[128,512]{1,0:T(8,128)(2,1)S(1)} %shard_map.89), channel_id=1, source_target_pairs={{0,24},{4,28},{8,16},{12,20},{16,8},{20,12},{24,0},{28,4},{1,25},{... | collective-permute-start | bytes 393224 | tf_op jit(solution)/shard_map/ppermute | solution.py:337
  17.7 11.2 %collective-permute-start.7 = (bf16[128,512]{1,0:T(8,128)(2,1)S(1)}, bf16[128,512]{1,0:T(8,128)(2,1)S(1)}, u32[]{:S(2)}, u32[]{:S(2)}) collective-permute-start(bf16[128,512]{1,0:T(8,128)(2,1)S(1)} %shard_map.89), channel_id=1, source_target_pairs={{0,16},{4,20},{8,24},{12,28},{16,0},{20,4},{24,8},{28,12},{1,17},{... | collective-permute-start | bytes 393224 | tf_op jit(solution)/shard_map/ppermute | solution.py:337
  19.4 27.6 %collective-permute-start.19 = (bf16[1,4,128,1024]{3,2,1,0:T(8,128)(2,1)S(1)}, bf16[1,4,128,1024]{3,2,1,0:T(8,128)(2,1)S(1)}, u32[]{:S(2)}, u32[]{:S(2)}) collective-permute-start(bf16[1,4,128,1024]{3,2,1,0:T(8,128)(2,1)S(1)} %get-tuple-element.125), channel_id=1, source_target_pairs={{0,1},{1,0},{2,3},{3,2},{4,5},{5,4},{6,7},{7,6},{8,9},{9,8},{10,11... | collective-permute-start | bytes 3145736 | tf_op jit(solution)/shard_map/ppermute | solution.py:337
  19.5 9.3 %collective-permute-start.6 = (bf16[2,128,512]{2,1,0:T(8,128)(2,1)S(1)}, bf16[2,128,512]{2,1,0:T(8,128)(2,1)S(1)}, u32[]{:S(2)}, u32[]{:S(2)}) collective-permute-start(bf16[2,128,512]{2,1,0:T(8,128)(2,1)S(1)} %pad_maximum_fusion.refs_0_), channel_id=1, source_target_pairs={{0,4},{4,0},{8,12},{12,8},{16,20},{20,16},{24,28},{28,24},{1,5},{5... | collective-permute-start | bytes 786440 | tf_op jit(solution)/shard_map/ppermute | solution.py:337
  24.0 28.3 %collective-permute-start.18 = (bf16[1,3,128,1024]{3,2,1,0:T(8,128)(2,1)S(1)}, bf16[1,3,128,1024]{3,2,1,0:T(8,128)(2,1)S(1)}, u32[]{:S(2)}, u32[]{:S(2)}) collective-permute-start(bf16[1,3,128,1024]{3,2,1,0:T(8,128)(2,1)S(1)} %get-tuple-element.120), channel_id=1, source_target_pairs={{0,3},{1,2},{2,1},{3,0},{4,7},{5,6},{6,5},{7,4},{8,11},{9,10},{10,... | collective-permute-start | bytes 2359304 | tf_op jit(solution)/shard_map/ppermute | solution.py:337
  28.9 1.5 %collective-permute-start.10 = (bf16[2,128,512]{2,1,0:T(8,128)(2,1)S(1)}, bf16[2,128,512]{2,1,0:T(8,128)(2,1)S(1)}, u32[]{:S(2)}, u32[]{:S(2)}) collective-permute-start(bf16[2,128,512]{2,1,0:T(8,128)(2,1)S(1)} %pad_maximum_fusion.refs_0_), channel_id=1, source_target_pairs={{0,1},{1,0},{2,3},{3,2},{4,5},{5,4},{6,7},{7,6},{8,9},{9,8},{10,11... | collective-permute-start | bytes 786440 | tf_op jit(solution)/shard_map/ppermute | solution.py:337
  28.9 3.0 %collective-permute-start.11 = (bf16[2,128,512]{2,1,0:T(8,128)(2,1)S(1)}, bf16[2,128,512]{2,1,0:T(8,128)(2,1)S(1)}, u32[]{:S(2)}, u32[]{:S(2)}) collective-permute-start(bf16[2,128,512]{2,1,0:T(8,128)(2,1)S(1)} %collective-permute-done.6.refs_1_), channel_id=1, source_target_pairs={{0,1},{1,0},{2,3},{3,2},{4,5},{5,4},{6,7},{7,6},{8,9},{9,8},{10,11... | collective-permute-start | bytes 786440 | tf_op jit(solution)/shard_map/ppermute | solution.py:337
  30.4 9.5 %collective-permute-start.9 = (bf16[1,128,512]{2,1,0:T(8,128)(2,1)S(1)}, bf16[1,128,512]{2,1,0:T(8,128)(2,1)S(1)}, u32[]{:S(2)}, u32[]{:S(2)}) collective-permute-start(bf16[1,128,512]{2,1,0:T(8,128)(2,1)S(1)} %bitcast.93), channel_id=1, source_target_pairs={{0,4},{4,0},{8,12},{12,8},{16,20},{20,16},{24,28},{28,24},{1,5},{5... | collective-permute-start | bytes 393224 | tf_op jit(solution)/shard_map/ppermute | solution.py:337
  34.4 5.5 %collective-permute-start.13 = (bf16[1,128,512]{2,1,0:T(8,128)(2,1)S(1)}, bf16[1,128,512]{2,1,0:T(8,128)(2,1)S(1)}, u32[]{:S(2)}, u32[]{:S(2)}) collective-permute-start(bf16[1,128,512]{2,1,0:T(8,128)(2,1)S(1)} %bitcast.90), channel_id=1, source_target_pairs={{0,4},{4,0},{8,12},{12,8},{16,20},{20,16},{24,28},{28,24},{1,5},{5... | collective-permute-start | bytes 393224 | tf_op jit(solution)/shard_map/ppermute | solution.py:337
  39.9 1.4 %collective-permute-start.14 = (bf16[1,128,512]{2,1,0:T(8,128)(2,1)S(1)}, bf16[1,128,512]{2,1,0:T(8,128)(2,1)S(1)}, u32[]{:S(2)}, u32[]{:S(2)}) collective-permute-start(bf16[1,128,512]{2,1,0:T(8,128)(2,1)S(1)} %bitcast.94), channel_id=1, source_target_pairs={{0,1},{1,0},{2,3},{3,2},{4,5},{5,4},{6,7},{7,6},{8,9},{9,8},{10,11... | collective-permute-start | bytes 393224 | tf_op jit(solution)/shard_map/ppermute | solution.py:337
  40.0 1.5 %collective-permute-start.15 = (bf16[1,128,512]{2,1,0:T(8,128)(2,1)S(1)}, bf16[1,128,512]{2,1,0:T(8,128)(2,1)S(1)}, u32[]{:S(2)}, u32[]{:S(2)}) collective-permute-start(bf16[1,128,512]{2,1,0:T(8,128)(2,1)S(1)} %collective-permute-done.9.refs_1_), channel_id=1, source_target_pairs={{0,1},{1,0},{2,3},{3,2},{4,5},{5,4},{6,7},{7,6},{8,9},{9,8},{10,11... | collective-permute-start | bytes 393224 | tf_op jit(solution)/shard_map/ppermute | solution.py:337
  40.5 1.7 %collective-permute-start.16 = (bf16[1,128,512]{2,1,0:T(8,128)(2,1)S(1)}, bf16[1,128,512]{2,1,0:T(8,128)(2,1)S(1)}, u32[]{:S(2)}, u32[]{:S(2)}) collective-permute-start(bf16[1,128,512]{2,1,0:T(8,128)(2,1)S(1)} %bitcast.91), channel_id=1, source_target_pairs={{0,1},{1,0},{2,3},{3,2},{4,5},{5,4},{6,7},{7,6},{8,9},{9,8},{10,11... | collective-permute-start | bytes 393224 | tf_op jit(solution)/shard_map/ppermute | solution.py:337
  41.3 1.9 %collective-permute-start.17 = (bf16[1,128,512]{2,1,0:T(8,128)(2,1)S(1)}, bf16[1,128,512]{2,1,0:T(8,128)(2,1)S(1)}, u32[]{:S(2)}, u32[]{:S(2)}) collective-permute-start(bf16[1,128,512]{2,1,0:T(8,128)(2,1)S(1)} %collective-permute-done.13.refs_3_), channel_id=1, source_target_pairs={{0,1},{1,0},{2,3},{3,2},{4,5},{5,4},{6,7},{7,6},{8,9},{9,8},{10,11... | collective-permute-start | bytes 393224 | tf_op jit(solution)/shard_map/ppermute | solution.py:337
  41.5 15.4 %collective-permute-start.4 = (bf16[1,1,128,1024]{3,2,1,0:T(8,128)(2,1)S(1)}, bf16[1,1,128,1024]{3,2,1,0:T(8,128)(2,1)S(1)}, u32[]{:S(2)}, u32[]{:S(2)}) collective-permute-start(bf16[1,1,128,1024]{3,2,1,0:T(8,128)(2,1)S(1)} %get-tuple-element.88), channel_id=1, source_target_pairs={{0,2},{1,3},{2,0},{3,1},{4,6},{5,7},{6,4},{7,5},{8,10},{9,11},{10,... | collective-permute-start | bytes 786440 | tf_op jit(solution)/shard_map/ppermute | solution.py:337
  42.2 16.8 %collective-permute-start.5 = (bf16[1,1,128,1024]{3,2,1,0:T(8,128)(2,1)S(1)}, bf16[1,1,128,1024]{3,2,1,0:T(8,128)(2,1)S(1)}, u32[]{:S(2)}, u32[]{:S(2)}) collective-permute-start(bf16[1,1,128,1024]{3,2,1,0:T(8,128)(2,1)S(1)} %get-tuple-element.89), channel_id=1, source_target_pairs={{0,3},{1,2},{2,1},{3,0},{4,7},{5,6},{6,5},{7,4},{8,11},{9,10},{10,... | collective-permute-start | bytes 786440 | tf_op jit(solution)/shard_map/ppermute | solution.py:337
  52.3 4.5 %collective-permute-start.20 = (f32[4,256]{1,0:T(4,128)S(1)}, f32[4,256]{1,0:T(4,128)S(1)}, u32[]{:S(2)}, u32[]{:S(2)}) collective-permute-start(f32[4,256]{1,0:T(4,128)S(1)} %slice_bitcast_fusion), channel_id=1, source_target_pairs={{0,1},{1,0},{2,3},{3,2},{4,5},{5,4},{6,7},{7,6},{8,9},{9,8},{10,11... | collective-permute-start | bytes 12296 | tf_op jit(solution)/shard_map/ppermute | solution.py:337
  64.0 5.1 %collective-permute-start.23 = (bf16[2,1024,256]{2,1,0:T(8,128)(2,1)S(1)}, bf16[2,1024,256]{2,1,0:T(8,128)(2,1)S(1)}, u32[]{:S(2)}, u32[]{:S(2)}) collective-permute-start(bf16[2,1024,256]{2,1,0:T(8,128)(2,1)S(1)} %shard_map.98), channel_id=1, source_target_pairs={{0,1},{1,0},{2,3},{3,2},{4,5},{5,4},{6,7},{7,6},{8,9},{9,8},{10,11... | collective-permute-start | bytes 3145736 | tf_op jit(solution)/shard_map/ppermute | solution.py:337
  69.4 9.2 %collective-permute-start.24 = (bf16[4,128,256]{2,1,0:T(8,128)(2,1)S(1)}, bf16[4,128,256]{2,1,0:T(8,128)(2,1)S(1)}, u32[]{:S(2)}, u32[]{:S(2)}) collective-permute-start(bf16[4,128,256]{2,1,0:T(8,128)(2,1)S(1)} %get-tuple-element.152), channel_id=1, source_target_pairs={{0,4},{1,5},{2,6},{3,7},{4,0},{5,1},{6,2},{7,3},{8,12},{9,13},{10,... | collective-permute-start | bytes 786440 | tf_op jit(solution)/shard_map/ppermute | solution.py:343
  71.0 13.7 %collective-permute-start.25 = (bf16[4,128,256]{2,1,0:T(8,128)(2,1)S(1)}, bf16[4,128,256]{2,1,0:T(8,128)(2,1)S(1)}, u32[]{:S(2)}, u32[]{:S(2)}) collective-permute-start(bf16[4,128,256]{2,1,0:T(8,128)(2,1)S(1)} %get-tuple-element.153), channel_id=1, source_target_pairs={{0,2},{1,3},{2,0},{3,1},{4,6},{5,7},{6,4},{7,5},{8,10},{9,11},{10,... | collective-permute-start | bytes 786440 | tf_op jit(solution)/shard_map/ppermute | solution.py:343
  71.6 13.0 %collective-permute-start.26 = (bf16[4,128,256]{2,1,0:T(8,128)(2,1)S(1)}, bf16[4,128,256]{2,1,0:T(8,128)(2,1)S(1)}, u32[]{:S(2)}, u32[]{:S(2)}) collective-permute-start(bf16[4,128,256]{2,1,0:T(8,128)(2,1)S(1)} %get-tuple-element.154), channel_id=1, source_target_pairs={{0,6},{1,7},{2,4},{3,5},{4,2},{5,3},{6,0},{7,1},{8,14},{9,15},{10,... | collective-permute-start | bytes 786440 | tf_op jit(solution)/shard_map/ppermute | solution.py:343
  73.0 16.0 %collective-permute-start.21 = (f32[4,256]{1,0:T(4,128)S(1)}, f32[4,256]{1,0:T(4,128)S(1)}, u32[]{:S(2)}, u32[]{:S(2)}) collective-permute-start(f32[4,256]{1,0:T(4,128)S(1)} %bitcast.108), channel_id=1, source_target_pairs={{0,2},{1,3},{2,0},{3,1},{4,6},{5,7},{6,4},{7,5},{8,10},{9,11},{10,... | collective-permute-start | bytes 12296 | tf_op jit(solution)/shard_map/ppermute | solution.py:337
  73.7 15.3 %collective-permute-start.22 = (f32[4,256]{1,0:T(4,128)S(1)}, f32[4,256]{1,0:T(4,128)S(1)}, u32[]{:S(2)}, u32[]{:S(2)}) collective-permute-start(f32[4,256]{1,0:T(4,128)S(1)} %bitcast.107), channel_id=1, source_target_pairs={{0,3},{1,2},{2,1},{3,0},{4,7},{5,6},{6,5},{7,4},{8,11},{9,10},{10,... | collective-permute-start | bytes 12296 | tf_op jit(solution)/shard_map/ppermute | solution.py:337
  84.9 4.8 %collective-permute-start.27 = (bf16[128,256]{1,0:T(8,128)(2,1)S(1)}, bf16[128,256]{1,0:T(8,128)(2,1)S(1)}, u32[]{:S(2)}, u32[]{:S(2)}) collective-permute-start(bf16[128,256]{1,0:T(8,128)(2,1)S(1)} %get-tuple-element.155), channel_id=1, source_target_pairs={{0,8},{4,12},{8,0},{12,4},{16,24},{20,28},{24,16},{28,20},{1,9},{5... | collective-permute-start | bytes 196616 | tf_op jit(solution)/shard_map/ppermute | solution.py:337
  85.4 6.6 %collective-permute-start.29 = (bf16[128,256]{1,0:T(8,128)(2,1)S(1)}, bf16[128,256]{1,0:T(8,128)(2,1)S(1)}, u32[]{:S(2)}, u32[]{:S(2)}) collective-permute-start(bf16[128,256]{1,0:T(8,128)(2,1)S(1)} %get-tuple-element.156), channel_id=1, source_target_pairs={{0,24},{4,28},{8,16},{12,20},{16,8},{20,12},{24,0},{28,4},{1,25},{... | collective-permute-start | bytes 196616 | tf_op jit(solution)/shard_map/ppermute | solution.py:337
  89.0 5.2 %collective-permute-start.28 = (bf16[128,256]{1,0:T(8,128)(2,1)S(1)}, bf16[128,256]{1,0:T(8,128)(2,1)S(1)}, u32[]{:S(2)}, u32[]{:S(2)}) collective-permute-start(bf16[128,256]{1,0:T(8,128)(2,1)S(1)} %get-tuple-element.157), channel_id=1, source_target_pairs={{0,16},{4,20},{8,24},{12,28},{16,0},{20,4},{24,8},{28,12},{1,17},{... | collective-permute-start | bytes 196616 | tf_op jit(solution)/shard_map/ppermute | solution.py:337

commit v10 on v9

--- a/solution.py
+++ b/solution.py
@@ -11,10 +11,10 @@
 MARGIN_BLOCK_SIZE = 64
 SHIFT = 6
 VMEM_LIMIT = 16 * 1024 * 1024
-WORK = 1 << 28
+WORK = 1 << 30
 MUCH = 1 << 35
 ME, CORE, DP, COUNTS = 0, 1, 2, 3
-TARGET, COEF = 0, 1
+TARGET, COEF, BLOCKS = 0, 1, 2
 F32, BF16 = jnp.float32, jnp.bfloat16
 
 
@@ -63,7 +63,7 @@
 
 
 def stacked(rows):
-    n, width = pad_rows(len(rows)), rows[0].shape[1]
+    n, width = -(-len(rows) // 8) * 8, rows[0].shape[1]
     row = iota((n, width), 0)
     out = jnp.zeros((n, width), rows[0].dtype)
     for i, r in enumerate(rows):
@@ -71,7 +71,9 @@
     return out
 
 
-def dispatch_kernel(plan, cap, info, routes, words, *outs):
+def dispatch_kernel(plan, cap, labels, info, routes, words, *outs):
+    if labels:
+        targets, *outs = outs
     wdev = words.shape[1]
     slots = iota((cap, wdev), 0).astype(F32)
     by_page = {}
@@ -95,53 +97,86 @@
         ]
         rows = dot(jnp.concatenate(picks, axis=0), words[page]).astype(BF16)
         for i, (_, out, place, p) in enumerate(some):
-            out[place, p] = rows[i * cap : (i + 1) * cap]
+            here = rows[i * cap : (i + 1) * cap]
+            if labels:
+                out[place, p * cap : (p + 1) * cap] = here
+            else:
+                out[place, p] = here
         n += len(some)
-
-
-def dispatch(info, routes, words, plan, cap, flops=0):
-    width = words.shape[2]
+    if labels:
+        block = stacked(
+            [
+                part.astype(F32)
+                for page in range(words.shape[0])
+                for part in (routes[page], targets[page] >> 6, targets[page] & 63)
+            ]
+        )
+        block = jnp.concatenate(
+            [block, jnp.zeros((block.shape[0], words.shape[2] - wdev), F32)], axis=1
+        ).astype(BF16)
+        for out in outs:
+            for place in range(out.shape[0]):
+                out[place, out.shape[1] - block.shape[0] :] = block
+
+
+def label_rows(pages):
+    return -(-3 * pages // 16) * 16
+
+
+def dispatch(info, routes, words, plan, cap, targets=None, flops=0):
+    pages, _, width = words.shape
+    labels = targets is not None
     out = [
-        jax.ShapeDtypeStruct((len(offsets), n_pages, cap, width), BF16)
+        jax.ShapeDtypeStruct(
+            (len(offsets), n_pages * cap + label_rows(pages), width)
+            if labels
+            else (len(offsets), n_pages, cap, width),
+            BF16,
+        )
         for offsets, _, n_pages in plan
     ]
+    operands = (routes, words) + ((targets,) if labels else ())
     return call(
-        functools.partial(dispatch_kernel, plan, cap),
+        functools.partial(dispatch_kernel, plan, cap, labels),
         1,
-        [all_of(routes), all_of(words)],
+        [all_of(x) for x in operands],
         [all_of(o) for o in out],
         out,
-        (info, routes, words),
+        (info, *operands),
         flops=flops,
     )
 
 
-def table_kernel(offsets, cap, info, meta, flags, bias, table, rank_out):
+def table_kernel(offsets, cap, own_blk, info, *refs):
+    *labels, flags, table, rank_out = refs
     me = info[ME]
-    n_homes, pages, _, wdev = meta.shape
+    n_homes, pages, wdev = len(offsets), flags.shape[0], rank_out.shape[2]
+    labels = [block[0].astype(F32)[:, :wdev] for block in labels]
+    label = lambda i, p, part: labels[i][3 * p + part : 3 * p + part + 1]
     nblk, all_blk = flags.shape[1:]
-    n_rows, pps = bias.shape[1:]
+    n_rows = table.shape[1]
     slots = iota((cap, wdev), 0).astype(F32)
     rank = ranks(
         stacked(
             [
-                (meta[i, p, 0:1, :] == me).astype(F32)
+                (label(i, p, 0) == me.astype(F32)).astype(F32)
                 for p in range(pages)
                 for i in range(n_homes)
             ]
         )
     )
-    first = me * (pps // MARGIN_BLOCK_SIZE)
-    block = iota((all_blk, pps), 1) >> SHIFT
-    spread = (iota((all_blk, pps), 0) == first + block).astype(BF16)
+    lane = iota((n_rows, 128), 1)
+    own = iota((all_blk, 128), 1) - BLOCKS
+    chosen = (own >= 0) & (own < own_blk) & (iota((all_blk, 128), 0) == me * own_blk + own)
+    chosen = chosen.astype(BF16)
     place = iota((1, wdev), 1) + 1
     for p in range(pages):
         t, idx = [], []
         for i, offset in enumerate(offsets):
             own = rank[p * n_homes + i : p * n_homes + i + 1]
             rank_out[p, i : i + 1] = own
-            target = meta[i, p, 1:2, :]
-            values = stacked([target >> 6, target & 63, place >> 6, place & 63]).astype(F32)
+            values = [label(i, p, 1), label(i, p, 2), place >> 6, place & 63]
+            values = stacked([v.astype(F32) for v in values])
             got = dot((slots == own).astype(BF16), values.astype(BF16), ((1,), (1,)))
             got = got.astype(jnp.int32)
             t.append(got[:, 0:1] * 64 + got[:, 1:2])
@@ -150,30 +185,32 @@
         t, idx = jnp.concatenate(t, axis=0), jnp.concatenate(idx, axis=0)
         word_block = jnp.maximum(idx, 0) >> SHIFT == iota((n_rows, nblk), 1)
         margin = dot(word_block.astype(BF16), flags[p].astype(BF16)).astype(BF16)
-        hit = dot(margin, spread)
-        own = iota((n_rows, pps), 1) >> SHIFT == t >> SHIFT
-        bias[p] = jnp.where((hit > 0.5) | own, 0.0, -jnp.inf).astype(BF16)
+        allowed = (dot(margin, chosen) > 0.5) | (lane - BLOCKS == t >> SHIFT)
         count = info[COUNTS + p]
         valid = (idx >= 0) & (idx < count)
         coef = jnp.where(valid, 64.0 / count.astype(F32), 0.0)
-        lane = iota((n_rows, 128), 1)
-        table[p] = jnp.where(lane == TARGET, t.astype(F32), jnp.where(lane == COEF, coef, 0.0))
-
-
-def tables(info, meta, flags, offsets, cap, pps, flops=0):
-    n_homes, pages, _, wdev = meta.shape
+        value = jnp.where(allowed, 1.0, 0.0)
+        table[p] = jnp.where(lane == TARGET, t.astype(F32), jnp.where(lane == COEF, coef, value))
+
+
+def tables(info, labels, flags, offsets, cap, pps, wdev, flops=0):
+    pages, n_homes = flags.shape[0], len(offsets)
+    rows = label_rows(pages)
     out = [
-        jax.ShapeDtypeStruct((pages, n_homes * cap, pps), BF16),
         jax.ShapeDtypeStruct((pages, n_homes * cap, 128), F32),
         jax.ShapeDtypeStruct((pages, pad_rows(n_homes), wdev), F32),
     ]
+    ends = [
+        pl.BlockSpec((1, rows, x.shape[2]), lambda p, info, at=x.shape[1] // rows - 1: (0, at, 0))
+        for x in labels
+    ]
     return call(
-        functools.partial(table_kernel, offsets, cap),
+        functools.partial(table_kernel, offsets, cap, pps // MARGIN_BLOCK_SIZE),
         1,
-        [all_of(meta), all_of(flags)],
+        ends + [all_of(flags)],
         [all_of(o) for o in out],
         out,
-        (info, meta, flags),
+        (info, *labels, flags),
         flops=flops,
     )
 
@@ -250,17 +287,22 @@
     )
 
 
-def page_kernel(n_homes, info, bias, table, rank, weight, patches, *refs):
-    *words, loss, x_t, dq = refs
+def page_kernel(rows_of_rank, info, weight, patches, *refs):
+    n_homes = len(rows_of_rank)
+    tables, ranks_of, words = (refs[i * n_homes : (i + 1) * n_homes] for i in range(3))
+    loss, x_t, dq = refs[3 * n_homes :]
     pps, width = patches.shape[1:]
-    cap = words[0].shape[2]
+    cap = words[0].shape[1]
     n_rows = n_homes * cap
     scale = 2.0 / math.sqrt(width)
-    x = jnp.concatenate([w[0, 0] for w in words], axis=0)
+    x = jnp.concatenate([w[0] for w in words], axis=0)
     scores = dot(x, weight[0]) * scale
-    is_target = iota((n_rows, pps), 1) == table[0, :, TARGET : TARGET + 1].astype(jnp.int32)
-    coef = table[0, :, COEF : COEF + 1]
-    masked = scores + bias[0].astype(F32)
+    lanes = jnp.concatenate([t[0] for t in tables], axis=0)
+    is_target = iota((n_rows, pps), 1) == lanes[:, TARGET : TARGET + 1].astype(jnp.int32)
+    coef = lanes[:, COEF : COEF + 1]
+    spread = iota((128, pps), 0) - BLOCKS == iota((128, pps), 1) >> SHIFT
+    allowed = dot(jnp.where(iota(lanes.shape, 1) < BLOCKS, 0.0, lanes).astype(BF16), spread.astype(BF16))
+    masked = jnp.where(allowed > 0.5, scores, -jnp.inf)
     top = jnp.max(masked, axis=1, keepdims=True)
     expo = jnp.exp(masked - top)
     total = jnp.sum(expo, axis=1, keepdims=True)
@@ -274,60 +316,79 @@
         back = jnp.concatenate([back, jnp.zeros((more, width), BF16)], axis=0)
         x = jnp.concatenate([x, jnp.zeros((more, width), BF16)], axis=0)
     dq[...] = back
-    slots = iota((cap, rank.shape[2]), 0).astype(F32)
-    for r in range(n_homes):
-        picked = jnp.where(slots == rank[0, r : r + 1, :], row_loss[r * cap : (r + 1) * cap], 0.0)
+    slots = iota((cap, loss.shape[2]), 0).astype(F32)
+    for r, row in enumerate(rows_of_rank):
+        rank = ranks_of[r][0, row : row + 1, :]
+        picked = jnp.where(slots == rank, row_loss[r * cap : (r + 1) * cap], 0.0)
         loss[0, r : r + 1, :] = jnp.sum(picked, axis=0, keepdims=True)
     x_t[...] = x.T
 
 
-def run_pages(info, weight, patches, table, words, first_page):
-    _, n_pages, cap, width = words[0][0].shape
-    wdev = table[2].shape[2]
-    n_homes = len(words)
+def run_pages(info, weight, patches, homes):
+    pages, _, width = patches.shape
+    wdev = homes[0][1][1].shape[2]
+    n_homes = len(homes)
+    cap = homes[0][2][1]
     n_rows = -(-n_homes * cap // 128) * 128
     out = [
-        jax.ShapeDtypeStruct((n_pages, n_homes, wdev), F32),
-        jax.ShapeDtypeStruct((width, n_pages * n_rows), BF16),
-        jax.ShapeDtypeStruct((n_pages * n_rows, width), BF16),
+        jax.ShapeDtypeStruct((pages, n_homes, wdev), F32),
+        jax.ShapeDtypeStruct((width, pages * n_rows), BF16),
+        jax.ShapeDtypeStruct((pages * n_rows, width), BF16),
     ]
-    inputs = (*table, weight, patches)
     return call(
-        functools.partial(page_kernel, n_homes),
-        n_pages,
-        [page_of(a, first_page) for a in inputs]
-        + [pl.BlockSpec((1, 1, cap, width), lambda p, info, i=i: (i, p, 0, 0)) for _, i in words],
+        functools.partial(page_kernel, [at for *_, (at, _) in homes]),
+        pages,
+        [page_of(weight), page_of(patches)]
+        + [pl.BlockSpec((1, cap, 128), lambda p, info, at=at: (p, at, 0)) for *_, (at, _) in homes]
+        + [page_of(table[1]) for _, table, _ in homes]
+        + [pl.BlockSpec((1, cap, width), lambda p, info: (0, p, 0))] * n_homes,
         [
             page_of(out[0]),
             pl.BlockSpec((width, n_rows), lambda p, info: (0, p)),
             pl.BlockSpec((n_rows, width), lambda p, info: (p, 0)),
         ],
         out,
-        (info, *inputs, *(w for w, _ in words)),
+        (
+            info,
+            weight,
+            patches,
+            *(table[0] for _, table, _ in homes),
+            *(table[1] for _, table, _ in homes),
+            *(rows for rows, _, _ in homes),
+        ),
     )
 
 
 def gradient_kernel(n_pairs, info, *refs):
-    *pairs, out = refs
+    pairs, (*before, out) = refs[: 2 * n_pairs], refs[2 * n_pairs :]
     got = sum(dot(pairs[i][...], pairs[i + 1][...]) for i in range(0, 2 * n_pairs, 2))
+    for part in before:
+        got = got + part[0]
     out[0] = got.astype(out.dtype)
 
 
-def gradient(info, other, dtype, n_y, pairs, flops=0):
+def gradient(info, dtype, n_y, pairs, cores, before=(), flops=0):
     width = pairs[0][0].shape[0]
     wcol = width // (2 * n_y)
-    out = jax.ShapeDtypeStruct((n_y, width, wcol), dtype)
-    column = lambda y, info: (0, 2 * y + jnp.bitwise_xor(info[CORE], other))
+    out = jax.ShapeDtypeStruct((len(cores) * n_y, width, wcol), dtype)
+
+    def column(i, info):
+        core = cores[0] if len(cores) == 1 else jnp.where(i < n_y, cores[0], cores[1])
+        return 0, 2 * (i % n_y) + jnp.bitwise_xor(info[CORE], core)
+
     specs = []
     for x_t, dq in pairs:
         specs += [all_of(x_t), pl.BlockSpec((dq.shape[0], wcol), column)]
+    if before:
+        first = before[1]
+        specs.append(pl.BlockSpec((1, width, wcol), lambda i, info: (first + i, 0, 0)))
     return call(
         functools.partial(gradient_kernel, len(pairs)),
-        n_y,
+        len(cores) * n_y,
         specs,
         page_of(out),
         out,
-        (info, *(x for pair in pairs for x in pair)),
+        (info, *(x for pair in pairs for x in pair), *before[:1]),
         flops=flops,
     )
 
@@ -370,69 +431,71 @@
     }
     info = jnp.concatenate([jnp.stack([me, core, my_dp]).astype(jnp.int32), counts])
     info, own, proj = lax.optimization_barrier((info, own, proj))
-    routes = routes.reshape(pages, 1, wdev)
-
-    pair = jnp.concatenate([routes, targets.reshape(pages, 1, wdev)], axis=1)
-    metas = [pair] + [exchange(pair, "seq", r) for r in range(1, n_seq)]
-    info, metas = lax.optimization_barrier((info, metas))
-    meta_near, meta_far = jnp.stack(metas[:2]), jnp.stack(metas[2:])
-
-    split = pages - 1
-    first = dispatch(info, routes, words, [((r,), 0, split) for r in far], cap)
-    info, proj, first = lax.optimization_barrier((info, proj, first))
-    first = [exchange(rows, "seq", r) for rows, r in zip(first, far)]
+    routes, targets = (x.reshape(pages, 1, wdev) for x in (routes, targets))
+
+    even, odd = far[0::2], far[1::2]
+    to_even = dispatch(info, routes, words, [((r,), 0, pages) for r in even], cap, targets)
+    info, proj, to_even = lax.optimization_barrier((info, proj, to_even))
+    from_even = [exchange(rows, "seq", r) for rows, r in zip(to_even, even)]
+    label_of = lambda rows: rows[:, pages * cap :]
+    labels = [label_of(to_even[0]), exchange(label_of(to_even[0]), "seq", 1)]
 
     piece = half_of(info, proj, width // 2)
     again = half_of(info, piece, width // 2)
+    info, again = lax.optimization_barrier((info, again))
     pieces = [piece] + [exchange(piece if k == 1 else again, "dp", 2 * k) for k in range(1, n_high)]
     group = n_high // 2
 
-    stay, across, *rest = dispatch(
-        info,
-        routes,
-        words,
-        [((r,), 0, pages) for r in near] + [((r,), split, pages - split) for r in far],
-        cap,
-        WORK,
-    )
-    pieces[1:group], rest, stay, across = lax.optimization_barrier(
-        (pieces[1:group], rest, stay, across)
-    )
+    stay, across, *to_odd = dispatch(
+        info, routes, words, [((r,), 0, pages) for r in near + odd], cap, flops=WORK
+    )
+    rows_of = lambda x: x.reshape(1, -1, width)
+    pieces[1:group], to_odd, stay, across = lax.optimization_barrier(
+        (pieces[1:group], to_odd, stay, across)
+    )
+    from_odd = [exchange(rows_of(rows), "seq", r) for rows, r in zip(to_odd, odd)]
     early = jnp.stack(pieces[:group])
     early = [early, exchange(early, "dp", 1)]
     late_offsets = [[2 * k + bit] for k in range(group, n_high) for bit in range(2)]
-    table_near = tables(info, meta_near, flags, near, cap, pps, WORK)
-    table_far = tables(info, meta_far, flags, far, cap, pps, WORK)
-    early, pieces[group:], table_near, table_far = lax.optimization_barrier(
-        (early, pieces[group:], table_near, table_far)
+    table_near = tables(info, labels, flags, near, cap, pps, wdev, 4 * WORK)
+    early, pieces[group:], table_near = lax.optimization_barrier(
+        (early, pieces[group:], table_near)
     )
     late = [jnp.stack([piece]) for piece in pieces[group:]]
 
+    late = [x for piece in late for x in (piece, exchange(piece, "dp", 1))]
     early += [exchange(some, "seq", 1) for some in early]
-    early, late[-1], first[0] = lax.optimization_barrier((early, late[-1], first[0]))
-    weight = weights(
-        info, patches, early, [[2 * k + bit for k in range(group)] for bit in range(2)], (), WORK
-    )
-    late = [x for piece in late for x in (piece, exchange(piece, "dp", 1))]
-    late, weight = lax.optimization_barrier((late, weight))
+    late, early, from_even, across = lax.optimization_barrier((late, early, from_even, across))
+    late += [exchange(piece, "seq", 1) for piece in late]
     across = exchange(across, "seq", 1)
-    late += [exchange(piece, "seq", 1) for piece in late]
-    rest = [exchange(rows, "seq", r) for rows, r in zip(rest, far)]
-    weight = weights(info, patches, late, late_offsets, [weight])
+
+    labels = [
+        x
+        for rows in from_even
+        for x in (label_of(rows), exchange(label_of(rows), "seq", 1))
+    ]
+    table_far = tables(info, labels, flags, far, cap, pps, wdev)
+    late, table_far = lax.optimization_barrier((late, table_far))
+    n, m = len(early) // 2, len(late) // 2
+    offsets = [[2 * k + bit for k in range(group)] for bit in range(2)] + late_offsets
+    weight = weights(info, patches, early[:n] + late[:m] + early[n:] + late[m:], offsets)
 
     run = functools.partial(run_pages, info, weight, patches)
-    loss, *pair_near = run(table_near, [(stay, 0), (across, 0)], 0)
-    near_loss = loss[:, 0] + exchange(loss[:, 1], "seq", 1)
-    first, pair_near = lax.optimization_barrier((first, pair_near))
-    loss_a, *pair_a = run(table_far, [(rows, 0) for rows in first], 0)
-    rest, pair_a, near_loss = lax.optimization_barrier((rest, pair_a, near_loss))
-    loss_b, *pair_b = run(table_far, [(rows, 0) for rows in rest], split)
-    losses = jnp.concatenate([loss_a, loss_b], axis=0)
-    far_loss = [exchange(losses[:, i], "seq", r) for i, r in enumerate(far)]
-
-    pairs = [pair_near, pair_a, pair_b]
-    sent = gradient(info, 1, BF16, n_y, pairs)
-    kept = gradient(info, 0, F32, n_y, pairs, MUCH)
+    loss, *pair_first = run(
+        [(rows_of(stay), table_near, (0, cap)), (rows_of(across), table_near, (1, cap))]
+        + [(rows, table_far, (2 * i, cap)) for i, rows in enumerate(from_even)]
+    )
+    word_loss = loss[:, 0] + exchange(loss[:, 1], "seq", 1)
+    for i, r in enumerate(even):
+        word_loss = word_loss + exchange(loss[:, 2 + i], "seq", r)
+    before = gradient(info, F32, n_y, [pair_first], (1, 0))
+    from_odd, before, word_loss = lax.optimization_barrier((from_odd, before, word_loss))
+    loss, *pair_last = run([(rows, table_far, (2 * i + 1, cap)) for i, rows in enumerate(from_odd)])
+    for i, r in enumerate(odd):
+        word_loss = word_loss + exchange(loss[:, i], "seq", r)
+
+    sent = gradient(info, BF16, n_y, [pair_last], (1,), (before, 0))
+    kept = gradient(info, F32, n_y, [pair_last], (0,), (before, n_y), MUCH)
     form = (n_y, n_high, 2, shard_rows, width // n_seq)
     terms = [kept.reshape(form), exchange(sent, "seq", 1).reshape(form)]
     part = lambda i, j: sum(
@@ -446,7 +509,7 @@
     grad = pick(total, (own["high"][0],))
     for k in range(1, n_high):
         grad = grad + exchange(pick(total, (own["high"][k],)).astype(BF16), "dp", 2 * k)
-    return (near_loss + sum(far_loss), grad)
+    return (word_loss, grad)
 
 
 def solution(mesh):

time: 95.1 us -> 95.1 us (level)
  waiting for transfers between devices: 24.7 us -> 29.7 us
  starting transfers between devices: 27.6 us -> 24 us
    ppermute x27 -> x24, waiting for transfers between devices: 13.8 us -> 18 us  [exchange(): return lax.ppermute(x, axis, [(i, i ^ offset) for i in range(n)])]
    ppermute x27 -> x24, starting transfers between devices: 24.1 us -> 20.4 us  [exchange(): return lax.ppermute(x, axis, [(i, i ^ offset) for i in range(n)])]
    pallas_call x13 -> x12, Pallas kernels: 35.3 us -> 34.7 us  [call(): pl.pallas_call(kernel, grid_spec=pltpu.PrefetchScalarGridSpec(num_scalar_...]
  transfers between devices with their start and end apart: 30 -> 27, of which waited for: 10 -> 11; matrix products, arithmetic and copies ran while one was open for 2% -> 1% of each run, Pallas kernels for 30% -> 29%
where the time goes in v10:
time: 95.1 us; the launch traced here: 94.8 us
  Pallas kernels  34.7 us (36%)
  waiting for transfers between devices  29.7 us (31%)
  starting transfers between devices  24 us (25%)
  local copies, waits for them, and re-layouts  3.04 us (3%)
  other arithmetic  2.44 us (3%)
    pallas_call x12, Pallas kernels, call(): pl.pallas_call(kernel, grid_spec=pltpu.PrefetchScalarGridSpec(num_scalar_...  34.7 us
    ppermute x24, starting transfers between devices, exchange(): return lax.ppermute(x, axis, [(i, i ^ offset) for i in range(n)])  20.4 us
    ppermute x24, waiting for transfers between devices, exchange(): return lax.ppermute(x, axis, [(i, i ^ offset) for i in range(n)])  18 us
    ppermute x3, waiting for transfers between devices, exchange_both(): lax.ppermute(x, ('dp', 'seq'), [(i, i ^ dp * n_seq + seq) for i in range(...  11.7 us
    ppermute x3, starting transfers between devices, exchange_both(): lax.ppermute(x, ('dp', 'seq'), [(i, i ^ dp * n_seq + seq) for i in range(...  3.55 us
    unnamed x15, local copies, waits for them, and re-layouts  2.3 us
  transfers between devices with their start and end apart: 27, of which 11 were waited for; matrix products, arithmetic and copies ran while one was open for 1% of the time, Pallas kernels for 29%

profile of v10, /device:TPU:0, one launch (start us, length us, event | category | flops | bytes accessed | tf_op | source)
XLA Modules:
  0.0 94.8 jit_solution(13975468079317691281)
XLA Ops:
  0.6 0.7 pad_add_fusion.info
  1.4 0.7 reshape.54.outs_0_
  2.1 1.6 %copy-done.1 = bf16[4,256,1024]{2,1,0:T(8,128)(2,1)S(1)} copy-done((bf16[4,256,1024]{2,1,0:T(8,128)(2,1)S(1)}, bf16[4,256,1024]{2,1,0:T(8,128)(2,1)}, u32[]{:S(2)}) %copy-start.1) | copy-done | bytes 2097176
  3.7 0.7 copy-done.4
  4.3 1.1 %shard_map.86 = bf16[1,528,1024]{2,1,0:T(8,128)(2,1)S(1)} custom-call(s32[7]{0:T(128)S(1)} %pad_add_fusion.info, s32[4,1,256]{2,1,0:T(1,128)S(1)} %bitcast.99, bf16[4,256,1024]{2,1,0:T(8,128)(2,1)S(1)} %copy-done.1, s32[4,1,256]{2,1,0:T(1,128)S(1)} %reshape.54.outs_0_), custom_call_target="tpu_custom_call" | custom-call | tf_op jit(solution)/shard_map/pallas_call | solution.py:36
  5.5 0.6 shard_map.87.proj
  6.1 3.1 %collective-permute-start = (bf16[128,512]{1,0:T(8,128)(2,1)S(1)}, bf16[128,512]{1,0:T(8,128)(2,1)S(1)}, u32[]{:S(2)}, u32[]{:S(2)}) collective-permute-start(bf16[128,512]{1,0:T(8,128)(2,1)S(1)} %shard_map.87.proj), channel_id=1, source_target_pairs={{0,8},{4,12},{8,0},{12,4},{16,24},{20,28},{24,16},{28,20},{1,9},{5... | collective-permute-start | bytes 393224 | tf_op jit(solution)/shard_map/ppermute | solution.py:398
  9.2 1.5 %collective-permute-start.10 = (bf16[1,528,1024]{2,1,0:T(8,128)(2,1)S(1)}, bf16[1,528,1024]{2,1,0:T(8,128)(2,1)S(1)}, u32[]{:S(2)}, u32[]{:S(2)}) collective-permute-start(bf16[1,528,1024]{2,1,0:T(8,128)(2,1)S(1)} %shard_map.86), channel_id=1, source_target_pairs={{0,2},{1,3},{2,0},{3,1},{4,6},{5,7},{6,4},{7,5},{8,10},{9,11},{10,... | collective-permute-start | bytes 3244040 | tf_op jit(solution)/shard_map/ppermute | solution.py:398
  10.7 0.5 shard_map.88
  11.2 2.7 %collective-permute-start.3 = (bf16[128,512]{1,0:T(8,128)(2,1)S(1)}, bf16[128,512]{1,0:T(8,128)(2,1)S(1)}, u32[]{:S(2)}, u32[]{:S(2)}) collective-permute-start(bf16[128,512]{1,0:T(8,128)(2,1)S(1)} %shard_map.88), channel_id=1, source_target_pairs={{0,16},{4,20},{8,24},{12,28},{16,0},{20,4},{24,8},{28,12},{1,17},{... | collective-permute-start | bytes 393224 | tf_op jit(solution)/shard_map/ppermute | solution.py:398
  14.2 1.7 %shard_map.89 = (bf16[1,4,128,1024]{3,2,1,0:T(8,128)(2,1)S(1)}, bf16[1,4,128,1024]{3,2,1,0:T(8,128)(2,1)S(1)}, bf16[1,4,128,1024]{3,2,1,0:T(8,128)(2,1)S(1)}) custom-call(s32[7]{0:T(128)S(1)} %pad_add_fusion.info, s32[4,1,256]{2,1,0:T(1,128)S(1)} %bitcast.100, bf16[4,256,1024]{2,1,0:T(8,128)(2,1)S(1)} %copy-done.2), custom_call_target="tpu_custom_call" | custom-call | flops 1073741824 | tf_op jit(solution)/shard_map/pallas_call | solution.py:36
  15.9 1.6 %collective-permute-start.2 = (bf16[2,128,512]{2,1,0:T(8,128)(2,1)S(1)}, bf16[2,128,512]{2,1,0:T(8,128)(2,1)S(1)}, u32[]{:S(2)}, u32[]{:S(2)}) collective-permute-start(bf16[2,128,512]{2,1,0:T(8,128)(2,1)S(1)} %pad_maximum_fusion.refs_0_), channel_id=1, source_target_pairs={{0,4},{4,0},{8,12},{12,8},{16,20},{20,16},{24,28},{28,24},{1,5},{5... | collective-permute-start | bytes 786440 | tf_op jit(solution)/shard_map/ppermute | solution.py:398
  17.4 2.6 %shard_map.90 = (f32[4,256,128]{2,1,0:T(8,128)S(1)}, f32[4,8,256]{2,1,0:T(8,128)S(1)}) custom-call(s32[7]{0:T(128)S(1)} %pad_add_fusion.info, bf16[1,16,1024]{2,1,0:T(8,128)(2,1)S(1)} %slice.17.refs_0_, bf16[1,16,1024]{2,1,0:T(8,128)(2,1)S(1)} %collective-permute-done.5.refs_1_, s32[4,16,32]{2,1,0:T(8,128)S(1)} %copy-done.3), custom_call_target="tpu_custom_call" | custom-call | flops 4294967296 | tf_op jit(solution)/shard_map/pallas_call | solution.py:36
  20.0 3.3 %collective-permute-done.3 = bf16[128,512]{1,0:T(8,128)(2,1)S(1)} collective-permute-done((bf16[128,512]{1,0:T(8,128)(2,1)S(1)}, bf16[128,512]{1,0:T(8,128)(2,1)S(1)}, u32[]{:S(2)}, u32[]{:S(2)}) %collective-permute-start.3) | collective-permute-done | bytes 131104 | tf_op jit(solution)/shard_map/ppermute | solution.py:398
  23.3 1.3 %collective-permute-done.2.refs_1_ = bf16[2,128,512]{2,1,0:T(8,128)(2,1)S(1)} collective-permute-done((bf16[2,128,512]{2,1,0:T(8,128)(2,1)S(1)}, bf16[2,128,512]{2,1,0:T(8,128)(2,1)S(1)}, u32[]{:S(2)}, u32[]{:S(2)}) %collective-permute-start.2) | collective-permute-done | bytes 262176 | tf_op jit(solution)/shard_map/ppermute | solution.py:398
  24.6 0.5 collective-permute-start.9
  25.1 1.5 %collective-permute-start.6 = (bf16[1,128,512]{2,1,0:T(8,128)(2,1)S(1)}, bf16[1,128,512]{2,1,0:T(8,128)(2,1)S(1)}, u32[]{:S(2)}, u32[]{:S(2)}) collective-permute-start(bf16[1,128,512]{2,1,0:T(8,128)(2,1)S(1)} %bitcast.92), channel_id=1, source_target_pairs={{0,4},{4,0},{8,12},{12,8},{16,20},{20,16},{24,28},{28,24},{1,5},{5... | collective-permute-start | bytes 393224 | tf_op jit(solution)/shard_map/ppermute | solution.py:398
  26.6 0.5 collective-permute-start.7
  27.2 4.3 %collective-permute-done.6.refs_3_ = bf16[1,128,512]{2,1,0:T(8,128)(2,1)S(1)} collective-permute-done((bf16[1,128,512]{2,1,0:T(8,128)(2,1)S(1)}, bf16[1,128,512]{2,1,0:T(8,128)(2,1)S(1)}, u32[]{:S(2)}, u32[]{:S(2)}) %collective-permute-start.6) | collective-permute-done | bytes 131104 | tf_op jit(solution)/shard_map/ppermute | solution.py:398
  31.5 1.8 %collective-permute-done.7.refs_5_ = bf16[1,128,512]{2,1,0:T(8,128)(2,1)S(1)} collective-permute-done((bf16[1,128,512]{2,1,0:T(8,128)(2,1)S(1)}, bf16[1,128,512]{2,1,0:T(8,128)(2,1)S(1)}, u32[]{:S(2)}, u32[]{:S(2)}) %collective-permute-start.7) | collective-permute-done | bytes 131104 | tf_op jit(solution)/shard_map/ppermute | solution.py:398
  33.4 1.1 %collective-permute-done.10.refs_8_ = bf16[1,528,1024]{2,1,0:T(8,128)(2,1)S(1)} collective-permute-done((bf16[1,528,1024]{2,1,0:T(8,128)(2,1)S(1)}, bf16[1,528,1024]{2,1,0:T(8,128)(2,1)S(1)}, u32[]{:S(2)}, u32[]{:S(2)}) %collective-permute-start.10) | collective-permute-done | bytes 1081376 | tf_op jit(solution)/shard_map/ppermute | solution.py:398
  34.5 1.6 %collective-permute-start.1 = (bf16[1,512,1024]{2,1,0:T(8,128)(2,1)S(1)}, bf16[1,512,1024]{2,1,0:T(8,128)(2,1)S(1)}, u32[]{:S(2)}, u32[]{:S(2)}) collective-permute-start(bf16[1,512,1024]{2,1,0:T(8,128)(2,1)S(1)} %bitcast.101), channel_id=1, source_target_pairs={{0,3},{1,2},{2,1},{3,0},{4,7},{5,6},{6,5},{7,4},{8,11},{9,10},{10,... | collective-permute-start | bytes 3145736 | tf_op jit(solution)/shard_map/ppermute | solution.py:398
  36.1 0.5 collective-permute-start.15
  36.6 0.9 collective-permute-done.15.refs_1_
  37.5 0.3 collective-permute-start.13
  38.0 2.6 %shard_map.91 = (f32[4,256,128]{2,1,0:T(8,128)S(1)}, f32[4,8,256]{2,1,0:T(8,128)S(1)}) custom-call(s32[7]{0:T(128)S(1)} %pad_add_fusion.info, bf16[1,16,1024]{2,1,0:T(8,128)(2,1)S(1)} %slice.18.refs_0_, bf16[1,16,1024]{2,1,0:T(8,128)(2,1)S(1)} %collective-permute-done.15.refs_1_, s32[4,16,32]{2,1,0:T(8,128)S(1)} %copy-done.3), custom_call_target="tpu_custom_call" | custom-call | tf_op jit(solution)/shard_map/pallas_call | solution.py:36
  40.6 6.3 %shard_map.92.weight = bf16[4,1024,512]{2,1,0:T(8,128)(2,1)S(1)} custom-call(s32[7]{0:T(128)S(1)} %pad_add_fusion.info, bf16[4,512,1024]{2,1,0:T(8,128)(2,1)S(1)} %copy-done, bf16[2,128,512]{2,1,0:T(8,128)(2,1)S(1)} %pad_maximum_fusion.refs_0_, bf16[2,128,512]{2,1,0:T(8,128)(2,1)S(1)} %collective-permute-done.2.refs_1_, bf16[1,128,512]{2,1,0:T(8,128)(2,1)S(1)} %bitcast.94, ...), custom_call_target="tpu_custom_call" | custom-call | tf_op jit(solution)/shard_map/pallas_call | solution.py:36
  47.0 7.2 %shard_map.93 = (f32[4,3,256]{2,1,0:T(4,128)S(1)}, bf16[1024,1536]{1,0:T(8,128)(2,1)S(1)}, bf16[1536,1024]{1,0:T(8,128)(2,1)S(1)}) custom-call(s32[7]{0:T(128)S(1)} %pad_add_fusion.info, bf16[4,1024,512]{2,1,0:T(8,128)(2,1)S(1)} %shard_map.92.weight, bf16[4,512,1024]{2,1,0:T(8,128)(2,1)S(1)} %copy-done, ...), custom_call_target="tpu_custom_call" | custom-call | tf_op jit(solution)/shard_map/pallas_call | solution.py:36
  54.2 0.4 collective-permute-start.17
  54.6 1.2 %collective-permute-start.18 = (f32[4,256]{1,0:T(4,128)S(1)}, f32[4,256]{1,0:T(4,128)S(1)}, u32[]{:S(2)}, u32[]{:S(2)}) collective-permute-start(f32[4,256]{1,0:T(4,128)S(1)} %get-tuple-element.131), channel_id=1, source_target_pairs={{0,2},{1,3},{2,0},{3,1},{4,6},{5,7},{6,4},{7,5},{8,10},{9,11},{10,... | collective-permute-start | bytes 12296 | tf_op jit(solution)/shard_map/ppermute | solution.py:398
  55.8 5.0 %shard_map.94.refs_2_ = f32[4,1024,256]{2,1,0:T(8,128)S(1)} custom-call(s32[7]{0:T(128)S(1)} %pad_add_fusion.info, bf16[1024,1536]{1,0:T(8,128)(2,1)S(1)} %get-tuple-element.107.refs_0_, bf16[1536,1024]{1,0:T(8,128)(2,1)S(1)} %get-tuple-element.108.refs_1_), custom_call_target="tpu_custom_call" | custom-call | tf_op jit(solution)/shard_map/pallas_call | solution.py:36
  60.9 4.1 %shard_map.95 = (f32[4,1,256]{2,1,0:T(1,128)S(1)}, bf16[1024,512]{1,0:T(8,128)(2,1)S(1)}, bf16[512,1024]{1,0:T(8,128)(2,1)S(1)}) custom-call(s32[7]{0:T(128)S(1)} %pad_add_fusion.info, bf16[4,1024,512]{2,1,0:T(8,128)(2,1)S(1)} %shard_map.92.weight, bf16[4,512,1024]{2,1,0:T(8,128)(2,1)S(1)} %copy-done, f32[4,256,128]{2,1,0:T(8,128)S(1)} %get-tuple-element.102.refs_2_.refs_0_, ...), custom_call_target="tpu_custom_call" | custom-call | tf_op jit(solution)/shard_map/pallas_call | solution.py:36
  65.0 1.6 %shard_map.97 = bf16[2,1024,256]{2,1,0:T(8,128)(2,1)S(1)} custom-call(s32[7]{0:T(128)S(1)} %pad_add_fusion.info, bf16[1024,512]{1,0:T(8,128)(2,1)S(1)} %get-tuple-element.113.refs_0_, bf16[512,1024]{1,0:T(8,128)(2,1)S(1)} %get-tuple-element.114.refs_1_, f32[4,1024,256]{2,1,0:T(8,128)S(1)} %shard_map.94.refs_2_), custom_call_target="tpu_custom_call" | custom-call | tf_op jit(solution)/shard_map/pallas_call | solution.py:36
  66.7 1.6 %shard_map.96 = f32[2,1024,256]{2,1,0:T(8,128)S(1)} custom-call(s32[7]{0:T(128)S(1)} %pad_add_fusion.info, bf16[1024,512]{1,0:T(8,128)(2,1)S(1)} %get-tuple-element.113.refs_0_, bf16[512,1024]{1,0:T(8,128)(2,1)S(1)} %get-tuple-element.114.refs_1_, f32[4,1024,256]{2,1,0:T(8,128)S(1)} %shard_map.94.refs_2_), custom_call_target="tpu_custom_call" | custom-call | flops 34359738368 | tf_op jit(solution)/shard_map/pallas_call | solution.py:36
  68.2 1.0 %collective-permute-done.20 = bf16[2,1024,256]{2,1,0:T(8,128)(2,1)S(1)} collective-permute-done((bf16[2,1024,256]{2,1,0:T(8,128)(2,1)S(1)}, bf16[2,1024,256]{2,1,0:T(8,128)(2,1)S(1)}, u32[]{:S(2)}, u32[]{:S(2)}) %collective-permute-start.20) | collective-permute-done | bytes 1048608 | tf_op jit(solution)/shard_map/ppermute | solution.py:398
  69.3 0.2 fusion.7
  69.5 1.6 %collective-permute-start.21 = (bf16[4,128,256]{2,1,0:T(8,128)(2,1)S(1)}, bf16[4,128,256]{2,1,0:T(8,128)(2,1)S(1)}, u32[]{:S(2)}, u32[]{:S(2)}) collective-permute-start(bf16[4,128,256]{2,1,0:T(8,128)(2,1)S(1)} %get-tuple-element.124), channel_id=1, source_target_pairs={{0,4},{1,5},{2,6},{3,7},{4,0},{5,1},{6,2},{7,3},{8,12},{9,13},{10,... | collective-permute-start | bytes 786440 | tf_op jit(solution)/shard_map/ppermute | solution.py:404
  71.0 0.8 collective-permute-start.22
  71.9 1.2 %collective-permute-start.23 = (bf16[4,128,256]{2,1,0:T(8,128)(2,1)S(1)}, bf16[4,128,256]{2,1,0:T(8,128)(2,1)S(1)}, u32[]{:S(2)}, u32[]{:S(2)}) collective-permute-start(bf16[4,128,256]{2,1,0:T(8,128)(2,1)S(1)} %get-tuple-element.126), channel_id=1, source_target_pairs={{0,6},{1,7},{2,4},{3,5},{4,2},{5,3},{6,0},{7,1},{8,14},{9,15},{10,... | collective-permute-start | bytes 786440 | tf_op jit(solution)/shard_map/ppermute | solution.py:404
  73.0 5.7 %collective-permute-done.21 = bf16[4,128,256]{2,1,0:T(8,128)(2,1)S(1)} collective-permute-done((bf16[4,128,256]{2,1,0:T(8,128)(2,1)S(1)}, bf16[4,128,256]{2,1,0:T(8,128)(2,1)S(1)}, u32[]{:S(2)}, u32[]{:S(2)}) %collective-permute-start.21) | collective-permute-done | bytes 262176 | tf_op jit(solution)/shard_map/ppermute | solution.py:404
  78.7 6.0 %collective-permute-done.22 = bf16[4,128,256]{2,1,0:T(8,128)(2,1)S(1)} collective-permute-done((bf16[4,128,256]{2,1,0:T(8,128)(2,1)S(1)}, bf16[4,128,256]{2,1,0:T(8,128)(2,1)S(1)}, u32[]{:S(2)}, u32[]{:S(2)}) %collective-permute-start.22) | collective-permute-done | bytes 262176 | tf_op jit(solution)/shard_map/ppermute | solution.py:404
  85.0 0.5 collective-permute-start.24
  85.5 2.6 %collective-permute-start.25 = (bf16[128,256]{1,0:T(8,128)(2,1)S(1)}, bf16[128,256]{1,0:T(8,128)(2,1)S(1)}, u32[]{:S(2)}, u32[]{:S(2)}) collective-permute-start(bf16[128,256]{1,0:T(8,128)(2,1)S(1)} %get-tuple-element.129), channel_id=1, source_target_pairs={{0,16},{4,20},{8,24},{12,28},{16,0},{20,4},{24,8},{28,12},{1,17},{... | collective-permute-start | bytes 196616 | tf_op jit(solution)/shard_map/ppermute | solution.py:398
  88.1 1.3 %collective-permute-start.26 = (bf16[128,256]{1,0:T(8,128)(2,1)S(1)}, bf16[128,256]{1,0:T(8,128)(2,1)S(1)}, u32[]{:S(2)}, u32[]{:S(2)}) collective-permute-start(bf16[128,256]{1,0:T(8,128)(2,1)S(1)} %get-tuple-element.128), channel_id=1, source_target_pairs={{0,24},{4,28},{8,16},{12,20},{16,8},{20,12},{24,0},{28,4},{1,25},{... | collective-permute-start | bytes 196616 | tf_op jit(solution)/shard_map/ppermute | solution.py:398
  89.4 3.0 %collective-permute-done.19 = f32[4,256]{1,0:T(4,128)S(1)} collective-permute-done((f32[4,256]{1,0:T(4,128)S(1)}, f32[4,256]{1,0:T(4,128)S(1)}, u32[]{:S(2)}, u32[]{:S(2)}) %collective-permute-start.19) | collective-permute-done | bytes 4128 | tf_op jit(solution)/shard_map/ppermute | solution.py:398
  92.4 0.6 add.47
  93.0 1.1 %collective-permute-done.26 = bf16[128,256]{1,0:T(8,128)(2,1)S(1)} collective-permute-done((bf16[128,256]{1,0:T(8,128)(2,1)S(1)}, bf16[128,256]{1,0:T(8,128)(2,1)S(1)}, u32[]{:S(2)}, u32[]{:S(2)}) %collective-permute-start.26) | collective-permute-done | bytes 65568 | tf_op jit(solution)/shard_map/ppermute | solution.py:398
  94.1 0.7 fusion.11
  (46 shorter events, 0.9 us)
Async XLA Ops:
  2.1 1.6 %copy-start.1 = (bf16[4,256,1024]{2,1,0:T(8,128)(2,1)S(1)}, bf16[4,256,1024]{2,1,0:T(8,128)(2,1)}, u32[]{:S(2)}) copy-start(bf16[4,256,1024]{2,1,0:T(8,128)(2,1)} %words.3) | copy-start | bytes 6291460
  3.7 0.7 copy-start.4
  4.3 1.1 %copy-start.6 = (bf16[128,1024]{1,0:T(8,128)(2,1)S(1)}, bf16[128,1024]{1,0:T(8,128)(2,1)}, u32[]{:S(2)}) copy-start(bf16[128,1024]{1,0:T(8,128)(2,1)} %proj) | copy-start | bytes 786436
  6.1 8.1 %copy-start.2 = (bf16[4,256,1024]{2,1,0:T(8,128)(2,1)S(1)}, bf16[4,256,1024]{2,1,0:T(8,128)(2,1)}, u32[]{:S(2)}) copy-start(bf16[4,256,1024]{2,1,0:T(8,128)(2,1)} %words.3) | copy-start | bytes 6291460
  6.1 8.1 %copy-start.5 = (s32[4,256,1]{1,2,0:T(1,128)S(1)}, s32[4,256,1]{1,2,0:T(1,128)}, u32[]{:S(2)}) copy-start(s32[4,256,1]{1,2,0:T(1,128)} %param.10) | copy-start | bytes 12292
  6.1 9.7 %collective-permute-start = (bf16[128,512]{1,0:T(8,128)(2,1)S(1)}, bf16[128,512]{1,0:T(8,128)(2,1)S(1)}, u32[]{:S(2)}, u32[]{:S(2)}) collective-permute-start(bf16[128,512]{1,0:T(8,128)(2,1)S(1)} %shard_map.87.proj), channel_id=1, source_target_pairs={{0,8},{4,12},{8,0},{12,4},{16,24},{20,28},{24,16},{28,20},{1,9},{5... | collective-permute-start | bytes 393224 | tf_op jit(solution)/shard_map/ppermute | solution.py:398
  9.2 25.3 %collective-permute-start.10 = (bf16[1,528,1024]{2,1,0:T(8,128)(2,1)S(1)}, bf16[1,528,1024]{2,1,0:T(8,128)(2,1)S(1)}, u32[]{:S(2)}, u32[]{:S(2)}) collective-permute-start(bf16[1,528,1024]{2,1,0:T(8,128)(2,1)S(1)} %shard_map.86), channel_id=1, source_target_pairs={{0,2},{1,3},{2,0},{3,1},{4,6},{5,7},{6,4},{7,5},{8,10},{9,11},{10,... | collective-permute-start | bytes 3244040 | tf_op jit(solution)/shard_map/ppermute | solution.py:398
  11.2 12.1 %collective-permute-start.3 = (bf16[128,512]{1,0:T(8,128)(2,1)S(1)}, bf16[128,512]{1,0:T(8,128)(2,1)S(1)}, u32[]{:S(2)}, u32[]{:S(2)}) collective-permute-start(bf16[128,512]{1,0:T(8,128)(2,1)S(1)} %shard_map.88), channel_id=1, source_target_pairs={{0,16},{4,20},{8,24},{12,28},{16,0},{20,4},{24,8},{28,12},{1,17},{... | collective-permute-start | bytes 393224 | tf_op jit(solution)/shard_map/ppermute | solution.py:398
  13.9 9.4 %collective-permute-start.4 = (bf16[128,512]{1,0:T(8,128)(2,1)S(1)}, bf16[128,512]{1,0:T(8,128)(2,1)S(1)}, u32[]{:S(2)}, u32[]{:S(2)}) collective-permute-start(bf16[128,512]{1,0:T(8,128)(2,1)S(1)} %shard_map.88), channel_id=1, source_target_pairs={{0,24},{4,28},{8,16},{12,20},{16,8},{20,12},{24,0},{28,4},{1,25},{... | collective-permute-start | bytes 393224 | tf_op jit(solution)/shard_map/ppermute | solution.py:398
  14.1 3.3 %copy-start.3 = (s32[4,16,32]{2,1,0:T(8,128)S(1)}, s32[4,16,32]{2,1,0:T(8,128)}, u32[]{:S(2)}) copy-start(s32[4,16,32]{2,1,0:T(8,128)} %refs_2_.3) | copy-start | bytes 24580
  14.1 3.3 %collective-permute-start.5 = (bf16[1,16,1024]{2,1,0:T(8,128)(2,1)S(1)}, bf16[1,16,1024]{2,1,0:T(8,128)(2,1)S(1)}, u32[]{:S(2)}, u32[]{:S(2)}) collective-permute-start(bf16[1,16,1024]{2,1,0:T(8,128)(2,1)S(1)} %slice.17.refs_0_), channel_id=1, source_target_pairs={{0,1},{1,0},{2,3},{3,2},{4,5},{5,4},{6,7},{7,6},{8,9},{9,8},{10,11... | collective-permute-start | bytes 98312 | tf_op jit(solution)/shard_map/ppermute | solution.py:398
  15.9 8.8 %collective-permute-start.2 = (bf16[2,128,512]{2,1,0:T(8,128)(2,1)S(1)}, bf16[2,128,512]{2,1,0:T(8,128)(2,1)S(1)}, u32[]{:S(2)}, u32[]{:S(2)}) collective-permute-start(bf16[2,128,512]{2,1,0:T(8,128)(2,1)S(1)} %pad_maximum_fusion.refs_0_), channel_id=1, source_target_pairs={{0,4},{4,0},{8,12},{12,8},{16,20},{20,16},{24,28},{28,24},{1,5},{5... | collective-permute-start | bytes 786440 | tf_op jit(solution)/shard_map/ppermute | solution.py:398
  17.4 23.2 %copy-start = (bf16[4,512,1024]{2,1,0:T(8,128)(2,1)S(1)}, bf16[4,512,1024]{2,1,0:T(8,128)(2,1)}, u32[]{:S(2)}) copy-start(bf16[4,512,1024]{2,1,0:T(8,128)(2,1)} %patches.5) | copy-start | bytes 12582916
  24.6 8.7 %collective-permute-start.8 = (bf16[2,128,512]{2,1,0:T(8,128)(2,1)S(1)}, bf16[2,128,512]{2,1,0:T(8,128)(2,1)S(1)}, u32[]{:S(2)}, u32[]{:S(2)}) collective-permute-start(bf16[2,128,512]{2,1,0:T(8,128)(2,1)S(1)} %pad_maximum_fusion.refs_0_), channel_id=1, source_target_pairs={{0,1},{1,0},{2,3},{3,2},{4,5},{5,4},{6,7},{7,6},{8,9},{9,8},{10,11... | collective-permute-start | bytes 786440 | tf_op jit(solution)/shard_map/ppermute | solution.py:398
  24.6 8.7 %collective-permute-start.9 = (bf16[2,128,512]{2,1,0:T(8,128)(2,1)S(1)}, bf16[2,128,512]{2,1,0:T(8,128)(2,1)S(1)}, u32[]{:S(2)}, u32[]{:S(2)}) collective-permute-start(bf16[2,128,512]{2,1,0:T(8,128)(2,1)S(1)} %collective-permute-done.2.refs_1_), channel_id=1, source_target_pairs={{0,1},{1,0},{2,3},{3,2},{4,5},{5,4},{6,7},{7,6},{8,9},{9,8},{10,11... | collective-permute-start | bytes 786440 | tf_op jit(solution)/shard_map/ppermute | solution.py:398
  25.1 6.4 %collective-permute-start.6 = (bf16[1,128,512]{2,1,0:T(8,128)(2,1)S(1)}, bf16[1,128,512]{2,1,0:T(8,128)(2,1)S(1)}, u32[]{:S(2)}, u32[]{:S(2)}) collective-permute-start(bf16[1,128,512]{2,1,0:T(8,128)(2,1)S(1)} %bitcast.92), channel_id=1, source_target_pairs={{0,4},{4,0},{8,12},{12,8},{16,20},{20,16},{24,28},{28,24},{1,5},{5... | collective-permute-start | bytes 393224 | tf_op jit(solution)/shard_map/ppermute | solution.py:398
  26.6 6.7 %collective-permute-start.7 = (bf16[1,128,512]{2,1,0:T(8,128)(2,1)S(1)}, bf16[1,128,512]{2,1,0:T(8,128)(2,1)S(1)}, u32[]{:S(2)}, u32[]{:S(2)}) collective-permute-start(bf16[1,128,512]{2,1,0:T(8,128)(2,1)S(1)} %bitcast.95), channel_id=1, source_target_pairs={{0,4},{4,0},{8,12},{12,8},{16,20},{20,16},{24,28},{28,24},{1,5},{5... | collective-permute-start | bytes 393224 | tf_op jit(solution)/shard_map/ppermute | solution.py:398
  34.5 12.5 %collective-permute-start.16 = (bf16[1,4,128,1024]{3,2,1,0:T(8,128)(2,1)S(1)}, bf16[1,4,128,1024]{3,2,1,0:T(8,128)(2,1)S(1)}, u32[]{:S(2)}, u32[]{:S(2)}) collective-permute-start(bf16[1,4,128,1024]{3,2,1,0:T(8,128)(2,1)S(1)} %get-tuple-element.106), channel_id=1, source_target_pairs={{0,1},{1,0},{2,3},{3,2},{4,5},{5,4},{6,7},{7,6},{8,9},{9,8},{10,11... | collective-permute-start | bytes 3145736 | tf_op jit(solution)/shard_map/ppermute | solution.py:398
  34.5 26.4 %collective-permute-start.1 = (bf16[1,512,1024]{2,1,0:T(8,128)(2,1)S(1)}, bf16[1,512,1024]{2,1,0:T(8,128)(2,1)S(1)}, u32[]{:S(2)}, u32[]{:S(2)}) collective-permute-start(bf16[1,512,1024]{2,1,0:T(8,128)(2,1)S(1)} %bitcast.101), channel_id=1, source_target_pairs={{0,3},{1,2},{2,1},{3,0},{4,7},{5,6},{6,5},{7,4},{8,11},{9,10},{10,... | collective-permute-start | bytes 3145736 | tf_op jit(solution)/shard_map/ppermute | solution.py:398
  36.1 1.7 %collective-permute-start.11 = (bf16[1,128,512]{2,1,0:T(8,128)(2,1)S(1)}, bf16[1,128,512]{2,1,0:T(8,128)(2,1)S(1)}, u32[]{:S(2)}, u32[]{:S(2)}) collective-permute-start(bf16[1,128,512]{2,1,0:T(8,128)(2,1)S(1)} %bitcast.93), channel_id=1, source_target_pairs={{0,1},{1,0},{2,3},{3,2},{4,5},{5,4},{6,7},{7,6},{8,9},{9,8},{10,11... | collective-permute-start | bytes 393224 | tf_op jit(solution)/shard_map/ppermute | solution.py:398
  36.1 1.4 %collective-permute-start.15 = (bf16[1,16,1024]{2,1,0:T(8,128)(2,1)S(1)}, bf16[1,16,1024]{2,1,0:T(8,128)(2,1)S(1)}, u32[]{:S(2)}, u32[]{:S(2)}) collective-permute-start(bf16[1,16,1024]{2,1,0:T(8,128)(2,1)S(1)} %slice.18.refs_0_), channel_id=1, source_target_pairs={{0,1},{1,0},{2,3},{3,2},{4,5},{5,4},{6,7},{7,6},{8,9},{9,8},{10,11... | collective-permute-start | bytes 98312 | tf_op jit(solution)/shard_map/ppermute | solution.py:398
  36.6 4.0 %collective-permute-start.12 = (bf16[1,128,512]{2,1,0:T(8,128)(2,1)S(1)}, bf16[1,128,512]{2,1,0:T(8,128)(2,1)S(1)}, u32[]{:S(2)}, u32[]{:S(2)}) collective-permute-start(bf16[1,128,512]{2,1,0:T(8,128)(2,1)S(1)} %collective-permute-done.6.refs_3_), channel_id=1, source_target_pairs={{0,1},{1,0},{2,3},{3,2},{4,5},{5,4},{6,7},{7,6},{8,9},{9,8},{10,11... | collective-permute-start | bytes 393224 | tf_op jit(solution)/shard_map/ppermute | solution.py:398
  37.5 3.1 %collective-permute-start.13 = (bf16[1,128,512]{2,1,0:T(8,128)(2,1)S(1)}, bf16[1,128,512]{2,1,0:T(8,128)(2,1)S(1)}, u32[]{:S(2)}, u32[]{:S(2)}) collective-permute-start(bf16[1,128,512]{2,1,0:T(8,128)(2,1)S(1)} %bitcast.96), channel_id=1, source_target_pairs={{0,1},{1,0},{2,3},{3,2},{4,5},{5,4},{6,7},{7,6},{8,9},{9,8},{10,11... | collective-permute-start | bytes 393224 | tf_op jit(solution)/shard_map/ppermute | solution.py:398
  37.9 2.8 %collective-permute-start.14 = (bf16[1,128,512]{2,1,0:T(8,128)(2,1)S(1)}, bf16[1,128,512]{2,1,0:T(8,128)(2,1)S(1)}, u32[]{:S(2)}, u32[]{:S(2)}) collective-permute-start(bf16[1,128,512]{2,1,0:T(8,128)(2,1)S(1)} %collective-permute-done.7.refs_5_), channel_id=1, source_target_pairs={{0,1},{1,0},{2,3},{3,2},{4,5},{5,4},{6,7},{7,6},{8,9},{9,8},{10,11... | collective-permute-start | bytes 393224 | tf_op jit(solution)/shard_map/ppermute | solution.py:398
  54.2 6.6 %collective-permute-start.17 = (f32[4,256]{1,0:T(4,128)S(1)}, f32[4,256]{1,0:T(4,128)S(1)}, u32[]{:S(2)}, u32[]{:S(2)}) collective-permute-start(f32[4,256]{1,0:T(4,128)S(1)} %get-tuple-element.130), channel_id=1, source_target_pairs={{0,1},{1,0},{2,3},{3,2},{4,5},{5,4},{6,7},{7,6},{8,9},{9,8},{10,11... | collective-permute-start | bytes 12296 | tf_op jit(solution)/shard_map/ppermute | solution.py:398
  54.6 6.2 %collective-permute-start.18 = (f32[4,256]{1,0:T(4,128)S(1)}, f32[4,256]{1,0:T(4,128)S(1)}, u32[]{:S(2)}, u32[]{:S(2)}) collective-permute-start(f32[4,256]{1,0:T(4,128)S(1)} %get-tuple-element.131), channel_id=1, source_target_pairs={{0,2},{1,3},{2,0},{3,1},{4,6},{5,7},{6,4},{7,5},{8,10},{9,11},{10,... | collective-permute-start | bytes 12296 | tf_op jit(solution)/shard_map/ppermute | solution.py:398
  66.5 2.7 %collective-permute-start.20 = (bf16[2,1024,256]{2,1,0:T(8,128)(2,1)S(1)}, bf16[2,1024,256]{2,1,0:T(8,128)(2,1)S(1)}, u32[]{:S(2)}, u32[]{:S(2)}) collective-permute-start(bf16[2,1024,256]{2,1,0:T(8,128)(2,1)S(1)} %shard_map.97), channel_id=1, source_target_pairs={{0,1},{1,0},{2,3},{3,2},{4,5},{5,4},{6,7},{7,6},{8,9},{9,8},{10,11... | collective-permute-start | bytes 3145736 | tf_op jit(solution)/shard_map/ppermute | solution.py:398
  69.5 9.2 %collective-permute-start.21 = (bf16[4,128,256]{2,1,0:T(8,128)(2,1)S(1)}, bf16[4,128,256]{2,1,0:T(8,128)(2,1)S(1)}, u32[]{:S(2)}, u32[]{:S(2)}) collective-permute-start(bf16[4,128,256]{2,1,0:T(8,128)(2,1)S(1)} %get-tuple-element.124), channel_id=1, source_target_pairs={{0,4},{1,5},{2,6},{3,7},{4,0},{5,1},{6,2},{7,3},{8,12},{9,13},{10,... | collective-permute-start | bytes 786440 | tf_op jit(solution)/shard_map/ppermute | solution.py:404
  71.0 13.7 %collective-permute-start.22 = (bf16[4,128,256]{2,1,0:T(8,128)(2,1)S(1)}, bf16[4,128,256]{2,1,0:T(8,128)(2,1)S(1)}, u32[]{:S(2)}, u32[]{:S(2)}) collective-permute-start(bf16[4,128,256]{2,1,0:T(8,128)(2,1)S(1)} %get-tuple-element.125), channel_id=1, source_target_pairs={{0,2},{1,3},{2,0},{3,1},{4,6},{5,7},{6,4},{7,5},{8,10},{9,11},{10,... | collective-permute-start | bytes 786440 | tf_op jit(solution)/shard_map/ppermute | solution.py:404
  71.9 12.9 %collective-permute-start.23 = (bf16[4,128,256]{2,1,0:T(8,128)(2,1)S(1)}, bf16[4,128,256]{2,1,0:T(8,128)(2,1)S(1)}, u32[]{:S(2)}, u32[]{:S(2)}) collective-permute-start(bf16[4,128,256]{2,1,0:T(8,128)(2,1)S(1)} %get-tuple-element.126), channel_id=1, source_target_pairs={{0,6},{1,7},{2,4},{3,5},{4,2},{5,3},{6,0},{7,1},{8,14},{9,15},{10,... | collective-permute-start | bytes 786440 | tf_op jit(solution)/shard_map/ppermute | solution.py:404
  85.0 8.1 %collective-permute-start.24 = (bf16[128,256]{1,0:T(8,128)(2,1)S(1)}, bf16[128,256]{1,0:T(8,128)(2,1)S(1)}, u32[]{:S(2)}, u32[]{:S(2)}) collective-permute-start(bf16[128,256]{1,0:T(8,128)(2,1)S(1)} %get-tuple-element.127), channel_id=1, source_target_pairs={{0,8},{4,12},{8,0},{12,4},{16,24},{20,28},{24,16},{28,20},{1,9},{5... | collective-permute-start | bytes 196616 | tf_op jit(solution)/shard_map/ppermute | solution.py:398
  85.5 7.6 %collective-permute-start.25 = (bf16[128,256]{1,0:T(8,128)(2,1)S(1)}, bf16[128,256]{1,0:T(8,128)(2,1)S(1)}, u32[]{:S(2)}, u32[]{:S(2)}) collective-permute-start(bf16[128,256]{1,0:T(8,128)(2,1)S(1)} %get-tuple-element.129), channel_id=1, source_target_pairs={{0,16},{4,20},{8,24},{12,28},{16,0},{20,4},{24,8},{28,12},{1,17},{... | collective-permute-start | bytes 196616 | tf_op jit(solution)/shard_map/ppermute | solution.py:398
  88.1 6.1 %collective-permute-start.26 = (bf16[128,256]{1,0:T(8,128)(2,1)S(1)}, bf16[128,256]{1,0:T(8,128)(2,1)S(1)}, u32[]{:S(2)}, u32[]{:S(2)}) collective-permute-start(bf16[128,256]{1,0:T(8,128)(2,1)S(1)} %get-tuple-element.128), channel_id=1, source_target_pairs={{0,24},{4,28},{8,16},{12,20},{16,8},{20,12},{24,0},{28,4},{1,25},{... | collective-permute-start | bytes 196616 | tf_op jit(solution)/shard_map/ppermute | solution.py:398
  89.4 3.0 %collective-permute-start.19 = (f32[4,256]{1,0:T(4,128)S(1)}, f32[4,256]{1,0:T(4,128)S(1)}, u32[]{:S(2)}, u32[]{:S(2)}) collective-permute-start(f32[4,256]{1,0:T(4,128)S(1)} %bitcast.105), channel_id=1, source_target_pairs={{0,3},{1,2},{2,1},{3,0},{4,7},{5,6},{6,5},{7,4},{8,11},{9,10},{10,... | collective-permute-start | bytes 12296 | tf_op jit(solution)/shard_map/ppermute | solution.py:398

commit v11 on v7

--- a/solution.py
+++ b/solution.py
@@ -12,8 +12,9 @@
 SHIFT = 6
 VMEM_LIMIT = 16 * 1024 * 1024
 WORK = 1<<31
+MUCH = 1 << 35
 ME, CORE, DP, COUNTS = 0, 1, 2, 3
-TARGET, COEF = 0, 1
+TARGET, COEF, BLOCKS = 0, 1, 2
 F32, BF16 = jnp.float32, jnp.bfloat16
 
 
@@ -115,11 +116,11 @@
     )
 
 
-def table_kernel(offsets, cap, info, meta, flags, bias, table, rank_out):
+def table_kernel(offsets, cap, own_blk, info, meta, flags, table, rank_out):
     me = info[ME]
     n_homes, pages, _, wdev = meta.shape
     nblk, all_blk = flags.shape[1:]
-    n_rows, pps = bias.shape[1:]
+    n_rows = table.shape[1]
     slots = iota((cap, wdev), 0).astype(F32)
     rank = ranks(
         stacked(
@@ -130,9 +131,10 @@
             ]
         )
     )
-    first = me * (pps // MARGIN_BLOCK_SIZE)
-    block = iota((all_blk, pps), 1) >> SHIFT
-    spread = (iota((all_blk, pps), 0) == first + block).astype(BF16)
+    lane = iota((n_rows, 128), 1)
+    own = iota((all_blk, 128), 1) - BLOCKS
+    chosen = (own >= 0) & (own < own_blk) & (iota((all_blk, 128), 0) == me * own_blk + own)
+    chosen = chosen.astype(BF16)
     place = iota((1, wdev), 1) + 1
     for p in range(pages):
         t, idx = [], []
@@ -149,25 +151,22 @@
         t, idx = jnp.concatenate(t, axis=0), jnp.concatenate(idx, axis=0)
         word_block = jnp.maximum(idx, 0) >> SHIFT == iota((n_rows, nblk), 1)
         margin = dot(word_block.astype(BF16), flags[p].astype(BF16)).astype(BF16)
-        hit = dot(margin, spread)
-        own = iota((n_rows, pps), 1) >> SHIFT == t >> SHIFT
-        bias[p] = jnp.where((hit > 0.5) | own, 0.0, -jnp.inf).astype(BF16)
+        allowed = (dot(margin, chosen) > 0.5) | (lane - BLOCKS == t >> SHIFT)
         count = info[COUNTS + p]
         valid = (idx >= 0) & (idx < count)
         coef = jnp.where(valid, 64.0 / count.astype(F32), 0.0)
-        lane = iota((n_rows, 128), 1)
-        table[p] = jnp.where(lane == TARGET, t.astype(F32), jnp.where(lane == COEF, coef, 0.0))
+        value = jnp.where(allowed, 1.0, 0.0)
+        table[p] = jnp.where(lane == TARGET, t.astype(F32), jnp.where(lane == COEF, coef, value))
 
 
 def tables(info, meta, flags, offsets, cap, pps, flops=0):
     n_homes, pages, _, wdev = meta.shape
     out = [
-        jax.ShapeDtypeStruct((pages, n_homes * cap, pps), BF16),
         jax.ShapeDtypeStruct((pages, n_homes * cap, 128), F32),
         jax.ShapeDtypeStruct((pages, pad_rows(n_homes), wdev), F32),
     ]
     return call(
-        functools.partial(table_kernel, offsets, cap),
+        functools.partial(table_kernel, offsets, cap, pps // MARGIN_BLOCK_SIZE),
         1,
         [all_of(meta), all_of(flags)],
         [all_of(o) for o in out],
@@ -181,17 +180,17 @@
     out[...] = proj[...]
 
 
-def half_of(info, proj):
+def half_of(info, proj, half):
     rows, width = proj.shape
-    out = jax.ShapeDtypeStruct((rows, width // 2), BF16)
+    out = jax.ShapeDtypeStruct((rows, half), BF16)
     return call(
         half_kernel,
         1,
-        [pl.BlockSpec((rows, width // 2), lambda p, info: (0, info[CORE]))],
+        [pl.BlockSpec((rows, half), lambda p, info: (0, info[CORE] if width > half else 0))],
         all_of(out),
         out,
         (info, proj),
-        flops=1 << 35,
+        flops=MUCH,
     )
 
 
@@ -249,7 +248,7 @@
     )
 
 
-def page_kernel(n_homes, info, bias, table, rank, weight, patches, *refs):
+def page_kernel(n_homes, info, table, rank, weight, patches, *refs):
     *words, loss, x_t, dq = refs
     pps, width = patches.shape[1:]
     cap = words[0].shape[2]
@@ -259,7 +258,10 @@
     scores = dot(x, weight[0]) * scale
     is_target = iota((n_rows, pps), 1) == table[0, :, TARGET : TARGET + 1].astype(jnp.int32)
     coef = table[0, :, COEF : COEF + 1]
-    masked = scores + bias[0].astype(F32)
+    lanes = table[0]
+    spread = iota((128, pps), 0) - BLOCKS == iota((128, pps), 1) >> SHIFT
+    marks = jnp.where(iota(lanes.shape, 1) < BLOCKS, 0.0, lanes).astype(BF16)
+    masked = jnp.where(dot(marks, spread.astype(BF16)) > 0.5, scores, -jnp.inf)
     top = jnp.max(masked, axis=1, keepdims=True)
     expo = jnp.exp(masked - top)
     total = jnp.sum(expo, axis=1, keepdims=True)
@@ -280,9 +282,9 @@
     x_t[...] = x.T
 
 
-def run_pages(info, weight, patches, table, words, first_page):
-    _, n_pages, cap, width = words[0][0].shape
-    wdev = table[2].shape[2]
+def run_pages(info, weight, patches, table, words, first_page, n_pages, at=0):
+    _, _, cap, width = words[0][0].shape
+    wdev = table[1].shape[2]
     n_homes = len(words)
     n_rows = -(-n_homes * cap // 128) * 128
     out = [
@@ -295,7 +297,7 @@
         functools.partial(page_kernel, n_homes),
         n_pages,
         [page_of(a, first_page) for a in inputs]
-        + [pl.BlockSpec((1, 1, cap, width), lambda p, info, i=i: (i, p, 0, 0)) for _, i in words],
+        + [pl.BlockSpec((1, 1, cap, width), lambda p, info, i=i: (i, p + at, 0, 0)) for _, i in words],
         [
             page_of(out[0]),
             pl.BlockSpec((width, n_rows), lambda p, info: (0, p)),
@@ -314,22 +316,29 @@
     out[0] = got.astype(out.dtype)
 
 
-def gradient(info, other, dtype, n_y, pairs, before=()):
+def gradient(info, dtype, n_y, pairs, cores, before=(), flops=0):
     width = pairs[0][0].shape[0]
     wcol = width // (2 * n_y)
-    out = jax.ShapeDtypeStruct((n_y, width, wcol), dtype)
-    column = lambda y, info: (0, 2 * y + jnp.bitwise_xor(info[CORE], other))
+    out = jax.ShapeDtypeStruct((len(cores) * n_y, width, wcol), dtype)
+
+    def column(i, info):
+        core = cores[0] if len(cores) == 1 else jnp.where(i < n_y, cores[0], cores[1])
+        return 0, 2 * (i % n_y) + jnp.bitwise_xor(info[CORE], core)
+
     specs = []
     for x_t, dq in pairs:
         specs += [all_of(x_t), pl.BlockSpec((dq.shape[0], wcol), column)]
+    if before:
+        first = before[1]
+        specs.append(pl.BlockSpec((1, width, wcol), lambda i, info: (first + i, 0, 0)))
     return call(
         functools.partial(gradient_kernel, len(pairs)),
-        n_y,
-        specs + [page_of(b) for b in before],
+        len(cores) * n_y,
+        specs,
         page_of(out),
         out,
-        (info, *(x for pair in pairs for x in pair), *before),
-        flops=64 * width * width * sum(dq.shape[0] for _, dq in pairs) if before else 0,
+        (info, *(x for pair in pairs for x in pair), *before[:1]),
+        flops=flops,
     )
 
 
@@ -379,7 +388,7 @@
     )
     info, proj, both = lax.optimization_barrier((info, proj, both))
     both = [exchange(rows, "seq", 2 * (k + 1)) for k, rows in enumerate(both)]
-    piece = half_of(info, proj)
+    piece = half_of(info, proj, width // 2)
     pieces = [piece] + [exchange(piece, "dp", 2 * k) for k in range(1, n_high)]
     group = n_high // 2
     stay, across, *rest = dispatch(
@@ -419,33 +428,33 @@
     rest = [exchange(rows, "seq", r) for rows, r in zip(rest, far)]
     weight = weights(info, patches, late, late_offsets, [weight])
     run = functools.partial(run_pages, info, weight, patches)
-    loss, *pair_near = run(table_near, [(stay, 0), (across, 0)], 0)
-    word_loss = [loss[:, 0], exchange(loss[:, 1], "seq", 1)]
-
-    both, meta_far, pair_near = lax.optimization_barrier((both, meta_far, pair_near))
+    near_words = [(stay, 0), (across, 0)]
+    some = pages // 2
+    loss, *pair_0 = run(table_near, near_words, 0, some)
+    both, meta_far, pair_0 = lax.optimization_barrier((both, meta_far, pair_0))
     first = [pair for rows in both for pair in ((rows, 0), (exchange(rows, "seq", 1), 1))]
-    before = [gradient(info, other, F32, n_y, [pair_near]) for other in range(2)]
-    info, before = lax.optimization_barrier((info, before))
+    loss_1, *pair_1 = run(table_near, near_words, some, pages - some, some)
+    loss = jnp.concatenate([loss, loss_1], axis=0)
+    near_loss = [loss[:, 0], exchange(loss[:, 1], "seq", 1)]
+    pair_1, meta_far = lax.optimization_barrier((pair_1, meta_far))
     table_far = tables(info, meta_far, flags, far, cap, pps)
-    loss_a, *pair_a = run(table_far, first, 0)
-    rest, pair_a = lax.optimization_barrier((rest, pair_a))
-    loss_b, *pair_b = run(table_far, [(rows, 0) for rows in rest], split)
+    loss_a, *pair_a = run(table_far, first, 0, split)
+    before = gradient(info, F32, n_y, [pair_0, pair_1], (1,))
+    rest, pair_a, before = lax.optimization_barrier((rest, pair_a, before))
+    loss_b, *pair_b = run(table_far, [(rows, 0) for rows in rest], split, pages - split)
     losses = jnp.concatenate([loss_a, loss_b], axis=0)
-    for i, r in enumerate(far):
-        word_loss.append(exchange(losses[:, i], "seq", r))
-
-    sent = gradient(info, 1, BF16, n_y, [pair_a, pair_b], [before[1]])
-    kept = gradient(info, 0, F32, n_y, [pair_a, pair_b], [before[0]])
+    word_loss = near_loss + [exchange(losses[:, i], "seq", r) for i, r in enumerate(far)]
+
+    sent = gradient(info, BF16, n_y, [pair_a, pair_b], (1,), (before, 0))
+    kept = gradient(info, F32, n_y, [pair_0, pair_1, pair_a, pair_b], (0,), flops=MUCH)
     form = (n_y, n_high, 2, shard_rows, width // n_seq)
     terms = [kept.reshape(form), exchange(sent, "seq", 1).reshape(form)]
     part = lambda i, j: sum(
         pick(t, (own["y"][i], None, own["low"][j])).astype(F32) for t in terms
     )
     total = part(0, 0)
-    for i in range(n_y):
-        for j in range(2):
-            if i or j:
-                total = total + exchange_both(part(i, j).astype(BF16), j, 2 * i)
+    for i, j in [(0, 1)] + [(i, j) for i in range(1, n_y) for j in (1, 0)]:
+        total = total + exchange_both(part(i, j).astype(BF16), j, 2 * i)
     grad = pick(total, (own["high"][0],))
     for k in range(1, n_high):
         grad = grad + exchange(pick(total, (own["high"][k],)).astype(BF16), "dp", 2 * k)

time: 92.4 us -> 91.1 us (0.986)
  starting transfers between devices: 25 us -> 26.7 us
  waiting for transfers between devices: 23.6 us -> 22.3 us
    ppermute x26, starting transfers between devices: 21.4 us -> 23.1 us  [exchange(): return lax.ppermute(x, axis, [(i, i ^ offset) for i in range(n)])]
    ppermute x3, waiting for transfers between devices: 10.9 us -> 9.79 us  [exchange_both(): lax.ppermute(x, ('dp', 'seq'), [(i, i ^ dp * n_seq + seq) for i in range(...]
    unnamed x21 -> x17, local copies, waits for them, and re-layouts: 2.32 us -> 2.31 us
  transfers between devices with their start and end apart: 29 -> 29, of which waited for: 11 -> 10; matrix products, arithmetic and copies ran while one was open for 3% -> 1% of each run, Pallas kernels for 38% -> 38%
where the time goes in v11:
time: 91.1 us; the launch traced here: 90.9 us
  Pallas kernels  36.2 us (40%)
  starting transfers between devices  26.7 us (29%)
  waiting for transfers between devices  22.3 us (24%)
  other arithmetic  2.49 us (3%)
  local copies, waits for them, and re-layouts  2.37 us (3%)
  between operations  0.92 us (1%)
    pallas_call x14, Pallas kernels, call(): pl.pallas_call(kernel, grid_spec=pltpu.PrefetchScalarGridSpec(num_scalar_...  36.2 us
    ppermute x26, starting transfers between devices, exchange(): return lax.ppermute(x, axis, [(i, i ^ offset) for i in range(n)])  23.1 us
    ppermute x26, waiting for transfers between devices, exchange(): return lax.ppermute(x, axis, [(i, i ^ offset) for i in range(n)])  12.5 us
    ppermute x3, waiting for transfers between devices, exchange_both(): lax.ppermute(x, ('dp', 'seq'), [(i, i ^ dp * n_seq + seq) for i in range(...  9.79 us
    ppermute x3, starting transfers between devices, exchange_both(): lax.ppermute(x, ('dp', 'seq'), [(i, i ^ dp * n_seq + seq) for i in range(...  3.55 us
    unnamed x17, local copies, waits for them, and re-layouts  2.31 us
  transfers between devices with their start and end apart: 29, of which 10 were waited for; matrix products, arithmetic and copies ran while one was open for 1% of the time, Pallas kernels for 38%

profile of v11, /device:TPU:0, one launch (start us, length us, event | category | flops | bytes accessed | tf_op | source)
XLA Modules:
  0.0 90.9 jit_solution(13180636592038522201)
XLA Ops:
  0.6 0.7 pad_add_fusion.2.info
  1.4 1.6 %copy-done.1 = bf16[4,256,1024]{2,1,0:T(8,128)(2,1)S(1)} copy-done((bf16[4,256,1024]{2,1,0:T(8,128)(2,1)S(1)}, bf16[4,256,1024]{2,1,0:T(8,128)(2,1)}, u32[]{:S(2)}) %copy-start.1) | copy-done | bytes 2097176
  3.0 0.7 copy-done.4
  3.7 1.3 %shard_map.86 = bf16[2,3,128,1024]{3,2,1,0:T(8,128)(2,1)S(1)} custom-call(s32[7]{0:T(128)S(1)} %pad_add_fusion.2.info, s32[4,1,256]{2,1,0:T(1,128)S(1)} %bitcast.100, bf16[4,256,1024]{2,1,0:T(8,128)(2,1)S(1)} %copy-done.1), custom_call_target="tpu_custom_call" | custom-call | tf_op jit(solution)/shard_map/pallas_call | solution.py:36
  5.0 3.0 %collective-permute-start.15 = (bf16[2,3,128,1024]{3,2,1,0:T(8,128)(2,1)S(1)}, bf16[2,3,128,1024]{3,2,1,0:T(8,128)(2,1)S(1)}, u32[]{:S(2)}, u32[]{:S(2)}) collective-permute-start(bf16[2,3,128,1024]{3,2,1,0:T(8,128)(2,1)S(1)} %shard_map.86), channel_id=1, source_target_pairs={{0,2},{1,3},{2,0},{3,1},{4,6},{5,7},{6,4},{7,5},{8,10},{9,11},{10,... | collective-permute-start | bytes 4718600 | tf_op jit(solution)/shard_map/ppermute | solution.py:347
  8.0 0.6 shard_map.87
  8.6 1.6 %collective-permute-start = (bf16[128,512]{1,0:T(8,128)(2,1)S(1)}, bf16[128,512]{1,0:T(8,128)(2,1)S(1)}, u32[]{:S(2)}, u32[]{:S(2)}) collective-permute-start(bf16[128,512]{1,0:T(8,128)(2,1)S(1)} %shard_map.87), channel_id=1, source_target_pairs={{0,8},{4,12},{8,0},{12,4},{16,24},{20,28},{24,16},{28,20},{1,9},{5... | collective-permute-start | bytes 393224 | tf_op jit(solution)/shard_map/ppermute | solution.py:347
  10.2 2.6 %collective-permute-start.2 = (bf16[128,512]{1,0:T(8,128)(2,1)S(1)}, bf16[128,512]{1,0:T(8,128)(2,1)S(1)}, u32[]{:S(2)}, u32[]{:S(2)}) collective-permute-start(bf16[128,512]{1,0:T(8,128)(2,1)S(1)} %shard_map.87), channel_id=1, source_target_pairs={{0,16},{4,20},{8,24},{12,28},{16,0},{20,4},{24,8},{28,12},{1,17},{... | collective-permute-start | bytes 393224 | tf_op jit(solution)/shard_map/ppermute | solution.py:347
  13.1 1.5 %shard_map.88 = (bf16[1,4,128,1024]{3,2,1,0:T(8,128)(2,1)S(1)}, bf16[1,4,128,1024]{3,2,1,0:T(8,128)(2,1)S(1)}, bf16[1,1,128,1024]{3,2,1,0:T(8,128)(2,1)S(1)}, bf16[1,1,128,1024]{3,2,1,0:T(8,128)(2,1)S(1)}) custom-call(s32[7]{0:T(128)S(1)} %pad_add_fusion.2.info, s32[4,1,256]{2,1,0:T(1,128)S(1)} %bitcast.102, bf16[4,256,1024]{2,1,0:T(8,128)(2,1)S(1)} %copy-done.2), custom_call_target="tpu_custom_call" | custom-call | flops 2147483648 | tf_op jit(solution)/shard_map/pallas_call | solution.py:36
  14.7 0.4 collective-permute-done
  15.3 1.5 %collective-permute-start.1 = (bf16[2,128,512]{2,1,0:T(8,128)(2,1)S(1)}, bf16[2,128,512]{2,1,0:T(8,128)(2,1)S(1)}, u32[]{:S(2)}, u32[]{:S(2)}) collective-permute-start(bf16[2,128,512]{2,1,0:T(8,128)(2,1)S(1)} %pad_maximum_fusion.refs_0_), channel_id=1, source_target_pairs={{0,4},{4,0},{8,12},{12,8},{16,20},{20,16},{24,28},{28,24},{1,5},{5... | collective-permute-start | bytes 786440 | tf_op jit(solution)/shard_map/ppermute | solution.py:347
  16.8 2.5 %shard_map.89 = (f32[4,256,128]{2,1,0:T(8,128)S(1)}, f32[4,8,256]{2,1,0:T(8,128)S(1)}) custom-call(s32[7]{0:T(128)S(1)} %pad_add_fusion.2.info, s32[2,4,2,256]{3,2,1,0:T(2,128)S(1)} %pad_add_fusion.meta, s32[4,16,32]{2,1,0:T(8,128)S(1)} %copy-done.3), custom_call_target="tpu_custom_call" | custom-call | flops 2147483648 | tf_op jit(solution)/shard_map/pallas_call | solution.py:36
  19.4 3.5 %collective-permute-done.2 = bf16[128,512]{1,0:T(8,128)(2,1)S(1)} collective-permute-done((bf16[128,512]{1,0:T(8,128)(2,1)S(1)}, bf16[128,512]{1,0:T(8,128)(2,1)S(1)}, u32[]{:S(2)}, u32[]{:S(2)}) %collective-permute-start.2) | collective-permute-done | bytes 131104 | tf_op jit(solution)/shard_map/ppermute | solution.py:347
  22.9 1.0 %collective-permute-done.1.refs_1_ = bf16[2,128,512]{2,1,0:T(8,128)(2,1)S(1)} collective-permute-done((bf16[2,128,512]{2,1,0:T(8,128)(2,1)S(1)}, bf16[2,128,512]{2,1,0:T(8,128)(2,1)S(1)}, u32[]{:S(2)}, u32[]{:S(2)}) %collective-permute-start.1) | collective-permute-done | bytes 262176 | tf_op jit(solution)/shard_map/ppermute | solution.py:347
  23.9 0.5 collective-permute-start.7
  24.4 1.5 %collective-permute-start.5 = (bf16[1,128,512]{2,1,0:T(8,128)(2,1)S(1)}, bf16[1,128,512]{2,1,0:T(8,128)(2,1)S(1)}, u32[]{:S(2)}, u32[]{:S(2)}) collective-permute-start(bf16[1,128,512]{2,1,0:T(8,128)(2,1)S(1)} %bitcast.93), channel_id=1, source_target_pairs={{0,4},{4,0},{8,12},{12,8},{16,20},{20,16},{24,28},{28,24},{1,5},{5... | collective-permute-start | bytes 393224 | tf_op jit(solution)/shard_map/ppermute | solution.py:347
  25.9 1.4 %collective-permute-start.8 = (bf16[1,128,512]{2,1,0:T(8,128)(2,1)S(1)}, bf16[1,128,512]{2,1,0:T(8,128)(2,1)S(1)}, u32[]{:S(2)}, u32[]{:S(2)}) collective-permute-start(bf16[1,128,512]{2,1,0:T(8,128)(2,1)S(1)} %bitcast.96), channel_id=1, source_target_pairs={{0,4},{4,0},{8,12},{12,8},{16,20},{20,16},{24,28},{28,24},{1,5},{5... | collective-permute-start | bytes 393224 | tf_op jit(solution)/shard_map/ppermute | solution.py:347
  27.3 4.0 %shard_map.90.refs_8_ = bf16[4,1024,512]{2,1,0:T(8,128)(2,1)S(1)} custom-call(s32[7]{0:T(128)S(1)} %pad_add_fusion.2.info, bf16[4,512,1024]{2,1,0:T(8,128)(2,1)S(1)} %copy-done, bf16[2,128,512]{2,1,0:T(8,128)(2,1)S(1)} %pad_maximum_fusion.refs_0_, bf16[2,128,512]{2,1,0:T(8,128)(2,1)S(1)} %collective-permute-done.1.refs_1_, ...), custom_call_target="tpu_custom_call" | custom-call | flops 2147483648 | tf_op jit(solution)/shard_map/pallas_call | solution.py:36
  31.3 1.3 %collective-permute-done.8.refs_3_ = bf16[1,128,512]{2,1,0:T(8,128)(2,1)S(1)} collective-permute-done((bf16[1,128,512]{2,1,0:T(8,128)(2,1)S(1)}, bf16[1,128,512]{2,1,0:T(8,128)(2,1)S(1)}, u32[]{:S(2)}, u32[]{:S(2)}) %collective-permute-start.8) | collective-permute-done | bytes 131104 | tf_op jit(solution)/shard_map/ppermute | solution.py:347
  32.6 0.5 collective-permute-start.10
  33.1 0.8 collective-permute-done.9.refs_4_
  34.2 0.3 collective-permute-start.16
  34.5 0.8 collective-permute-done.12.refs_7_
  35.3 3.8 %shard_map.91.weight = bf16[4,1024,512]{2,1,0:T(8,128)(2,1)S(1)} custom-call(s32[7]{0:T(128)S(1)} %pad_add_fusion.2.info, bf16[4,512,1024]{2,1,0:T(8,128)(2,1)S(1)} %copy-done, bf16[1,128,512]{2,1,0:T(8,128)(2,1)S(1)} %bitcast.95, bf16[1,128,512]{2,1,0:T(8,128)(2,1)S(1)} %collective-permute-done.5.refs_1_, bf16[1,128,512]{2,1,0:T(8,128)(2,1)S(1)} %bitcast.98, ...), custom_call_target="tpu_custom_call" | custom-call | tf_op jit(solution)/shard_map/pallas_call | solution.py:36
  39.1 3.1 %shard_map.92 = (f32[2,2,256]{2,1,0:T(2,128)S(1)}, bf16[1024,512]{1,0:T(8,128)(2,1)S(1)}, bf16[512,1024]{1,0:T(8,128)(2,1)S(1)}) custom-call(s32[7]{0:T(128)S(1)} %pad_add_fusion.2.info, f32[4,256,128]{2,1,0:T(8,128)S(1)} %get-tuple-element.79.table, f32[4,8,256]{2,1,0:T(8,128)S(1)} %get-tuple-element.80.rank, bf16[4,1024,512]{2,1,0:T(8,128)(2,1)S(1)} %shard_map.91.weight, ...), custom_call_target="tpu_custom_call" | custom-call | tf_op jit(solution)/shard_map/pallas_call | solution.py:36
  42.2 0.6 collective-permute-done.16.meta
  42.8 1.7 %collective-permute-start.18 = (bf16[1,1,128,1024]{3,2,1,0:T(8,128)(2,1)S(1)}, bf16[1,1,128,1024]{3,2,1,0:T(8,128)(2,1)S(1)}, u32[]{:S(2)}, u32[]{:S(2)}) collective-permute-start(bf16[1,1,128,1024]{3,2,1,0:T(8,128)(2,1)S(1)} %get-tuple-element.110), channel_id=1, source_target_pairs={{0,2},{1,3},{2,0},{3,1},{4,6},{5,7},{6,4},{7,5},{8,10},{9,11},{10,... | collective-permute-start | bytes 786440 | tf_op jit(solution)/shard_map/ppermute | solution.py:347
  44.6 3.1 %shard_map.93 = (f32[2,2,256]{2,1,0:T(2,128)S(1)}, bf16[1024,512]{1,0:T(8,128)(2,1)S(1)}, bf16[512,1024]{1,0:T(8,128)(2,1)S(1)}) custom-call(s32[7]{0:T(128)S(1)} %pad_add_fusion.2.info, f32[4,256,128]{2,1,0:T(8,128)S(1)} %get-tuple-element.79.table, f32[4,8,256]{2,1,0:T(8,128)S(1)} %get-tuple-element.80.rank, bf16[4,1024,512]{2,1,0:T(8,128)(2,1)S(1)} %shard_map.91.weight, ...), custom_call_target="tpu_custom_call" | custom-call | tf_op jit(solution)/shard_map/pallas_call | solution.py:36
  47.7 0.3 collective-permute-start.14
  48.1 2.5 %shard_map.94 = (f32[4,256,128]{2,1,0:T(8,128)S(1)}, f32[4,8,256]{2,1,0:T(8,128)S(1)}) custom-call(s32[7]{0:T(128)S(1)} %pad_add_fusion.2.info, s32[2,4,2,256]{3,2,1,0:T(2,128)S(1)} %collective-permute-done.16.meta, s32[4,16,32]{2,1,0:T(8,128)S(1)} %copy-done.3), custom_call_target="tpu_custom_call" | custom-call | tf_op jit(solution)/shard_map/pallas_call | solution.py:36
  50.6 2.2 %shard_map.96.refs_4_ = f32[2,1024,256]{2,1,0:T(8,128)S(1)} custom-call(s32[7]{0:T(128)S(1)} %pad_add_fusion.2.info, bf16[1024,512]{1,0:T(8,128)(2,1)S(1)} %get-tuple-element.114.refs_0_, bf16[512,1024]{1,0:T(8,128)(2,1)S(1)} %get-tuple-element.115.refs_1_, bf16[1024,512]{1,0:T(8,128)(2,1)S(1)} %get-tuple-element.116.refs_2_, ...), custom_call_target="tpu_custom_call" | custom-call | tf_op jit(solution)/shard_map/pallas_call | solution.py:36
  52.8 4.2 %shard_map.95 = (f32[3,2,256]{2,1,0:T(2,128)S(1)}, bf16[1024,768]{1,0:T(8,128)(2,1)S(1)}, bf16[768,1024]{1,0:T(8,128)(2,1)S(1)}) custom-call(s32[7]{0:T(128)S(1)} %pad_add_fusion.2.info, f32[4,256,128]{2,1,0:T(8,128)S(1)} %get-tuple-element.106.table, f32[4,8,256]{2,1,0:T(8,128)S(1)} %get-tuple-element.107.rank, bf16[4,1024,512]{2,1,0:T(8,128)(2,1)S(1)} %shard_map.91.weight, ...), custom_call_target="tpu_custom_call" | custom-call | tf_op jit(solution)/shard_map/pallas_call | solution.py:36
  57.1 1.7 %shard_map.97 = (f32[1,2,256]{2,1,0:T(2,128)S(1)}, bf16[1024,256]{1,0:T(8,128)(2,1)S(1)}, bf16[256,1024]{1,0:T(8,128)(2,1)S(1)}) custom-call(s32[7]{0:T(128)S(1)} %pad_add_fusion.2.info, f32[4,256,128]{2,1,0:T(8,128)S(1)} %get-tuple-element.106.table, f32[4,8,256]{2,1,0:T(8,128)S(1)} %get-tuple-element.107.rank, bf16[4,1024,512]{2,1,0:T(8,128)(2,1)S(1)} %shard_map.91.weight, ...), custom_call_target="tpu_custom_call" | custom-call | tf_op jit(solution)/shard_map/pallas_call | solution.py:36
  58.8 2.3 %shard_map.99 = bf16[2,1024,256]{2,1,0:T(8,128)(2,1)S(1)} custom-call(s32[7]{0:T(128)S(1)} %pad_add_fusion.2.info, bf16[1024,768]{1,0:T(8,128)(2,1)S(1)} %get-tuple-element.121.refs_4_.refs_0_, bf16[768,1024]{1,0:T(8,128)(2,1)S(1)} %get-tuple-element.122.refs_5_.refs_1_, bf16[1024,256]{1,0:T(8,128)(2,1)S(1)} %get-tuple-element.123.refs_6_.refs_2_, ...), custom_call_target="tpu_custom_call" | custom-call | tf_op jit(solution)/shard_map/pallas_call | solution.py:36
  61.1 0.3 collective-permute-start.22
  61.4 3.5 %shard_map.98 = f32[2,1024,256]{2,1,0:T(8,128)S(1)} custom-call(s32[7]{0:T(128)S(1)} %pad_add_fusion.2.info, bf16[1024,512]{1,0:T(8,128)(2,1)S(1)} %get-tuple-element.114.refs_0_, bf16[512,1024]{1,0:T(8,128)(2,1)S(1)} %get-tuple-element.115.refs_1_, bf16[1024,512]{1,0:T(8,128)(2,1)S(1)} %get-tuple-element.116.refs_2_, ...), custom_call_target="tpu_custom_call" | custom-call | flops 34359738368 | tf_op jit(solution)/shard_map/pallas_call | solution.py:36
  65.1 1.8 %collective-permute-start.25 = (bf16[4,128,256]{2,1,0:T(8,128)(2,1)S(1)}, bf16[4,128,256]{2,1,0:T(8,128)(2,1)S(1)}, u32[]{:S(2)}, u32[]{:S(2)}) collective-permute-start(bf16[4,128,256]{2,1,0:T(8,128)(2,1)S(1)} %get-tuple-element.136), channel_id=1, source_target_pairs={{0,2},{1,3},{2,0},{3,1},{4,6},{5,7},{6,4},{7,5},{8,10},{9,11},{10,... | collective-permute-start | bytes 786440 | tf_op jit(solution)/shard_map/ppermute | solution.py:353
  66.9 1.4 %collective-permute-start.24 = (bf16[4,128,256]{2,1,0:T(8,128)(2,1)S(1)}, bf16[4,128,256]{2,1,0:T(8,128)(2,1)S(1)}, u32[]{:S(2)}, u32[]{:S(2)}) collective-permute-start(bf16[4,128,256]{2,1,0:T(8,128)(2,1)S(1)} %get-tuple-element.135), channel_id=1, source_target_pairs={{0,6},{1,7},{2,4},{3,5},{4,2},{5,3},{6,0},{7,1},{8,14},{9,15},{10,... | collective-permute-start | bytes 786440 | tf_op jit(solution)/shard_map/ppermute | solution.py:353
  68.3 0.3 collective-permute-start.23
  68.7 0.8 collective-permute-start.21
  69.5 9.8 %collective-permute-done.25 = bf16[4,128,256]{2,1,0:T(8,128)(2,1)S(1)} collective-permute-done((bf16[4,128,256]{2,1,0:T(8,128)(2,1)S(1)}, bf16[4,128,256]{2,1,0:T(8,128)(2,1)S(1)}, u32[]{:S(2)}, u32[]{:S(2)}) %collective-permute-start.25) | collective-permute-done | bytes 262176 | tf_op jit(solution)/shard_map/ppermute | solution.py:353
  79.3 1.7 %collective-permute-start.20 = (f32[4,256]{1,0:T(4,128)S(1)}, f32[4,256]{1,0:T(4,128)S(1)}, u32[]{:S(2)}, u32[]{:S(2)}) collective-permute-start(f32[4,256]{1,0:T(4,128)S(1)} %bitcast.108), channel_id=1, source_target_pairs={{0,2},{1,3},{2,0},{3,1},{4,6},{5,7},{6,4},{7,5},{8,10},{9,11},{10,... | collective-permute-start | bytes 12296 | tf_op jit(solution)/shard_map/ppermute | solution.py:347
  81.3 3.7 %collective-permute-start.28 = (bf16[128,256]{1,0:T(8,128)(2,1)S(1)}, bf16[128,256]{1,0:T(8,128)(2,1)S(1)}, u32[]{:S(2)}, u32[]{:S(2)}) collective-permute-start(bf16[128,256]{1,0:T(8,128)(2,1)S(1)} %get-tuple-element.138), channel_id=1, source_target_pairs={{0,24},{4,28},{8,16},{12,20},{16,8},{20,12},{24,0},{28,4},{1,25},{... | collective-permute-start | bytes 196616 | tf_op jit(solution)/shard_map/ppermute | solution.py:347
  84.9 0.8 collective-permute-start.26
  85.7 0.6 fusion.19
  86.3 1.5 %collective-permute-done.28 = bf16[128,256]{1,0:T(8,128)(2,1)S(1)} collective-permute-done((bf16[128,256]{1,0:T(8,128)(2,1)S(1)}, bf16[128,256]{1,0:T(8,128)(2,1)S(1)}, u32[]{:S(2)}, u32[]{:S(2)}) %collective-permute-start.28) | collective-permute-done | bytes 65568 | tf_op jit(solution)/shard_map/ppermute | solution.py:347
  87.8 2.5 %collective-permute-done.27 = bf16[128,256]{1,0:T(8,128)(2,1)S(1)} collective-permute-done((bf16[128,256]{1,0:T(8,128)(2,1)S(1)}, bf16[128,256]{1,0:T(8,128)(2,1)S(1)}, u32[]{:S(2)}, u32[]{:S(2)}) %collective-permute-start.27) | collective-permute-done | bytes 65568 | tf_op jit(solution)/shard_map/ppermute | solution.py:347
  90.3 0.7 fusion.11
  (56 shorter events, 1.5 us)
Async XLA Ops:
  1.4 1.6 %copy-start.1 = (bf16[4,256,1024]{2,1,0:T(8,128)(2,1)S(1)}, bf16[4,256,1024]{2,1,0:T(8,128)(2,1)}, u32[]{:S(2)}) copy-start(bf16[4,256,1024]{2,1,0:T(8,128)(2,1)} %words.3) | copy-start | bytes 6291460
  3.0 0.7 copy-start.4
  3.7 4.3 %copy-start.5 = (bf16[128,1024]{1,0:T(8,128)(2,1)S(1)}, bf16[128,1024]{1,0:T(8,128)(2,1)}, u32[]{:S(2)}) copy-start(bf16[128,1024]{1,0:T(8,128)(2,1)} %proj) | copy-start | bytes 786436
  4.9 8.1 %copy-start.6 = (s32[4,256]{1,0:T(4,128)S(1)}, s32[4,256]{1,0:T(4,128)}, u32[]{:S(2)}) copy-start(s32[4,256]{1,0:T(4,128)} %param.11) | copy-start | bytes 12292
  5.0 8.2 %copy-start.2 = (bf16[4,256,1024]{2,1,0:T(8,128)(2,1)S(1)}, bf16[4,256,1024]{2,1,0:T(8,128)(2,1)}, u32[]{:S(2)}) copy-start(bf16[4,256,1024]{2,1,0:T(8,128)(2,1)} %words.3) | copy-start | bytes 6291460
  5.0 37.8 %collective-permute-start.15 = (bf16[2,3,128,1024]{3,2,1,0:T(8,128)(2,1)S(1)}, bf16[2,3,128,1024]{3,2,1,0:T(8,128)(2,1)S(1)}, u32[]{:S(2)}, u32[]{:S(2)}) collective-permute-start(bf16[2,3,128,1024]{3,2,1,0:T(8,128)(2,1)S(1)} %shard_map.86), channel_id=1, source_target_pairs={{0,2},{1,3},{2,0},{3,1},{4,6},{5,7},{6,4},{7,5},{8,10},{9,11},{10,... | collective-permute-start | bytes 4718600 | tf_op jit(solution)/shard_map/ppermute | solution.py:347
  8.6 6.5 %collective-permute-start = (bf16[128,512]{1,0:T(8,128)(2,1)S(1)}, bf16[128,512]{1,0:T(8,128)(2,1)S(1)}, u32[]{:S(2)}, u32[]{:S(2)}) collective-permute-start(bf16[128,512]{1,0:T(8,128)(2,1)S(1)} %shard_map.87), channel_id=1, source_target_pairs={{0,8},{4,12},{8,0},{12,4},{16,24},{20,28},{24,16},{28,20},{1,9},{5... | collective-permute-start | bytes 393224 | tf_op jit(solution)/shard_map/ppermute | solution.py:347
  10.2 12.6 %collective-permute-start.2 = (bf16[128,512]{1,0:T(8,128)(2,1)S(1)}, bf16[128,512]{1,0:T(8,128)(2,1)S(1)}, u32[]{:S(2)}, u32[]{:S(2)}) collective-permute-start(bf16[128,512]{1,0:T(8,128)(2,1)S(1)} %shard_map.87), channel_id=1, source_target_pairs={{0,16},{4,20},{8,24},{12,28},{16,0},{20,4},{24,8},{28,12},{1,17},{... | collective-permute-start | bytes 393224 | tf_op jit(solution)/shard_map/ppermute | solution.py:347
  12.8 10.1 %collective-permute-start.3 = (bf16[128,512]{1,0:T(8,128)(2,1)S(1)}, bf16[128,512]{1,0:T(8,128)(2,1)S(1)}, u32[]{:S(2)}, u32[]{:S(2)}) collective-permute-start(bf16[128,512]{1,0:T(8,128)(2,1)S(1)} %shard_map.87), channel_id=1, source_target_pairs={{0,24},{4,28},{8,16},{12,20},{16,8},{20,12},{24,0},{28,4},{1,25},{... | collective-permute-start | bytes 393224 | tf_op jit(solution)/shard_map/ppermute | solution.py:347
  13.0 3.8 %copy-start.3 = (s32[4,16,32]{2,1,0:T(8,128)S(1)}, s32[4,16,32]{2,1,0:T(8,128)}, u32[]{:S(2)}) copy-start(s32[4,16,32]{2,1,0:T(8,128)} %flags.3) | copy-start | bytes 24580
  13.1 2.2 %collective-permute-start.4 = (s32[4,2,256]{2,1,0:T(2,128)S(1)}, s32[4,2,256]{2,1,0:T(2,128)S(1)}, u32[]{:S(2)}, u32[]{:S(2)}) collective-permute-start(s32[4,2,256]{2,1,0:T(2,128)S(1)} %get-tuple-element.143), channel_id=1, source_target_pairs={{0,1},{1,0},{2,3},{3,2},{4,5},{5,4},{6,7},{7,6},{8,9},{9,8},{10,11... | collective-permute-start | bytes 24584 | tf_op jit(solution)/shard_map/ppermute | solution.py:347
  15.1 24.1 %collective-permute-start.13 = (bf16[1,4,128,1024]{3,2,1,0:T(8,128)(2,1)S(1)}, bf16[1,4,128,1024]{3,2,1,0:T(8,128)(2,1)S(1)}, u32[]{:S(2)}, u32[]{:S(2)}) collective-permute-start(bf16[1,4,128,1024]{3,2,1,0:T(8,128)(2,1)S(1)} %get-tuple-element.96), channel_id=1, source_target_pairs={{0,1},{1,0},{2,3},{3,2},{4,5},{5,4},{6,7},{7,6},{8,9},{9,8},{10,11... | collective-permute-start | bytes 3145736 | tf_op jit(solution)/shard_map/ppermute | solution.py:347
  15.3 8.6 %collective-permute-start.1 = (bf16[2,128,512]{2,1,0:T(8,128)(2,1)S(1)}, bf16[2,128,512]{2,1,0:T(8,128)(2,1)S(1)}, u32[]{:S(2)}, u32[]{:S(2)}) collective-permute-start(bf16[2,128,512]{2,1,0:T(8,128)(2,1)S(1)} %pad_maximum_fusion.refs_0_), channel_id=1, source_target_pairs={{0,4},{4,0},{8,12},{12,8},{16,20},{20,16},{24,28},{28,24},{1,5},{5... | collective-permute-start | bytes 786440 | tf_op jit(solution)/shard_map/ppermute | solution.py:347
  16.8 10.5 %copy-start = (bf16[4,512,1024]{2,1,0:T(8,128)(2,1)S(1)}, bf16[4,512,1024]{2,1,0:T(8,128)(2,1)}, u32[]{:S(2)}) copy-start(bf16[4,512,1024]{2,1,0:T(8,128)(2,1)} %patches.11) | copy-start | bytes 12582916
  23.9 2.0 %collective-permute-start.6 = (bf16[2,128,512]{2,1,0:T(8,128)(2,1)S(1)}, bf16[2,128,512]{2,1,0:T(8,128)(2,1)S(1)}, u32[]{:S(2)}, u32[]{:S(2)}) collective-permute-start(bf16[2,128,512]{2,1,0:T(8,128)(2,1)S(1)} %pad_maximum_fusion.refs_0_), channel_id=1, source_target_pairs={{0,1},{1,0},{2,3},{3,2},{4,5},{5,4},{6,7},{7,6},{8,9},{9,8},{10,11... | collective-permute-start | bytes 786440 | tf_op jit(solution)/shard_map/ppermute | solution.py:347
  23.9 2.0 %collective-permute-start.7 = (bf16[2,128,512]{2,1,0:T(8,128)(2,1)S(1)}, bf16[2,128,512]{2,1,0:T(8,128)(2,1)S(1)}, u32[]{:S(2)}, u32[]{:S(2)}) collective-permute-start(bf16[2,128,512]{2,1,0:T(8,128)(2,1)S(1)} %collective-permute-done.1.refs_1_), channel_id=1, source_target_pairs={{0,1},{1,0},{2,3},{3,2},{4,5},{5,4},{6,7},{7,6},{8,9},{9,8},{10,11... | collective-permute-start | bytes 786440 | tf_op jit(solution)/shard_map/ppermute | solution.py:347
  24.4 6.9 %collective-permute-start.5 = (bf16[1,128,512]{2,1,0:T(8,128)(2,1)S(1)}, bf16[1,128,512]{2,1,0:T(8,128)(2,1)S(1)}, u32[]{:S(2)}, u32[]{:S(2)}) collective-permute-start(bf16[1,128,512]{2,1,0:T(8,128)(2,1)S(1)} %bitcast.93), channel_id=1, source_target_pairs={{0,4},{4,0},{8,12},{12,8},{16,20},{20,16},{24,28},{28,24},{1,5},{5... | collective-permute-start | bytes 393224 | tf_op jit(solution)/shard_map/ppermute | solution.py:347
  25.9 6.7 %collective-permute-start.8 = (bf16[1,128,512]{2,1,0:T(8,128)(2,1)S(1)}, bf16[1,128,512]{2,1,0:T(8,128)(2,1)S(1)}, u32[]{:S(2)}, u32[]{:S(2)}) collective-permute-start(bf16[1,128,512]{2,1,0:T(8,128)(2,1)S(1)} %bitcast.96), channel_id=1, source_target_pairs={{0,4},{4,0},{8,12},{12,8},{16,20},{20,16},{24,28},{28,24},{1,5},{5... | collective-permute-start | bytes 393224 | tf_op jit(solution)/shard_map/ppermute | solution.py:347
  32.6 1.3 %collective-permute-start.9 = (bf16[1,128,512]{2,1,0:T(8,128)(2,1)S(1)}, bf16[1,128,512]{2,1,0:T(8,128)(2,1)S(1)}, u32[]{:S(2)}, u32[]{:S(2)}) collective-permute-start(bf16[1,128,512]{2,1,0:T(8,128)(2,1)S(1)} %bitcast.94), channel_id=1, source_target_pairs={{0,1},{1,0},{2,3},{3,2},{4,5},{5,4},{6,7},{7,6},{8,9},{9,8},{10,11... | collective-permute-start | bytes 393224 | tf_op jit(solution)/shard_map/ppermute | solution.py:347
  32.6 1.5 %collective-permute-start.10 = (bf16[1,128,512]{2,1,0:T(8,128)(2,1)S(1)}, bf16[1,128,512]{2,1,0:T(8,128)(2,1)S(1)}, u32[]{:S(2)}, u32[]{:S(2)}) collective-permute-start(bf16[1,128,512]{2,1,0:T(8,128)(2,1)S(1)} %collective-permute-done.5.refs_1_), channel_id=1, source_target_pairs={{0,1},{1,0},{2,3},{3,2},{4,5},{5,4},{6,7},{7,6},{8,9},{9,8},{10,11... | collective-permute-start | bytes 393224 | tf_op jit(solution)/shard_map/ppermute | solution.py:347
  33.1 1.3 %collective-permute-start.11 = (bf16[1,128,512]{2,1,0:T(8,128)(2,1)S(1)}, bf16[1,128,512]{2,1,0:T(8,128)(2,1)S(1)}, u32[]{:S(2)}, u32[]{:S(2)}) collective-permute-start(bf16[1,128,512]{2,1,0:T(8,128)(2,1)S(1)} %bitcast.97), channel_id=1, source_target_pairs={{0,1},{1,0},{2,3},{3,2},{4,5},{5,4},{6,7},{7,6},{8,9},{9,8},{10,11... | collective-permute-start | bytes 393224 | tf_op jit(solution)/shard_map/ppermute | solution.py:347
  34.0 1.3 %collective-permute-start.12 = (bf16[1,128,512]{2,1,0:T(8,128)(2,1)S(1)}, bf16[1,128,512]{2,1,0:T(8,128)(2,1)S(1)}, u32[]{:S(2)}, u32[]{:S(2)}) collective-permute-start(bf16[1,128,512]{2,1,0:T(8,128)(2,1)S(1)} %collective-permute-done.8.refs_3_), channel_id=1, source_target_pairs={{0,1},{1,0},{2,3},{3,2},{4,5},{5,4},{6,7},{7,6},{8,9},{9,8},{10,11... | collective-permute-start | bytes 393224 | tf_op jit(solution)/shard_map/ppermute | solution.py:347
  34.2 8.6 %collective-permute-start.16 = (s32[2,4,2,256]{3,2,1,0:T(2,128)S(1)}, s32[2,4,2,256]{3,2,1,0:T(2,128)S(1)}, u32[]{:S(2)}, u32[]{:S(2)}) collective-permute-start(s32[2,4,2,256]{3,2,1,0:T(2,128)S(1)} %pad_add_fusion.meta), channel_id=1, source_target_pairs={{0,2},{1,3},{2,0},{3,1},{4,6},{5,7},{6,4},{7,5},{8,10},{9,11},{10,... | collective-permute-start | bytes 49160 | tf_op jit(solution)/shard_map/ppermute | solution.py:347
  42.7 10.1 %collective-permute-start.17 = (bf16[2,3,128,1024]{3,2,1,0:T(8,128)(2,1)S(1)}, bf16[2,3,128,1024]{3,2,1,0:T(8,128)(2,1)S(1)}, u32[]{:S(2)}, u32[]{:S(2)}) collective-permute-start(bf16[2,3,128,1024]{3,2,1,0:T(8,128)(2,1)S(1)} %collective-permute-done.15.refs_0_), channel_id=1, source_target_pairs={{0,1},{1,0},{2,3},{3,2},{4,5},{5,4},{6,7},{7,6},{8,9},{9,8},{10,11... | collective-permute-start | bytes 4718600 | tf_op jit(solution)/shard_map/ppermute | solution.py:347
  42.8 14.3 %collective-permute-start.18 = (bf16[1,1,128,1024]{3,2,1,0:T(8,128)(2,1)S(1)}, bf16[1,1,128,1024]{3,2,1,0:T(8,128)(2,1)S(1)}, u32[]{:S(2)}, u32[]{:S(2)}) collective-permute-start(bf16[1,1,128,1024]{3,2,1,0:T(8,128)(2,1)S(1)} %get-tuple-element.110), channel_id=1, source_target_pairs={{0,2},{1,3},{2,0},{3,1},{4,6},{5,7},{6,4},{7,5},{8,10},{9,11},{10,... | collective-permute-start | bytes 786440 | tf_op jit(solution)/shard_map/ppermute | solution.py:347
  44.5 12.6 %collective-permute-start.19 = (bf16[1,1,128,1024]{3,2,1,0:T(8,128)(2,1)S(1)}, bf16[1,1,128,1024]{3,2,1,0:T(8,128)(2,1)S(1)}, u32[]{:S(2)}, u32[]{:S(2)}) collective-permute-start(bf16[1,1,128,1024]{3,2,1,0:T(8,128)(2,1)S(1)} %get-tuple-element.111), channel_id=1, source_target_pairs={{0,3},{1,2},{2,1},{3,0},{4,7},{5,6},{6,5},{7,4},{8,11},{9,10},{10,... | collective-permute-start | bytes 786440 | tf_op jit(solution)/shard_map/ppermute | solution.py:347
  47.7 37.2 %collective-permute-start.14 = (f32[4,256]{1,0:T(4,128)S(1)}, f32[4,256]{1,0:T(4,128)S(1)}, u32[]{:S(2)}, u32[]{:S(2)}) collective-permute-start(f32[4,256]{1,0:T(4,128)S(1)} %fusion.20), channel_id=1, source_target_pairs={{0,1},{1,0},{2,3},{3,2},{4,5},{5,4},{6,7},{7,6},{8,9},{9,8},{10,11... | collective-permute-start | bytes 12296 | tf_op jit(solution)/shard_map/ppermute | solution.py:347
  61.1 3.8 %collective-permute-start.22 = (bf16[2,1024,256]{2,1,0:T(8,128)(2,1)S(1)}, bf16[2,1024,256]{2,1,0:T(8,128)(2,1)S(1)}, u32[]{:S(2)}, u32[]{:S(2)}) collective-permute-start(bf16[2,1024,256]{2,1,0:T(8,128)(2,1)S(1)} %shard_map.99), channel_id=1, source_target_pairs={{0,1},{1,0},{2,3},{3,2},{4,5},{5,4},{6,7},{7,6},{8,9},{9,8},{10,11... | collective-permute-start | bytes 3145736 | tf_op jit(solution)/shard_map/ppermute | solution.py:347
  65.1 14.2 %collective-permute-start.25 = (bf16[4,128,256]{2,1,0:T(8,128)(2,1)S(1)}, bf16[4,128,256]{2,1,0:T(8,128)(2,1)S(1)}, u32[]{:S(2)}, u32[]{:S(2)}) collective-permute-start(bf16[4,128,256]{2,1,0:T(8,128)(2,1)S(1)} %get-tuple-element.136), channel_id=1, source_target_pairs={{0,2},{1,3},{2,0},{3,1},{4,6},{5,7},{6,4},{7,5},{8,10},{9,11},{10,... | collective-permute-start | bytes 786440 | tf_op jit(solution)/shard_map/ppermute | solution.py:353
  66.9 14.2 %collective-permute-start.24 = (bf16[4,128,256]{2,1,0:T(8,128)(2,1)S(1)}, bf16[4,128,256]{2,1,0:T(8,128)(2,1)S(1)}, u32[]{:S(2)}, u32[]{:S(2)}) collective-permute-start(bf16[4,128,256]{2,1,0:T(8,128)(2,1)S(1)} %get-tuple-element.135), channel_id=1, source_target_pairs={{0,6},{1,7},{2,4},{3,5},{4,2},{5,3},{6,0},{7,1},{8,14},{9,15},{10,... | collective-permute-start | bytes 786440 | tf_op jit(solution)/shard_map/ppermute | solution.py:353
  68.3 12.7 %collective-permute-start.23 = (bf16[4,128,256]{2,1,0:T(8,128)(2,1)S(1)}, bf16[4,128,256]{2,1,0:T(8,128)(2,1)S(1)}, u32[]{:S(2)}, u32[]{:S(2)}) collective-permute-start(bf16[4,128,256]{2,1,0:T(8,128)(2,1)S(1)} %get-tuple-element.134), channel_id=1, source_target_pairs={{0,4},{1,5},{2,6},{3,7},{4,0},{5,1},{6,2},{7,3},{8,12},{9,13},{10,... | collective-permute-start | bytes 786440 | tf_op jit(solution)/shard_map/ppermute | solution.py:353
  68.7 17.0 %collective-permute-start.21 = (f32[4,256]{1,0:T(4,128)S(1)}, f32[4,256]{1,0:T(4,128)S(1)}, u32[]{:S(2)}, u32[]{:S(2)}) collective-permute-start(f32[4,256]{1,0:T(4,128)S(1)} %bitcast.107), channel_id=1, source_target_pairs={{0,3},{1,2},{2,1},{3,0},{4,7},{5,6},{6,5},{7,4},{8,11},{9,10},{10,... | collective-permute-start | bytes 12296 | tf_op jit(solution)/shard_map/ppermute | solution.py:347
  79.3 6.4 %collective-permute-start.20 = (f32[4,256]{1,0:T(4,128)S(1)}, f32[4,256]{1,0:T(4,128)S(1)}, u32[]{:S(2)}, u32[]{:S(2)}) collective-permute-start(f32[4,256]{1,0:T(4,128)S(1)} %bitcast.108), channel_id=1, source_target_pairs={{0,2},{1,3},{2,0},{3,1},{4,6},{5,7},{6,4},{7,5},{8,10},{9,11},{10,... | collective-permute-start | bytes 12296 | tf_op jit(solution)/shard_map/ppermute | solution.py:347
  81.3 6.5 %collective-permute-start.28 = (bf16[128,256]{1,0:T(8,128)(2,1)S(1)}, bf16[128,256]{1,0:T(8,128)(2,1)S(1)}, u32[]{:S(2)}, u32[]{:S(2)}) collective-permute-start(bf16[128,256]{1,0:T(8,128)(2,1)S(1)} %get-tuple-element.138), channel_id=1, source_target_pairs={{0,24},{4,28},{8,16},{12,20},{16,8},{20,12},{24,0},{28,4},{1,25},{... | collective-permute-start | bytes 196616 | tf_op jit(solution)/shard_map/ppermute | solution.py:347
  84.9 5.3 %collective-permute-start.27 = (bf16[128,256]{1,0:T(8,128)(2,1)S(1)}, bf16[128,256]{1,0:T(8,128)(2,1)S(1)}, u32[]{:S(2)}, u32[]{:S(2)}) collective-permute-start(bf16[128,256]{1,0:T(8,128)(2,1)S(1)} %get-tuple-element.139), channel_id=1, source_target_pairs={{0,16},{4,20},{8,24},{12,28},{16,0},{20,4},{24,8},{28,12},{1,17},{... | collective-permute-start | bytes 196616 | tf_op jit(solution)/shard_map/ppermute | solution.py:347
  84.9 5.3 %collective-permute-start.26 = (bf16[128,256]{1,0:T(8,128)(2,1)S(1)}, bf16[128,256]{1,0:T(8,128)(2,1)S(1)}, u32[]{:S(2)}, u32[]{:S(2)}) collective-permute-start(bf16[128,256]{1,0:T(8,128)(2,1)S(1)} %get-tuple-element.137), channel_id=1, source_target_pairs={{0,8},{4,12},{8,0},{12,4},{16,24},{20,28},{24,16},{28,20},{1,9},{5... | collective-permute-start | bytes 196616 | tf_op jit(solution)/shard_map/ppermute | solution.py:347

commit v12 on v11

--- a/solution.py
+++ b/solution.py
@@ -46,6 +46,18 @@
         compiler_params=pltpu.CompilerParams(vmem_limit_bytes=VMEM_LIMIT),
         cost_estimate=pl.CostEstimate(flops=flops, bytes_accessed=0, transcendentals=0),
         input_output_aliases=aliases,
+    )(*operands)
+
+
+def call_whole(kernel, out_shape, operands, flops=0):
+    vmem = pl.BlockSpec(memory_space=pltpu.VMEM)
+    return pl.pallas_call(
+        kernel,
+        in_specs=[pl.BlockSpec(memory_space=pltpu.SMEM)] + [vmem] * (len(operands) - 1),
+        out_specs=[vmem] * len(out_shape),
+        out_shape=out_shape,
+        compiler_params=pltpu.CompilerParams(vmem_limit_bytes=VMEM_LIMIT),
+        cost_estimate=pl.CostEstimate(flops=flops, bytes_accessed=0, transcendentals=0),
     )(*operands)
 
 
@@ -105,14 +117,8 @@
         jax.ShapeDtypeStruct((len(offsets), n_pages, cap, width), BF16)
         for offsets, _, n_pages in plan
     ]
-    return call(
-        functools.partial(dispatch_kernel, plan, cap),
-        1,
-        [all_of(routes), all_of(words)],
-        [all_of(o) for o in out],
-        out,
-        (info, routes, words),
-        flops=flops,
+    return call_whole(
+        functools.partial(dispatch_kernel, plan, cap), out, (info, routes, words), flops
     )
 
 
@@ -165,33 +171,23 @@
         jax.ShapeDtypeStruct((pages, n_homes * cap, 128), F32),
         jax.ShapeDtypeStruct((pages, pad_rows(n_homes), wdev), F32),
     ]
-    return call(
+    return call_whole(
         functools.partial(table_kernel, offsets, cap, pps // MARGIN_BLOCK_SIZE),
-        1,
-        [all_of(meta), all_of(flags)],
-        [all_of(o) for o in out],
         out,
         (info, meta, flags),
-        flops=flops,
+        flops,
     )
 
 
 def half_kernel(info, proj, out):
-    out[...] = proj[...]
-
-
-def half_of(info, proj, half):
+    half = out.shape[1]
+    out[...] = proj[:, pl.ds(pl.multiple_of(info[CORE] * half, half), half)]
+
+
+def half_of(info, proj):
     rows, width = proj.shape
-    out = jax.ShapeDtypeStruct((rows, half), BF16)
-    return call(
-        half_kernel,
-        1,
-        [pl.BlockSpec((rows, half), lambda p, info: (0, info[CORE] if width > half else 0))],
-        all_of(out),
-        out,
-        (info, proj),
-        flops=MUCH,
-    )
+    out = [jax.ShapeDtypeStruct((rows, width // 2), BF16)]
+    return call_whole(half_kernel, out, (info, proj), MUCH)[0]
 
 
 def weights_kernel(offsets, info, patches, *refs):
@@ -308,38 +304,27 @@
     )
 
 
-def gradient_kernel(n_pairs, info, *refs):
-    pairs, (*before, out) = refs[: 2 * n_pairs], refs[2 * n_pairs :]
-    got = sum(dot(pairs[i][...], pairs[i + 1][...]) for i in range(0, len(pairs), 2))
-    for part in before:
-        got = got + part[0]
-    out[0] = got.astype(out.dtype)
-
-
-def gradient(info, dtype, n_y, pairs, cores, before=(), flops=0):
+def gradient_kernel(core, info, *refs):
+    *pairs, out = refs
+    n_y, _, wcol = out.shape
+
+    def block(y, _):
+        column = pl.multiple_of((2 * y + jnp.bitwise_xor(info[CORE], core)) * wcol, wcol)
+        got = sum(
+            dot(pairs[i][...], pairs[i + 1][:, pl.ds(column, wcol)])
+            for i in range(0, len(pairs), 2)
+        )
+        out[y] = got.astype(out.dtype)
+        return 0
+
+    lax.fori_loop(0, n_y, block, 0)
+
+
+def gradient(info, core, dtype, n_y, pairs, flops=0):
     width = pairs[0][0].shape[0]
-    wcol = width // (2 * n_y)
-    out = jax.ShapeDtypeStruct((len(cores) * n_y, width, wcol), dtype)
-
-    def column(i, info):
-        core = cores[0] if len(cores) == 1 else jnp.where(i < n_y, cores[0], cores[1])
-        return 0, 2 * (i % n_y) + jnp.bitwise_xor(info[CORE], core)
-
-    specs = []
-    for x_t, dq in pairs:
-        specs += [all_of(x_t), pl.BlockSpec((dq.shape[0], wcol), column)]
-    if before:
-        first = before[1]
-        specs.append(pl.BlockSpec((1, width, wcol), lambda i, info: (first + i, 0, 0)))
-    return call(
-        functools.partial(gradient_kernel, len(pairs)),
-        len(cores) * n_y,
-        specs,
-        page_of(out),
-        out,
-        (info, *(x for pair in pairs for x in pair), *before[:1]),
-        flops=flops,
-    )
+    out = [jax.ShapeDtypeStruct((n_y, width, width // (2 * n_y)), dtype)]
+    operands = (info, *(x for pair in pairs for x in pair))
+    return call_whole(functools.partial(gradient_kernel, core), out, operands, flops)[0]
 
 
 def exchange(x, axis, offset):
@@ -388,7 +373,7 @@
     )
     info, proj, both = lax.optimization_barrier((info, proj, both))
     both = [exchange(rows, "seq", 2 * (k + 1)) for k, rows in enumerate(both)]
-    piece = half_of(info, proj, width // 2)
+    piece = half_of(info, proj)
     pieces = [piece] + [exchange(piece, "dp", 2 * k) for k in range(1, n_high)]
     group = n_high // 2
     stay, across, *rest = dispatch(
@@ -439,21 +424,21 @@
     pair_1, meta_far = lax.optimization_barrier((pair_1, meta_far))
     table_far = tables(info, meta_far, flags, far, cap, pps)
     loss_a, *pair_a = run(table_far, first, 0, split)
-    before = gradient(info, F32, n_y, [pair_0, pair_1], (1,))
-    rest, pair_a, before = lax.optimization_barrier((rest, pair_a, before))
+    rest, pair_a = lax.optimization_barrier((rest, pair_a))
     loss_b, *pair_b = run(table_far, [(rows, 0) for rows in rest], split, pages - split)
     losses = jnp.concatenate([loss_a, loss_b], axis=0)
     word_loss = near_loss + [exchange(losses[:, i], "seq", r) for i, r in enumerate(far)]
 
-    sent = gradient(info, BF16, n_y, [pair_a, pair_b], (1,), (before, 0))
-    kept = gradient(info, F32, n_y, [pair_0, pair_1, pair_a, pair_b], (0,), flops=MUCH)
+    pairs = [pair_0, pair_1, pair_a, pair_b]
+    sent = gradient(info, 1, BF16, n_y, pairs)
+    kept = gradient(info, 0, F32, n_y, pairs, MUCH)
     form = (n_y, n_high, 2, shard_rows, width // n_seq)
     terms = [kept.reshape(form), exchange(sent, "seq", 1).reshape(form)]
     part = lambda i, j: sum(
         pick(t, (own["y"][i], None, own["low"][j])).astype(F32) for t in terms
     )
     total = part(0, 0)
-    for i, j in [(0, 1)] + [(i, j) for i in range(1, n_y) for j in (1, 0)]:
+    for i, j in [(i, j) for i in range(1, n_y) for j in (0, 1)] + [(0, 1)]:
         total = total + exchange_both(part(i, j).astype(BF16), j, 2 * i)
     grad = pick(total, (own["high"][0],))
     for k in range(1, n_high):

time: 91.1 us -> 92.3 us (1.013)
  waiting for transfers between devices: 22.3 us -> 25.2 us
  Pallas kernels: 36.2 us -> 34.4 us
    pallas_call x14 -> x6, Pallas kernels: 36.2 us -> 19.8 us  [call(): pl.pallas_call(kernel, grid_spec=pltpu.PrefetchScalarGridSpec(num_scalar_...]
    pallas_call x0 -> x7, Pallas kernels: none -> 14.6 us  [call_whole(): pl.pallas_call(kernel, in_specs=[pl.BlockSpec(memory_space=pltpu.SMEM)] +...]
    ppermute x26, waiting for transfers between devices: 12.5 us -> 15.9 us  [exchange(): return lax.ppermute(x, axis, [(i, i ^ offset) for i in range(n)])]
  transfers between devices with their start and end apart: 29 -> 29, of which waited for: 10 -> 12; matrix products, arithmetic and copies ran while one was open for 1% -> 1% of each run, Pallas kernels for 38% -> 36%
where the time goes in v12:
time: 92.3 us; the launch traced here: 92.1 us
  Pallas kernels  34.4 us (37%)
  starting transfers between devices  26.7 us (29%)
  waiting for transfers between devices  25.2 us (27%)
  other arithmetic  2.52 us (3%)
  local copies, waits for them, and re-layouts  2.37 us (3%)
    ppermute x26, starting transfers between devices, exchange(): return lax.ppermute(x, axis, [(i, i ^ offset) for i in range(n)])  23.1 us
    pallas_call x6, Pallas kernels, call(): pl.pallas_call(kernel, grid_spec=pltpu.PrefetchScalarGridSpec(num_scalar_...  19.8 us
    ppermute x26, waiting for transfers between devices, exchange(): return lax.ppermute(x, axis, [(i, i ^ offset) for i in range(n)])  15.9 us
    pallas_call x7, Pallas kernels, call_whole(): pl.pallas_call(kernel, in_specs=[pl.BlockSpec(memory_space=pltpu.SMEM)] +...  14.6 us
    ppermute x3, waiting for transfers between devices, exchange_both(): lax.ppermute(x, ('dp', 'seq'), [(i, i ^ dp * n_seq + seq) for i in range(...  9.32 us
    ppermute x3, starting transfers between devices, exchange_both(): lax.ppermute(x, ('dp', 'seq'), [(i, i ^ dp * n_seq + seq) for i in range(...  3.55 us
    unnamed x17, local copies, waits for them, and re-layouts  2.31 us
  transfers between devices with their start and end apart: 29, of which 12 were waited for; matrix products, arithmetic and copies ran while one was open for 1% of the time, Pallas kernels for 36%

profile of v12, /device:TPU:0, one launch (start us, length us, event | category | flops | bytes accessed | tf_op | source)
XLA Modules:
  0.0 92.1 jit_solution(18029275266404953329)
XLA Ops:
  0.6 0.7 pad_add_fusion.2.info
  1.4 1.6 %copy-done.1 = bf16[4,256,1024]{2,1,0:T(8,128)(2,1)S(1)} copy-done((bf16[4,256,1024]{2,1,0:T(8,128)(2,1)S(1)}, bf16[4,256,1024]{2,1,0:T(8,128)(2,1)}, u32[]{:S(2)}) %copy-start.1) | copy-done | bytes 2097176
  3.0 0.7 copy-done.4
  3.7 1.3 %shard_map.86 = bf16[2,3,128,1024]{3,2,1,0:T(8,128)(2,1)S(1)} custom-call(s32[7]{0:T(128)S(1)} %pad_add_fusion.2.info, s32[4,1,256]{2,1,0:T(1,128)S(1)} %bitcast.100, bf16[4,256,1024]{2,1,0:T(8,128)(2,1)S(1)} %copy-done.1), custom_call_target="tpu_custom_call" | custom-call | tf_op jit(solution)/shard_map/pallas_call | solution.py:54
  5.0 3.0 %collective-permute-start.15 = (bf16[2,3,128,1024]{3,2,1,0:T(8,128)(2,1)S(1)}, bf16[2,3,128,1024]{3,2,1,0:T(8,128)(2,1)S(1)}, u32[]{:S(2)}, u32[]{:S(2)}) collective-permute-start(bf16[2,3,128,1024]{3,2,1,0:T(8,128)(2,1)S(1)} %shard_map.86), channel_id=1, source_target_pairs={{0,2},{1,3},{2,0},{3,1},{4,6},{5,7},{6,4},{7,5},{8,10},{9,11},{10,... | collective-permute-start | bytes 4718600 | tf_op jit(solution)/shard_map/ppermute | solution.py:332
  8.0 0.6 shard_map.87
  8.6 1.6 %collective-permute-start = (bf16[128,512]{1,0:T(8,128)(2,1)S(1)}, bf16[128,512]{1,0:T(8,128)(2,1)S(1)}, u32[]{:S(2)}, u32[]{:S(2)}) collective-permute-start(bf16[128,512]{1,0:T(8,128)(2,1)S(1)} %shard_map.87), channel_id=1, source_target_pairs={{0,8},{4,12},{8,0},{12,4},{16,24},{20,28},{24,16},{28,20},{1,9},{5... | collective-permute-start | bytes 393224 | tf_op jit(solution)/shard_map/ppermute | solution.py:332
  10.2 2.6 %collective-permute-start.2 = (bf16[128,512]{1,0:T(8,128)(2,1)S(1)}, bf16[128,512]{1,0:T(8,128)(2,1)S(1)}, u32[]{:S(2)}, u32[]{:S(2)}) collective-permute-start(bf16[128,512]{1,0:T(8,128)(2,1)S(1)} %shard_map.87), channel_id=1, source_target_pairs={{0,16},{4,20},{8,24},{12,28},{16,0},{20,4},{24,8},{28,12},{1,17},{... | collective-permute-start | bytes 393224 | tf_op jit(solution)/shard_map/ppermute | solution.py:332
  13.1 1.5 %shard_map.88 = (bf16[1,4,128,1024]{3,2,1,0:T(8,128)(2,1)S(1)}, bf16[1,4,128,1024]{3,2,1,0:T(8,128)(2,1)S(1)}, bf16[1,1,128,1024]{3,2,1,0:T(8,128)(2,1)S(1)}, bf16[1,1,128,1024]{3,2,1,0:T(8,128)(2,1)S(1)}) custom-call(s32[7]{0:T(128)S(1)} %pad_add_fusion.2.info, s32[4,1,256]{2,1,0:T(1,128)S(1)} %bitcast.102, bf16[4,256,1024]{2,1,0:T(8,128)(2,1)S(1)} %copy-done.2), custom_call_target="tpu_custom_call" | custom-call | flops 2147483648 | tf_op jit(solution)/shard_map/pallas_call | solution.py:54
  14.7 0.4 collective-permute-done
  15.3 1.6 %collective-permute-start.1 = (bf16[2,128,512]{2,1,0:T(8,128)(2,1)S(1)}, bf16[2,128,512]{2,1,0:T(8,128)(2,1)S(1)}, u32[]{:S(2)}, u32[]{:S(2)}) collective-permute-start(bf16[2,128,512]{2,1,0:T(8,128)(2,1)S(1)} %pad_maximum_fusion.refs_0_), channel_id=1, source_target_pairs={{0,4},{4,0},{8,12},{12,8},{16,20},{20,16},{24,28},{28,24},{1,5},{5... | collective-permute-start | bytes 786440 | tf_op jit(solution)/shard_map/ppermute | solution.py:332
  16.8 2.5 %shard_map.89 = (f32[4,256,128]{2,1,0:T(8,128)S(1)}, f32[4,8,256]{2,1,0:T(8,128)S(1)}) custom-call(s32[7]{0:T(128)S(1)} %pad_add_fusion.2.info, s32[2,4,2,256]{3,2,1,0:T(2,128)S(1)} %pad_add_fusion.meta, s32[4,16,32]{2,1,0:T(8,128)S(1)} %copy-done.3), custom_call_target="tpu_custom_call" | custom-call | flops 2147483648 | tf_op jit(solution)/shard_map/pallas_call | solution.py:54
  19.4 3.5 %collective-permute-done.2 = bf16[128,512]{1,0:T(8,128)(2,1)S(1)} collective-permute-done((bf16[128,512]{1,0:T(8,128)(2,1)S(1)}, bf16[128,512]{1,0:T(8,128)(2,1)S(1)}, u32[]{:S(2)}, u32[]{:S(2)}) %collective-permute-start.2) | collective-permute-done | bytes 131104 | tf_op jit(solution)/shard_map/ppermute | solution.py:332
  22.9 1.0 %collective-permute-done.1.refs_1_ = bf16[2,128,512]{2,1,0:T(8,128)(2,1)S(1)} collective-permute-done((bf16[2,128,512]{2,1,0:T(8,128)(2,1)S(1)}, bf16[2,128,512]{2,1,0:T(8,128)(2,1)S(1)}, u32[]{:S(2)}, u32[]{:S(2)}) %collective-permute-start.1) | collective-permute-done | bytes 262176 | tf_op jit(solution)/shard_map/ppermute | solution.py:332
  23.9 0.5 collective-permute-start.7
  24.4 1.5 %collective-permute-start.5 = (bf16[1,128,512]{2,1,0:T(8,128)(2,1)S(1)}, bf16[1,128,512]{2,1,0:T(8,128)(2,1)S(1)}, u32[]{:S(2)}, u32[]{:S(2)}) collective-permute-start(bf16[1,128,512]{2,1,0:T(8,128)(2,1)S(1)} %bitcast.93), channel_id=1, source_target_pairs={{0,4},{4,0},{8,12},{12,8},{16,20},{20,16},{24,28},{28,24},{1,5},{5... | collective-permute-start | bytes 393224 | tf_op jit(solution)/shard_map/ppermute | solution.py:332
  25.9 1.4 %collective-permute-start.8 = (bf16[1,128,512]{2,1,0:T(8,128)(2,1)S(1)}, bf16[1,128,512]{2,1,0:T(8,128)(2,1)S(1)}, u32[]{:S(2)}, u32[]{:S(2)}) collective-permute-start(bf16[1,128,512]{2,1,0:T(8,128)(2,1)S(1)} %bitcast.96), channel_id=1, source_target_pairs={{0,4},{4,0},{8,12},{12,8},{16,20},{20,16},{24,28},{28,24},{1,5},{5... | collective-permute-start | bytes 393224 | tf_op jit(solution)/shard_map/ppermute | solution.py:332
  27.3 4.0 %shard_map.90.refs_8_ = bf16[4,1024,512]{2,1,0:T(8,128)(2,1)S(1)} custom-call(s32[7]{0:T(128)S(1)} %pad_add_fusion.2.info, bf16[4,512,1024]{2,1,0:T(8,128)(2,1)S(1)} %copy-done, bf16[2,128,512]{2,1,0:T(8,128)(2,1)S(1)} %pad_maximum_fusion.refs_0_, bf16[2,128,512]{2,1,0:T(8,128)(2,1)S(1)} %collective-permute-done.1.refs_1_, ...), custom_call_target="tpu_custom_call" | custom-call | flops 2147483648 | tf_op jit(solution)/shard_map/pallas_call | solution.py:36
  31.3 1.3 %collective-permute-done.8.refs_3_ = bf16[1,128,512]{2,1,0:T(8,128)(2,1)S(1)} collective-permute-done((bf16[1,128,512]{2,1,0:T(8,128)(2,1)S(1)}, bf16[1,128,512]{2,1,0:T(8,128)(2,1)S(1)}, u32[]{:S(2)}, u32[]{:S(2)}) %collective-permute-start.8) | collective-permute-done | bytes 131104 | tf_op jit(solution)/shard_map/ppermute | solution.py:332
  32.6 0.5 collective-permute-start.11
  33.1 0.8 collective-permute-done.10.refs_5_
  34.2 0.3 collective-permute-start.16
  34.5 0.8 collective-permute-done.9.refs_4_
  35.3 3.8 %shard_map.91.weight = bf16[4,1024,512]{2,1,0:T(8,128)(2,1)S(1)} custom-call(s32[7]{0:T(128)S(1)} %pad_add_fusion.2.info, bf16[4,512,1024]{2,1,0:T(8,128)(2,1)S(1)} %copy-done, bf16[1,128,512]{2,1,0:T(8,128)(2,1)S(1)} %bitcast.95, bf16[1,128,512]{2,1,0:T(8,128)(2,1)S(1)} %collective-permute-done.5.refs_1_, bf16[1,128,512]{2,1,0:T(8,128)(2,1)S(1)} %bitcast.98, ...), custom_call_target="tpu_custom_call" | custom-call | tf_op jit(solution)/shard_map/pallas_call | solution.py:36
  39.1 3.1 %shard_map.92 = (f32[2,2,256]{2,1,0:T(2,128)S(1)}, bf16[1024,512]{1,0:T(8,128)(2,1)S(1)}, bf16[512,1024]{1,0:T(8,128)(2,1)S(1)}) custom-call(s32[7]{0:T(128)S(1)} %pad_add_fusion.2.info, f32[4,256,128]{2,1,0:T(8,128)S(1)} %get-tuple-element.78.table, f32[4,8,256]{2,1,0:T(8,128)S(1)} %get-tuple-element.79.rank, bf16[4,1024,512]{2,1,0:T(8,128)(2,1)S(1)} %shard_map.91.weight, ...), custom_call_target="tpu_custom_call" | custom-call | tf_op jit(solution)/shard_map/pallas_call | solution.py:36
  42.2 0.6 collective-permute-done.16.meta
  42.8 1.7 %collective-permute-start.18 = (bf16[1,1,128,1024]{3,2,1,0:T(8,128)(2,1)S(1)}, bf16[1,1,128,1024]{3,2,1,0:T(8,128)(2,1)S(1)}, u32[]{:S(2)}, u32[]{:S(2)}) collective-permute-start(bf16[1,1,128,1024]{3,2,1,0:T(8,128)(2,1)S(1)} %get-tuple-element.109), channel_id=1, source_target_pairs={{0,2},{1,3},{2,0},{3,1},{4,6},{5,7},{6,4},{7,5},{8,10},{9,11},{10,... | collective-permute-start | bytes 786440 | tf_op jit(solution)/shard_map/ppermute | solution.py:332
  44.6 3.1 %shard_map.93 = (f32[2,2,256]{2,1,0:T(2,128)S(1)}, bf16[1024,512]{1,0:T(8,128)(2,1)S(1)}, bf16[512,1024]{1,0:T(8,128)(2,1)S(1)}) custom-call(s32[7]{0:T(128)S(1)} %pad_add_fusion.2.info, f32[4,256,128]{2,1,0:T(8,128)S(1)} %get-tuple-element.78.table, f32[4,8,256]{2,1,0:T(8,128)S(1)} %get-tuple-element.79.rank, bf16[4,1024,512]{2,1,0:T(8,128)(2,1)S(1)} %shard_map.91.weight, ...), custom_call_target="tpu_custom_call" | custom-call | tf_op jit(solution)/shard_map/pallas_call | solution.py:36
  47.7 0.3 collective-permute-start.14
  48.1 2.5 %shard_map.94 = (f32[4,256,128]{2,1,0:T(8,128)S(1)}, f32[4,8,256]{2,1,0:T(8,128)S(1)}) custom-call(s32[7]{0:T(128)S(1)} %pad_add_fusion.2.info, s32[2,4,2,256]{3,2,1,0:T(2,128)S(1)} %collective-permute-done.16.meta, s32[4,16,32]{2,1,0:T(8,128)S(1)} %copy-done.3), custom_call_target="tpu_custom_call" | custom-call | tf_op jit(solution)/shard_map/pallas_call | solution.py:54
  50.6 4.2 %shard_map.95 = (f32[3,2,256]{2,1,0:T(2,128)S(1)}, bf16[1024,768]{1,0:T(8,128)(2,1)S(1)}, bf16[768,1024]{1,0:T(8,128)(2,1)S(1)}) custom-call(s32[7]{0:T(128)S(1)} %pad_add_fusion.2.info, f32[4,256,128]{2,1,0:T(8,128)S(1)} %get-tuple-element.105.table, f32[4,8,256]{2,1,0:T(8,128)S(1)} %get-tuple-element.106.rank, bf16[4,1024,512]{2,1,0:T(8,128)(2,1)S(1)} %shard_map.91.weight, ...), custom_call_target="tpu_custom_call" | custom-call | tf_op jit(solution)/shard_map/pallas_call | solution.py:36
  54.9 1.9 %collective-permute-done.19.refs_1_ = bf16[1,1,128,1024]{3,2,1,0:T(8,128)(2,1)S(1)} collective-permute-done((bf16[1,1,128,1024]{3,2,1,0:T(8,128)(2,1)S(1)}, bf16[1,1,128,1024]{3,2,1,0:T(8,128)(2,1)S(1)}, u32[]{:S(2)}, u32[]{:S(2)}) %collective-permute-start.19) | collective-permute-done | bytes 262176 | tf_op jit(solution)/shard_map/ppermute | solution.py:332
  56.7 1.7 %shard_map.96 = (f32[1,2,256]{2,1,0:T(2,128)S(1)}, bf16[1024,256]{1,0:T(8,128)(2,1)S(1)}, bf16[256,1024]{1,0:T(8,128)(2,1)S(1)}) custom-call(s32[7]{0:T(128)S(1)} %pad_add_fusion.2.info, f32[4,256,128]{2,1,0:T(8,128)S(1)} %get-tuple-element.105.table, f32[4,8,256]{2,1,0:T(8,128)S(1)} %get-tuple-element.106.rank, bf16[4,1024,512]{2,1,0:T(8,128)(2,1)S(1)} %shard_map.91.weight, ...), custom_call_target="tpu_custom_call" | custom-call | tf_op jit(solution)/shard_map/pallas_call | solution.py:36
  58.4 3.1 %shard_map.98 = bf16[2,1024,256]{2,1,0:T(8,128)(2,1)S(1)} custom-call(s32[7]{0:T(128)S(1)} %pad_add_fusion.2.info, bf16[1024,512]{1,0:T(8,128)(2,1)S(1)} %get-tuple-element.116.refs_0_, bf16[512,1024]{1,0:T(8,128)(2,1)S(1)} %get-tuple-element.117.refs_1_, bf16[1024,512]{1,0:T(8,128)(2,1)S(1)} %get-tuple-element.118.refs_2_, ...), custom_call_target="tpu_custom_call" | custom-call | tf_op jit(solution)/shard_map/pallas_call | solution.py:54
  61.8 3.1 %shard_map.97 = f32[2,1024,256]{2,1,0:T(8,128)S(1)} custom-call(s32[7]{0:T(128)S(1)} %pad_add_fusion.2.info, bf16[1024,512]{1,0:T(8,128)(2,1)S(1)} %get-tuple-element.116.refs_0_, bf16[512,1024]{1,0:T(8,128)(2,1)S(1)} %get-tuple-element.117.refs_1_, bf16[1024,512]{1,0:T(8,128)(2,1)S(1)} %get-tuple-element.118.refs_2_, ...), custom_call_target="tpu_custom_call" | custom-call | flops 34359738368 | tf_op jit(solution)/shard_map/pallas_call | solution.py:54
  65.1 1.8 %collective-permute-start.23 = (bf16[4,128,256]{2,1,0:T(8,128)(2,1)S(1)}, bf16[4,128,256]{2,1,0:T(8,128)(2,1)S(1)}, u32[]{:S(2)}, u32[]{:S(2)}) collective-permute-start(bf16[4,128,256]{2,1,0:T(8,128)(2,1)S(1)} %get-tuple-element.132), channel_id=1, source_target_pairs={{0,2},{1,3},{2,0},{3,1},{4,6},{5,7},{6,4},{7,5},{8,10},{9,11},{10,... | collective-permute-start | bytes 786440 | tf_op jit(solution)/shard_map/ppermute | solution.py:338
  67.0 1.4 %collective-permute-start.24 = (bf16[4,128,256]{2,1,0:T(8,128)(2,1)S(1)}, bf16[4,128,256]{2,1,0:T(8,128)(2,1)S(1)}, u32[]{:S(2)}, u32[]{:S(2)}) collective-permute-start(bf16[4,128,256]{2,1,0:T(8,128)(2,1)S(1)} %get-tuple-element.133), channel_id=1, source_target_pairs={{0,6},{1,7},{2,4},{3,5},{4,2},{5,3},{6,0},{7,1},{8,14},{9,15},{10,... | collective-permute-start | bytes 786440 | tf_op jit(solution)/shard_map/ppermute | solution.py:338
  68.4 0.3 collective-permute-start.25
  68.7 1.8 %collective-permute-start.20 = (f32[4,256]{1,0:T(4,128)S(1)}, f32[4,256]{1,0:T(4,128)S(1)}, u32[]{:S(2)}, u32[]{:S(2)}) collective-permute-start(f32[4,256]{1,0:T(4,128)S(1)} %bitcast.107), channel_id=1, source_target_pairs={{0,2},{1,3},{2,0},{3,1},{4,6},{5,7},{6,4},{7,5},{8,10},{9,11},{10,... | collective-permute-start | bytes 12296 | tf_op jit(solution)/shard_map/ppermute | solution.py:332
  70.5 8.9 %collective-permute-done.23 = bf16[4,128,256]{2,1,0:T(8,128)(2,1)S(1)} collective-permute-done((bf16[4,128,256]{2,1,0:T(8,128)(2,1)S(1)}, bf16[4,128,256]{2,1,0:T(8,128)(2,1)S(1)}, u32[]{:S(2)}, u32[]{:S(2)}) %collective-permute-start.23) | collective-permute-done | bytes 262176 | tf_op jit(solution)/shard_map/ppermute | solution.py:338
  79.4 0.8 collective-permute-start.21
  80.2 0.5 collective-permute-done.25
  80.9 1.8 %collective-permute-start.26 = (bf16[128,256]{1,0:T(8,128)(2,1)S(1)}, bf16[128,256]{1,0:T(8,128)(2,1)S(1)}, u32[]{:S(2)}, u32[]{:S(2)}) collective-permute-start(bf16[128,256]{1,0:T(8,128)(2,1)S(1)} %get-tuple-element.135), channel_id=1, source_target_pairs={{0,8},{4,12},{8,0},{12,4},{16,24},{20,28},{24,16},{28,20},{1,9},{5... | collective-permute-start | bytes 196616 | tf_op jit(solution)/shard_map/ppermute | solution.py:332
  82.7 2.6 %collective-permute-start.27 = (bf16[128,256]{1,0:T(8,128)(2,1)S(1)}, bf16[128,256]{1,0:T(8,128)(2,1)S(1)}, u32[]{:S(2)}, u32[]{:S(2)}) collective-permute-start(bf16[128,256]{1,0:T(8,128)(2,1)S(1)} %get-tuple-element.137), channel_id=1, source_target_pairs={{0,16},{4,20},{8,24},{12,28},{16,0},{20,4},{24,8},{28,12},{1,17},{... | collective-permute-start | bytes 196616 | tf_op jit(solution)/shard_map/ppermute | solution.py:332
  85.3 0.6 fusion.19
  85.9 4.4 %collective-permute-done.27 = bf16[128,256]{1,0:T(8,128)(2,1)S(1)} collective-permute-done((bf16[128,256]{1,0:T(8,128)(2,1)S(1)}, bf16[128,256]{1,0:T(8,128)(2,1)S(1)}, u32[]{:S(2)}, u32[]{:S(2)}) %collective-permute-start.27) | collective-permute-done | bytes 65568 | tf_op jit(solution)/shard_map/ppermute | solution.py:332
  90.4 1.0 %collective-permute-done.28 = bf16[128,256]{1,0:T(8,128)(2,1)S(1)} collective-permute-done((bf16[128,256]{1,0:T(8,128)(2,1)S(1)}, bf16[128,256]{1,0:T(8,128)(2,1)S(1)}, u32[]{:S(2)}, u32[]{:S(2)}) %collective-permute-start.28) | collective-permute-done | bytes 65568 | tf_op jit(solution)/shard_map/ppermute | solution.py:332
  91.4 0.7 fusion.11
  (55 shorter events, 1.8 us)
Async XLA Ops:
  1.4 1.6 %copy-start.1 = (bf16[4,256,1024]{2,1,0:T(8,128)(2,1)S(1)}, bf16[4,256,1024]{2,1,0:T(8,128)(2,1)}, u32[]{:S(2)}) copy-start(bf16[4,256,1024]{2,1,0:T(8,128)(2,1)} %words.3) | copy-start | bytes 6291460
  3.0 0.7 copy-start.4
  3.7 4.3 %copy-start.5 = (bf16[128,1024]{1,0:T(8,128)(2,1)S(1)}, bf16[128,1024]{1,0:T(8,128)(2,1)}, u32[]{:S(2)}) copy-start(bf16[128,1024]{1,0:T(8,128)(2,1)} %proj) | copy-start | bytes 786436
  4.9 8.1 %copy-start.6 = (s32[4,256]{1,0:T(4,128)S(1)}, s32[4,256]{1,0:T(4,128)}, u32[]{:S(2)}) copy-start(s32[4,256]{1,0:T(4,128)} %param.11) | copy-start | bytes 12292
  5.0 8.2 %copy-start.2 = (bf16[4,256,1024]{2,1,0:T(8,128)(2,1)S(1)}, bf16[4,256,1024]{2,1,0:T(8,128)(2,1)}, u32[]{:S(2)}) copy-start(bf16[4,256,1024]{2,1,0:T(8,128)(2,1)} %words.3) | copy-start | bytes 6291460
  5.0 37.8 %collective-permute-start.15 = (bf16[2,3,128,1024]{3,2,1,0:T(8,128)(2,1)S(1)}, bf16[2,3,128,1024]{3,2,1,0:T(8,128)(2,1)S(1)}, u32[]{:S(2)}, u32[]{:S(2)}) collective-permute-start(bf16[2,3,128,1024]{3,2,1,0:T(8,128)(2,1)S(1)} %shard_map.86), channel_id=1, source_target_pairs={{0,2},{1,3},{2,0},{3,1},{4,6},{5,7},{6,4},{7,5},{8,10},{9,11},{10,... | collective-permute-start | bytes 4718600 | tf_op jit(solution)/shard_map/ppermute | solution.py:332
  8.6 6.5 %collective-permute-start = (bf16[128,512]{1,0:T(8,128)(2,1)S(1)}, bf16[128,512]{1,0:T(8,128)(2,1)S(1)}, u32[]{:S(2)}, u32[]{:S(2)}) collective-permute-start(bf16[128,512]{1,0:T(8,128)(2,1)S(1)} %shard_map.87), channel_id=1, source_target_pairs={{0,8},{4,12},{8,0},{12,4},{16,24},{20,28},{24,16},{28,20},{1,9},{5... | collective-permute-start | bytes 393224 | tf_op jit(solution)/shard_map/ppermute | solution.py:332
  10.2 12.6 %collective-permute-start.2 = (bf16[128,512]{1,0:T(8,128)(2,1)S(1)}, bf16[128,512]{1,0:T(8,128)(2,1)S(1)}, u32[]{:S(2)}, u32[]{:S(2)}) collective-permute-start(bf16[128,512]{1,0:T(8,128)(2,1)S(1)} %shard_map.87), channel_id=1, source_target_pairs={{0,16},{4,20},{8,24},{12,28},{16,0},{20,4},{24,8},{28,12},{1,17},{... | collective-permute-start | bytes 393224 | tf_op jit(solution)/shard_map/ppermute | solution.py:332
  12.8 10.1 %collective-permute-start.3 = (bf16[128,512]{1,0:T(8,128)(2,1)S(1)}, bf16[128,512]{1,0:T(8,128)(2,1)S(1)}, u32[]{:S(2)}, u32[]{:S(2)}) collective-permute-start(bf16[128,512]{1,0:T(8,128)(2,1)S(1)} %shard_map.87), channel_id=1, source_target_pairs={{0,24},{4,28},{8,16},{12,20},{16,8},{20,12},{24,0},{28,4},{1,25},{... | collective-permute-start | bytes 393224 | tf_op jit(solution)/shard_map/ppermute | solution.py:332
  13.0 3.8 %copy-start.3 = (s32[4,16,32]{2,1,0:T(8,128)S(1)}, s32[4,16,32]{2,1,0:T(8,128)}, u32[]{:S(2)}) copy-start(s32[4,16,32]{2,1,0:T(8,128)} %flags.3) | copy-start | bytes 24580
  13.1 2.2 %collective-permute-start.4 = (s32[4,2,256]{2,1,0:T(2,128)S(1)}, s32[4,2,256]{2,1,0:T(2,128)S(1)}, u32[]{:S(2)}, u32[]{:S(2)}) collective-permute-start(s32[4,2,256]{2,1,0:T(2,128)S(1)} %get-tuple-element.141), channel_id=1, source_target_pairs={{0,1},{1,0},{2,3},{3,2},{4,5},{5,4},{6,7},{7,6},{8,9},{9,8},{10,11... | collective-permute-start | bytes 24584 | tf_op jit(solution)/shard_map/ppermute | solution.py:332
  15.1 24.1 %collective-permute-start.13 = (bf16[1,4,128,1024]{3,2,1,0:T(8,128)(2,1)S(1)}, bf16[1,4,128,1024]{3,2,1,0:T(8,128)(2,1)S(1)}, u32[]{:S(2)}, u32[]{:S(2)}) collective-permute-start(bf16[1,4,128,1024]{3,2,1,0:T(8,128)(2,1)S(1)} %get-tuple-element.95), channel_id=1, source_target_pairs={{0,1},{1,0},{2,3},{3,2},{4,5},{5,4},{6,7},{7,6},{8,9},{9,8},{10,11... | collective-permute-start | bytes 3145736 | tf_op jit(solution)/shard_map/ppermute | solution.py:332
  15.3 8.6 %collective-permute-start.1 = (bf16[2,128,512]{2,1,0:T(8,128)(2,1)S(1)}, bf16[2,128,512]{2,1,0:T(8,128)(2,1)S(1)}, u32[]{:S(2)}, u32[]{:S(2)}) collective-permute-start(bf16[2,128,512]{2,1,0:T(8,128)(2,1)S(1)} %pad_maximum_fusion.refs_0_), channel_id=1, source_target_pairs={{0,4},{4,0},{8,12},{12,8},{16,20},{20,16},{24,28},{28,24},{1,5},{5... | collective-permute-start | bytes 786440 | tf_op jit(solution)/shard_map/ppermute | solution.py:332
  16.8 10.5 %copy-start = (bf16[4,512,1024]{2,1,0:T(8,128)(2,1)S(1)}, bf16[4,512,1024]{2,1,0:T(8,128)(2,1)}, u32[]{:S(2)}) copy-start(bf16[4,512,1024]{2,1,0:T(8,128)(2,1)} %patches.11) | copy-start | bytes 12582916
  23.9 2.0 %collective-permute-start.6 = (bf16[2,128,512]{2,1,0:T(8,128)(2,1)S(1)}, bf16[2,128,512]{2,1,0:T(8,128)(2,1)S(1)}, u32[]{:S(2)}, u32[]{:S(2)}) collective-permute-start(bf16[2,128,512]{2,1,0:T(8,128)(2,1)S(1)} %pad_maximum_fusion.refs_0_), channel_id=1, source_target_pairs={{0,1},{1,0},{2,3},{3,2},{4,5},{5,4},{6,7},{7,6},{8,9},{9,8},{10,11... | collective-permute-start | bytes 786440 | tf_op jit(solution)/shard_map/ppermute | solution.py:332
  23.9 2.0 %collective-permute-start.7 = (bf16[2,128,512]{2,1,0:T(8,128)(2,1)S(1)}, bf16[2,128,512]{2,1,0:T(8,128)(2,1)S(1)}, u32[]{:S(2)}, u32[]{:S(2)}) collective-permute-start(bf16[2,128,512]{2,1,0:T(8,128)(2,1)S(1)} %collective-permute-done.1.refs_1_), channel_id=1, source_target_pairs={{0,1},{1,0},{2,3},{3,2},{4,5},{5,4},{6,7},{7,6},{8,9},{9,8},{10,11... | collective-permute-start | bytes 786440 | tf_op jit(solution)/shard_map/ppermute | solution.py:332
  24.4 6.9 %collective-permute-start.5 = (bf16[1,128,512]{2,1,0:T(8,128)(2,1)S(1)}, bf16[1,128,512]{2,1,0:T(8,128)(2,1)S(1)}, u32[]{:S(2)}, u32[]{:S(2)}) collective-permute-start(bf16[1,128,512]{2,1,0:T(8,128)(2,1)S(1)} %bitcast.93), channel_id=1, source_target_pairs={{0,4},{4,0},{8,12},{12,8},{16,20},{20,16},{24,28},{28,24},{1,5},{5... | collective-permute-start | bytes 393224 | tf_op jit(solution)/shard_map/ppermute | solution.py:332
  25.9 6.7 %collective-permute-start.8 = (bf16[1,128,512]{2,1,0:T(8,128)(2,1)S(1)}, bf16[1,128,512]{2,1,0:T(8,128)(2,1)S(1)}, u32[]{:S(2)}, u32[]{:S(2)}) collective-permute-start(bf16[1,128,512]{2,1,0:T(8,128)(2,1)S(1)} %bitcast.96), channel_id=1, source_target_pairs={{0,4},{4,0},{8,12},{12,8},{16,20},{20,16},{24,28},{28,24},{1,5},{5... | collective-permute-start | bytes 393224 | tf_op jit(solution)/shard_map/ppermute | solution.py:332
  32.6 1.3 %collective-permute-start.10 = (bf16[1,128,512]{2,1,0:T(8,128)(2,1)S(1)}, bf16[1,128,512]{2,1,0:T(8,128)(2,1)S(1)}, u32[]{:S(2)}, u32[]{:S(2)}) collective-permute-start(bf16[1,128,512]{2,1,0:T(8,128)(2,1)S(1)} %collective-permute-done.5.refs_1_), channel_id=1, source_target_pairs={{0,1},{1,0},{2,3},{3,2},{4,5},{5,4},{6,7},{7,6},{8,9},{9,8},{10,11... | collective-permute-start | bytes 393224 | tf_op jit(solution)/shard_map/ppermute | solution.py:332
  32.6 1.5 %collective-permute-start.11 = (bf16[1,128,512]{2,1,0:T(8,128)(2,1)S(1)}, bf16[1,128,512]{2,1,0:T(8,128)(2,1)S(1)}, u32[]{:S(2)}, u32[]{:S(2)}) collective-permute-start(bf16[1,128,512]{2,1,0:T(8,128)(2,1)S(1)} %bitcast.97), channel_id=1, source_target_pairs={{0,1},{1,0},{2,3},{3,2},{4,5},{5,4},{6,7},{7,6},{8,9},{9,8},{10,11... | collective-permute-start | bytes 393224 | tf_op jit(solution)/shard_map/ppermute | solution.py:332
  33.1 1.3 %collective-permute-start.12 = (bf16[1,128,512]{2,1,0:T(8,128)(2,1)S(1)}, bf16[1,128,512]{2,1,0:T(8,128)(2,1)S(1)}, u32[]{:S(2)}, u32[]{:S(2)}) collective-permute-start(bf16[1,128,512]{2,1,0:T(8,128)(2,1)S(1)} %collective-permute-done.8.refs_3_), channel_id=1, source_target_pairs={{0,1},{1,0},{2,3},{3,2},{4,5},{5,4},{6,7},{7,6},{8,9},{9,8},{10,11... | collective-permute-start | bytes 393224 | tf_op jit(solution)/shard_map/ppermute | solution.py:332
  34.0 1.3 %collective-permute-start.9 = (bf16[1,128,512]{2,1,0:T(8,128)(2,1)S(1)}, bf16[1,128,512]{2,1,0:T(8,128)(2,1)S(1)}, u32[]{:S(2)}, u32[]{:S(2)}) collective-permute-start(bf16[1,128,512]{2,1,0:T(8,128)(2,1)S(1)} %bitcast.94), channel_id=1, source_target_pairs={{0,1},{1,0},{2,3},{3,2},{4,5},{5,4},{6,7},{7,6},{8,9},{9,8},{10,11... | collective-permute-start | bytes 393224 | tf_op jit(solution)/shard_map/ppermute | solution.py:332
  34.2 8.6 %collective-permute-start.16 = (s32[2,4,2,256]{3,2,1,0:T(2,128)S(1)}, s32[2,4,2,256]{3,2,1,0:T(2,128)S(1)}, u32[]{:S(2)}, u32[]{:S(2)}) collective-permute-start(s32[2,4,2,256]{3,2,1,0:T(2,128)S(1)} %pad_add_fusion.meta), channel_id=1, source_target_pairs={{0,2},{1,3},{2,0},{3,1},{4,6},{5,7},{6,4},{7,5},{8,10},{9,11},{10,... | collective-permute-start | bytes 49160 | tf_op jit(solution)/shard_map/ppermute | solution.py:332
  42.8 7.9 %collective-permute-start.17 = (bf16[2,3,128,1024]{3,2,1,0:T(8,128)(2,1)S(1)}, bf16[2,3,128,1024]{3,2,1,0:T(8,128)(2,1)S(1)}, u32[]{:S(2)}, u32[]{:S(2)}) collective-permute-start(bf16[2,3,128,1024]{3,2,1,0:T(8,128)(2,1)S(1)} %collective-permute-done.15.refs_0_), channel_id=1, source_target_pairs={{0,1},{1,0},{2,3},{3,2},{4,5},{5,4},{6,7},{7,6},{8,9},{9,8},{10,11... | collective-permute-start | bytes 4718600 | tf_op jit(solution)/shard_map/ppermute | solution.py:332
  42.8 12.1 %collective-permute-start.18 = (bf16[1,1,128,1024]{3,2,1,0:T(8,128)(2,1)S(1)}, bf16[1,1,128,1024]{3,2,1,0:T(8,128)(2,1)S(1)}, u32[]{:S(2)}, u32[]{:S(2)}) collective-permute-start(bf16[1,1,128,1024]{3,2,1,0:T(8,128)(2,1)S(1)} %get-tuple-element.109), channel_id=1, source_target_pairs={{0,2},{1,3},{2,0},{3,1},{4,6},{5,7},{6,4},{7,5},{8,10},{9,11},{10,... | collective-permute-start | bytes 786440 | tf_op jit(solution)/shard_map/ppermute | solution.py:332
  44.5 12.2 %collective-permute-start.19 = (bf16[1,1,128,1024]{3,2,1,0:T(8,128)(2,1)S(1)}, bf16[1,1,128,1024]{3,2,1,0:T(8,128)(2,1)S(1)}, u32[]{:S(2)}, u32[]{:S(2)}) collective-permute-start(bf16[1,1,128,1024]{3,2,1,0:T(8,128)(2,1)S(1)} %get-tuple-element.110), channel_id=1, source_target_pairs={{0,3},{1,2},{2,1},{3,0},{4,7},{5,6},{6,5},{7,4},{8,11},{9,10},{10,... | collective-permute-start | bytes 786440 | tf_op jit(solution)/shard_map/ppermute | solution.py:332
  47.7 37.5 %collective-permute-start.14 = (f32[4,256]{1,0:T(4,128)S(1)}, f32[4,256]{1,0:T(4,128)S(1)}, u32[]{:S(2)}, u32[]{:S(2)}) collective-permute-start(f32[4,256]{1,0:T(4,128)S(1)} %fusion.20), channel_id=1, source_target_pairs={{0,1},{1,0},{2,3},{3,2},{4,5},{5,4},{6,7},{7,6},{8,9},{9,8},{10,11... | collective-permute-start | bytes 12296 | tf_op jit(solution)/shard_map/ppermute | solution.py:332
  61.5 3.3 %collective-permute-start.22 = (bf16[2,1024,256]{2,1,0:T(8,128)(2,1)S(1)}, bf16[2,1024,256]{2,1,0:T(8,128)(2,1)S(1)}, u32[]{:S(2)}, u32[]{:S(2)}) collective-permute-start(bf16[2,1024,256]{2,1,0:T(8,128)(2,1)S(1)} %shard_map.98), channel_id=1, source_target_pairs={{0,1},{1,0},{2,3},{3,2},{4,5},{5,4},{6,7},{7,6},{8,9},{9,8},{10,11... | collective-permute-start | bytes 3145736 | tf_op jit(solution)/shard_map/ppermute | solution.py:332
  65.1 14.2 %collective-permute-start.23 = (bf16[4,128,256]{2,1,0:T(8,128)(2,1)S(1)}, bf16[4,128,256]{2,1,0:T(8,128)(2,1)S(1)}, u32[]{:S(2)}, u32[]{:S(2)}) collective-permute-start(bf16[4,128,256]{2,1,0:T(8,128)(2,1)S(1)} %get-tuple-element.132), channel_id=1, source_target_pairs={{0,2},{1,3},{2,0},{3,1},{4,6},{5,7},{6,4},{7,5},{8,10},{9,11},{10,... | collective-permute-start | bytes 786440 | tf_op jit(solution)/shard_map/ppermute | solution.py:338
  67.0 13.2 %collective-permute-start.24 = (bf16[4,128,256]{2,1,0:T(8,128)(2,1)S(1)}, bf16[4,128,256]{2,1,0:T(8,128)(2,1)S(1)}, u32[]{:S(2)}, u32[]{:S(2)}) collective-permute-start(bf16[4,128,256]{2,1,0:T(8,128)(2,1)S(1)} %get-tuple-element.133), channel_id=1, source_target_pairs={{0,6},{1,7},{2,4},{3,5},{4,2},{5,3},{6,0},{7,1},{8,14},{9,15},{10,... | collective-permute-start | bytes 786440 | tf_op jit(solution)/shard_map/ppermute | solution.py:338
  68.4 12.3 %collective-permute-start.25 = (bf16[4,128,256]{2,1,0:T(8,128)(2,1)S(1)}, bf16[4,128,256]{2,1,0:T(8,128)(2,1)S(1)}, u32[]{:S(2)}, u32[]{:S(2)}) collective-permute-start(bf16[4,128,256]{2,1,0:T(8,128)(2,1)S(1)} %get-tuple-element.134), channel_id=1, source_target_pairs={{0,4},{1,5},{2,6},{3,7},{4,0},{5,1},{6,2},{7,3},{8,12},{9,13},{10,... | collective-permute-start | bytes 786440 | tf_op jit(solution)/shard_map/ppermute | solution.py:338
  68.7 16.6 %collective-permute-start.20 = (f32[4,256]{1,0:T(4,128)S(1)}, f32[4,256]{1,0:T(4,128)S(1)}, u32[]{:S(2)}, u32[]{:S(2)}) collective-permute-start(f32[4,256]{1,0:T(4,128)S(1)} %bitcast.107), channel_id=1, source_target_pairs={{0,2},{1,3},{2,0},{3,1},{4,6},{5,7},{6,4},{7,5},{8,10},{9,11},{10,... | collective-permute-start | bytes 12296 | tf_op jit(solution)/shard_map/ppermute | solution.py:332
  79.4 5.9 %collective-permute-start.21 = (f32[4,256]{1,0:T(4,128)S(1)}, f32[4,256]{1,0:T(4,128)S(1)}, u32[]{:S(2)}, u32[]{:S(2)}) collective-permute-start(f32[4,256]{1,0:T(4,128)S(1)} %bitcast.108), channel_id=1, source_target_pairs={{0,3},{1,2},{2,1},{3,0},{4,7},{5,6},{6,5},{7,4},{8,11},{9,10},{10,... | collective-permute-start | bytes 12296 | tf_op jit(solution)/shard_map/ppermute | solution.py:332
  80.9 5.1 %collective-permute-start.26 = (bf16[128,256]{1,0:T(8,128)(2,1)S(1)}, bf16[128,256]{1,0:T(8,128)(2,1)S(1)}, u32[]{:S(2)}, u32[]{:S(2)}) collective-permute-start(bf16[128,256]{1,0:T(8,128)(2,1)S(1)} %get-tuple-element.135), channel_id=1, source_target_pairs={{0,8},{4,12},{8,0},{12,4},{16,24},{20,28},{24,16},{28,20},{1,9},{5... | collective-permute-start | bytes 196616 | tf_op jit(solution)/shard_map/ppermute | solution.py:332
  82.7 7.7 %collective-permute-start.27 = (bf16[128,256]{1,0:T(8,128)(2,1)S(1)}, bf16[128,256]{1,0:T(8,128)(2,1)S(1)}, u32[]{:S(2)}, u32[]{:S(2)}) collective-permute-start(bf16[128,256]{1,0:T(8,128)(2,1)S(1)} %get-tuple-element.137), channel_id=1, source_target_pairs={{0,16},{4,20},{8,24},{12,28},{16,0},{20,4},{24,8},{28,12},{1,17},{... | collective-permute-start | bytes 196616 | tf_op jit(solution)/shard_map/ppermute | solution.py:332
  85.3 6.1 %collective-permute-start.28 = (bf16[128,256]{1,0:T(8,128)(2,1)S(1)}, bf16[128,256]{1,0:T(8,128)(2,1)S(1)}, u32[]{:S(2)}, u32[]{:S(2)}) collective-permute-start(bf16[128,256]{1,0:T(8,128)(2,1)S(1)} %get-tuple-element.136), channel_id=1, source_target_pairs={{0,24},{4,28},{8,16},{12,20},{16,8},{20,12},{24,0},{28,4},{1,25},{... | collective-permute-start | bytes 196616 | tf_op jit(solution)/shard_map/ppermute | solution.py:332

commit v13 on v12

--- a/solution.py
+++ b/solution.py
@@ -11,6 +11,7 @@
 MARGIN_BLOCK_SIZE = 64
 SHIFT = 6
 VMEM_LIMIT = 16 * 1024 * 1024
+FIRST_LIMIT = 54 * 1024 * 1024
 WORK = 1<<31
 MUCH = 1 << 35
 ME, CORE, DP, COUNTS = 0, 1, 2, 3
@@ -83,7 +84,7 @@
     return out
 
 
-def dispatch_kernel(plan, cap, info, routes, words, *outs):
+def dispatch_kernel(plan, cap, info, routes, words, *outs, ready=lambda page: None):
     wdev = words.shape[1]
     slots = iota((cap, wdev), 0).astype(F32)
     by_page = {}
@@ -105,6 +106,7 @@
         picks = [
             (slots == rank[n + i : n + i + 1]).astype(BF16) for i in range(len(some))
         ]
+        ready(page)
         rows = dot(jnp.concatenate(picks, axis=0), words[page]).astype(BF16)
         for i, (_, out, place, p) in enumerate(some):
             out[place, p] = rows[i * cap : (i + 1) * cap]
@@ -120,6 +122,43 @@
     return call_whole(
         functools.partial(dispatch_kernel, plan, cap), out, (info, routes, words), flops
     )
+
+
+def first_dispatch_kernel(plan, cap, info, routes, words, *refs):
+    *outs, held_routes, held_words, sems = refs
+    n_pages = held_words.shape[0]
+    get_routes = pltpu.make_async_copy(routes, held_routes, sems.at[n_pages])
+    get_words = [
+        pltpu.make_async_copy(words.at[p], held_words.at[p], sems.at[p]) for p in range(n_pages)
+    ]
+    get_routes.start()
+    for copy in get_words:
+        copy.start()
+    get_routes.wait()
+    ready = lambda page: get_words[page].wait()
+    dispatch_kernel(plan, cap, info, held_routes, held_words, *outs, ready=ready)
+
+
+def first_dispatch(info, routes, words, plan, cap):
+    _, wdev, width = words.shape
+    n_pages = max(first_page + n for _, first_page, n in plan)
+    out = [
+        jax.ShapeDtypeStruct((len(offsets), n, cap, width), BF16) for offsets, _, n in plan
+    ]
+    anywhere, vmem = pl.BlockSpec(memory_space=pl.ANY), pl.BlockSpec(memory_space=pltpu.VMEM)
+    return pl.pallas_call(
+        functools.partial(first_dispatch_kernel, plan, cap),
+        in_specs=[pl.BlockSpec(memory_space=pltpu.SMEM), anywhere, anywhere],
+        out_specs=[vmem] * len(out),
+        out_shape=out,
+        scratch_shapes=[
+            pltpu.VMEM(routes.shape, jnp.int32),
+            pltpu.VMEM((n_pages, wdev, width), BF16),
+            pltpu.SemaphoreType.DMA((n_pages + 1,)),
+        ],
+        compiler_params=pltpu.CompilerParams(vmem_limit_bytes=FIRST_LIMIT),
+        cost_estimate=pl.CostEstimate(flops=0, bytes_accessed=0, transcendentals=0),
+    )(info, routes, words)
 
 
 def table_kernel(offsets, cap, own_blk, info, meta, flags, table, rank_out):
@@ -306,6 +345,7 @@
 
 def gradient_kernel(core, info, *refs):
     *pairs, out = refs
+    before = [pairs.pop()] if len(pairs) % 2 else []
     n_y, _, wcol = out.shape
 
     def block(y, _):
@@ -314,16 +354,18 @@
             dot(pairs[i][...], pairs[i + 1][:, pl.ds(column, wcol)])
             for i in range(0, len(pairs), 2)
         )
+        for part in before:
+            got = got + part[y]
         out[y] = got.astype(out.dtype)
         return 0
 
     lax.fori_loop(0, n_y, block, 0)
 
 
-def gradient(info, core, dtype, n_y, pairs, flops=0):
+def gradient(info, core, dtype, n_y, pairs, before=(), flops=0):
     width = pairs[0][0].shape[0]
     out = [jax.ShapeDtypeStruct((n_y, width, width // (2 * n_y)), dtype)]
-    operands = (info, *(x for pair in pairs for x in pair))
+    operands = (info, *(x for pair in pairs for x in pair), *before)
     return call_whole(functools.partial(gradient_kernel, core), out, operands, flops)[0]
 
 
@@ -368,7 +410,7 @@
     routes = routes.reshape(pages, 1, wdev)
 
     split = pages - 1
-    both = dispatch(
+    both = first_dispatch(
         info, routes, words, [((2 * k, 2 * k + 1), 0, split) for k in range(1, n_y)], cap
     )
     info, proj, both = lax.optimization_barrier((info, proj, both))
@@ -424,21 +466,22 @@
     pair_1, meta_far = lax.optimization_barrier((pair_1, meta_far))
     table_far = tables(info, meta_far, flags, far, cap, pps)
     loss_a, *pair_a = run(table_far, first, 0, split)
-    rest, pair_a = lax.optimization_barrier((rest, pair_a))
+    before = gradient(info, 1, F32, n_y, [pair_0, pair_1])
+    rest, pair_a, before = lax.optimization_barrier((rest, pair_a, before))
     loss_b, *pair_b = run(table_far, [(rows, 0) for rows in rest], split, pages - split)
     losses = jnp.concatenate([loss_a, loss_b], axis=0)
     word_loss = near_loss + [exchange(losses[:, i], "seq", r) for i, r in enumerate(far)]
 
     pairs = [pair_0, pair_1, pair_a, pair_b]
-    sent = gradient(info, 1, BF16, n_y, pairs)
-    kept = gradient(info, 0, F32, n_y, pairs, MUCH)
+    sent = gradient(info, 1, BF16, n_y, [pair_a, pair_b], [before])
+    kept = gradient(info, 0, F32, n_y, pairs, (), MUCH)
     form = (n_y, n_high, 2, shard_rows, width // n_seq)
     terms = [kept.reshape(form), exchange(sent, "seq", 1).reshape(form)]
     part = lambda i, j: sum(
         pick(t, (own["y"][i], None, own["low"][j])).astype(F32) for t in terms
     )
     total = part(0, 0)
-    for i, j in [(i, j) for i in range(1, n_y) for j in (0, 1)] + [(0, 1)]:
+    for i, j in [(0, 1)] + [(i, j) for i in range(1, n_y) for j in (1, 0)]:
         total = total + exchange_both(part(i, j).astype(BF16), j, 2 * i)
     grad = pick(total, (own["high"][0],))
     for k in range(1, n_high):

time: 92.3 us -> 91.5 us (level)
  Pallas kernels: 34.4 us -> 37.9 us
  waiting for transfers between devices: 25.2 us -> 22.5 us
  local copies, waits for them, and re-layouts: 2.37 us -> 0.11 us
    pallas_call x0 -> x1, Pallas kernels: none -> 4 us  [first_dispatch(): pl.pallas_call(functools.partial(first_dispatch_kernel, plan, cap), in_sp...]
    ppermute x26, waiting for transfers between devices: 15.9 us -> 12.7 us  [exchange(): return lax.ppermute(x, axis, [(i, i ^ offset) for i in range(n)])]
    unnamed x17, local copies, waits for them, and re-layouts: 2.31 us -> 0.05 us
  transfers between devices with their start and end apart: 29 -> 29, of which waited for: 12 -> 10; matrix products, arithmetic and copies ran while one was open for 1% -> 1% of each run, Pallas kernels for 36% -> 37%
where the time goes in v13:
time: 91.5 us; the launch traced here: 91.3 us
  Pallas kernels  37.9 us (41%)
  starting transfers between devices  26.7 us (29%)
  waiting for transfers between devices  22.5 us (25%)
  other arithmetic  3.07 us (3%)
  between operations  0.95 us (1%)
    ppermute x26, starting transfers between devices, exchange(): return lax.ppermute(x, axis, [(i, i ^ offset) for i in range(n)])  23.2 us
    pallas_call x6, Pallas kernels, call(): pl.pallas_call(kernel, grid_spec=pltpu.PrefetchScalarGridSpec(num_scalar_...  19.7 us
    pallas_call x7, Pallas kernels, call_whole(): pl.pallas_call(kernel, in_specs=[pl.BlockSpec(memory_space=pltpu.SMEM)] +...  14.2 us
    ppermute x26, waiting for transfers between devices, exchange(): return lax.ppermute(x, axis, [(i, i ^ offset) for i in range(n)])  12.7 us
    ppermute x3, waiting for transfers between devices, exchange_both(): lax.ppermute(x, ('dp', 'seq'), [(i, i ^ dp * n_seq + seq) for i in range(...  9.79 us
    pallas_call x1, Pallas kernels, first_dispatch(): pl.pallas_call(functools.partial(first_dispatch_kernel, plan, cap), in_sp...  4 us
    ppermute x3, starting transfers between devices, exchange_both(): lax.ppermute(x, ('dp', 'seq'), [(i, i ^ dp * n_seq + seq) for i in range(...  3.55 us
  transfers between devices with their start and end apart: 29, of which 10 were waited for; matrix products, arithmetic and copies ran while one was open for 1% of the time, Pallas kernels for 37%

profile of v13, /device:TPU:0, one launch (start us, length us, event | category | flops | bytes accessed | tf_op | source)
XLA Modules:
  0.0 91.3 jit_solution(11249838757372229531)
XLA Ops:
  0.6 1.3 %pad_add_fusion.2.info = s32[7]{0:T(128)} fusion(s32[4]{0:T(128)} %param.12, s32[1]{0:T(128)} %bitcast.2, s32[1]{0:T(128)} %bitcast.1, s32[1]{0:T(128)} %bitcast), kind=kLoop, calls=%fused_computation.39 | loop fusion | flops 21 | bytes 56 | tf_op jit(solution)/shard_map/concatenate | solution.py:408
  2.0 4.0 %shard_map.86 = bf16[2,3,128,1024]{3,2,1,0:T(8,128)(2,1)} custom-call(s32[7]{0:T(128)} %pad_add_fusion.2.info, s32[4,1,256]{2,1,0:T(1,128)} %bitcast.100, bf16[4,256,1024]{2,1,0:T(8,128)(2,1)} %words.3), custom_call_target="tpu_custom_call" | custom-call | tf_op jit(solution)/shard_map/pallas_call | solution.py:149
  6.0 3.0 %collective-permute-start.15 = (bf16[2,3,128,1024]{3,2,1,0:T(8,128)(2,1)}, bf16[2,3,128,1024]{3,2,1,0:T(8,128)(2,1)S(1)}, u32[]{:S(2)}, u32[]{:S(2)}) collective-permute-start(bf16[2,3,128,1024]{3,2,1,0:T(8,128)(2,1)} %shard_map.86), channel_id=1, source_target_pairs={{0,2},{1,3},{2,0},{3,1},{4,6},{5,7},{6,4},{7,5},{8,10},{9,11},{10,... | collective-permute-start | bytes 4718600 | tf_op jit(solution)/shard_map/ppermute | solution.py:374
  9.0 0.6 shard_map.87
  9.6 1.6 %collective-permute-start = (bf16[128,512]{1,0:T(8,128)(2,1)S(1)}, bf16[128,512]{1,0:T(8,128)(2,1)S(1)}, u32[]{:S(2)}, u32[]{:S(2)}) collective-permute-start(bf16[128,512]{1,0:T(8,128)(2,1)S(1)} %shard_map.87), channel_id=1, source_target_pairs={{0,8},{4,12},{8,0},{12,4},{16,24},{20,28},{24,16},{28,20},{1,9},{5... | collective-permute-start | bytes 393224 | tf_op jit(solution)/shard_map/ppermute | solution.py:374
  11.3 2.6 %collective-permute-start.2 = (bf16[128,512]{1,0:T(8,128)(2,1)S(1)}, bf16[128,512]{1,0:T(8,128)(2,1)S(1)}, u32[]{:S(2)}, u32[]{:S(2)}) collective-permute-start(bf16[128,512]{1,0:T(8,128)(2,1)S(1)} %shard_map.87), channel_id=1, source_target_pairs={{0,16},{4,20},{8,24},{12,28},{16,0},{20,4},{24,8},{28,12},{1,17},{... | collective-permute-start | bytes 393224 | tf_op jit(solution)/shard_map/ppermute | solution.py:374
  13.8 0.2 collective-permute-start.3
  14.2 1.5 %shard_map.88 = (bf16[1,4,128,1024]{3,2,1,0:T(8,128)(2,1)S(1)}, bf16[1,4,128,1024]{3,2,1,0:T(8,128)(2,1)S(1)}, bf16[1,1,128,1024]{3,2,1,0:T(8,128)(2,1)S(1)}, bf16[1,1,128,1024]{3,2,1,0:T(8,128)(2,1)S(1)}) custom-call(s32[7]{0:T(128)S(1)} %copy-done.2, s32[4,1,256]{2,1,0:T(1,128)S(1)} %bitcast.102, bf16[4,256,1024]{2,1,0:T(8,128)(2,1)S(1)} %copy-done.1), custom_call_target="tpu_custom_call" | custom-call | flops 2147483648 | tf_op jit(solution)/shard_map/pallas_call | solution.py:55
  15.7 0.4 collective-permute-done
  16.3 1.6 %collective-permute-start.1 = (bf16[2,128,512]{2,1,0:T(8,128)(2,1)S(1)}, bf16[2,128,512]{2,1,0:T(8,128)(2,1)S(1)}, u32[]{:S(2)}, u32[]{:S(2)}) collective-permute-start(bf16[2,128,512]{2,1,0:T(8,128)(2,1)S(1)} %pad_maximum_fusion.refs_0_), channel_id=1, source_target_pairs={{0,4},{4,0},{8,12},{12,8},{16,20},{20,16},{24,28},{28,24},{1,5},{5... | collective-permute-start | bytes 786440 | tf_op jit(solution)/shard_map/ppermute | solution.py:374
  17.9 2.5 %shard_map.89 = (f32[4,256,128]{2,1,0:T(8,128)S(1)}, f32[4,8,256]{2,1,0:T(8,128)S(1)}) custom-call(s32[7]{0:T(128)S(1)} %copy-done.2, s32[2,4,2,256]{3,2,1,0:T(2,128)S(1)} %pad_add_fusion.meta, s32[4,16,32]{2,1,0:T(8,128)S(1)} %copy-done.3), custom_call_target="tpu_custom_call" | custom-call | flops 2147483648 | tf_op jit(solution)/shard_map/pallas_call | solution.py:55
  20.4 3.4 %collective-permute-done.2 = bf16[128,512]{1,0:T(8,128)(2,1)S(1)} collective-permute-done((bf16[128,512]{1,0:T(8,128)(2,1)S(1)}, bf16[128,512]{1,0:T(8,128)(2,1)S(1)}, u32[]{:S(2)}, u32[]{:S(2)}) %collective-permute-start.2) | collective-permute-done | bytes 131104 | tf_op jit(solution)/shard_map/ppermute | solution.py:374
  23.9 1.0 %collective-permute-done.1.refs_1_ = bf16[2,128,512]{2,1,0:T(8,128)(2,1)S(1)} collective-permute-done((bf16[2,128,512]{2,1,0:T(8,128)(2,1)S(1)}, bf16[2,128,512]{2,1,0:T(8,128)(2,1)S(1)}, u32[]{:S(2)}, u32[]{:S(2)}) %collective-permute-start.1) | collective-permute-done | bytes 262176 | tf_op jit(solution)/shard_map/ppermute | solution.py:374
  24.9 0.5 collective-permute-start.7
  25.4 1.5 %collective-permute-start.5 = (bf16[1,128,512]{2,1,0:T(8,128)(2,1)S(1)}, bf16[1,128,512]{2,1,0:T(8,128)(2,1)S(1)}, u32[]{:S(2)}, u32[]{:S(2)}) collective-permute-start(bf16[1,128,512]{2,1,0:T(8,128)(2,1)S(1)} %bitcast.93), channel_id=1, source_target_pairs={{0,4},{4,0},{8,12},{12,8},{16,20},{20,16},{24,28},{28,24},{1,5},{5... | collective-permute-start | bytes 393224 | tf_op jit(solution)/shard_map/ppermute | solution.py:374
  26.9 1.4 %collective-permute-start.8 = (bf16[1,128,512]{2,1,0:T(8,128)(2,1)S(1)}, bf16[1,128,512]{2,1,0:T(8,128)(2,1)S(1)}, u32[]{:S(2)}, u32[]{:S(2)}) collective-permute-start(bf16[1,128,512]{2,1,0:T(8,128)(2,1)S(1)} %bitcast.96), channel_id=1, source_target_pairs={{0,4},{4,0},{8,12},{12,8},{16,20},{20,16},{24,28},{28,24},{1,5},{5... | collective-permute-start | bytes 393224 | tf_op jit(solution)/shard_map/ppermute | solution.py:374
  28.3 4.0 %shard_map.90.refs_8_ = bf16[4,1024,512]{2,1,0:T(8,128)(2,1)S(1)} custom-call(s32[7]{0:T(128)S(1)} %copy-done.2, bf16[4,512,1024]{2,1,0:T(8,128)(2,1)S(1)} %copy-done, bf16[2,128,512]{2,1,0:T(8,128)(2,1)S(1)} %pad_maximum_fusion.refs_0_, bf16[2,128,512]{2,1,0:T(8,128)(2,1)S(1)} %collective-permute-done.1.refs_1_, ...), custom_call_target="tpu_custom_call" | custom-call | flops 2147483648 | tf_op jit(solution)/shard_map/pallas_call | solution.py:37
  32.3 1.3 %collective-permute-done.8.refs_3_ = bf16[1,128,512]{2,1,0:T(8,128)(2,1)S(1)} collective-permute-done((bf16[1,128,512]{2,1,0:T(8,128)(2,1)S(1)}, bf16[1,128,512]{2,1,0:T(8,128)(2,1)S(1)}, u32[]{:S(2)}, u32[]{:S(2)}) %collective-permute-start.8) | collective-permute-done | bytes 131104 | tf_op jit(solution)/shard_map/ppermute | solution.py:374
  33.7 0.5 collective-permute-start.10
  34.2 0.8 collective-permute-done.9.refs_4_
  35.2 0.3 collective-permute-start.16
  35.5 0.8 collective-permute-done.12.refs_7_
  36.4 3.8 %shard_map.91.weight = bf16[4,1024,512]{2,1,0:T(8,128)(2,1)S(1)} custom-call(s32[7]{0:T(128)S(1)} %copy-done.2, bf16[4,512,1024]{2,1,0:T(8,128)(2,1)S(1)} %copy-done, bf16[1,128,512]{2,1,0:T(8,128)(2,1)S(1)} %bitcast.95, bf16[1,128,512]{2,1,0:T(8,128)(2,1)S(1)} %collective-permute-done.5.refs_1_, bf16[1,128,512]{2,1,0:T(8,128)(2,1)S(1)} %bitcast.98, ...), custom_call_target="tpu_custom_call" | custom-call | tf_op jit(solution)/shard_map/pallas_call | solution.py:37
  40.2 3.0 %shard_map.92 = (f32[2,2,256]{2,1,0:T(2,128)S(1)}, bf16[1024,512]{1,0:T(8,128)(2,1)S(1)}, bf16[512,1024]{1,0:T(8,128)(2,1)S(1)}) custom-call(s32[7]{0:T(128)S(1)} %copy-done.2, f32[4,256,128]{2,1,0:T(8,128)S(1)} %get-tuple-element.79.table, f32[4,8,256]{2,1,0:T(8,128)S(1)} %get-tuple-element.80.rank, bf16[4,1024,512]{2,1,0:T(8,128)(2,1)S(1)} %shard_map.91.weight, ...), custom_call_target="tpu_custom_call" | custom-call | tf_op jit(solution)/shard_map/pallas_call | solution.py:37
  43.2 0.8 collective-permute-done.16.meta
  44.0 1.7 %collective-permute-start.18 = (bf16[1,1,128,1024]{3,2,1,0:T(8,128)(2,1)S(1)}, bf16[1,1,128,1024]{3,2,1,0:T(8,128)(2,1)S(1)}, u32[]{:S(2)}, u32[]{:S(2)}) collective-permute-start(bf16[1,1,128,1024]{3,2,1,0:T(8,128)(2,1)S(1)} %get-tuple-element.110), channel_id=1, source_target_pairs={{0,2},{1,3},{2,0},{3,1},{4,6},{5,7},{6,4},{7,5},{8,10},{9,11},{10,... | collective-permute-start | bytes 786440 | tf_op jit(solution)/shard_map/ppermute | solution.py:374
  45.9 3.0 %shard_map.93 = (f32[2,2,256]{2,1,0:T(2,128)S(1)}, bf16[1024,512]{1,0:T(8,128)(2,1)S(1)}, bf16[512,1024]{1,0:T(8,128)(2,1)S(1)}) custom-call(s32[7]{0:T(128)S(1)} %copy-done.2, f32[4,256,128]{2,1,0:T(8,128)S(1)} %get-tuple-element.79.table, f32[4,8,256]{2,1,0:T(8,128)S(1)} %get-tuple-element.80.rank, bf16[4,1024,512]{2,1,0:T(8,128)(2,1)S(1)} %shard_map.91.weight, ...), custom_call_target="tpu_custom_call" | custom-call | tf_op jit(solution)/shard_map/pallas_call | solution.py:37
  48.9 0.3 collective-permute-start.14
  49.3 2.5 %shard_map.94 = (f32[4,256,128]{2,1,0:T(8,128)S(1)}, f32[4,8,256]{2,1,0:T(8,128)S(1)}) custom-call(s32[7]{0:T(128)S(1)} %copy-done.2, s32[2,4,2,256]{3,2,1,0:T(2,128)S(1)} %collective-permute-done.16.meta, s32[4,16,32]{2,1,0:T(8,128)S(1)} %copy-done.3), custom_call_target="tpu_custom_call" | custom-call | tf_op jit(solution)/shard_map/pallas_call | solution.py:55
  51.8 2.0 %shard_map.96.refs_4_ = f32[2,1024,256]{2,1,0:T(8,128)S(1)} custom-call(s32[7]{0:T(128)S(1)} %copy-done.2, bf16[1024,512]{1,0:T(8,128)(2,1)S(1)} %get-tuple-element.114.refs_0_, bf16[512,1024]{1,0:T(8,128)(2,1)S(1)} %get-tuple-element.115.refs_1_, bf16[1024,512]{1,0:T(8,128)(2,1)S(1)} %get-tuple-element.116.refs_2_, ...), custom_call_target="tpu_custom_call" | custom-call | tf_op jit(solution)/shard_map/pallas_call | solution.py:55
  53.8 4.2 %shard_map.95 = (f32[3,2,256]{2,1,0:T(2,128)S(1)}, bf16[1024,768]{1,0:T(8,128)(2,1)S(1)}, bf16[768,1024]{1,0:T(8,128)(2,1)S(1)}) custom-call(s32[7]{0:T(128)S(1)} %copy-done.2, f32[4,256,128]{2,1,0:T(8,128)S(1)} %get-tuple-element.106.table, f32[4,8,256]{2,1,0:T(8,128)S(1)} %get-tuple-element.107.rank, bf16[4,1024,512]{2,1,0:T(8,128)(2,1)S(1)} %shard_map.91.weight, ...), custom_call_target="tpu_custom_call" | custom-call | tf_op jit(solution)/shard_map/pallas_call | solution.py:37
  58.1 1.7 %shard_map.97 = (f32[1,2,256]{2,1,0:T(2,128)S(1)}, bf16[1024,256]{1,0:T(8,128)(2,1)S(1)}, bf16[256,1024]{1,0:T(8,128)(2,1)S(1)}) custom-call(s32[7]{0:T(128)S(1)} %copy-done.2, f32[4,256,128]{2,1,0:T(8,128)S(1)} %get-tuple-element.106.table, f32[4,8,256]{2,1,0:T(8,128)S(1)} %get-tuple-element.107.rank, bf16[4,1024,512]{2,1,0:T(8,128)(2,1)S(1)} %shard_map.91.weight, ...), custom_call_target="tpu_custom_call" | custom-call | tf_op jit(solution)/shard_map/pallas_call | solution.py:37
  59.8 2.0 %shard_map.99 = bf16[2,1024,256]{2,1,0:T(8,128)(2,1)S(1)} custom-call(s32[7]{0:T(128)S(1)} %copy-done.2, bf16[1024,768]{1,0:T(8,128)(2,1)S(1)} %get-tuple-element.121.refs_4_.refs_0_, bf16[768,1024]{1,0:T(8,128)(2,1)S(1)} %get-tuple-element.122.refs_5_.refs_1_, bf16[1024,256]{1,0:T(8,128)(2,1)S(1)} %get-tuple-element.123.refs_6_.refs_2_, ...), custom_call_target="tpu_custom_call" | custom-call | tf_op jit(solution)/shard_map/pallas_call | solution.py:55
  61.8 0.3 collective-permute-start.22
  62.1 3.1 %shard_map.98 = f32[2,1024,256]{2,1,0:T(8,128)S(1)} custom-call(s32[7]{0:T(128)S(1)} %copy-done.2, bf16[1024,512]{1,0:T(8,128)(2,1)S(1)} %get-tuple-element.114.refs_0_, bf16[512,1024]{1,0:T(8,128)(2,1)S(1)} %get-tuple-element.115.refs_1_, bf16[1024,512]{1,0:T(8,128)(2,1)S(1)} %get-tuple-element.116.refs_2_, ...), custom_call_target="tpu_custom_call" | custom-call | flops 34359738368 | tf_op jit(solution)/shard_map/pallas_call | solution.py:55
  65.2 0.2 fusion.7
  65.4 1.8 %collective-permute-start.25 = (bf16[4,128,256]{2,1,0:T(8,128)(2,1)S(1)}, bf16[4,128,256]{2,1,0:T(8,128)(2,1)S(1)}, u32[]{:S(2)}, u32[]{:S(2)}) collective-permute-start(bf16[4,128,256]{2,1,0:T(8,128)(2,1)S(1)} %get-tuple-element.136), channel_id=1, source_target_pairs={{0,2},{1,3},{2,0},{3,1},{4,6},{5,7},{6,4},{7,5},{8,10},{9,11},{10,... | collective-permute-start | bytes 786440 | tf_op jit(solution)/shard_map/ppermute | solution.py:380
  67.2 1.4 %collective-permute-start.24 = (bf16[4,128,256]{2,1,0:T(8,128)(2,1)S(1)}, bf16[4,128,256]{2,1,0:T(8,128)(2,1)S(1)}, u32[]{:S(2)}, u32[]{:S(2)}) collective-permute-start(bf16[4,128,256]{2,1,0:T(8,128)(2,1)S(1)} %get-tuple-element.135), channel_id=1, source_target_pairs={{0,6},{1,7},{2,4},{3,5},{4,2},{5,3},{6,0},{7,1},{8,14},{9,15},{10,... | collective-permute-start | bytes 786440 | tf_op jit(solution)/shard_map/ppermute | solution.py:380
  68.6 0.3 collective-permute-start.23
  69.0 0.8 collective-permute-start.21
  69.8 9.8 %collective-permute-done.25 = bf16[4,128,256]{2,1,0:T(8,128)(2,1)S(1)} collective-permute-done((bf16[4,128,256]{2,1,0:T(8,128)(2,1)S(1)}, bf16[4,128,256]{2,1,0:T(8,128)(2,1)S(1)}, u32[]{:S(2)}, u32[]{:S(2)}) %collective-permute-start.25) | collective-permute-done | bytes 262176 | tf_op jit(solution)/shard_map/ppermute | solution.py:380
  79.6 1.7 %collective-permute-start.20 = (f32[4,256]{1,0:T(4,128)S(1)}, f32[4,256]{1,0:T(4,128)S(1)}, u32[]{:S(2)}, u32[]{:S(2)}) collective-permute-start(f32[4,256]{1,0:T(4,128)S(1)} %bitcast.108), channel_id=1, source_target_pairs={{0,2},{1,3},{2,0},{3,1},{4,6},{5,7},{6,4},{7,5},{8,10},{9,11},{10,... | collective-permute-start | bytes 12296 | tf_op jit(solution)/shard_map/ppermute | solution.py:374
  81.6 3.7 %collective-permute-start.28 = (bf16[128,256]{1,0:T(8,128)(2,1)S(1)}, bf16[128,256]{1,0:T(8,128)(2,1)S(1)}, u32[]{:S(2)}, u32[]{:S(2)}) collective-permute-start(bf16[128,256]{1,0:T(8,128)(2,1)S(1)} %get-tuple-element.138), channel_id=1, source_target_pairs={{0,24},{4,28},{8,16},{12,20},{16,8},{20,12},{24,0},{28,4},{1,25},{... | collective-permute-start | bytes 196616 | tf_op jit(solution)/shard_map/ppermute | solution.py:374
  85.3 0.8 collective-permute-start.26
  86.1 0.6 fusion.19
  86.7 1.5 %collective-permute-done.28 = bf16[128,256]{1,0:T(8,128)(2,1)S(1)} collective-permute-done((bf16[128,256]{1,0:T(8,128)(2,1)S(1)}, bf16[128,256]{1,0:T(8,128)(2,1)S(1)}, u32[]{:S(2)}, u32[]{:S(2)}) %collective-permute-start.28) | collective-permute-done | bytes 65568 | tf_op jit(solution)/shard_map/ppermute | solution.py:374
  88.1 2.4 %collective-permute-done.27 = bf16[128,256]{1,0:T(8,128)(2,1)S(1)} collective-permute-done((bf16[128,256]{1,0:T(8,128)(2,1)S(1)}, bf16[128,256]{1,0:T(8,128)(2,1)S(1)}, u32[]{:S(2)}, u32[]{:S(2)}) %collective-permute-start.27) | collective-permute-done | bytes 65568 | tf_op jit(solution)/shard_map/ppermute | solution.py:374
  90.6 0.7 fusion.11
  (56 shorter events, 1.0 us)
Async XLA Ops:
  0.6 8.4 %copy-start.5 = (bf16[128,1024]{1,0:T(8,128)(2,1)S(1)}, bf16[128,1024]{1,0:T(8,128)(2,1)}, u32[]{:S(2)}) copy-start(bf16[128,1024]{1,0:T(8,128)(2,1)} %proj) | copy-start | bytes 786436
  2.0 7.1 %copy-start.2 = (s32[7]{0:T(128)S(1)}, s32[7]{0:T(128)}, u32[]{:S(2)}) copy-start(s32[7]{0:T(128)} %pad_add_fusion.2.info) | copy-start | bytes 88
  6.0 8.1 %copy-start.6 = (s32[4,256]{1,0:T(4,128)S(1)}, s32[4,256]{1,0:T(4,128)}, u32[]{:S(2)}) copy-start(s32[4,256]{1,0:T(4,128)} %param.11) | copy-start | bytes 12292
  6.0 8.1 %copy-start.4 = (s32[4,256,1]{1,2,0:T(1,128)S(1)}, s32[4,256,1]{1,2,0:T(1,128)}, u32[]{:S(2)}) copy-start(s32[4,256,1]{1,2,0:T(1,128)} %param.10) | copy-start | bytes 12292
  6.0 8.2 %copy-start.1 = (bf16[4,256,1024]{2,1,0:T(8,128)(2,1)S(1)}, bf16[4,256,1024]{2,1,0:T(8,128)(2,1)}, u32[]{:S(2)}) copy-start(bf16[4,256,1024]{2,1,0:T(8,128)(2,1)} %words.3) | copy-start | bytes 6291460
  6.0 38.0 %collective-permute-start.15 = (bf16[2,3,128,1024]{3,2,1,0:T(8,128)(2,1)}, bf16[2,3,128,1024]{3,2,1,0:T(8,128)(2,1)S(1)}, u32[]{:S(2)}, u32[]{:S(2)}) collective-permute-start(bf16[2,3,128,1024]{3,2,1,0:T(8,128)(2,1)} %shard_map.86), channel_id=1, source_target_pairs={{0,2},{1,3},{2,0},{3,1},{4,6},{5,7},{6,4},{7,5},{8,10},{9,11},{10,... | collective-permute-start | bytes 4718600 | tf_op jit(solution)/shard_map/ppermute | solution.py:374
  9.6 6.5 %collective-permute-start = (bf16[128,512]{1,0:T(8,128)(2,1)S(1)}, bf16[128,512]{1,0:T(8,128)(2,1)S(1)}, u32[]{:S(2)}, u32[]{:S(2)}) collective-permute-start(bf16[128,512]{1,0:T(8,128)(2,1)S(1)} %shard_map.87), channel_id=1, source_target_pairs={{0,8},{4,12},{8,0},{12,4},{16,24},{20,28},{24,16},{28,20},{1,9},{5... | collective-permute-start | bytes 393224 | tf_op jit(solution)/shard_map/ppermute | solution.py:374
  11.3 12.6 %collective-permute-start.2 = (bf16[128,512]{1,0:T(8,128)(2,1)S(1)}, bf16[128,512]{1,0:T(8,128)(2,1)S(1)}, u32[]{:S(2)}, u32[]{:S(2)}) collective-permute-start(bf16[128,512]{1,0:T(8,128)(2,1)S(1)} %shard_map.87), channel_id=1, source_target_pairs={{0,16},{4,20},{8,24},{12,28},{16,0},{20,4},{24,8},{28,12},{1,17},{... | collective-permute-start | bytes 393224 | tf_op jit(solution)/shard_map/ppermute | solution.py:374
  13.8 10.1 %collective-permute-start.3 = (bf16[128,512]{1,0:T(8,128)(2,1)S(1)}, bf16[128,512]{1,0:T(8,128)(2,1)S(1)}, u32[]{:S(2)}, u32[]{:S(2)}) collective-permute-start(bf16[128,512]{1,0:T(8,128)(2,1)S(1)} %shard_map.87), channel_id=1, source_target_pairs={{0,24},{4,28},{8,16},{12,20},{16,8},{20,12},{24,0},{28,4},{1,25},{... | collective-permute-start | bytes 393224 | tf_op jit(solution)/shard_map/ppermute | solution.py:374
  14.1 3.8 %copy-start.3 = (s32[4,16,32]{2,1,0:T(8,128)S(1)}, s32[4,16,32]{2,1,0:T(8,128)}, u32[]{:S(2)}) copy-start(s32[4,16,32]{2,1,0:T(8,128)} %flags.3) | copy-start | bytes 24580
  14.1 2.2 %collective-permute-start.4 = (s32[4,2,256]{2,1,0:T(2,128)S(1)}, s32[4,2,256]{2,1,0:T(2,128)S(1)}, u32[]{:S(2)}, u32[]{:S(2)}) collective-permute-start(s32[4,2,256]{2,1,0:T(2,128)S(1)} %get-tuple-element.143), channel_id=1, source_target_pairs={{0,1},{1,0},{2,3},{3,2},{4,5},{5,4},{6,7},{7,6},{8,9},{9,8},{10,11... | collective-permute-start | bytes 24584 | tf_op jit(solution)/shard_map/ppermute | solution.py:374
  16.1 24.1 %collective-permute-start.13 = (bf16[1,4,128,1024]{3,2,1,0:T(8,128)(2,1)S(1)}, bf16[1,4,128,1024]{3,2,1,0:T(8,128)(2,1)S(1)}, u32[]{:S(2)}, u32[]{:S(2)}) collective-permute-start(bf16[1,4,128,1024]{3,2,1,0:T(8,128)(2,1)S(1)} %get-tuple-element.96), channel_id=1, source_target_pairs={{0,1},{1,0},{2,3},{3,2},{4,5},{5,4},{6,7},{7,6},{8,9},{9,8},{10,11... | collective-permute-start | bytes 3145736 | tf_op jit(solution)/shard_map/ppermute | solution.py:374
  16.3 8.6 %collective-permute-start.1 = (bf16[2,128,512]{2,1,0:T(8,128)(2,1)S(1)}, bf16[2,128,512]{2,1,0:T(8,128)(2,1)S(1)}, u32[]{:S(2)}, u32[]{:S(2)}) collective-permute-start(bf16[2,128,512]{2,1,0:T(8,128)(2,1)S(1)} %pad_maximum_fusion.refs_0_), channel_id=1, source_target_pairs={{0,4},{4,0},{8,12},{12,8},{16,20},{20,16},{24,28},{28,24},{1,5},{5... | collective-permute-start | bytes 786440 | tf_op jit(solution)/shard_map/ppermute | solution.py:374
  17.9 10.5 %copy-start = (bf16[4,512,1024]{2,1,0:T(8,128)(2,1)S(1)}, bf16[4,512,1024]{2,1,0:T(8,128)(2,1)}, u32[]{:S(2)}) copy-start(bf16[4,512,1024]{2,1,0:T(8,128)(2,1)} %patches.11) | copy-start | bytes 12582916
  24.9 2.0 %collective-permute-start.6 = (bf16[2,128,512]{2,1,0:T(8,128)(2,1)S(1)}, bf16[2,128,512]{2,1,0:T(8,128)(2,1)S(1)}, u32[]{:S(2)}, u32[]{:S(2)}) collective-permute-start(bf16[2,128,512]{2,1,0:T(8,128)(2,1)S(1)} %pad_maximum_fusion.refs_0_), channel_id=1, source_target_pairs={{0,1},{1,0},{2,3},{3,2},{4,5},{5,4},{6,7},{7,6},{8,9},{9,8},{10,11... | collective-permute-start | bytes 786440 | tf_op jit(solution)/shard_map/ppermute | solution.py:374
  24.9 2.0 %collective-permute-start.7 = (bf16[2,128,512]{2,1,0:T(8,128)(2,1)S(1)}, bf16[2,128,512]{2,1,0:T(8,128)(2,1)S(1)}, u32[]{:S(2)}, u32[]{:S(2)}) collective-permute-start(bf16[2,128,512]{2,1,0:T(8,128)(2,1)S(1)} %collective-permute-done.1.refs_1_), channel_id=1, source_target_pairs={{0,1},{1,0},{2,3},{3,2},{4,5},{5,4},{6,7},{7,6},{8,9},{9,8},{10,11... | collective-permute-start | bytes 786440 | tf_op jit(solution)/shard_map/ppermute | solution.py:374
  25.4 6.9 %collective-permute-start.5 = (bf16[1,128,512]{2,1,0:T(8,128)(2,1)S(1)}, bf16[1,128,512]{2,1,0:T(8,128)(2,1)S(1)}, u32[]{:S(2)}, u32[]{:S(2)}) collective-permute-start(bf16[1,128,512]{2,1,0:T(8,128)(2,1)S(1)} %bitcast.93), channel_id=1, source_target_pairs={{0,4},{4,0},{8,12},{12,8},{16,20},{20,16},{24,28},{28,24},{1,5},{5... | collective-permute-start | bytes 393224 | tf_op jit(solution)/shard_map/ppermute | solution.py:374
  26.9 6.7 %collective-permute-start.8 = (bf16[1,128,512]{2,1,0:T(8,128)(2,1)S(1)}, bf16[1,128,512]{2,1,0:T(8,128)(2,1)S(1)}, u32[]{:S(2)}, u32[]{:S(2)}) collective-permute-start(bf16[1,128,512]{2,1,0:T(8,128)(2,1)S(1)} %bitcast.96), channel_id=1, source_target_pairs={{0,4},{4,0},{8,12},{12,8},{16,20},{20,16},{24,28},{28,24},{1,5},{5... | collective-permute-start | bytes 393224 | tf_op jit(solution)/shard_map/ppermute | solution.py:374
  33.7 1.3 %collective-permute-start.9 = (bf16[1,128,512]{2,1,0:T(8,128)(2,1)S(1)}, bf16[1,128,512]{2,1,0:T(8,128)(2,1)S(1)}, u32[]{:S(2)}, u32[]{:S(2)}) collective-permute-start(bf16[1,128,512]{2,1,0:T(8,128)(2,1)S(1)} %bitcast.94), channel_id=1, source_target_pairs={{0,1},{1,0},{2,3},{3,2},{4,5},{5,4},{6,7},{7,6},{8,9},{9,8},{10,11... | collective-permute-start | bytes 393224 | tf_op jit(solution)/shard_map/ppermute | solution.py:374
  33.7 1.5 %collective-permute-start.10 = (bf16[1,128,512]{2,1,0:T(8,128)(2,1)S(1)}, bf16[1,128,512]{2,1,0:T(8,128)(2,1)S(1)}, u32[]{:S(2)}, u32[]{:S(2)}) collective-permute-start(bf16[1,128,512]{2,1,0:T(8,128)(2,1)S(1)} %collective-permute-done.5.refs_1_), channel_id=1, source_target_pairs={{0,1},{1,0},{2,3},{3,2},{4,5},{5,4},{6,7},{7,6},{8,9},{9,8},{10,11... | collective-permute-start | bytes 393224 | tf_op jit(solution)/shard_map/ppermute | solution.py:374
  34.2 1.3 %collective-permute-start.11 = (bf16[1,128,512]{2,1,0:T(8,128)(2,1)S(1)}, bf16[1,128,512]{2,1,0:T(8,128)(2,1)S(1)}, u32[]{:S(2)}, u32[]{:S(2)}) collective-permute-start(bf16[1,128,512]{2,1,0:T(8,128)(2,1)S(1)} %bitcast.97), channel_id=1, source_target_pairs={{0,1},{1,0},{2,3},{3,2},{4,5},{5,4},{6,7},{7,6},{8,9},{9,8},{10,11... | collective-permute-start | bytes 393224 | tf_op jit(solution)/shard_map/ppermute | solution.py:374
  35.0 1.3 %collective-permute-start.12 = (bf16[1,128,512]{2,1,0:T(8,128)(2,1)S(1)}, bf16[1,128,512]{2,1,0:T(8,128)(2,1)S(1)}, u32[]{:S(2)}, u32[]{:S(2)}) collective-permute-start(bf16[1,128,512]{2,1,0:T(8,128)(2,1)S(1)} %collective-permute-done.8.refs_3_), channel_id=1, source_target_pairs={{0,1},{1,0},{2,3},{3,2},{4,5},{5,4},{6,7},{7,6},{8,9},{9,8},{10,11... | collective-permute-start | bytes 393224 | tf_op jit(solution)/shard_map/ppermute | solution.py:374
  35.2 8.8 %collective-permute-start.16 = (s32[2,4,2,256]{3,2,1,0:T(2,128)S(1)}, s32[2,4,2,256]{3,2,1,0:T(2,128)S(1)}, u32[]{:S(2)}, u32[]{:S(2)}) collective-permute-start(s32[2,4,2,256]{3,2,1,0:T(2,128)S(1)} %pad_add_fusion.meta), channel_id=1, source_target_pairs={{0,2},{1,3},{2,0},{3,1},{4,6},{5,7},{6,4},{7,5},{8,10},{9,11},{10,... | collective-permute-start | bytes 49160 | tf_op jit(solution)/shard_map/ppermute | solution.py:374
  44.0 9.8 %collective-permute-start.17 = (bf16[2,3,128,1024]{3,2,1,0:T(8,128)(2,1)S(1)}, bf16[2,3,128,1024]{3,2,1,0:T(8,128)(2,1)S(1)}, u32[]{:S(2)}, u32[]{:S(2)}) collective-permute-start(bf16[2,3,128,1024]{3,2,1,0:T(8,128)(2,1)S(1)} %collective-permute-done.15.refs_0_), channel_id=1, source_target_pairs={{0,1},{1,0},{2,3},{3,2},{4,5},{5,4},{6,7},{7,6},{8,9},{9,8},{10,11... | collective-permute-start | bytes 4718600 | tf_op jit(solution)/shard_map/ppermute | solution.py:374
  44.0 14.0 %collective-permute-start.18 = (bf16[1,1,128,1024]{3,2,1,0:T(8,128)(2,1)S(1)}, bf16[1,1,128,1024]{3,2,1,0:T(8,128)(2,1)S(1)}, u32[]{:S(2)}, u32[]{:S(2)}) collective-permute-start(bf16[1,1,128,1024]{3,2,1,0:T(8,128)(2,1)S(1)} %get-tuple-element.110), channel_id=1, source_target_pairs={{0,2},{1,3},{2,0},{3,1},{4,6},{5,7},{6,4},{7,5},{8,10},{9,11},{10,... | collective-permute-start | bytes 786440 | tf_op jit(solution)/shard_map/ppermute | solution.py:374
  45.7 12.3 %collective-permute-start.19 = (bf16[1,1,128,1024]{3,2,1,0:T(8,128)(2,1)S(1)}, bf16[1,1,128,1024]{3,2,1,0:T(8,128)(2,1)S(1)}, u32[]{:S(2)}, u32[]{:S(2)}) collective-permute-start(bf16[1,1,128,1024]{3,2,1,0:T(8,128)(2,1)S(1)} %get-tuple-element.111), channel_id=1, source_target_pairs={{0,3},{1,2},{2,1},{3,0},{4,7},{5,6},{6,5},{7,4},{8,11},{9,10},{10,... | collective-permute-start | bytes 786440 | tf_op jit(solution)/shard_map/ppermute | solution.py:374
  48.9 36.3 %collective-permute-start.14 = (f32[4,256]{1,0:T(4,128)S(1)}, f32[4,256]{1,0:T(4,128)S(1)}, u32[]{:S(2)}, u32[]{:S(2)}) collective-permute-start(f32[4,256]{1,0:T(4,128)S(1)} %fusion.20), channel_id=1, source_target_pairs={{0,1},{1,0},{2,3},{3,2},{4,5},{5,4},{6,7},{7,6},{8,9},{9,8},{10,11... | collective-permute-start | bytes 12296 | tf_op jit(solution)/shard_map/ppermute | solution.py:374
  61.8 3.4 %collective-permute-start.22 = (bf16[2,1024,256]{2,1,0:T(8,128)(2,1)S(1)}, bf16[2,1024,256]{2,1,0:T(8,128)(2,1)S(1)}, u32[]{:S(2)}, u32[]{:S(2)}) collective-permute-start(bf16[2,1024,256]{2,1,0:T(8,128)(2,1)S(1)} %shard_map.99), channel_id=1, source_target_pairs={{0,1},{1,0},{2,3},{3,2},{4,5},{5,4},{6,7},{7,6},{8,9},{9,8},{10,11... | collective-permute-start | bytes 3145736 | tf_op jit(solution)/shard_map/ppermute | solution.py:374
  65.4 14.2 %collective-permute-start.25 = (bf16[4,128,256]{2,1,0:T(8,128)(2,1)S(1)}, bf16[4,128,256]{2,1,0:T(8,128)(2,1)S(1)}, u32[]{:S(2)}, u32[]{:S(2)}) collective-permute-start(bf16[4,128,256]{2,1,0:T(8,128)(2,1)S(1)} %get-tuple-element.136), channel_id=1, source_target_pairs={{0,2},{1,3},{2,0},{3,1},{4,6},{5,7},{6,4},{7,5},{8,10},{9,11},{10,... | collective-permute-start | bytes 786440 | tf_op jit(solution)/shard_map/ppermute | solution.py:380
  67.2 14.2 %collective-permute-start.24 = (bf16[4,128,256]{2,1,0:T(8,128)(2,1)S(1)}, bf16[4,128,256]{2,1,0:T(8,128)(2,1)S(1)}, u32[]{:S(2)}, u32[]{:S(2)}) collective-permute-start(bf16[4,128,256]{2,1,0:T(8,128)(2,1)S(1)} %get-tuple-element.135), channel_id=1, source_target_pairs={{0,6},{1,7},{2,4},{3,5},{4,2},{5,3},{6,0},{7,1},{8,14},{9,15},{10,... | collective-permute-start | bytes 786440 | tf_op jit(solution)/shard_map/ppermute | solution.py:380
  68.6 12.7 %collective-permute-start.23 = (bf16[4,128,256]{2,1,0:T(8,128)(2,1)S(1)}, bf16[4,128,256]{2,1,0:T(8,128)(2,1)S(1)}, u32[]{:S(2)}, u32[]{:S(2)}) collective-permute-start(bf16[4,128,256]{2,1,0:T(8,128)(2,1)S(1)} %get-tuple-element.134), channel_id=1, source_target_pairs={{0,4},{1,5},{2,6},{3,7},{4,0},{5,1},{6,2},{7,3},{8,12},{9,13},{10,... | collective-permute-start | bytes 786440 | tf_op jit(solution)/shard_map/ppermute | solution.py:380
  69.0 17.0 %collective-permute-start.21 = (f32[4,256]{1,0:T(4,128)S(1)}, f32[4,256]{1,0:T(4,128)S(1)}, u32[]{:S(2)}, u32[]{:S(2)}) collective-permute-start(f32[4,256]{1,0:T(4,128)S(1)} %bitcast.107), channel_id=1, source_target_pairs={{0,3},{1,2},{2,1},{3,0},{4,7},{5,6},{6,5},{7,4},{8,11},{9,10},{10,... | collective-permute-start | bytes 12296 | tf_op jit(solution)/shard_map/ppermute | solution.py:374
  79.6 6.4 %collective-permute-start.20 = (f32[4,256]{1,0:T(4,128)S(1)}, f32[4,256]{1,0:T(4,128)S(1)}, u32[]{:S(2)}, u32[]{:S(2)}) collective-permute-start(f32[4,256]{1,0:T(4,128)S(1)} %bitcast.108), channel_id=1, source_target_pairs={{0,2},{1,3},{2,0},{3,1},{4,6},{5,7},{6,4},{7,5},{8,10},{9,11},{10,... | collective-permute-start | bytes 12296 | tf_op jit(solution)/shard_map/ppermute | solution.py:374
  81.6 6.5 %collective-permute-start.28 = (bf16[128,256]{1,0:T(8,128)(2,1)S(1)}, bf16[128,256]{1,0:T(8,128)(2,1)S(1)}, u32[]{:S(2)}, u32[]{:S(2)}) collective-permute-start(bf16[128,256]{1,0:T(8,128)(2,1)S(1)} %get-tuple-element.138), channel_id=1, source_target_pairs={{0,24},{4,28},{8,16},{12,20},{16,8},{20,12},{24,0},{28,4},{1,25},{... | collective-permute-start | bytes 196616 | tf_op jit(solution)/shard_map/ppermute | solution.py:374
  85.3 5.3 %collective-permute-start.27 = (bf16[128,256]{1,0:T(8,128)(2,1)S(1)}, bf16[128,256]{1,0:T(8,128)(2,1)S(1)}, u32[]{:S(2)}, u32[]{:S(2)}) collective-permute-start(bf16[128,256]{1,0:T(8,128)(2,1)S(1)} %get-tuple-element.139), channel_id=1, source_target_pairs={{0,16},{4,20},{8,24},{12,28},{16,0},{20,4},{24,8},{28,12},{1,17},{... | collective-permute-start | bytes 196616 | tf_op jit(solution)/shard_map/ppermute | solution.py:374
  85.3 5.3 %collective-permute-start.26 = (bf16[128,256]{1,0:T(8,128)(2,1)S(1)}, bf16[128,256]{1,0:T(8,128)(2,1)S(1)}, u32[]{:S(2)}, u32[]{:S(2)}) collective-permute-start(bf16[128,256]{1,0:T(8,128)(2,1)S(1)} %get-tuple-element.137), channel_id=1, source_target_pairs={{0,8},{4,12},{8,0},{12,4},{16,24},{20,28},{24,16},{28,20},{1,9},{5... | collective-permute-start | bytes 196616 | tf_op jit(solution)/shard_map/ppermute | solution.py:374

commit v14 on v13

--- a/solution.py
+++ b/solution.py
@@ -410,7 +410,7 @@
     routes = routes.reshape(pages, 1, wdev)
 
     split = pages - 1
-    both = first_dispatch(
+    both = dispatch(
         info, routes, words, [((2 * k, 2 * k + 1), 0, split) for k in range(1, n_y)], cap
     )
     info, proj, both = lax.optimization_barrier((info, proj, both))

time: 91.5 us -> 90.3 us (0.987)
  Pallas kernels: 37.9 us -> 35.3 us
  local copies, waits for them, and re-layouts: 0.11 us -> 2.37 us
    pallas_call x1 -> x0, Pallas kernels: 4 us -> none  [first_dispatch(): pl.pallas_call(functools.partial(first_dispatch_kernel, plan, cap), in_sp...]
    unnamed x17, local copies, waits for them, and re-layouts: 0.05 us -> 2.31 us
    pallas_call x7 -> x8, Pallas kernels: 14.2 us -> 15.5 us  [call_whole(): pl.pallas_call(kernel, in_specs=[pl.BlockSpec(memory_space=pltpu.SMEM)] +...]
  transfers between devices with their start and end apart: 29 -> 29, of which waited for: 10 -> 10; matrix products, arithmetic and copies ran while one was open for 1% -> 1% of each run, Pallas kernels for 37% -> 38%
where the time goes in v14:
time: 90.3 us; the launch traced here: 90.1 us
  Pallas kernels  35.3 us (39%)
  starting transfers between devices  26.7 us (30%)
  waiting for transfers between devices  22.3 us (25%)
  other arithmetic  2.49 us (3%)
  local copies, waits for them, and re-layouts  2.37 us (3%)
  between operations  0.92 us (1%)
    ppermute x26, starting transfers between devices, exchange(): return lax.ppermute(x, axis, [(i, i ^ offset) for i in range(n)])  23.2 us
    pallas_call x6, Pallas kernels, call(): pl.pallas_call(kernel, grid_spec=pltpu.PrefetchScalarGridSpec(num_scalar_...  19.8 us
    pallas_call x8, Pallas kernels, call_whole(): pl.pallas_call(kernel, in_specs=[pl.BlockSpec(memory_space=pltpu.SMEM)] +...  15.5 us
    ppermute x26, waiting for transfers between devices, exchange(): return lax.ppermute(x, axis, [(i, i ^ offset) for i in range(n)])  12.5 us
    ppermute x3, waiting for transfers between devices, exchange_both(): lax.ppermute(x, ('dp', 'seq'), [(i, i ^ dp * n_seq + seq) for i in range(...  9.79 us
    ppermute x3, starting transfers between devices, exchange_both(): lax.ppermute(x, ('dp', 'seq'), [(i, i ^ dp * n_seq + seq) for i in range(...  3.55 us
    unnamed x17, local copies, waits for them, and re-layouts  2.31 us
  transfers between devices with their start and end apart: 29, of which 10 were waited for; matrix products, arithmetic and copies ran while one was open for 1% of the time, Pallas kernels for 38%

profile of v14, /device:TPU:0, one launch (start us, length us, event | category | flops | bytes accessed | tf_op | source)
XLA Modules:
  0.0 90.1 jit_solution(2081587951310593555)
XLA Ops:
  0.6 0.7 pad_add_fusion.2.info
  1.4 1.6 %copy-done.1 = bf16[4,256,1024]{2,1,0:T(8,128)(2,1)S(1)} copy-done((bf16[4,256,1024]{2,1,0:T(8,128)(2,1)S(1)}, bf16[4,256,1024]{2,1,0:T(8,128)(2,1)}, u32[]{:S(2)}) %copy-start.1) | copy-done | bytes 2097176
  3.0 0.7 copy-done.4
  3.7 1.3 %shard_map.86 = bf16[2,3,128,1024]{3,2,1,0:T(8,128)(2,1)S(1)} custom-call(s32[7]{0:T(128)S(1)} %pad_add_fusion.2.info, s32[4,1,256]{2,1,0:T(1,128)S(1)} %bitcast.100, bf16[4,256,1024]{2,1,0:T(8,128)(2,1)S(1)} %copy-done.1), custom_call_target="tpu_custom_call" | custom-call | tf_op jit(solution)/shard_map/pallas_call | solution.py:55
  5.0 3.0 %collective-permute-start.15 = (bf16[2,3,128,1024]{3,2,1,0:T(8,128)(2,1)S(1)}, bf16[2,3,128,1024]{3,2,1,0:T(8,128)(2,1)S(1)}, u32[]{:S(2)}, u32[]{:S(2)}) collective-permute-start(bf16[2,3,128,1024]{3,2,1,0:T(8,128)(2,1)S(1)} %shard_map.86), channel_id=1, source_target_pairs={{0,2},{1,3},{2,0},{3,1},{4,6},{5,7},{6,4},{7,5},{8,10},{9,11},{10,... | collective-permute-start | bytes 4718600 | tf_op jit(solution)/shard_map/ppermute | solution.py:374
  8.0 0.6 shard_map.87
  8.6 1.6 %collective-permute-start = (bf16[128,512]{1,0:T(8,128)(2,1)S(1)}, bf16[128,512]{1,0:T(8,128)(2,1)S(1)}, u32[]{:S(2)}, u32[]{:S(2)}) collective-permute-start(bf16[128,512]{1,0:T(8,128)(2,1)S(1)} %shard_map.87), channel_id=1, source_target_pairs={{0,8},{4,12},{8,0},{12,4},{16,24},{20,28},{24,16},{28,20},{1,9},{5... | collective-permute-start | bytes 393224 | tf_op jit(solution)/shard_map/ppermute | solution.py:374
  10.2 2.6 %collective-permute-start.2 = (bf16[128,512]{1,0:T(8,128)(2,1)S(1)}, bf16[128,512]{1,0:T(8,128)(2,1)S(1)}, u32[]{:S(2)}, u32[]{:S(2)}) collective-permute-start(bf16[128,512]{1,0:T(8,128)(2,1)S(1)} %shard_map.87), channel_id=1, source_target_pairs={{0,16},{4,20},{8,24},{12,28},{16,0},{20,4},{24,8},{28,12},{1,17},{... | collective-permute-start | bytes 393224 | tf_op jit(solution)/shard_map/ppermute | solution.py:374
  13.1 1.5 %shard_map.88 = (bf16[1,4,128,1024]{3,2,1,0:T(8,128)(2,1)S(1)}, bf16[1,4,128,1024]{3,2,1,0:T(8,128)(2,1)S(1)}, bf16[1,1,128,1024]{3,2,1,0:T(8,128)(2,1)S(1)}, bf16[1,1,128,1024]{3,2,1,0:T(8,128)(2,1)S(1)}) custom-call(s32[7]{0:T(128)S(1)} %pad_add_fusion.2.info, s32[4,1,256]{2,1,0:T(1,128)S(1)} %bitcast.102, bf16[4,256,1024]{2,1,0:T(8,128)(2,1)S(1)} %copy-done.2), custom_call_target="tpu_custom_call" | custom-call | flops 2147483648 | tf_op jit(solution)/shard_map/pallas_call | solution.py:55
  14.7 0.4 collective-permute-done
  15.3 1.6 %collective-permute-start.1 = (bf16[2,128,512]{2,1,0:T(8,128)(2,1)S(1)}, bf16[2,128,512]{2,1,0:T(8,128)(2,1)S(1)}, u32[]{:S(2)}, u32[]{:S(2)}) collective-permute-start(bf16[2,128,512]{2,1,0:T(8,128)(2,1)S(1)} %pad_maximum_fusion.refs_0_), channel_id=1, source_target_pairs={{0,4},{4,0},{8,12},{12,8},{16,20},{20,16},{24,28},{28,24},{1,5},{5... | collective-permute-start | bytes 786440 | tf_op jit(solution)/shard_map/ppermute | solution.py:374
  16.8 2.5 %shard_map.89 = (f32[4,256,128]{2,1,0:T(8,128)S(1)}, f32[4,8,256]{2,1,0:T(8,128)S(1)}) custom-call(s32[7]{0:T(128)S(1)} %pad_add_fusion.2.info, s32[2,4,2,256]{3,2,1,0:T(2,128)S(1)} %pad_add_fusion.meta, s32[4,16,32]{2,1,0:T(8,128)S(1)} %copy-done.3), custom_call_target="tpu_custom_call" | custom-call | flops 2147483648 | tf_op jit(solution)/shard_map/pallas_call | solution.py:55
  19.4 3.5 %collective-permute-done.2 = bf16[128,512]{1,0:T(8,128)(2,1)S(1)} collective-permute-done((bf16[128,512]{1,0:T(8,128)(2,1)S(1)}, bf16[128,512]{1,0:T(8,128)(2,1)S(1)}, u32[]{:S(2)}, u32[]{:S(2)}) %collective-permute-start.2) | collective-permute-done | bytes 131104 | tf_op jit(solution)/shard_map/ppermute | solution.py:374
  22.9 1.0 %collective-permute-done.1.refs_1_ = bf16[2,128,512]{2,1,0:T(8,128)(2,1)S(1)} collective-permute-done((bf16[2,128,512]{2,1,0:T(8,128)(2,1)S(1)}, bf16[2,128,512]{2,1,0:T(8,128)(2,1)S(1)}, u32[]{:S(2)}, u32[]{:S(2)}) %collective-permute-start.1) | collective-permute-done | bytes 262176 | tf_op jit(solution)/shard_map/ppermute | solution.py:374
  23.9 0.5 collective-permute-start.7
  24.4 1.5 %collective-permute-start.5 = (bf16[1,128,512]{2,1,0:T(8,128)(2,1)S(1)}, bf16[1,128,512]{2,1,0:T(8,128)(2,1)S(1)}, u32[]{:S(2)}, u32[]{:S(2)}) collective-permute-start(bf16[1,128,512]{2,1,0:T(8,128)(2,1)S(1)} %bitcast.93), channel_id=1, source_target_pairs={{0,4},{4,0},{8,12},{12,8},{16,20},{20,16},{24,28},{28,24},{1,5},{5... | collective-permute-start | bytes 393224 | tf_op jit(solution)/shard_map/ppermute | solution.py:374
  25.9 1.4 %collective-permute-start.8 = (bf16[1,128,512]{2,1,0:T(8,128)(2,1)S(1)}, bf16[1,128,512]{2,1,0:T(8,128)(2,1)S(1)}, u32[]{:S(2)}, u32[]{:S(2)}) collective-permute-start(bf16[1,128,512]{2,1,0:T(8,128)(2,1)S(1)} %bitcast.96), channel_id=1, source_target_pairs={{0,4},{4,0},{8,12},{12,8},{16,20},{20,16},{24,28},{28,24},{1,5},{5... | collective-permute-start | bytes 393224 | tf_op jit(solution)/shard_map/ppermute | solution.py:374
  27.3 4.0 %shard_map.90.refs_8_ = bf16[4,1024,512]{2,1,0:T(8,128)(2,1)S(1)} custom-call(s32[7]{0:T(128)S(1)} %pad_add_fusion.2.info, bf16[4,512,1024]{2,1,0:T(8,128)(2,1)S(1)} %copy-done, bf16[2,128,512]{2,1,0:T(8,128)(2,1)S(1)} %pad_maximum_fusion.refs_0_, bf16[2,128,512]{2,1,0:T(8,128)(2,1)S(1)} %collective-permute-done.1.refs_1_, ...), custom_call_target="tpu_custom_call" | custom-call | flops 2147483648 | tf_op jit(solution)/shard_map/pallas_call | solution.py:37
  31.3 1.3 %collective-permute-done.8.refs_3_ = bf16[1,128,512]{2,1,0:T(8,128)(2,1)S(1)} collective-permute-done((bf16[1,128,512]{2,1,0:T(8,128)(2,1)S(1)}, bf16[1,128,512]{2,1,0:T(8,128)(2,1)S(1)}, u32[]{:S(2)}, u32[]{:S(2)}) %collective-permute-start.8) | collective-permute-done | bytes 131104 | tf_op jit(solution)/shard_map/ppermute | solution.py:374
  32.6 0.5 collective-permute-start.10
  33.1 0.8 collective-permute-done.9.refs_4_
  34.2 0.3 collective-permute-start.16
  34.5 0.8 collective-permute-done.12.refs_7_
  35.3 3.8 %shard_map.91.weight = bf16[4,1024,512]{2,1,0:T(8,128)(2,1)S(1)} custom-call(s32[7]{0:T(128)S(1)} %pad_add_fusion.2.info, bf16[4,512,1024]{2,1,0:T(8,128)(2,1)S(1)} %copy-done, bf16[1,128,512]{2,1,0:T(8,128)(2,1)S(1)} %bitcast.95, bf16[1,128,512]{2,1,0:T(8,128)(2,1)S(1)} %collective-permute-done.5.refs_1_, bf16[1,128,512]{2,1,0:T(8,128)(2,1)S(1)} %bitcast.98, ...), custom_call_target="tpu_custom_call" | custom-call | tf_op jit(solution)/shard_map/pallas_call | solution.py:37
  39.1 3.1 %shard_map.92 = (f32[2,2,256]{2,1,0:T(2,128)S(1)}, bf16[1024,512]{1,0:T(8,128)(2,1)S(1)}, bf16[512,1024]{1,0:T(8,128)(2,1)S(1)}) custom-call(s32[7]{0:T(128)S(1)} %pad_add_fusion.2.info, f32[4,256,128]{2,1,0:T(8,128)S(1)} %get-tuple-element.79.table, f32[4,8,256]{2,1,0:T(8,128)S(1)} %get-tuple-element.80.rank, bf16[4,1024,512]{2,1,0:T(8,128)(2,1)S(1)} %shard_map.91.weight, ...), custom_call_target="tpu_custom_call" | custom-call | tf_op jit(solution)/shard_map/pallas_call | solution.py:37
  42.2 0.6 collective-permute-done.16.meta
  42.8 1.7 %collective-permute-start.18 = (bf16[1,1,128,1024]{3,2,1,0:T(8,128)(2,1)S(1)}, bf16[1,1,128,1024]{3,2,1,0:T(8,128)(2,1)S(1)}, u32[]{:S(2)}, u32[]{:S(2)}) collective-permute-start(bf16[1,1,128,1024]{3,2,1,0:T(8,128)(2,1)S(1)} %get-tuple-element.110), channel_id=1, source_target_pairs={{0,2},{1,3},{2,0},{3,1},{4,6},{5,7},{6,4},{7,5},{8,10},{9,11},{10,... | collective-permute-start | bytes 786440 | tf_op jit(solution)/shard_map/ppermute | solution.py:374
  44.6 3.1 %shard_map.93 = (f32[2,2,256]{2,1,0:T(2,128)S(1)}, bf16[1024,512]{1,0:T(8,128)(2,1)S(1)}, bf16[512,1024]{1,0:T(8,128)(2,1)S(1)}) custom-call(s32[7]{0:T(128)S(1)} %pad_add_fusion.2.info, f32[4,256,128]{2,1,0:T(8,128)S(1)} %get-tuple-element.79.table, f32[4,8,256]{2,1,0:T(8,128)S(1)} %get-tuple-element.80.rank, bf16[4,1024,512]{2,1,0:T(8,128)(2,1)S(1)} %shard_map.91.weight, ...), custom_call_target="tpu_custom_call" | custom-call | tf_op jit(solution)/shard_map/pallas_call | solution.py:37
  47.7 0.3 collective-permute-start.14
  48.1 2.5 %shard_map.94 = (f32[4,256,128]{2,1,0:T(8,128)S(1)}, f32[4,8,256]{2,1,0:T(8,128)S(1)}) custom-call(s32[7]{0:T(128)S(1)} %pad_add_fusion.2.info, s32[2,4,2,256]{3,2,1,0:T(2,128)S(1)} %collective-permute-done.16.meta, s32[4,16,32]{2,1,0:T(8,128)S(1)} %copy-done.3), custom_call_target="tpu_custom_call" | custom-call | tf_op jit(solution)/shard_map/pallas_call | solution.py:55
  50.6 2.0 %shard_map.96.refs_4_ = f32[2,1024,256]{2,1,0:T(8,128)S(1)} custom-call(s32[7]{0:T(128)S(1)} %pad_add_fusion.2.info, bf16[1024,512]{1,0:T(8,128)(2,1)S(1)} %get-tuple-element.114.refs_0_, bf16[512,1024]{1,0:T(8,128)(2,1)S(1)} %get-tuple-element.115.refs_1_, bf16[1024,512]{1,0:T(8,128)(2,1)S(1)} %get-tuple-element.116.refs_2_, ...), custom_call_target="tpu_custom_call" | custom-call | tf_op jit(solution)/shard_map/pallas_call | solution.py:55
  52.6 4.2 %shard_map.95 = (f32[3,2,256]{2,1,0:T(2,128)S(1)}, bf16[1024,768]{1,0:T(8,128)(2,1)S(1)}, bf16[768,1024]{1,0:T(8,128)(2,1)S(1)}) custom-call(s32[7]{0:T(128)S(1)} %pad_add_fusion.2.info, f32[4,256,128]{2,1,0:T(8,128)S(1)} %get-tuple-element.106.table, f32[4,8,256]{2,1,0:T(8,128)S(1)} %get-tuple-element.107.rank, bf16[4,1024,512]{2,1,0:T(8,128)(2,1)S(1)} %shard_map.91.weight, ...), custom_call_target="tpu_custom_call" | custom-call | tf_op jit(solution)/shard_map/pallas_call | solution.py:37
  56.8 1.7 %shard_map.97 = (f32[1,2,256]{2,1,0:T(2,128)S(1)}, bf16[1024,256]{1,0:T(8,128)(2,1)S(1)}, bf16[256,1024]{1,0:T(8,128)(2,1)S(1)}) custom-call(s32[7]{0:T(128)S(1)} %pad_add_fusion.2.info, f32[4,256,128]{2,1,0:T(8,128)S(1)} %get-tuple-element.106.table, f32[4,8,256]{2,1,0:T(8,128)S(1)} %get-tuple-element.107.rank, bf16[4,1024,512]{2,1,0:T(8,128)(2,1)S(1)} %shard_map.91.weight, ...), custom_call_target="tpu_custom_call" | custom-call | tf_op jit(solution)/shard_map/pallas_call | solution.py:37
  58.6 2.0 %shard_map.99 = bf16[2,1024,256]{2,1,0:T(8,128)(2,1)S(1)} custom-call(s32[7]{0:T(128)S(1)} %pad_add_fusion.2.info, bf16[1024,768]{1,0:T(8,128)(2,1)S(1)} %get-tuple-element.121.refs_4_.refs_0_, bf16[768,1024]{1,0:T(8,128)(2,1)S(1)} %get-tuple-element.122.refs_5_.refs_1_, bf16[1024,256]{1,0:T(8,128)(2,1)S(1)} %get-tuple-element.123.refs_6_.refs_2_, ...), custom_call_target="tpu_custom_call" | custom-call | tf_op jit(solution)/shard_map/pallas_call | solution.py:55
  60.6 0.3 collective-permute-start.22
  60.9 3.1 %shard_map.98 = f32[2,1024,256]{2,1,0:T(8,128)S(1)} custom-call(s32[7]{0:T(128)S(1)} %pad_add_fusion.2.info, bf16[1024,512]{1,0:T(8,128)(2,1)S(1)} %get-tuple-element.114.refs_0_, bf16[512,1024]{1,0:T(8,128)(2,1)S(1)} %get-tuple-element.115.refs_1_, bf16[1024,512]{1,0:T(8,128)(2,1)S(1)} %get-tuple-element.116.refs_2_, ...), custom_call_target="tpu_custom_call" | custom-call | flops 34359738368 | tf_op jit(solution)/shard_map/pallas_call | solution.py:55
  64.2 1.8 %collective-permute-start.25 = (bf16[4,128,256]{2,1,0:T(8,128)(2,1)S(1)}, bf16[4,128,256]{2,1,0:T(8,128)(2,1)S(1)}, u32[]{:S(2)}, u32[]{:S(2)}) collective-permute-start(bf16[4,128,256]{2,1,0:T(8,128)(2,1)S(1)} %get-tuple-element.136), channel_id=1, source_target_pairs={{0,2},{1,3},{2,0},{3,1},{4,6},{5,7},{6,4},{7,5},{8,10},{9,11},{10,... | collective-permute-start | bytes 786440 | tf_op jit(solution)/shard_map/ppermute | solution.py:380
  66.0 1.4 %collective-permute-start.24 = (bf16[4,128,256]{2,1,0:T(8,128)(2,1)S(1)}, bf16[4,128,256]{2,1,0:T(8,128)(2,1)S(1)}, u32[]{:S(2)}, u32[]{:S(2)}) collective-permute-start(bf16[4,128,256]{2,1,0:T(8,128)(2,1)S(1)} %get-tuple-element.135), channel_id=1, source_target_pairs={{0,6},{1,7},{2,4},{3,5},{4,2},{5,3},{6,0},{7,1},{8,14},{9,15},{10,... | collective-permute-start | bytes 786440 | tf_op jit(solution)/shard_map/ppermute | solution.py:380
  67.4 0.3 collective-permute-start.23
  67.8 0.8 collective-permute-start.21
  68.6 9.8 %collective-permute-done.25 = bf16[4,128,256]{2,1,0:T(8,128)(2,1)S(1)} collective-permute-done((bf16[4,128,256]{2,1,0:T(8,128)(2,1)S(1)}, bf16[4,128,256]{2,1,0:T(8,128)(2,1)S(1)}, u32[]{:S(2)}, u32[]{:S(2)}) %collective-permute-start.25) | collective-permute-done | bytes 262176 | tf_op jit(solution)/shard_map/ppermute | solution.py:380
  78.4 1.7 %collective-permute-start.20 = (f32[4,256]{1,0:T(4,128)S(1)}, f32[4,256]{1,0:T(4,128)S(1)}, u32[]{:S(2)}, u32[]{:S(2)}) collective-permute-start(f32[4,256]{1,0:T(4,128)S(1)} %bitcast.108), channel_id=1, source_target_pairs={{0,2},{1,3},{2,0},{3,1},{4,6},{5,7},{6,4},{7,5},{8,10},{9,11},{10,... | collective-permute-start | bytes 12296 | tf_op jit(solution)/shard_map/ppermute | solution.py:374
  80.4 3.7 %collective-permute-start.28 = (bf16[128,256]{1,0:T(8,128)(2,1)S(1)}, bf16[128,256]{1,0:T(8,128)(2,1)S(1)}, u32[]{:S(2)}, u32[]{:S(2)}) collective-permute-start(bf16[128,256]{1,0:T(8,128)(2,1)S(1)} %get-tuple-element.138), channel_id=1, source_target_pairs={{0,24},{4,28},{8,16},{12,20},{16,8},{20,12},{24,0},{28,4},{1,25},{... | collective-permute-start | bytes 196616 | tf_op jit(solution)/shard_map/ppermute | solution.py:374
  84.1 0.8 collective-permute-start.26
  84.9 0.6 fusion.19
  85.5 1.5 %collective-permute-done.28 = bf16[128,256]{1,0:T(8,128)(2,1)S(1)} collective-permute-done((bf16[128,256]{1,0:T(8,128)(2,1)S(1)}, bf16[128,256]{1,0:T(8,128)(2,1)S(1)}, u32[]{:S(2)}, u32[]{:S(2)}) %collective-permute-start.28) | collective-permute-done | bytes 65568 | tf_op jit(solution)/shard_map/ppermute | solution.py:374
  86.9 2.4 %collective-permute-done.27 = bf16[128,256]{1,0:T(8,128)(2,1)S(1)} collective-permute-done((bf16[128,256]{1,0:T(8,128)(2,1)S(1)}, bf16[128,256]{1,0:T(8,128)(2,1)S(1)}, u32[]{:S(2)}, u32[]{:S(2)}) %collective-permute-start.27) | collective-permute-done | bytes 65568 | tf_op jit(solution)/shard_map/ppermute | solution.py:374
  89.4 0.7 fusion.11
  (56 shorter events, 1.4 us)
Async XLA Ops:
  1.4 1.6 %copy-start.1 = (bf16[4,256,1024]{2,1,0:T(8,128)(2,1)S(1)}, bf16[4,256,1024]{2,1,0:T(8,128)(2,1)}, u32[]{:S(2)}) copy-start(bf16[4,256,1024]{2,1,0:T(8,128)(2,1)} %words.3) | copy-start | bytes 6291460
  3.0 0.7 copy-start.4
  3.7 4.3 %copy-start.5 = (bf16[128,1024]{1,0:T(8,128)(2,1)S(1)}, bf16[128,1024]{1,0:T(8,128)(2,1)}, u32[]{:S(2)}) copy-start(bf16[128,1024]{1,0:T(8,128)(2,1)} %proj) | copy-start | bytes 786436
  4.9 8.1 %copy-start.6 = (s32[4,256]{1,0:T(4,128)S(1)}, s32[4,256]{1,0:T(4,128)}, u32[]{:S(2)}) copy-start(s32[4,256]{1,0:T(4,128)} %param.11) | copy-start | bytes 12292
  5.0 8.2 %copy-start.2 = (bf16[4,256,1024]{2,1,0:T(8,128)(2,1)S(1)}, bf16[4,256,1024]{2,1,0:T(8,128)(2,1)}, u32[]{:S(2)}) copy-start(bf16[4,256,1024]{2,1,0:T(8,128)(2,1)} %words.3) | copy-start | bytes 6291460
  5.0 37.8 %collective-permute-start.15 = (bf16[2,3,128,1024]{3,2,1,0:T(8,128)(2,1)S(1)}, bf16[2,3,128,1024]{3,2,1,0:T(8,128)(2,1)S(1)}, u32[]{:S(2)}, u32[]{:S(2)}) collective-permute-start(bf16[2,3,128,1024]{3,2,1,0:T(8,128)(2,1)S(1)} %shard_map.86), channel_id=1, source_target_pairs={{0,2},{1,3},{2,0},{3,1},{4,6},{5,7},{6,4},{7,5},{8,10},{9,11},{10,... | collective-permute-start | bytes 4718600 | tf_op jit(solution)/shard_map/ppermute | solution.py:374
  8.6 6.5 %collective-permute-start = (bf16[128,512]{1,0:T(8,128)(2,1)S(1)}, bf16[128,512]{1,0:T(8,128)(2,1)S(1)}, u32[]{:S(2)}, u32[]{:S(2)}) collective-permute-start(bf16[128,512]{1,0:T(8,128)(2,1)S(1)} %shard_map.87), channel_id=1, source_target_pairs={{0,8},{4,12},{8,0},{12,4},{16,24},{20,28},{24,16},{28,20},{1,9},{5... | collective-permute-start | bytes 393224 | tf_op jit(solution)/shard_map/ppermute | solution.py:374
  10.2 12.6 %collective-permute-start.2 = (bf16[128,512]{1,0:T(8,128)(2,1)S(1)}, bf16[128,512]{1,0:T(8,128)(2,1)S(1)}, u32[]{:S(2)}, u32[]{:S(2)}) collective-permute-start(bf16[128,512]{1,0:T(8,128)(2,1)S(1)} %shard_map.87), channel_id=1, source_target_pairs={{0,16},{4,20},{8,24},{12,28},{16,0},{20,4},{24,8},{28,12},{1,17},{... | collective-permute-start | bytes 393224 | tf_op jit(solution)/shard_map/ppermute | solution.py:374
  12.8 10.1 %collective-permute-start.3 = (bf16[128,512]{1,0:T(8,128)(2,1)S(1)}, bf16[128,512]{1,0:T(8,128)(2,1)S(1)}, u32[]{:S(2)}, u32[]{:S(2)}) collective-permute-start(bf16[128,512]{1,0:T(8,128)(2,1)S(1)} %shard_map.87), channel_id=1, source_target_pairs={{0,24},{4,28},{8,16},{12,20},{16,8},{20,12},{24,0},{28,4},{1,25},{... | collective-permute-start | bytes 393224 | tf_op jit(solution)/shard_map/ppermute | solution.py:374
  13.0 3.8 %copy-start.3 = (s32[4,16,32]{2,1,0:T(8,128)S(1)}, s32[4,16,32]{2,1,0:T(8,128)}, u32[]{:S(2)}) copy-start(s32[4,16,32]{2,1,0:T(8,128)} %flags.3) | copy-start | bytes 24580
  13.1 2.2 %collective-permute-start.4 = (s32[4,2,256]{2,1,0:T(2,128)S(1)}, s32[4,2,256]{2,1,0:T(2,128)S(1)}, u32[]{:S(2)}, u32[]{:S(2)}) collective-permute-start(s32[4,2,256]{2,1,0:T(2,128)S(1)} %get-tuple-element.143), channel_id=1, source_target_pairs={{0,1},{1,0},{2,3},{3,2},{4,5},{5,4},{6,7},{7,6},{8,9},{9,8},{10,11... | collective-permute-start | bytes 24584 | tf_op jit(solution)/shard_map/ppermute | solution.py:374
  15.1 24.1 %collective-permute-start.13 = (bf16[1,4,128,1024]{3,2,1,0:T(8,128)(2,1)S(1)}, bf16[1,4,128,1024]{3,2,1,0:T(8,128)(2,1)S(1)}, u32[]{:S(2)}, u32[]{:S(2)}) collective-permute-start(bf16[1,4,128,1024]{3,2,1,0:T(8,128)(2,1)S(1)} %get-tuple-element.96), channel_id=1, source_target_pairs={{0,1},{1,0},{2,3},{3,2},{4,5},{5,4},{6,7},{7,6},{8,9},{9,8},{10,11... | collective-permute-start | bytes 3145736 | tf_op jit(solution)/shard_map/ppermute | solution.py:374
  15.3 8.6 %collective-permute-start.1 = (bf16[2,128,512]{2,1,0:T(8,128)(2,1)S(1)}, bf16[2,128,512]{2,1,0:T(8,128)(2,1)S(1)}, u32[]{:S(2)}, u32[]{:S(2)}) collective-permute-start(bf16[2,128,512]{2,1,0:T(8,128)(2,1)S(1)} %pad_maximum_fusion.refs_0_), channel_id=1, source_target_pairs={{0,4},{4,0},{8,12},{12,8},{16,20},{20,16},{24,28},{28,24},{1,5},{5... | collective-permute-start | bytes 786440 | tf_op jit(solution)/shard_map/ppermute | solution.py:374
  16.8 10.5 %copy-start = (bf16[4,512,1024]{2,1,0:T(8,128)(2,1)S(1)}, bf16[4,512,1024]{2,1,0:T(8,128)(2,1)}, u32[]{:S(2)}) copy-start(bf16[4,512,1024]{2,1,0:T(8,128)(2,1)} %patches.11) | copy-start | bytes 12582916
  23.9 2.0 %collective-permute-start.6 = (bf16[2,128,512]{2,1,0:T(8,128)(2,1)S(1)}, bf16[2,128,512]{2,1,0:T(8,128)(2,1)S(1)}, u32[]{:S(2)}, u32[]{:S(2)}) collective-permute-start(bf16[2,128,512]{2,1,0:T(8,128)(2,1)S(1)} %pad_maximum_fusion.refs_0_), channel_id=1, source_target_pairs={{0,1},{1,0},{2,3},{3,2},{4,5},{5,4},{6,7},{7,6},{8,9},{9,8},{10,11... | collective-permute-start | bytes 786440 | tf_op jit(solution)/shard_map/ppermute | solution.py:374
  23.9 2.0 %collective-permute-start.7 = (bf16[2,128,512]{2,1,0:T(8,128)(2,1)S(1)}, bf16[2,128,512]{2,1,0:T(8,128)(2,1)S(1)}, u32[]{:S(2)}, u32[]{:S(2)}) collective-permute-start(bf16[2,128,512]{2,1,0:T(8,128)(2,1)S(1)} %collective-permute-done.1.refs_1_), channel_id=1, source_target_pairs={{0,1},{1,0},{2,3},{3,2},{4,5},{5,4},{6,7},{7,6},{8,9},{9,8},{10,11... | collective-permute-start | bytes 786440 | tf_op jit(solution)/shard_map/ppermute | solution.py:374
  24.4 6.9 %collective-permute-start.5 = (bf16[1,128,512]{2,1,0:T(8,128)(2,1)S(1)}, bf16[1,128,512]{2,1,0:T(8,128)(2,1)S(1)}, u32[]{:S(2)}, u32[]{:S(2)}) collective-permute-start(bf16[1,128,512]{2,1,0:T(8,128)(2,1)S(1)} %bitcast.93), channel_id=1, source_target_pairs={{0,4},{4,0},{8,12},{12,8},{16,20},{20,16},{24,28},{28,24},{1,5},{5... | collective-permute-start | bytes 393224 | tf_op jit(solution)/shard_map/ppermute | solution.py:374
  25.9 6.7 %collective-permute-start.8 = (bf16[1,128,512]{2,1,0:T(8,128)(2,1)S(1)}, bf16[1,128,512]{2,1,0:T(8,128)(2,1)S(1)}, u32[]{:S(2)}, u32[]{:S(2)}) collective-permute-start(bf16[1,128,512]{2,1,0:T(8,128)(2,1)S(1)} %bitcast.96), channel_id=1, source_target_pairs={{0,4},{4,0},{8,12},{12,8},{16,20},{20,16},{24,28},{28,24},{1,5},{5... | collective-permute-start | bytes 393224 | tf_op jit(solution)/shard_map/ppermute | solution.py:374
  32.6 1.3 %collective-permute-start.9 = (bf16[1,128,512]{2,1,0:T(8,128)(2,1)S(1)}, bf16[1,128,512]{2,1,0:T(8,128)(2,1)S(1)}, u32[]{:S(2)}, u32[]{:S(2)}) collective-permute-start(bf16[1,128,512]{2,1,0:T(8,128)(2,1)S(1)} %bitcast.94), channel_id=1, source_target_pairs={{0,1},{1,0},{2,3},{3,2},{4,5},{5,4},{6,7},{7,6},{8,9},{9,8},{10,11... | collective-permute-start | bytes 393224 | tf_op jit(solution)/shard_map/ppermute | solution.py:374
  32.6 1.5 %collective-permute-start.10 = (bf16[1,128,512]{2,1,0:T(8,128)(2,1)S(1)}, bf16[1,128,512]{2,1,0:T(8,128)(2,1)S(1)}, u32[]{:S(2)}, u32[]{:S(2)}) collective-permute-start(bf16[1,128,512]{2,1,0:T(8,128)(2,1)S(1)} %collective-permute-done.5.refs_1_), channel_id=1, source_target_pairs={{0,1},{1,0},{2,3},{3,2},{4,5},{5,4},{6,7},{7,6},{8,9},{9,8},{10,11... | collective-permute-start | bytes 393224 | tf_op jit(solution)/shard_map/ppermute | solution.py:374
  33.1 1.3 %collective-permute-start.11 = (bf16[1,128,512]{2,1,0:T(8,128)(2,1)S(1)}, bf16[1,128,512]{2,1,0:T(8,128)(2,1)S(1)}, u32[]{:S(2)}, u32[]{:S(2)}) collective-permute-start(bf16[1,128,512]{2,1,0:T(8,128)(2,1)S(1)} %bitcast.97), channel_id=1, source_target_pairs={{0,1},{1,0},{2,3},{3,2},{4,5},{5,4},{6,7},{7,6},{8,9},{9,8},{10,11... | collective-permute-start | bytes 393224 | tf_op jit(solution)/shard_map/ppermute | solution.py:374
  34.0 1.3 %collective-permute-start.12 = (bf16[1,128,512]{2,1,0:T(8,128)(2,1)S(1)}, bf16[1,128,512]{2,1,0:T(8,128)(2,1)S(1)}, u32[]{:S(2)}, u32[]{:S(2)}) collective-permute-start(bf16[1,128,512]{2,1,0:T(8,128)(2,1)S(1)} %collective-permute-done.8.refs_3_), channel_id=1, source_target_pairs={{0,1},{1,0},{2,3},{3,2},{4,5},{5,4},{6,7},{7,6},{8,9},{9,8},{10,11... | collective-permute-start | bytes 393224 | tf_op jit(solution)/shard_map/ppermute | solution.py:374
  34.2 8.6 %collective-permute-start.16 = (s32[2,4,2,256]{3,2,1,0:T(2,128)S(1)}, s32[2,4,2,256]{3,2,1,0:T(2,128)S(1)}, u32[]{:S(2)}, u32[]{:S(2)}) collective-permute-start(s32[2,4,2,256]{3,2,1,0:T(2,128)S(1)} %pad_add_fusion.meta), channel_id=1, source_target_pairs={{0,2},{1,3},{2,0},{3,1},{4,6},{5,7},{6,4},{7,5},{8,10},{9,11},{10,... | collective-permute-start | bytes 49160 | tf_op jit(solution)/shard_map/ppermute | solution.py:374
  42.8 9.8 %collective-permute-start.17 = (bf16[2,3,128,1024]{3,2,1,0:T(8,128)(2,1)S(1)}, bf16[2,3,128,1024]{3,2,1,0:T(8,128)(2,1)S(1)}, u32[]{:S(2)}, u32[]{:S(2)}) collective-permute-start(bf16[2,3,128,1024]{3,2,1,0:T(8,128)(2,1)S(1)} %collective-permute-done.15.refs_0_), channel_id=1, source_target_pairs={{0,1},{1,0},{2,3},{3,2},{4,5},{5,4},{6,7},{7,6},{8,9},{9,8},{10,11... | collective-permute-start | bytes 4718600 | tf_op jit(solution)/shard_map/ppermute | solution.py:374
  42.8 14.1 %collective-permute-start.18 = (bf16[1,1,128,1024]{3,2,1,0:T(8,128)(2,1)S(1)}, bf16[1,1,128,1024]{3,2,1,0:T(8,128)(2,1)S(1)}, u32[]{:S(2)}, u32[]{:S(2)}) collective-permute-start(bf16[1,1,128,1024]{3,2,1,0:T(8,128)(2,1)S(1)} %get-tuple-element.110), channel_id=1, source_target_pairs={{0,2},{1,3},{2,0},{3,1},{4,6},{5,7},{6,4},{7,5},{8,10},{9,11},{10,... | collective-permute-start | bytes 786440 | tf_op jit(solution)/shard_map/ppermute | solution.py:374
  44.5 12.3 %collective-permute-start.19 = (bf16[1,1,128,1024]{3,2,1,0:T(8,128)(2,1)S(1)}, bf16[1,1,128,1024]{3,2,1,0:T(8,128)(2,1)S(1)}, u32[]{:S(2)}, u32[]{:S(2)}) collective-permute-start(bf16[1,1,128,1024]{3,2,1,0:T(8,128)(2,1)S(1)} %get-tuple-element.111), channel_id=1, source_target_pairs={{0,3},{1,2},{2,1},{3,0},{4,7},{5,6},{6,5},{7,4},{8,11},{9,10},{10,... | collective-permute-start | bytes 786440 | tf_op jit(solution)/shard_map/ppermute | solution.py:374
  47.7 36.3 %collective-permute-start.14 = (f32[4,256]{1,0:T(4,128)S(1)}, f32[4,256]{1,0:T(4,128)S(1)}, u32[]{:S(2)}, u32[]{:S(2)}) collective-permute-start(f32[4,256]{1,0:T(4,128)S(1)} %fusion.20), channel_id=1, source_target_pairs={{0,1},{1,0},{2,3},{3,2},{4,5},{5,4},{6,7},{7,6},{8,9},{9,8},{10,11... | collective-permute-start | bytes 12296 | tf_op jit(solution)/shard_map/ppermute | solution.py:374
  60.6 3.4 %collective-permute-start.22 = (bf16[2,1024,256]{2,1,0:T(8,128)(2,1)S(1)}, bf16[2,1024,256]{2,1,0:T(8,128)(2,1)S(1)}, u32[]{:S(2)}, u32[]{:S(2)}) collective-permute-start(bf16[2,1024,256]{2,1,0:T(8,128)(2,1)S(1)} %shard_map.99), channel_id=1, source_target_pairs={{0,1},{1,0},{2,3},{3,2},{4,5},{5,4},{6,7},{7,6},{8,9},{9,8},{10,11... | collective-permute-start | bytes 3145736 | tf_op jit(solution)/shard_map/ppermute | solution.py:374
  64.2 14.2 %collective-permute-start.25 = (bf16[4,128,256]{2,1,0:T(8,128)(2,1)S(1)}, bf16[4,128,256]{2,1,0:T(8,128)(2,1)S(1)}, u32[]{:S(2)}, u32[]{:S(2)}) collective-permute-start(bf16[4,128,256]{2,1,0:T(8,128)(2,1)S(1)} %get-tuple-element.136), channel_id=1, source_target_pairs={{0,2},{1,3},{2,0},{3,1},{4,6},{5,7},{6,4},{7,5},{8,10},{9,11},{10,... | collective-permute-start | bytes 786440 | tf_op jit(solution)/shard_map/ppermute | solution.py:380
  66.0 14.2 %collective-permute-start.24 = (bf16[4,128,256]{2,1,0:T(8,128)(2,1)S(1)}, bf16[4,128,256]{2,1,0:T(8,128)(2,1)S(1)}, u32[]{:S(2)}, u32[]{:S(2)}) collective-permute-start(bf16[4,128,256]{2,1,0:T(8,128)(2,1)S(1)} %get-tuple-element.135), channel_id=1, source_target_pairs={{0,6},{1,7},{2,4},{3,5},{4,2},{5,3},{6,0},{7,1},{8,14},{9,15},{10,... | collective-permute-start | bytes 786440 | tf_op jit(solution)/shard_map/ppermute | solution.py:380
  67.4 12.7 %collective-permute-start.23 = (bf16[4,128,256]{2,1,0:T(8,128)(2,1)S(1)}, bf16[4,128,256]{2,1,0:T(8,128)(2,1)S(1)}, u32[]{:S(2)}, u32[]{:S(2)}) collective-permute-start(bf16[4,128,256]{2,1,0:T(8,128)(2,1)S(1)} %get-tuple-element.134), channel_id=1, source_target_pairs={{0,4},{1,5},{2,6},{3,7},{4,0},{5,1},{6,2},{7,3},{8,12},{9,13},{10,... | collective-permute-start | bytes 786440 | tf_op jit(solution)/shard_map/ppermute | solution.py:380
  67.8 17.0 %collective-permute-start.21 = (f32[4,256]{1,0:T(4,128)S(1)}, f32[4,256]{1,0:T(4,128)S(1)}, u32[]{:S(2)}, u32[]{:S(2)}) collective-permute-start(f32[4,256]{1,0:T(4,128)S(1)} %bitcast.107), channel_id=1, source_target_pairs={{0,3},{1,2},{2,1},{3,0},{4,7},{5,6},{6,5},{7,4},{8,11},{9,10},{10,... | collective-permute-start | bytes 12296 | tf_op jit(solution)/shard_map/ppermute | solution.py:374
  78.4 6.4 %collective-permute-start.20 = (f32[4,256]{1,0:T(4,128)S(1)}, f32[4,256]{1,0:T(4,128)S(1)}, u32[]{:S(2)}, u32[]{:S(2)}) collective-permute-start(f32[4,256]{1,0:T(4,128)S(1)} %bitcast.108), channel_id=1, source_target_pairs={{0,2},{1,3},{2,0},{3,1},{4,6},{5,7},{6,4},{7,5},{8,10},{9,11},{10,... | collective-permute-start | bytes 12296 | tf_op jit(solution)/shard_map/ppermute | solution.py:374
  80.4 6.5 %collective-permute-start.28 = (bf16[128,256]{1,0:T(8,128)(2,1)S(1)}, bf16[128,256]{1,0:T(8,128)(2,1)S(1)}, u32[]{:S(2)}, u32[]{:S(2)}) collective-permute-start(bf16[128,256]{1,0:T(8,128)(2,1)S(1)} %get-tuple-element.138), channel_id=1, source_target_pairs={{0,24},{4,28},{8,16},{12,20},{16,8},{20,12},{24,0},{28,4},{1,25},{... | collective-permute-start | bytes 196616 | tf_op jit(solution)/shard_map/ppermute | solution.py:374
  84.1 5.3 %collective-permute-start.27 = (bf16[128,256]{1,0:T(8,128)(2,1)S(1)}, bf16[128,256]{1,0:T(8,128)(2,1)S(1)}, u32[]{:S(2)}, u32[]{:S(2)}) collective-permute-start(bf16[128,256]{1,0:T(8,128)(2,1)S(1)} %get-tuple-element.139), channel_id=1, source_target_pairs={{0,16},{4,20},{8,24},{12,28},{16,0},{20,4},{24,8},{28,12},{1,17},{... | collective-permute-start | bytes 196616 | tf_op jit(solution)/shard_map/ppermute | solution.py:374
  84.1 5.3 %collective-permute-start.26 = (bf16[128,256]{1,0:T(8,128)(2,1)S(1)}, bf16[128,256]{1,0:T(8,128)(2,1)S(1)}, u32[]{:S(2)}, u32[]{:S(2)}) collective-permute-start(bf16[128,256]{1,0:T(8,128)(2,1)S(1)} %get-tuple-element.137), channel_id=1, source_target_pairs={{0,8},{4,12},{8,0},{12,4},{16,24},{20,28},{24,16},{28,20},{1,9},{5... | collective-permute-start | bytes 196616 | tf_op jit(solution)/shard_map/ppermute | solution.py:374
